TPU v7x, 32 devices: a whole 2x2x4 slice. The times are simulated.
32 devices in a mesh: dp: 8 (over z, x), tensor: 4 (over y, core).
Axes of the slice: x: 2, y: 2, z: 4, core: 2. Of those that a mesh axis runs over, the one named last changes fastest.
Arguments:
- codes_in: int32 [16, 1024, 4], P('dp', 'tensor'), may hold values from 0 to 2047, as said below
- codes_out: int32 [16, 1024, 4], P('dp', 'tensor'), may hold values from 0 to 2047, as said below
- pad_mask: int32 [16, 1024, 4], P('dp', 'tensor'), may hold values from 0 to 1, as said below
- text_table: bfloat16 [256, 1024], replicated, may hold values from -6 to 6
- text_index: int32 [16, 64], P('dp'), may hold values from 0 to 255
- attend_in: float32 [1024, 6, 1024], P('dp', None, 'tensor'), may hold values from -0.1875 to 0.1875
- attend_out: float32 [2, 1024, 1024], P(None, 'tensor', 'dp'), may hold values from -0.75 to 0.75
- expand_weights: float32 [1024, 4096], P('dp', 'tensor'), may hold values from -0.1875 to 0.1875
- shrink_weights: float32 [4096, 1024], P('tensor', 'dp'), may hold values from -0.09375 to 0.09375
- attend_in_momentum: float32 [1024, 6, 1024], P('dp', None, 'tensor'), may hold values from -0.0024414062 to 0.0024414062
- attend_out_momentum: float32 [2, 1024, 1024], P(None, 'tensor', 'dp'), may hold values from -0.0024414062 to 0.0024414062
- expand_momentum: float32 [1024, 4096], P('dp', 'tensor'), may hold values from -0.0024414062 to 0.0024414062
- shrink_momentum: float32 [4096, 1024], P('tensor', 'dp'), may hold values from -0.0024414062 to 0.0024414062
- embed_table: float32 [4, 2048, 1024], P(None, ('dp', 'tensor')), may hold values from -4 to 4
- head_table: float32 [4, 2048, 1024], P(None, ('dp', 'tensor')), may hold values from -0.1875 to 0.1875
- norm_params: float32 [8, 1024], replicated, may hold values from -2 to 1.4, as said below
- embed_first: float32 [4, 2048, 1024], P(None, ('dp', 'tensor')), may hold values from -4.7683716e-06 to 4.7683716e-06
- embed_second: float32 [4, 2048, 1024], P(None, ('dp', 'tensor')), may hold values from 6.3329935e-13 to 2.0489097e-12
- head_first: float32 [4, 2048, 1024], P(None, ('dp', 'tensor')), may hold values from -9.1552734e-05 to 9.1552734e-05
- head_second: float32 [4, 2048, 1024], P(None, ('dp', 'tensor')), may hold values from 1.7508864e-10 to 5.7742e-10
- norm_first: float32 [8, 1024], replicated, may hold values from -0.0029296875 to 0.0029296875
- norm_second: float32 [8, 1024], replicated, may hold values from 6.103516e-08 to 2.4414064e-07
Outputs:
- loss_sum: float32 [], replicated
- token_count: float32 [], replicated
- attend_in_new: float32 [1024, 6, 1024], P('dp', None, 'tensor')
- attend_out_new: float32 [2, 1024, 1024], P(None, 'tensor', 'dp')
- expand_new: float32 [1024, 4096], P('dp', 'tensor')
- shrink_new: float32 [4096, 1024], P('tensor', 'dp')
- attend_in_next: float32 [1024, 6, 1024], P('dp', None, 'tensor')
- attend_out_next: float32 [2, 1024, 1024], P(None, 'tensor', 'dp')
- expand_next: float32 [1024, 4096], P('dp', 'tensor')
- shrink_next: float32 [4096, 1024], P('tensor', 'dp')
- embed_new: float32 [4, 2048, 1024], P(None, ('dp', 'tensor'))
- head_new: float32 [4, 2048, 1024], P(None, ('dp', 'tensor'))
- norm_new: float32 [8, 1024], replicated
- embed_first_new: float32 [4, 2048, 1024], P(None, ('dp', 'tensor'))
- embed_second_new: float32 [4, 2048, 1024], P(None, ('dp', 'tensor'))
- head_first_new: float32 [4, 2048, 1024], P(None, ('dp', 'tensor'))
- head_second_new: float32 [4, 2048, 1024], P(None, ('dp', 'tensor'))
- norm_first_new: float32 [8, 1024], replicated
- norm_second_new: float32 [8, 1024], replicated
Inputs may be any that keep to these rules, and one draw needn't show every extreme that they name: `codes_in`: each clip has a length from 128 to 1024, longer on average in later groups of 2 clips; one clip of each group, drawn, has length 1024. In codebook k, frame s holds a code where k <= s < length + k, else 2048 - 1. codes_out[c, t] is the code of frame t + 1 by the same rule, so codes_out[c, t] = codes_in[c, t + 1] below the last frame. `pad_mask`: 1 exactly where codebook k of frame t + 1 holds a live code by that rule. `norm_params`: rows 0, 2, 4, 6 are gains, rows 1, 3, 5, 7 shifts.
All inputs are finite; a program needn't handle non-finite values.
Results may differ from a plain program's by a relative error of at most 0.025.
Values may be sent and summed in bfloat16 or wider, within the bound.
No kernel may reach another device: no remote copies, remote signals or barrier semaphores. Data moves between devices by JAX's collectives and lax.ppermute only.
A program may use at most 256 MiB of HBM per device.

v0:
```python
import math

import jax
import jax.numpy as jnp
from jax import lax
from jax.sharding import PartitionSpec as P

HEAD_DIM = 64
MUON_ROWS = 32
STEP = 10


HIGHEST = lax.Precision.HIGHEST
NEWTON = (3.4445, -4.775, 2.0315)
BETA_ONE = 0.9
BETA_TWO = 0.95
ADAM_EPS = 1e-08
DECAY = 0.01
MOMENTUM = 0.95


def as_sent(array):
    return jax.tree.map(lambda a: a.astype(jnp.bfloat16) if a.dtype == jnp.float32 else a, array)


def layer_norm(values, gain, shift):
    centred = values - jnp.mean(values, -1, keepdims=True)
    variance = jnp.mean(centred * centred, -1, keepdims=True)
    return centred * lax.rsqrt(variance + 1e-05) * gain + shift


def norm_back(values, gain, shift, grad):
    result, backward = jax.vjp(layer_norm, values, gain, shift)
    return backward(grad)


def exact_gelu(values):
    return jax.nn.gelu(values, approximate=False)


def sinusoid(first, length, width):
    half = width // 2
    rates = jnp.exp(jnp.arange(half, dtype=jnp.float32) * (-math.log(10000.0) / half))
    places = (first + jnp.arange(length, dtype=jnp.int32)).astype(jnp.float32)
    angles = places[:, None] * rates[None, :]
    return jnp.concatenate([jnp.sin(angles), jnp.cos(angles)], -1)


def split_heads(values):
    return values.reshape(values.shape[:2] + (-1, HEAD_DIM))


def spread_rows(values):
    return lax.all_gather(values.astype(jnp.bfloat16), "tensor", axis=0, tiled=True)


def pulled(grad):
    return lax.all_gather(grad.astype(jnp.bfloat16), "tensor", axis=0, tiled=True)


def pushed(partial_value):
    return lax.psum_scatter(
        partial_value.astype(jnp.bfloat16), "tensor", scatter_dimension=0, tiled=True
    ).astype(jnp.float32)


def collect(left, weight):
    return lax.psum_scatter(
        jnp.einsum("fcn,nd->fcd", left, weight, preferred_element_type=jnp.float32),
        "tensor",
        scatter_dimension=0,
        tiled=True,
    )


def slot_of(codes, rows_each, groups, place):
    owner = codes // rows_each % groups
    local = codes // (rows_each * groups) * rows_each + codes % rows_each
    return jnp.where(owner == place, local, -1)


def embed_rows(table, slots):
    total = None
    for codebook in range(table.shape[0]):
        slot = slots[:, :, codebook]
        picked = jnp.take(table[codebook], jnp.maximum(slot, 0), axis=0).astype(jnp.float32)
        picked = jnp.where((slot >= 0)[:, :, None], picked, 0.0)
        total = picked if total is None else total + picked
    return total


def table_grad(grad_rows, slots, rows_count):
    width = grad_rows.shape[-1]
    flat_grad = grad_rows.reshape(-1, width).astype(jnp.float32)
    flat_slots = slots.reshape(flat_grad.shape[0], -1)
    segments = jnp.where(flat_slots >= 0, flat_slots, rows_count)
    return jnp.stack(
        [
            jax.ops.segment_sum(flat_grad, segments[:, codebook], num_segments=rows_count + 1)[
                :rows_count
            ]
            for codebook in range(flat_slots.shape[1])
        ],
        0,
    )


def scores_of(part, key_rows, first, causal):
    scores = (
        jnp.einsum("qchd,kchd->chqk", part, key_rows, preferred_element_type=jnp.float32) * 0.125
    )
    if causal:
        allowed = (first + jnp.arange(part.shape[0]))[:, None] >= jnp.arange(key_rows.shape[0])[
            None, :
        ]
        scores = jnp.where(allowed[None, None], scores, -jnp.inf)
    return scores


def attend(queries, key_rows, value_rows, causal):
    frames, clips, heads_local, depth = queries.shape
    span = min(512, frames)
    grouped = queries.reshape(frames // span, span, clips, heads_local, depth)
    firsts = jnp.arange(frames // span) * span

    def one_block(inputs):
        part, first = inputs
        scores = scores_of(part, key_rows, first, causal)
        row_max = jnp.max(scores, -1, keepdims=True)
        expo = jnp.exp(scores - row_max)
        total = jnp.sum(expo, -1, keepdims=True)
        probs = (expo / total).astype(jnp.bfloat16)
        mixed = jnp.einsum("chqk,kchd->qchd", probs, value_rows, preferred_element_type=jnp.float32)
        return (mixed.astype(jnp.bfloat16), (row_max + jnp.log(total))[..., 0])

    mixed, log_total = lax.map(one_block, (grouped, firsts))
    return (mixed.reshape(frames, clips, heads_local * depth), log_total)


def attend_back(queries, key_rows, value_rows, log_total, grad_mixed, causal):
    frames, clips, heads_local, depth = queries.shape
    span = min(512, frames)
    grouped = queries.reshape(frames // span, span, clips, heads_local, depth)
    grad_grouped = grad_mixed.reshape(grouped.shape)
    firsts = jnp.arange(frames // span) * span

    def one_block(carry, inputs):
        grad_keys, grad_values = carry
        part, grad_part, log_part, first = inputs
        scores = scores_of(part, key_rows, first, causal)
        probs = jnp.exp(scores - log_part[..., None])
        grad_probs = jnp.einsum(
            "qchd,kchd->chqk", grad_part, value_rows, preferred_element_type=jnp.float32
        )
        grad_scores = (
            probs * (grad_probs - jnp.sum(probs * grad_probs, -1, keepdims=True))
        ).astype(jnp.bfloat16)
        grad_query = (
            jnp.einsum("chqk,kchd->qchd", grad_scores, key_rows, preferred_element_type=jnp.float32)
            * 0.125
        )
        grad_keys = (
            grad_keys
            + jnp.einsum("chqk,qchd->kchd", grad_scores, part, preferred_element_type=jnp.float32)
            * 0.125
        )
        grad_values = grad_values + jnp.einsum(
            "chqk,qchd->kchd",
            probs.astype(jnp.bfloat16),
            grad_part,
            preferred_element_type=jnp.float32,
        )
        return ((grad_keys, grad_values), grad_query)

    empty = jnp.zeros(key_rows.shape, jnp.float32)
    (grad_keys, grad_values), grad_query = lax.scan(
        one_block, (empty, empty), (grouped, grad_grouped, log_total, firsts)
    )
    return (grad_query.reshape(queries.shape), grad_keys, grad_values)


def layer_forward(residual, gains, weights, memory):
    attend_in, attend_out, expand, shrink = weights
    normed_one = spread_rows(layer_norm(residual, gains[0], gains[1]))
    triple = jnp.einsum(
        "fcd,djn->fcjn", normed_one, attend_in[:, 0:3], preferred_element_type=jnp.float32
    ).astype(jnp.bfloat16)
    self_parts = tuple((split_heads(triple[:, :, member]) for member in range(3)))
    self_mixed, self_total = attend(self_parts[0], self_parts[1], self_parts[2], True)
    residual_one = residual + collect(self_mixed, attend_out[0])
    normed_two = spread_rows(layer_norm(residual_one, gains[2], gains[3]))
    cross_q = jnp.einsum(
        "fcd,dn->fcn", normed_two, attend_in[:, 3], preferred_element_type=jnp.float32
    ).astype(jnp.bfloat16)
    cross_kv = jnp.einsum(
        "scd,djn->scjn", memory, attend_in[:, 4:6], preferred_element_type=jnp.float32
    ).astype(jnp.bfloat16)
    cross_parts = (
        split_heads(cross_q),
        split_heads(cross_kv[:, :, 0]),
        split_heads(cross_kv[:, :, 1]),
    )
    cross_mixed, cross_total = attend(cross_parts[0], cross_parts[1], cross_parts[2], False)
    residual_two = residual_one + collect(cross_mixed, attend_out[1])
    normed_three = spread_rows(layer_norm(residual_two, gains[4], gains[5]))
    upper = jnp.einsum("fcd,dn->fcn", normed_three, expand, preferred_element_type=jnp.float32)
    active = exact_gelu(upper).astype(jnp.bfloat16)
    residual_three = residual_two + collect(active, shrink)
    kept = (
        residual,
        residual_one,
        residual_two,
        normed_one,
        normed_two,
        normed_three,
        self_parts,
        self_mixed,
        self_total,
        cross_parts,
        cross_mixed,
        cross_total,
        upper,
        active,
    )
    return (residual_three, kept)


def layer_backward(grad, kept, gains, weights, memory):
    attend_in, attend_out, expand, shrink = weights
    (
        residual,
        residual_one,
        residual_two,
        normed_one,
        normed_two,
        normed_three,
        self_parts,
        self_mixed,
        self_total,
        cross_parts,
        cross_mixed,
        cross_total,
        upper,
        active,
    ) = kept
    frames, clips = normed_one.shape[:2]
    grad_rows = pulled(grad)
    grad_active = jnp.einsum("fcd,nd->fcn", grad_rows, shrink, preferred_element_type=jnp.float32)
    grad_shrink = jnp.einsum("fcn,fcd->nd", active, grad_rows, preferred_element_type=jnp.float32)
    grad_upper = jax.vjp(exact_gelu, upper)[1](grad_active)[0].astype(jnp.bfloat16)
    grad_expand = jnp.einsum(
        "fcd,fcn->dn", normed_three, grad_upper, preferred_element_type=jnp.float32
    )
    grad_normed = pushed(
        jnp.einsum("fcn,dn->fcd", grad_upper, expand, preferred_element_type=jnp.float32)
    )
    grad_resid, gain_three, shift_three = norm_back(residual_two, gains[4], gains[5], grad_normed)
    grad = grad + grad_resid
    grad_rows = pulled(grad)
    grad_mixed = jnp.einsum(
        "fcd,nd->fcn", grad_rows, attend_out[1], preferred_element_type=jnp.float32
    ).astype(jnp.bfloat16)
    grad_cross_out = jnp.einsum(
        "fcn,fcd->nd", cross_mixed, grad_rows, preferred_element_type=jnp.float32
    )
    grad_q, grad_k, grad_v = attend_back(
        cross_parts[0], cross_parts[1], cross_parts[2], cross_total, split_heads(grad_mixed), False
    )
    grad_q = grad_q.astype(jnp.bfloat16).reshape(frames, clips, -1)
    grad_kv = (
        jnp.stack([grad_k, grad_v], 2).astype(jnp.bfloat16).reshape(memory.shape[0], clips, 2, -1)
    )
    grad_cross_q = jnp.einsum("fcd,fcn->dn", normed_two, grad_q, preferred_element_type=jnp.float32)
    grad_cross_kv = jnp.einsum("scd,scjn->djn", memory, grad_kv, preferred_element_type=jnp.float32)
    grad_normed = pushed(
        jnp.einsum("fcn,dn->fcd", grad_q, attend_in[:, 3], preferred_element_type=jnp.float32)
    )
    grad_resid, gain_two, shift_two = norm_back(residual_one, gains[2], gains[3], grad_normed)
    grad = grad + grad_resid
    grad_rows = pulled(grad)
    grad_mixed = jnp.einsum(
        "fcd,nd->fcn", grad_rows, attend_out[0], preferred_element_type=jnp.float32
    ).astype(jnp.bfloat16)
    grad_self_out = jnp.einsum(
        "fcn,fcd->nd", self_mixed, grad_rows, preferred_element_type=jnp.float32
    )
    grad_q, grad_k, grad_v = attend_back(
        self_parts[0], self_parts[1], self_parts[2], self_total, split_heads(grad_mixed), True
    )
    grad_triple = (
        jnp.stack([grad_q, grad_k, grad_v], 2).astype(jnp.bfloat16).reshape(frames, clips, 3, -1)
    )
    grad_self_in = jnp.einsum(
        "fcd,fcjn->djn", normed_one, grad_triple, preferred_element_type=jnp.float32
    )
    grad_normed = pushed(
        jnp.einsum(
            "fcjn,djn->fcd", grad_triple, attend_in[:, 0:3], preferred_element_type=jnp.float32
        )
    )
    grad_resid, gain_one, shift_one = norm_back(residual, gains[0], gains[1], grad_normed)
    grad = grad + grad_resid
    grad_in = jnp.concatenate([grad_self_in, grad_cross_q[:, None], grad_cross_kv], 1)
    grad_out = jnp.stack([grad_self_out, grad_cross_out], 0)
    grad_gains = [gain_one, shift_one, gain_two, shift_two, gain_three, shift_three]
    return (grad, (grad_in, grad_out, grad_expand, grad_shrink), grad_gains)


def gram_of(part):
    return jnp.einsum("brc,bsc->brs", part, part, precision=HIGHEST)


def newton(blocks, total):
    grams = total(tuple((gram_of(part) for part in blocks)))
    sizes = tuple(
        (jnp.sqrt(jnp.trace(gram, axis1=1, axis2=2))[:, None, None] + 1e-07 for gram in grams)
    )
    current = tuple((part / size for part, size in zip(blocks, sizes)))
    grams = tuple((gram / (size * size) for gram, size in zip(grams, sizes)))
    for repeat in range(5):
        if repeat > 0:
            grams = total(tuple((gram_of(part) for part in current)))
        current = tuple(
            (
                NEWTON[0] * part
                + jnp.einsum(
                    "brs,bsc->brc",
                    NEWTON[1] * gram
                    + NEWTON[2] * jnp.einsum("brs,bst->brt", gram, gram, precision=HIGHEST),
                    part,
                    precision=HIGHEST,
                )
                for part, gram in zip(current, grams)
            )
        )
    return current


def tensor_total(grams):
    return lax.psum(grams, "tensor")


def data_total(grams):
    return jax.tree.map(lambda part: part.astype(jnp.float32), lax.psum(as_sent(grams), "dp"))


def adam(weight, first, second, gradient, rate, decay):
    first = BETA_ONE * first + (1.0 - BETA_ONE) * gradient
    second = BETA_TWO * second + (1.0 - BETA_TWO) * gradient * gradient
    direction = (
        first / (1.0 - BETA_ONE**STEP) / (jnp.sqrt(second / (1.0 - BETA_TWO**STEP)) + ADAM_EPS)
    )
    return (weight - rate * (direction + decay * weight), first, second)


def body(
    codes_in,
    codes_out,
    pad_mask,
    text_table,
    text_index,
    attend_in,
    attend_out,
    expand_weights,
    shrink_weights,
    attend_in_momentum,
    attend_out_momentum,
    expand_momentum,
    shrink_momentum,
    embed_table,
    head_table,
    norm_params,
    embed_first,
    embed_second,
    head_first,
    head_second,
    norm_first,
    norm_second,
):
    codes_now = jnp.transpose(codes_in, (1, 0, 2))
    codes_next = jnp.transpose(codes_out, (1, 0, 2))
    mask_now = jnp.transpose(pad_mask, (1, 0, 2))
    frames_local, clip_count, books = codes_now.shape
    width = norm_params.shape[1]
    token_count = lax.psum(jnp.sum(mask_now.astype(jnp.float32)), ("dp", "tensor"))
    memory = jnp.take(text_table, jnp.transpose(text_index), axis=0)
    groups = 1
    place = 0
    table_rows, head_rows = (
        lax.all_gather(embed_table.astype(jnp.bfloat16), ("dp", "tensor"), axis=1, tiled=True),
        lax.all_gather(head_table.astype(jnp.bfloat16), ("dp", "tensor"), axis=1, tiled=True),
    )
    weights = (
        lax.all_gather(attend_in.astype(jnp.bfloat16), "dp", axis=0, tiled=True),
        lax.all_gather(attend_out.astype(jnp.bfloat16), "dp", axis=2, tiled=True),
        lax.all_gather(expand_weights.astype(jnp.bfloat16), "dp", axis=0, tiled=True),
        lax.all_gather(shrink_weights.astype(jnp.bfloat16), "dp", axis=1, tiled=True),
    )
    codes_all, next_all, mask_all = (codes_now, codes_next, mask_now)
    rows_each = head_rows.shape[1]
    rows_count = head_rows.shape[1]
    local_ids = jnp.arange(rows_count)
    vocab_ids = (local_ids // rows_each * groups + place) * rows_each + local_ids % rows_each
    slots = slot_of(codes_all, rows_each, groups, place)
    counted_all = mask_all.astype(jnp.float32)
    embedded = embed_rows(table_rows, slots)
    first_frame = lax.axis_index("tensor") * frames_local
    residual = embedded + sinusoid(first_frame, frames_local, width)[:, None, :]
    output, kept = layer_forward(residual, norm_params, weights, memory)
    final_rows = layer_norm(output, norm_params[6], norm_params[7]).astype(jnp.bfloat16)
    frames_rows = final_rows.shape[0]
    total_rows = frames_rows * clip_count
    span = min(512, total_rows)
    blocks = total_rows // span

    def head_block(carry, inputs):
        grad_head, loss_local = carry
        rows_part, wanted, weight_part = inputs
        logits = jnp.einsum("td,kvd->tkv", rows_part, head_rows, preferred_element_type=jnp.float32)
        expo_sum = jnp.sum(jnp.exp(logits), -1)
        is_target = vocab_ids[None, None, :] == wanted[:, :, None]
        picked = jnp.sum(jnp.where(is_target, logits, 0.0), -1)
        log_total = jnp.log(expo_sum)
        loss_local = loss_local - jnp.sum((picked - log_total) * weight_part)
        grad_logits = (
            (jnp.exp(logits - log_total[:, :, None]) - is_target.astype(jnp.float32))
            * (weight_part / token_count)[:, :, None]
        ).astype(jnp.bfloat16)
        grad_head = grad_head + jnp.einsum(
            "tkv,td->kvd", grad_logits, rows_part, preferred_element_type=jnp.float32
        )
        grad_part = jnp.einsum(
            "tkv,kvd->td", grad_logits, head_rows, preferred_element_type=jnp.float32
        )
        return ((grad_head, loss_local), grad_part)

    start_carry = (jnp.zeros(head_rows.shape, jnp.float32), jnp.zeros((), jnp.float32))
    (grad_head, loss_local), grad_final = lax.scan(
        head_block,
        start_carry,
        (
            final_rows.reshape(blocks, span, width),
            next_all.reshape(blocks, span, books),
            counted_all.reshape(blocks, span, books),
        ),
    )
    grad_final = grad_final.reshape(frames_rows, clip_count, width)
    grad_resid, gain_final, shift_final = norm_back(
        output, norm_params[6], norm_params[7], grad_final
    )
    grad_embedded, grad_layer, grad_gains = layer_backward(
        grad_resid, kept, norm_params, weights, memory
    )
    grad_embed_rows = grad_embedded.astype(jnp.bfloat16)
    grad_table = table_grad(grad_embed_rows, slots, rows_count)
    grad_table, grad_head = (
        lax.psum_scatter(grad_table, ("dp", "tensor"), scatter_dimension=1, tiled=True),
        lax.psum_scatter(grad_head, ("dp", "tensor"), scatter_dimension=1, tiled=True),
    )
    grad_in, grad_out, grad_expand, grad_shrink = (
        lax.psum_scatter(
            grad_layer[0].astype(jnp.bfloat16), "dp", scatter_dimension=0, tiled=True
        ).astype(jnp.float32),
        lax.psum_scatter(
            grad_layer[1].astype(jnp.bfloat16), "dp", scatter_dimension=2, tiled=True
        ).astype(jnp.float32),
        lax.psum_scatter(
            grad_layer[2].astype(jnp.bfloat16), "dp", scatter_dimension=0, tiled=True
        ).astype(jnp.float32),
        lax.psum_scatter(
            grad_layer[3].astype(jnp.bfloat16), "dp", scatter_dimension=1, tiled=True
        ).astype(jnp.float32),
    )
    loss_sum, grad_norm = lax.psum(
        (loss_local, jnp.stack(grad_gains + [gain_final, shift_final], 0)), ("dp", "tensor")
    )
    next_in = MOMENTUM * attend_in_momentum + grad_in
    next_out = MOMENTUM * attend_out_momentum + grad_out
    next_expand = MOMENTUM * expand_momentum + grad_expand
    next_shrink = MOMENTUM * shrink_momentum + grad_shrink
    rows_data, members, cols_in = next_in.shape
    cols_expand = next_expand.shape[1]
    cols_data = next_shrink.shape[1]
    blocks_in = (
        next_in.reshape(rows_data // MUON_ROWS, MUON_ROWS, members, cols_in)
        .transpose(2, 0, 1, 3)
        .reshape(-1, MUON_ROWS, cols_in)
    )
    blocks_expand = next_expand.reshape(-1, MUON_ROWS, cols_expand)
    count_out = next_out.size // (MUON_ROWS * cols_data)
    blocks_data = jnp.concatenate(
        [next_out.reshape(-1, MUON_ROWS, cols_data), next_shrink.reshape(-1, MUON_ROWS, cols_data)],
        0,
    )
    ortho_in, ortho_expand = newton((blocks_in, blocks_expand), tensor_total)
    ortho_data = newton((blocks_data,), data_total)[0]
    ortho_in = (
        ortho_in.reshape(members, rows_data // MUON_ROWS, MUON_ROWS, cols_in)
        .transpose(1, 2, 0, 3)
        .reshape(next_in.shape)
    )
    ortho_out = ortho_data[:count_out].reshape(next_out.shape)
    ortho_shrink = ortho_data[count_out:].reshape(next_shrink.shape)
    attend_in_new = attend_in * (1.0 - 0.5 * DECAY) - 0.5 * ortho_in
    attend_out_new = attend_out * (1.0 - 1.0 * DECAY) - 1.0 * ortho_out
    expand_new = expand_weights * (1.0 - 0.5 * DECAY) - 0.5 * ortho_expand.reshape(
        next_expand.shape
    )
    shrink_new = shrink_weights * (1.0 - 0.5 * DECAY) - 0.5 * ortho_shrink
    embed_new, embed_first_new, embed_second_new = adam(
        embed_table, embed_first, embed_second, grad_table, 0.1, DECAY
    )
    head_new, head_first_new, head_second_new = adam(
        head_table, head_first, head_second, grad_head, 0.03, DECAY
    )
    norm_new, norm_first_new, norm_second_new = adam(
        norm_params, norm_first, norm_second, grad_norm, 0.5, 0.0
    )
    return (
        loss_sum,
        token_count,
        attend_in_new,
        attend_out_new,
        expand_new,
        shrink_new,
        next_in,
        next_out,
        next_expand,
        next_shrink,
        embed_new,
        head_new,
        norm_new,
        embed_first_new,
        embed_second_new,
        head_first_new,
        head_second_new,
        norm_first_new,
        norm_second_new,
    )


def solution(mesh):
    return jax.shard_map(
        body,
        mesh=mesh,
        in_specs=(
            P("dp", "tensor", None),
            P("dp", "tensor", None),
            P("dp", "tensor", None),
            P(),
            P("dp", None),
            P("dp", None, "tensor"),
            P(None, "tensor", "dp"),
            P("dp", "tensor"),
            P("tensor", "dp"),
            P("dp", None, "tensor"),
            P(None, "tensor", "dp"),
            P("dp", "tensor"),
            P("tensor", "dp"),
            P(None, ("dp", "tensor"), None),
            P(None, ("dp", "tensor"), None),
            P(),
            P(None, ("dp", "tensor"), None),
            P(None, ("dp", "tensor"), None),
            P(None, ("dp", "tensor"), None),
            P(None, ("dp", "tensor"), None),
            P(),
            P(),
        ),
        out_specs=(
            P(),
            P(),
            P("dp", None, "tensor"),
            P(None, "tensor", "dp"),
            P("dp", "tensor"),
            P("tensor", "dp"),
            P("dp", None, "tensor"),
            P(None, "tensor", "dp"),
            P("dp", "tensor"),
            P("tensor", "dp"),
            P(None, ("dp", "tensor"), None),
            P(None, ("dp", "tensor"), None),
            P(),
            P(None, ("dp", "tensor"), None),
            P(None, ("dp", "tensor"), None),
            P(None, ("dp", "tensor"), None),
            P(None, ("dp", "tensor"), None),
            P(),
            P(),
        ),
        check_vma=False,
    )
```

profile of v0, /device:TPU:0, one launch (start us, length us, event | category | flops | bytes accessed | tf_op | source)
XLA Modules:
  0.0 2824.5 jit_solution(11287826173642289330)
XLA Ops:
  16.3 112.9 %all-gather.13.cloned.1.call-done = bf16[4,2048,1024]{2,1,0:T(8,128)(2,1)} async-done(((bf16[4,64,1024]{2,1,0:T(8,128)(2,1)}), bf16[4,2048,1024]{2,1,0:T(8,128)(2,1)}) %all-gather.13.cloned.1.call-update) | async-done | bytes 16777232 | tf_op jit(solution)/shard_map/all_gather | solution.py:390
  129.2 12.5 slice_bitcast_fusion.7
  182.4 10.7 all-gather.17.cloned.1.call-done
  193.1 34.9 %all-gather.15.cloned.1.call-done = bf16[1024,2,1024]{2,0,1:T(8,128)(2,1)} async-done(((bf16[256,2,1024]{2,0,1:T(8,128)(2,1)}), bf16[1024,2,1024]{2,0,1:T(8,128)(2,1)}) %all-gather.15.cloned.1.call-update) | async-done | bytes 4194320 | tf_op jit(solution)/shard_map/all_gather | solution.py:54
  239.5 30.3 %while.60 = (s32[]{:T(128)}, bf16[2,512,2,4,64]{1,4,3,2,0:T(8,128)(2,1)}, f32[2,2,4,512]{3,2,1,0:T(4,128)S(1)}, s32[2]{0:T(128)S(1)}, bf16[2,512,2,4,64]{1,4,3,2...) while((s32[]{:T(128)}, ...), condition=%wide.region_5.7_spmd, body=%wide.region_2.6_spmd.sunk | while | flops 1124856320 | bytes 68292808 | solution.py:136
  282.5 71.8 %reduce-scatter.17.cloned.1.call-done = f32[256,2,1024]{2,0,1:T(8,128)} async-done(((f32[1024,2,1024]{2,0,1:T(8,128)}), f32[256,2,1024]{2,0,1:T(8,128)}) %reduce-scatter.17.cloned.1.call-update) | async-done | bytes 2097168 | tf_op jit(solution)/shard_map/reduce_scatter | solution.py:68
  364.3 30.4 %all-gather.21.cloned.1.call-done = bf16[1024,2,1024]{2,0,1:T(8,128)(2,1)} async-done(((bf16[256,2,1024]{2,0,1:T(8,128)(2,1)}), bf16[1024,2,1024]{2,0,1:T(8,128)(2,1)}) %all-gather.21.cloned.1.call-update) | async-done | bytes 4194320 | tf_op jit(solution)/shard_map/all_gather | solution.py:54
  427.8 70.0 %reduce-scatter.19.cloned.1.call-done = f32[256,2,1024]{2,0,1:T(8,128)} async-done(((f32[1024,2,1024]{2,0,1:T(8,128)}), f32[256,2,1024]{2,0,1:T(8,128)}) %reduce-scatter.19.cloned.1.call-update) | async-done | bytes 2097168 | tf_op jit(solution)/shard_map/reduce_scatter | solution.py:68
  503.6 46.3 %all-gather.25.cloned.1.call-done = bf16[1024,1024]{1,0:T(8,128)(2,1)} async-done(((bf16[128,1024]{1,0:T(8,128)(2,1)}), bf16[1024,1024]{1,0:T(8,128)(2,1)}) %all-gather.25.cloned.1.call-update) | async-done | bytes 2097168 | tf_op jit(solution)/shard_map/all_gather | solution.py:396
  549.9 35.2 %all-gather.23.cloned.1.call-done = bf16[1024,2,1024]{2,0,1:T(8,128)(2,1)} async-done(((bf16[256,2,1024]{2,0,1:T(8,128)(2,1)}), bf16[1024,2,1024]{2,0,1:T(8,128)(2,1)}) %all-gather.23.cloned.1.call-update) | async-done | bytes 4194320 | tf_op jit(solution)/shard_map/all_gather | solution.py:54
  585.0 9.9 fusion.109
  598.2 20.3 multiply_convert_fusion.2
  618.5 21.0 all-gather.27.cloned.1.call-done
  639.5 10.6 fusion.103
  653.5 38.3 %psum.127 = f32[]{:T(128)} all-reduce(f32[]{:T(128)} %convert_reduce_fusion.3), channel_id=1, replica_groups=mesh['dp'=8,'tensor'=4] {'dp','tensor'}, use_global_device_ids=true, to_apply=%region_24.26 | all-reduce | flops 1 | bytes 8 | tf_op jit(solution)/shard_map/psum | solution.py:385
  692.1 28.0 reduce-scatter.21.cloned.1.call-done
  728.6 110.2 %all-gather.29.cloned.1.call-done = bf16[4,2048,1024]{2,1,0:T(8,128)(2,1)} async-done(((bf16[4,64,1024]{2,1,0:T(8,128)(2,1)}), bf16[4,2048,1024]{2,1,0:T(8,128)(2,1)}) %all-gather.29.cloned.1.call-update) | async-done | bytes 16777232 | tf_op jit(solution)/shard_map/all_gather | solution.py:391
  838.8 17.2 exponential_reduce_fusion
  857.8 19.7 fusion.215
  888.7 32.8 %all-gather.31.cloned.1.call-done = bf16[1024,2,1024]{2,0,1:T(8,128)(2,1)} async-done(((bf16[256,2,1024]{2,0,1:T(8,128)(2,1)}), bf16[1024,2,1024]{2,0,1:T(8,128)(2,1)}) %all-gather.31.cloned.1.call-update) | async-done | bytes 4194320 | tf_op jit(solution)/shard_map/all_gather | solution.py:58
  921.5 11.8 add_convert_fusion
  941.8 44.6 %reduce-scatter.23.cloned.1.call-done = bf16[256,2,1024]{2,0,1:T(8,128)(2,1)} async-done(((bf16[1024,2,1024]{2,0,1:T(8,128)(2,1)}), bf16[256,2,1024]{2,0,1:T(8,128)(2,1)}) %reduce-scatter.23.cloned.1.call-update) | async-done | bytes 1048592 | tf_op jit(solution)/shard_map/reduce_scatter | solution.py:62
  995.4 34.4 %all-gather.33.cloned.1.call-done = bf16[1024,2,1024]{2,0,1:T(8,128)(2,1)} async-done(((bf16[256,2,1024]{2,0,1:T(8,128)(2,1)}), bf16[1024,2,1024]{2,0,1:T(8,128)(2,1)}) %all-gather.33.cloned.1.call-update) | async-done | bytes 4194320 | tf_op jit(solution)/shard_map/all_gather | solution.py:58
  1044.1 10.6 while.62
  1065.3 9.5 bitcast_convert_fusion.2
  1079.3 30.7 %reduce-scatter.25.cloned.1.call-done = bf16[256,2,1024]{2,0,1:T(8,128)(2,1)} async-done(((bf16[1024,2,1024]{2,0,1:T(8,128)(2,1)}), bf16[256,2,1024]{2,0,1:T(8,128)(2,1)}) %reduce-scatter.25.cloned.1.call-update) | async-done | bytes 1048592 | tf_op jit(solution)/shard_map/reduce_scatter | solution.py:62
  1118.1 63.5 %reduce-scatter.39.cloned.1.call-done = bf16[128,1024]{1,0:T(8,128)(2,1)} async-done(((bf16[1024,1024]{1,0:T(8,128)(2,1)}), bf16[128,1024]{1,0:T(8,128)(2,1)}) %reduce-scatter.39.cloned.1.call-update) | async-done | bytes 262160
  1192.6 24.7 all-gather.35.cloned.1.call-done
  1234.3 90.3 %while.63 = (s32[]{:T(128)}, f32[1024,2,4,64]{0,3,2,1:T(8,128)}, f32[1024,2,4,64]{0,3,2,1:T(8,128)}, bf16[2,512,2,4,64]{1,4,3,2,0:T(8,128)(2,1)}, bf16[2,512,2,4...) while((s32[]{:T(128)}, f32[1024,2,4,64]{0,3,2,1:T(8,128)}, ...), condition=%wide.region_38.40_spmd.clone, body=%wide.region_36.39_spmd.clone.sunk | while | flops 2750673408 | bytes 197251344 | solution.py:176
  1246.0 10.7 multiply_reduce_fusion.11
  1256.8 10.8 multiply_convert_fusion.6
  1267.6 7.2 fusion.410
  1284.5 7.2 bitcast_add_fusion.5
  1291.7 10.7 multiply_reduce_fusion.11
  1302.4 10.8 multiply_convert_fusion.6
  1349.8 64.8 %all-reduce.22.cloned.1.call-done = bf16[48,32,32]{2,1,0:T(8,128)(2,1)} async-done(((bf16[48,32,32]{2,1,0:T(8,128)(2,1)}), bf16[48,32,32]{2,1,0:T(8,128)(2,1)}) %all-reduce.22.cloned.1.call-update) | async-done | bytes 98320 | tf_op jit(solution)/shard_map/psum | solution.py:344
  1425.6 66.7 %all-reduce.24.cloned.1.call-done = bf16[48,32,32]{2,1,0:T(8,128)(2,1)} async-done(((bf16[48,32,32]{2,1,0:T(8,128)(2,1)}), bf16[48,32,32]{2,1,0:T(8,128)(2,1)}) %all-reduce.24.cloned.1.call-update) | async-done | bytes 98320 | tf_op jit(solution)/shard_map/psum | solution.py:344
  1496.9 72.9 %reduce-scatter.27.cloned.1.call-done = bf16[128,6,256]{2,0,1:T(8,128)(2,1)} async-done(((bf16[1024,6,256]{2,0,1:T(8,128)(2,1)}), bf16[128,6,256]{2,0,1:T(8,128)(2,1)}) %reduce-scatter.27.cloned.1.call-update) | async-done | bytes 393232 | tf_op jit(solution)/shard_map/reduce_scatter | solution.py:461
  1572.6 71.7 %all-reduce.26.cloned.1.call-done = bf16[48,32,32]{2,1,0:T(8,128)(2,1)} async-done(((bf16[48,32,32]{2,1,0:T(8,128)(2,1)}), bf16[48,32,32]{2,1,0:T(8,128)(2,1)}) %all-reduce.26.cloned.1.call-update) | async-done | bytes 98320 | tf_op jit(solution)/shard_map/psum | solution.py:344
  1645.9 33.0 %all-reduce.12.cloned.1.call-done = f32[24,32,32]{2,1,0:T(8,128)} async-done(((f32[24,32,32]{2,1,0:T(8,128)}), f32[24,32,32]{2,1,0:T(8,128)}) %all-reduce.12.cloned.1.call-update) | async-done | bytes 98320 | tf_op jit(solution)/shard_map/psum | solution.py:340
  1686.7 31.8 %all-reduce.14.cloned.1.call-done = f32[24,32,32]{2,1,0:T(8,128)} async-done(((f32[24,32,32]{2,1,0:T(8,128)}), f32[24,32,32]{2,1,0:T(8,128)}) %all-reduce.14.cloned.1.call-update) | async-done | bytes 98320 | tf_op jit(solution)/shard_map/psum | solution.py:340
  1726.6 30.4 %all-reduce.16.cloned.1.call-done = f32[24,32,32]{2,1,0:T(8,128)} async-done(((f32[24,32,32]{2,1,0:T(8,128)}), f32[24,32,32]{2,1,0:T(8,128)}) %all-reduce.16.cloned.1.call-update) | async-done | bytes 98320 | tf_op jit(solution)/shard_map/psum | solution.py:340
  1761.3 7.8 bitcast_convert_fusion
  1769.2 9.4 bitcast_convert_fusion.1
  1778.8 53.2 %all-reduce.28.cloned.1.call-done = bf16[48,32,32]{2,1,0:T(8,128)(2,1)} async-done(((bf16[48,32,32]{2,1,0:T(8,128)(2,1)}), bf16[48,32,32]{2,1,0:T(8,128)(2,1)}) %all-reduce.28.cloned.1.call-update) | async-done | bytes 98320 | tf_op jit(solution)/shard_map/psum | solution.py:344
  1836.8 30.0 %all-reduce.18.cloned.1.call-done = f32[24,32,32]{2,1,0:T(8,128)} async-done(((f32[24,32,32]{2,1,0:T(8,128)}), f32[24,32,32]{2,1,0:T(8,128)}) %all-reduce.18.cloned.1.call-update) | async-done | bytes 98320 | tf_op jit(solution)/shard_map/psum | solution.py:340
  1872.0 21.1 fusion.197
  1894.6 19.3 reduce-scatter.31.cloned.1.call-done
  1925.9 9.6 scatter_custom_fusion.3
  1935.4 9.5 scatter_custom_fusion.2
  1944.9 9.7 scatter_custom_fusion.1
  1954.6 9.5 scatter_custom_fusion
  1964.1 8.5 slice_bitcast_fusion
  1972.6 8.4 slice_bitcast_fusion.1
  1991.7 20.3 pad_maximum_fusion
  2014.7 11.1 psum.138
  2027.5 11.7 psum.139
  2040.6 10.7 psum.140
  2052.6 12.2 psum.141
  2066.2 11.4 psum.142
  2084.8 10.5 all-reduce.20.cloned.1.call-done
  2101.1 59.2 %all-reduce = (f32[]{:T(128)}, f32[8,1024]{1,0:T(8,128)S(1)}) all-reduce(f32[]{:T(128)S(6)} %sub.175, f32[8,1024]{1,0:T(8,128)S(1)} %stack.97), channel_id=1, replica_groups=mesh['dp'=8,'tensor'=4] {'dp','tensor'}, use_global_device_ids=true, to_apply=%region_22.24 | all-reduce | flops 8193 | bytes 65544 | tf_op jit(solution)/shard_map/psum | solution.py:474
  2160.9 291.9 %reduce-scatter.35.cloned.1.call-done = f32[4,64,1024]{2,1,0:T(8,128)} async-done(((f32[4,2048,1024]{2,1,0:T(8,128)}), f32[4,64,1024]{2,1,0:T(8,128)}) %reduce-scatter.35.cloned.1.call-update) | async-done | bytes 1048592 | tf_op jit(solution)/shard_map/reduce_scatter | solution.py:458
  2457.1 356.0 %reduce-scatter.33.cloned.1.call-done = f32[4,64,1024]{2,1,0:T(8,128)} async-done(((f32[4,2048,1024]{2,1,0:T(8,128)}), f32[4,64,1024]{2,1,0:T(8,128)}) %reduce-scatter.33.cloned.1.call-update) | async-done | bytes 1048592 | tf_op jit(solution)/shard_map/reduce_scatter | solution.py:457
  (634 shorter events, 440.4 us)
Async XLA Ops:
  7.2 353.3 %copy-start = (bf16[256,1024]{1,0:T(8,128)(2,1)S(1)}, bf16[256,1024]{1,0:T(8,128)(2,1)}, u32[]{:S(2)}) copy-start(bf16[256,1024]{1,0:T(8,128)(2,1)} %param.35) | copy-start | bytes 1572868
  7.2 122.0 %all-gather.13.cloned.1.call-start = ((), (), s32[]{:S(2)}) async-start(), calls=%async_computation.12 | async-start | bytes 17301504 | tf_op jit(solution)/shard_map/all_gather | solution.py:390
  9.4 183.7 %all-gather.17.cloned.1.call-start = ((), (), s32[]{:S(2)}) async-start(), calls=%async_computation.14 | async-start | bytes 3538944 | tf_op jit(solution)/shard_map/all_gather | solution.py:394
  11.6 216.4 %all-gather.15.cloned.1.call-start = ((), (), s32[]{:S(2)}) async-start(), calls=%async_computation.13 | async-start | bytes 5242880 | tf_op jit(solution)/shard_map/all_gather | solution.py:54
  12.3 129.4 %copy-start.66 = (s32[256,2,4]{0,2,1:T(4,128)}, s32[256,2,4]{0,2,1:T(4,128)S(1)}, u32[]{:S(2)}) copy-start(s32[256,2,4]{0,2,1:T(4,128)S(1)} %fusion.177) | copy-start | bytes 24580
  16.3 163.3 %copy-start.69 = (f32[1,1024]{1,0:T(1,128)}, f32[1,1024]{1,0:T(1,128)S(1)}, u32[]{:S(2)}) copy-start(f32[1,1024]{1,0:T(1,128)S(1)} %get-tuple-element.537) | copy-start | bytes 12292
  178.4 49.6 %copy-start.74 = (f32[256,2]{0,1:T(2,128)}, f32[256,2]{0,1:T(2,128)S(1)}, u32[]{:S(2)}) copy-start(f32[256,2]{0,1:T(2,128)S(1)} %broadcast_multiply_fusion.3) | copy-start | bytes 6148
  179.6 48.3 %copy-start.83 = (f32[256,2]{0,1:T(2,128)}, f32[256,2]{0,1:T(2,128)S(1)}, u32[]{:S(2)}) copy-start(f32[256,2]{0,1:T(2,128)S(1)} %fusion.182) | copy-start | bytes 6148
  181.2 95.3 %all-gather.19.cloned.1.call-start = ((), (), s32[]{:S(2)}) async-start(), calls=%async_computation.15 | async-start | bytes 1179648 | tf_op jit(solution)/shard_map/all_gather | solution.py:395
  181.9 172.3 %reduce-scatter.17.cloned.1.call-start = ((), (), s32[]{:S(2)}) async-start(), calls=%async_computation.16 | async-start | bytes 10485760 | tf_op jit(solution)/shard_map/reduce_scatter | solution.py:68
  282.4 76.2 %copy-start.61 = (f32[1,1024]{1,0:T(1,128)S(1)}, f32[1,1024]{1,0:T(1,128)}, u32[]{:S(2)}) copy-start(f32[1,1024]{1,0:T(1,128)} %get-tuple-element.535) | copy-start | bytes 12292
  282.4 76.2 %copy-start.100 = (f32[1,1024]{1,0:T(1,128)S(1)}, f32[1,1024]{1,0:T(1,128)}, u32[]{:S(2)}) copy-start(f32[1,1024]{1,0:T(1,128)} %get-tuple-element.534) | copy-start | bytes 12292
  282.4 112.2 %all-gather.21.cloned.1.call-start = ((), (), s32[]{:S(2)}) async-start(), calls=%async_computation.17 | async-start | bytes 5242880 | tf_op jit(solution)/shard_map/all_gather | solution.py:54
  356.8 758.8 %copy-start.7 = (f32[256,2,1024]{2,0,1:T(8,128)}, f32[256,2,1024]{2,0,1:T(8,128)S(1)}, u32[]{:S(2)}) copy-start(f32[256,2,1024]{2,0,1:T(8,128)S(1)} %get-tuple-element.501) | copy-start | bytes 6291460
  360.0 137.8 %reduce-scatter.19.cloned.1.call-start = ((), (), s32[]{:S(2)}) async-start(), calls=%async_computation.18 | async-start | bytes 10485760 | tf_op jit(solution)/shard_map/reduce_scatter | solution.py:68
  426.0 123.9 %all-gather.25.cloned.1.call-start = ((), (), s32[]{:S(2)}) async-start(), calls=%async_computation.20 | async-start | bytes 2359296 | tf_op jit(solution)/shard_map/all_gather | solution.py:396
  427.7 73.3 %copy-start.68 = (f32[1,1024]{1,0:T(1,128)S(1)}, f32[1,1024]{1,0:T(1,128)}, u32[]{:S(2)}) copy-start(f32[1,1024]{1,0:T(1,128)} %get-tuple-element.533) | copy-start | bytes 12292
  427.8 73.3 %copy-start.99 = (f32[1,1024]{1,0:T(1,128)S(1)}, f32[1,1024]{1,0:T(1,128)}, u32[]{:S(2)}) copy-start(f32[1,1024]{1,0:T(1,128)} %get-tuple-element.532) | copy-start | bytes 12292
  427.8 157.2 %all-gather.23.cloned.1.call-start = ((), (), s32[]{:S(2)}) async-start(), calls=%async_computation.19 | async-start | bytes 5242880 | tf_op jit(solution)/shard_map/all_gather | solution.py:54
  502.5 137.0 %all-gather.27.cloned.1.call-start = ((), (), s32[]{:S(2)}) async-start(), calls=%async_computation.21 | async-start | bytes 2359296 | tf_op jit(solution)/shard_map/all_gather | solution.py:397
  503.3 216.7 %reduce-scatter.21.cloned.1.call-start = ((), (), s32[]{:S(2)}) async-start(), calls=%async_computation.22 | async-start | bytes 10485760 | tf_op jit(solution)/shard_map/reduce_scatter | solution.py:68
  650.1 41.6 %copy-start.102 = (s32[2,256,4]{1,2,0:T(4,128)S(1)}, s32[2,256,4]{1,2,0:T(4,128)}, u32[]{:S(2)}) copy-start(s32[2,256,4]{1,2,0:T(4,128)} %param.33) | copy-start | bytes 24580
  650.2 188.6 %all-gather.29.cloned.1.call-start = ((), (), s32[]{:S(2)}) async-start(), calls=%async_computation.23 | async-start | bytes 17301504 | tf_op jit(solution)/shard_map/all_gather | solution.py:391
  652.3 269.2 %all-gather.31.cloned.1.call-start = ((), (), s32[]{:S(2)}) async-start(), calls=%async_computation.24 | async-start | bytes 5242880 | tf_op jit(solution)/shard_map/all_gather | solution.py:58
  692.0 165.8 %copy-start.103 = (s32[512,4]{0,1:T(4,128)}, s32[512,4]{0,1:T(4,128)S(1)}, u32[]{:S(2)}) copy-start(s32[512,4]{0,1:T(4,128)S(1)} %copy.132) | copy-start | bytes 24580
  692.0 165.8 %copy-start.107 = (s32[2048]{0:T(1024)}, s32[2048]{0:T(1024)S(1)}, u32[]{:S(2)}) copy-start(s32[2048]{0:T(1024)S(1)} %fusion.175) | copy-start | bytes 24580
  888.7 97.7 %reduce-scatter.23.cloned.1.call-start = ((), (), s32[]{:S(2)}) async-start(), calls=%async_computation.25 | async-start | bytes 5242880 | tf_op jit(solution)/shard_map/reduce_scatter | solution.py:62
  941.8 88.1 %all-gather.33.cloned.1.call-start = ((), (), s32[]{:S(2)}) async-start(), calls=%async_computation.26 | async-start | bytes 5242880 | tf_op jit(solution)/shard_map/all_gather | solution.py:58
  995.2 114.8 %reduce-scatter.25.cloned.1.call-start = ((), (), s32[]{:S(2)}) async-start(), calls=%async_computation.27 | async-start | bytes 5242880 | tf_op jit(solution)/shard_map/reduce_scatter | solution.py:62
  1065.3 116.3 %reduce-scatter.39.cloned.1.call-start = ((), (), s32[]{:S(2)}) async-start(), calls=%async_computation.45 | async-start | bytes 2359296
  1074.8 37.8 %copy-start.92 = (f32[256,2]{0,1:T(2,128)S(1)}, f32[256,2]{0,1:T(2,128)}, u32[]{:S(2)}) copy-start(f32[256,2]{0,1:T(2,128)} %copy-done.91) | copy-start | bytes 6148
  1074.8 37.8 %copy-start.79 = (f32[256,2]{0,1:T(2,128)S(1)}, f32[256,2]{0,1:T(2,128)}, u32[]{:S(2)}) copy-start(f32[256,2]{0,1:T(2,128)} %copy-done.78) | copy-start | bytes 6148
  1078.9 138.4 %all-gather.35.cloned.1.call-start = ((), (), s32[]{:S(2)}) async-start(), calls=%async_computation.28 | async-start | bytes 5242880 | tf_op jit(solution)/shard_map/all_gather | solution.py:58
  1115.6 69.0 %copy-start.87 = (f32[256,2]{0,1:T(2,128)}, f32[256,2]{0,1:T(2,128)S(1)}, u32[]{:S(2)}) copy-start(f32[256,2]{0,1:T(2,128)S(1)} %negate_multiply_fusion.2) | copy-start | bytes 6148
  1115.6 69.2 %copy-start.60 = (bf16[64,2,1024]{2,1,0:T(2,128)(2,1)S(1)}, bf16[64,2,1024]{2,1,0:T(2,128)(2,1)}, u32[]{:S(2)}) copy-start(bf16[64,2,1024]{2,1,0:T(2,128)(2,1)} %copy-done.59) | copy-start | bytes 786436
  1115.7 69.2 %copy-start.118 = (pred[64,2]{0,1:T(4,128)(4,1)S(1)}, pred[64,2]{0,1:T(4,128)(4,1)}, u32[]{:S(2)}) copy-start(pred[64,2]{0,1:T(4,128)(4,1)} %copy-done.117) | copy-start | bytes 388
  1117.4 69.0 %copy-start.39 = (bf16[1024,2,256]{0,2,1:T(8,128)(2,1)S(1)}, bf16[1024,2,256]{0,2,1:T(8,128)(2,1)}, u32[]{:S(2)}) copy-start(bf16[1024,2,256]{0,2,1:T(8,128)(2,1)} %reshape.441) | copy-start | bytes 3145732
  1117.4 222.5 %reduce-scatter.37.cloned.1.call-start = ((), (), s32[]{:S(2)}) async-start(), calls=%async_computation.44 | async-start | bytes 1179648
  1223.0 191.6 %all-reduce.22.cloned.1.call-start = ((), (), s32[]{:S(2)}) async-start(), calls=%async_computation.35 | async-start | bytes 786432 | tf_op jit(solution)/shard_map/psum | solution.py:344
  1341.0 77.6 %copy-start.51 = (f32[2,256,128]{2,1,0:T(8,128)}, f32[2,256,128]{2,1,0:T(8,128)S(1)}, u32[]{:S(2)}) copy-start(f32[2,256,128]{2,1,0:T(8,128)S(1)} %convert_add_fusion.3) | copy-start | bytes 786436
  1343.2 71.4 %copy-start.76 = (pred[32,32]{1,0:T(8,128)(4,1)S(1)}, pred[32,32]{1,0:T(8,128)(4,1)}, u32[]{:S(2)}) copy-start(pred[32,32]{1,0:T(8,128)(4,1)} %iota_compare_fusion.2) | copy-start | bytes 3076
  1343.2 149.1 %all-reduce.24.cloned.1.call-start = ((), (), s32[]{:S(2)}) async-start(), calls=%async_computation.36 | async-start | bytes 786432 | tf_op jit(solution)/shard_map/psum | solution.py:344
  1421.7 148.1 %reduce-scatter.27.cloned.1.call-start = ((), (), s32[]{:S(2)}) async-start(), calls=%async_computation.29 | async-start | bytes 3538944 | tf_op jit(solution)/shard_map/reduce_scatter | solution.py:461
  1425.1 144.7 %copy-start.52 = (f32[128,6,256]{2,0,1:T(8,128)S(1)}, f32[128,6,256]{2,0,1:T(8,128)}, u32[]{:S(2)}) copy-start(f32[128,6,256]{2,0,1:T(8,128)} %param.41) | copy-start | bytes 2359300
  1425.1 219.2 %all-reduce.26.cloned.1.call-start = ((), (), s32[]{:S(2)}) async-start(), calls=%async_computation.37 | async-start | bytes 786432 | tf_op jit(solution)/shard_map/psum | solution.py:344
  1496.9 182.1 %all-reduce.12.cloned.1.call-start = ((), (), s32[]{:S(2)}) async-start(), calls=%async_computation.30 | async-start | bytes 786432 | tf_op jit(solution)/shard_map/psum | solution.py:340
  1570.9 112.3 %copy-start.33 = (f32[128,6,256]{2,0,1:T(8,128)}, f32[128,6,256]{2,0,1:T(8,128)S(1)}, u32[]{:S(2)}) copy-start(f32[128,6,256]{2,0,1:T(8,128)S(1)} %convert_add_fusion) | copy-start | bytes 2359300
  1572.6 145.9 %all-reduce.14.cloned.1.call-start = ((), (), s32[]{:S(2)}) async-start(), calls=%async_computation.31 | async-start | bytes 786432 | tf_op jit(solution)/shard_map/psum | solution.py:340
  1685.7 71.3 %all-reduce.16.cloned.1.call-start = ((), (), s32[]{:S(2)}) async-start(), calls=%async_computation.32 | async-start | bytes 786432 | tf_op jit(solution)/shard_map/psum | solution.py:340
  1724.2 107.8 %all-reduce.28.cloned.1.call-start = ((), (), s32[]{:S(2)}) async-start(), calls=%async_computation.38 | async-start | bytes 786432 | tf_op jit(solution)/shard_map/psum | solution.py:344
  1726.4 140.4 %all-reduce.18.cloned.1.call-start = ((), (), s32[]{:S(2)}) async-start(), calls=%async_computation.33 | async-start | bytes 786432 | tf_op jit(solution)/shard_map/psum | solution.py:340
  1761.3 152.6 %reduce-scatter.31.cloned.1.call-start = ((), (), s32[]{:S(2)}) async-start(), calls=%async_computation.41 | async-start | bytes 5242880 | tf_op jit(solution)/shard_map/reduce_scatter | solution.py:62
  1769.1 243.6 %reduce-scatter.29.cloned.1.call-start = ((), (), s32[]{:S(2)}) async-start(), calls=%async_computation.40 | async-start | bytes 2359296 | tf_op jit(solution)/shard_map/reduce_scatter | solution.py:467
  1778.6 300.8 %all-reduce.30.cloned.1.call-start = ((), (), s32[]{:S(2)}) async-start(), calls=%async_computation.39 | async-start | bytes 786432 | tf_op jit(solution)/shard_map/psum | solution.py:344
  1836.7 258.5 %all-reduce.20.cloned.1.call-start = ((), (), s32[]{:S(2)}) async-start(), calls=%async_computation.34 | async-start | bytes 786432 | tf_op jit(solution)/shard_map/psum | solution.py:340
  1871.9 580.9 %reduce-scatter.35.cloned.1.call-start = ((), (), s32[]{:S(2)}) async-start(), calls=%async_computation.43 | async-start | bytes 34603008 | tf_op jit(solution)/shard_map/reduce_scatter | solution.py:458
  1893.3 919.8 %reduce-scatter.33.cloned.1.call-start = ((), (), s32[]{:S(2)}) async-start(), calls=%async_computation.42 | async-start | bytes 34603008 | tf_op jit(solution)/shard_map/reduce_scatter | solution.py:457
  2039.4 39.1 %copy-start.46 = (f32[128,1024]{1,0:T(8,128)S(1)}, f32[128,1024]{1,0:T(8,128)}, u32[]{:S(2)}) copy-start(f32[128,1024]{1,0:T(8,128)} %param.39) | copy-start | bytes 1572868
  2083.9 76.4 %copy-start.65 = (f32[8,1024]{1,0:T(8,128)S(1)}, f32[8,1024]{1,0:T(8,128)}, u32[]{:S(2)}) copy-start(f32[8,1024]{1,0:T(8,128)} %param.47) | copy-start | bytes 98308
  2083.9 76.4 %copy-start.85 = (f32[8,1024]{1,0:T(8,128)S(1)}, f32[8,1024]{1,0:T(8,128)}, u32[]{:S(2)}) copy-start(f32[8,1024]{1,0:T(8,128)} %param.52) | copy-start | bytes 98308
  2083.9 76.4 %copy-start.86 = (f32[8,1024]{1,0:T(8,128)S(1)}, f32[8,1024]{1,0:T(8,128)}, u32[]{:S(2)}) copy-start(f32[8,1024]{1,0:T(8,128)} %param.53) | copy-start | bytes 98308
  2083.9 368.9 %copy-start.36 = (f32[4,64,1024]{2,1,0:T(8,128)S(1)}, f32[4,64,1024]{2,1,0:T(8,128)}, u32[]{:S(2)}) copy-start(f32[4,64,1024]{2,1,0:T(8,128)} %param.46) | copy-start | bytes 3145732
  2101.1 712.0 %copy-start.37 = (f32[4,64,1024]{2,1,0:T(8,128)S(1)}, f32[4,64,1024]{2,1,0:T(8,128)}, u32[]{:S(2)}) copy-start(f32[4,64,1024]{2,1,0:T(8,128)} %param.45) | copy-start | bytes 3145732
  2452.8 364.4 %copy-start.1 = (bf16[256,1024]{1,0:T(8,128)(2,1)S(1)}, bf16[256,1024]{1,0:T(8,128)(2,1)}, u32[]{:S(2)}) copy-start(bf16[256,1024]{1,0:T(8,128)(2,1)} %param.35) | copy-start | bytes 1572868
  (107 other events, 1154.2 us)
Sparse Core Ops, SparseCore 0:
  11.6 117.6 all-gather.12
  131.9 61.2 all-gather.16
  195.3 32.6 all-gather.14
  230.4 39.5 all-gather.18
  282.5 71.6 reduce-scatter.16
  360.2 34.4 all-gather.20
  426.1 71.6 reduce-scatter.18
  500.5 49.2 all-gather.24
  552.0 32.9 all-gather.22
  587.5 51.9 all-gather.26
  650.3 69.6 reduce-scatter.20
  723.8 114.9 all-gather.28
  888.8 32.6 all-gather.30
  941.9 44.4 reduce-scatter.22
  995.3 34.4 all-gather.32
  1065.4 44.5 reduce-scatter.24
  1113.8 67.7 reduce-scatter.38
  1183.6 33.5 all-gather.34
  1223.1 63.4 reduce-scatter.36
  1343.3 71.2 all-reduce.21
  1421.8 70.3 all-reduce.23
  1495.8 73.9 reduce-scatter.26
  1573.7 70.5 all-reduce.25
  1647.2 31.6 all-reduce.11
  1685.8 32.5 all-reduce.13
  1724.3 32.6 all-reduce.15
  1760.8 71.2 all-reduce.27
  1835.1 31.6 all-reduce.17
  1869.4 44.4 reduce-scatter.30
  1917.7 67.9 reduce-scatter.28
  1989.9 70.2 all-reduce.29
  2063.2 32.0 all-reduce.19
  2097.5 355.2 reduce-scatter.34
  2455.2 357.7 reduce-scatter.32
where the time goes:
time: 2830 us; the launch traced here: 2820 us
  waiting for transfers between devices  1930 us (68%)
  matrix products  326 us (12%)
  other arithmetic  201 us (7%)
  local copies, waits for them, and re-layouts  187 us (7%)
  blocking collectives  155 us (5%)
    reduce_scatter x1, waiting for transfers between devices, body(): lax.psum_scatter(grad_table, ('dp', 'tensor'), scatter_dimension=1, tiled...  356 us
    reduce_scatter x1, waiting for transfers between devices, body(): lax.psum_scatter(grad_head, ('dp', 'tensor'), scatter_dimension=1, tiled=...  292 us
    psum x5, waiting for transfers between devices, data_total(): lax.psum(as_sent(grams), 'dp')  256 us
    reduce_scatter x3, waiting for transfers between devices, collect(): lax.psum_scatter(jnp.einsum('fcn,nd->fcd', left, weight, preferred_elemen...  170 us
    psum x5, waiting for transfers between devices, tensor_total(): return lax.psum(grams, 'tensor')  136 us
    all_gather x1, waiting for transfers between devices, body(): lax.all_gather(embed_table.astype(jnp.bfloat16), ('dp', 'tensor'), axis=1...  113 us
    all_gather x1, waiting for transfers between devices, body(): lax.all_gather(head_table.astype(jnp.bfloat16), ('dp', 'tensor'), axis=1,...  110 us
    all_gather x3, waiting for transfers between devices, spread_rows(): lax.all_gather(values.astype(jnp.bfloat16), 'tensor', axis=0, tiled=True)  100 us
  transfers between devices with their start and end apart: 34, of which 30 were waited for; matrix products, arithmetic and copies ran while one was open for 18% of the time, Pallas kernels for 0%

commit v1 on v0

v1 whole, which is shorter than its diff:
```python
import functools
import math

import jax
import jax.numpy as jnp
from jax import lax
from jax.sharding import Mesh
from jax.sharding import PartitionSpec as P

HEAD_DIM = 64
MUON_ROWS = 32
STEP = 10

HIGHEST = lax.Precision.HIGHEST
NEWTON = (3.4445, -4.775, 2.0315)
BETA_ONE = 0.9
BETA_TWO = 0.95
ADAM_EPS = 1e-08
DECAY = 0.01
MOMENTUM = 0.95
BF16 = jnp.bfloat16
F32 = jnp.float32


def layer_norm(values, gain, shift):
    centred = values - jnp.mean(values, -1, keepdims=True)
    variance = jnp.mean(centred * centred, -1, keepdims=True)
    return centred * lax.rsqrt(variance + 1e-05) * gain + shift


def norm_back(values, gain, shift, grad):
    result, backward = jax.vjp(layer_norm, values, gain, shift)
    return backward(grad)


def exact_gelu(values):
    return jax.nn.gelu(values, approximate=False)


def sinusoid(first, length, width):
    half = width // 2
    rates = jnp.exp(jnp.arange(half, dtype=jnp.float32) * (-math.log(10000.0) / half))
    places = (first + jnp.arange(length, dtype=jnp.int32)).astype(jnp.float32)
    angles = places[:, None] * rates[None, :]
    return jnp.concatenate([jnp.sin(angles), jnp.cos(angles)], -1)


def scores_of(part, key_rows, first, causal):
    scores = (
        jnp.einsum("qchd,kchd->chqk", part, key_rows, preferred_element_type=jnp.float32) * 0.125
    )
    if causal:
        allowed = (first + jnp.arange(part.shape[0]))[:, None] >= jnp.arange(key_rows.shape[0])[
            None, :
        ]
        scores = jnp.where(allowed[None, None], scores, -jnp.inf)
    return scores


def attend(queries, key_rows, value_rows, causal):
    frames, clips, heads_local, depth = queries.shape
    span = min(512, frames)
    grouped = queries.reshape(frames // span, span, clips, heads_local, depth)
    firsts = jnp.arange(frames // span) * span

    def one_block(inputs):
        part, first = inputs
        scores = scores_of(part, key_rows, first, causal)
        row_max = jnp.max(scores, -1, keepdims=True)
        expo = jnp.exp(scores - row_max)
        total = jnp.sum(expo, -1, keepdims=True)
        probs = (expo / total).astype(jnp.bfloat16)
        mixed = jnp.einsum("chqk,kchd->qchd", probs, value_rows, preferred_element_type=jnp.float32)
        return (mixed.astype(jnp.bfloat16), (row_max + jnp.log(total))[..., 0])

    mixed, log_total = lax.map(one_block, (grouped, firsts))
    return (mixed.reshape(frames, clips, heads_local * depth), log_total)


def attend_back(queries, key_rows, value_rows, log_total, grad_mixed, causal):
    frames, clips, heads_local, depth = queries.shape
    span = min(512, frames)
    grouped = queries.reshape(frames // span, span, clips, heads_local, depth)
    grad_grouped = grad_mixed.reshape(grouped.shape)
    firsts = jnp.arange(frames // span) * span

    def one_block(carry, inputs):
        grad_keys, grad_values = carry
        part, grad_part, log_part, first = inputs
        scores = scores_of(part, key_rows, first, causal)
        probs = jnp.exp(scores - log_part[..., None])
        grad_probs = jnp.einsum(
            "qchd,kchd->chqk", grad_part, value_rows, preferred_element_type=jnp.float32
        )
        grad_scores = (
            probs * (grad_probs - jnp.sum(probs * grad_probs, -1, keepdims=True))
        ).astype(jnp.bfloat16)
        grad_query = (
            jnp.einsum("chqk,kchd->qchd", grad_scores, key_rows, preferred_element_type=jnp.float32)
            * 0.125
        )
        grad_keys = (
            grad_keys
            + jnp.einsum("chqk,qchd->kchd", grad_scores, part, preferred_element_type=jnp.float32)
            * 0.125
        )
        grad_values = grad_values + jnp.einsum(
            "chqk,qchd->kchd",
            probs.astype(jnp.bfloat16),
            grad_part,
            preferred_element_type=jnp.float32,
        )
        return ((grad_keys, grad_values), grad_query)

    empty = jnp.zeros(key_rows.shape, jnp.float32)
    (grad_keys, grad_values), grad_query = lax.scan(
        one_block, (empty, empty), (grouped, grad_grouped, log_total, firsts)
    )
    return (grad_query.reshape(queries.shape), grad_keys, grad_values)


def adam(weight, first, second, gradient, rate, decay):
    first = BETA_ONE * first + (1.0 - BETA_ONE) * gradient
    second = BETA_TWO * second + (1.0 - BETA_TWO) * gradient * gradient
    direction = (
        first / (1.0 - BETA_ONE**STEP) / (jnp.sqrt(second / (1.0 - BETA_TWO**STEP)) + ADAM_EPS)
    )
    return (weight - rate * (direction + decay * weight), first, second)


class Grid:
    def __init__(self, sizes):
        self.sizes = sizes

    def index(self, axis):
        return lax.axis_index(axis)

    def rotate(self, value, axis):
        size = self.sizes[axis]
        return lax.ppermute(value, axis, [(i, (i + 1) % size) for i in range(size)])

    def swap(self, value, axis, step):
        return lax.ppermute(value, axis, [(i, i ^ step) for i in range(self.sizes[axis])])

    def total(self, value, axes):
        for axis in axes:
            step = 1
            while step < self.sizes[axis]:
                value = value + self.swap(value, axis, step)
                step *= 2
        return value

    def gather(self, shard, axes):
        held = [(shard, {})]
        for axis in axes:
            wave, found = held, list(held)
            for step in range(1, self.sizes[axis]):
                wave = [
                    (self.rotate(value, axis), {**moved, axis: step}) for value, moved in wave
                ]
                found += wave
            held = found
        return held

    def source(self, moved, axis):
        return lax.rem(lax.axis_index(axis) + self.sizes[axis] - moved.get(axis, 0), self.sizes[axis])

    def scatter(self, axis, pick):
        size = self.sizes[axis]
        place = lax.axis_index(axis)
        running = pick(lax.rem(place + size - 1, size))
        for step in range(1, size):
            arrived = self.rotate(running.astype(BF16), axis)
            running = arrived.astype(F32) + pick(lax.rem(place + 2 * size - step - 1, size)).astype(F32)
        return running


def chosen(array, index, axis):
    return lax.dynamic_index_in_dim(array, index, axis, keepdims=False)


def newton(grams):
    count, _, rows = grams.shape
    repeats = rows // MUON_ROWS
    band = jnp.arange(rows) // MUON_ROWS
    mask = band[:, None] == band[None, :]
    eye = jnp.eye(rows, dtype=F32)
    gram = jnp.where(mask, jnp.tile(grams, (1, repeats, 1)), 0.0)
    diagonal = jnp.sum(gram * eye, -1).reshape(count, repeats, MUON_ROWS)
    size = jnp.sqrt(jnp.sum(diagonal, -1, keepdims=True)) + 1e-07
    size = jnp.broadcast_to(size, diagonal.shape).reshape(count, rows, 1)
    gram = gram / (size * size)

    def times(left, right):
        return jnp.einsum("brs,bst->brt", left, right, precision=HIGHEST)

    factor = None
    for repeat in range(5):
        mixing = NEWTON[0] * eye + NEWTON[1] * gram + NEWTON[2] * times(gram, gram)
        factor = mixing if factor is None else times(mixing, factor)
        if repeat < 4:
            gram = times(mixing, times(gram, mixing))
    return factor / size


def folded_gram(part):
    count, rows, _ = part.shape
    gram = jnp.einsum("brc,bsc->brs", part, part, precision=HIGHEST)
    band = jnp.arange(rows) // MUON_ROWS
    gram = jnp.where(band[:, None] == band[None, :], gram, 0.0)
    return jnp.sum(gram.reshape(count, rows // MUON_ROWS, MUON_ROWS, rows), 1)


def orthogonal(factor, part):
    return jnp.einsum("brs,bsc->brc", factor, part, precision=HIGHEST)


def body(
    grid,
    codes_in,
    codes_out,
    pad_mask,
    text_table,
    text_index,
    attend_in,
    attend_out,
    expand_weights,
    shrink_weights,
    attend_in_momentum,
    attend_out_momentum,
    expand_momentum,
    shrink_momentum,
    embed_table,
    head_table,
    norm_params,
    embed_first,
    embed_second,
    head_first,
    head_second,
    norm_first,
    norm_second,
):
    sizes = grid.sizes
    at_z, at_x, at_y, at_c = (grid.index(axis) for axis in ("z", "x", "y", "c"))
    width = norm_params.shape[1]
    clips, frames_part, books = codes_in.shape
    inner = sizes["c"]
    group = sizes["z"] * sizes["x"]
    split = sizes["y"] * inner
    frames = frames_part * split
    own_frames = frames // inner
    rows_in, members, cols_in = attend_in.shape
    cols_out = attend_out.shape[2]
    quarters = expand_weights.shape[1] // cols_in
    table_rows = embed_table.shape[1]

    token_count = grid.total(
        jnp.sum(pad_mask.astype(F32)).reshape(1, 1), ("c", "y", "x", "z")
    )[0, 0]

    codes = jnp.stack([codes_in, codes_out, pad_mask], 0).transpose(0, 3, 1, 2)
    pieces = grid.gather(codes, ("c", "y"))
    codes = jnp.zeros((3, books, clips, sizes["y"], inner, frames_part), jnp.int32)
    for piece, moved in pieces:
        codes = lax.dynamic_update_slice(
            codes,
            piece[:, :, :, None, None],
            (0, 0, 0, grid.source(moved, "y"), grid.source(moved, "c"), 0),
        )
    codes = codes.reshape(3, books, clips, frames)
    codes_all = codes[0]
    mine = chosen(codes, at_y, 2)
    next_codes, counted = mine[1].T, mine[2].T.astype(F32)

    def dp_place(moved):
        return grid.source(moved, "z") * sizes["x"] + grid.source(moved, "x")

    table = jnp.zeros((books, group * table_rows, width), BF16)
    for piece, moved in grid.gather(embed_table.astype(BF16), ("z", "x")):
        table = lax.dynamic_update_slice(table, piece, (0, dp_place(moved) * table_rows, 0))
    at_tensor = at_y * inner + at_c
    owner = codes_all // table_rows % split
    local = codes_all // (table_rows * split) * table_rows + codes_all % table_rows
    slots = jnp.where(owner == at_tensor, local, -1)
    slots = slots.reshape(books, clips, inner, own_frames)

    def one_hot(places):
        return (places[..., None] == jnp.arange(group * table_rows)).astype(BF16)

    hot = one_hot(slots)
    partial = jnp.einsum("kyrfv,kvd->yrfd", hot, table, preferred_element_type=F32)
    both = grid.scatter("c", lambda target: chosen(partial, target, 1))
    embedded = grid.scatter("y", lambda target: chosen(both, target, 0))
    residual = embedded + sinusoid(at_c * own_frames, own_frames, width)

    def gather_rows(shard, axes):
        count, rows, cols = shard.shape
        full = jnp.zeros((count, group * rows, sizes["y"] * cols), BF16)
        for piece, moved in grid.gather(shard, axes):
            full = lax.dynamic_update_slice(
                full, piece, (0, dp_place(moved) * rows, grid.source(moved, "y") * cols)
            )
        return full

    def gather_cols(shard, axes):
        count, rows, cols = shard.shape
        full = jnp.zeros((count, sizes["y"] * rows, group * cols), BF16)
        for piece, moved in grid.gather(shard, axes):
            full = lax.dynamic_update_slice(
                full, piece, (0, grid.source(moved, "y") * rows, dp_place(moved) * cols)
            )
        return full

    turned_in = attend_in.transpose(1, 0, 2)
    weight_in = gather_rows(turned_in.astype(BF16), ("z", "x", "y"))
    cols_pack = jnp.concatenate(
        [attend_out, shrink_weights.reshape(quarters, cols_in, cols_out)], 0
    )
    weight_cols = gather_cols(cols_pack.astype(BF16), ("z", "y", "x"))
    weight_out, weight_shrink = weight_cols[:2], weight_cols[2:]
    turned_expand = expand_weights.reshape(rows_in, quarters, cols_in).transpose(1, 0, 2)
    weight_expand = gather_rows(turned_expand.astype(BF16), ("y", "z", "x"))
    head_place = []
    head = jnp.zeros((books, group * sizes["y"] * table_rows, width), BF16)
    for piece, moved in grid.gather(head_table.astype(BF16), ("x", "z", "y")):
        place = dp_place(moved) * sizes["y"] + grid.source(moved, "y")
        head = lax.dynamic_update_slice(head, piece, (0, place * table_rows, 0))
    head_index = jnp.arange(group * sizes["y"] * table_rows)
    head_ids = (head_index // table_rows * inner + at_c) * table_rows + head_index % table_rows

    def spread(rows):
        rows = rows.astype(BF16)
        full = jnp.zeros((inner,) + rows.shape, BF16)
        for piece, moved in grid.gather(rows, ("c",)):
            full = lax.dynamic_update_slice(full, piece[None], (grid.source(moved, "c"), 0, 0))
        return full.reshape(frames, width)

    def collect(partial_rows):
        parts = partial_rows.reshape(inner, own_frames, width)
        running = chosen(parts, lax.rem(at_c + inner - 1, inner), 0)
        for step in range(1, inner):
            arrived = grid.rotate(running, "c")
            running = arrived + chosen(parts, lax.rem(at_c + 2 * inner - step - 1, inner), 0)
        return running

    def heads_of(values):
        return values.reshape(values.shape[0], 1, -1, HEAD_DIM)

    def product(left, right):
        return jnp.dot(left, right, preferred_element_type=F32)

    gains = norm_params
    memory = jnp.take(text_table, chosen(text_index, at_y, 0), axis=0)

    normed_one = spread(layer_norm(residual, gains[0], gains[1]))
    triple = jnp.einsum(
        "fd,jdn->jfn", normed_one, weight_in[:3], preferred_element_type=F32
    ).astype(BF16)
    self_parts = tuple(heads_of(triple[member]) for member in range(3))
    self_mixed, self_total = attend(*self_parts, True)
    self_mixed = self_mixed[:, 0]
    residual_one = residual + collect(product(self_mixed, weight_out[0]))

    normed_two = spread(layer_norm(residual_one, gains[2], gains[3]))
    cross_q = product(normed_two, weight_in[3]).astype(BF16)
    cross_kv = jnp.einsum(
        "sd,jdn->jsn", memory, weight_in[4:6], preferred_element_type=F32
    ).astype(BF16)
    cross_parts = (heads_of(cross_q), heads_of(cross_kv[0]), heads_of(cross_kv[1]))
    cross_mixed, cross_total = attend(*cross_parts, False)
    cross_mixed = cross_mixed[:, 0]
    residual_two = residual_one + collect(product(cross_mixed, weight_out[1]))

    normed_three = spread(layer_norm(residual_two, gains[4], gains[5]))
    upper = jnp.einsum("fd,bdn->bfn", normed_three, weight_expand, preferred_element_type=F32)
    active = exact_gelu(upper).astype(BF16)
    residual_three = residual_two + collect(
        jnp.einsum("bfn,bnd->fd", active, weight_shrink, preferred_element_type=F32)
    )

    final = spread(layer_norm(residual_three, gains[6], gains[7]))
    logits = jnp.einsum("fd,kvd->kfv", final, head, preferred_element_type=F32)
    row_max = jnp.max(logits, -1)
    is_target = head_ids[None, None, :] == next_codes.T[:, :, None]
    picked = jnp.sum(jnp.where(is_target, logits, 0.0), -1)
    row_sum = jnp.sum(jnp.exp(logits - row_max[..., None]), -1)
    top = row_max
    stats = grid.gather(jnp.stack([row_max, row_sum, picked], 0), ("c",))
    for piece, _ in stats[1:]:
        top = jnp.maximum(top, piece[0])
    row_sum = sum(piece[1] * jnp.exp(piece[0] - top) for piece, _ in stats)
    picked = sum(piece[2] for piece, _ in stats)
    log_total = top + jnp.log(row_sum)
    live = counted.T
    loss_local = jnp.where(at_c == 0, jnp.sum((log_total - picked) * live), 0.0)
    grad_logits = (
        (jnp.exp(logits - log_total[..., None]) - is_target.astype(F32))
        * (live / token_count)[..., None]
    ).astype(BF16)
    grad_head = jnp.einsum("kfv,fd->kvd", grad_logits, final, preferred_element_type=F32)
    grad_final = collect(
        jnp.einsum("kfv,kvd->fd", grad_logits, head, preferred_element_type=F32)
    )

    def scatter_head(value):
        value = value.reshape(books, sizes["z"], sizes["x"], sizes["y"], table_rows, width)
        value = grid.scatter("y", lambda target: chosen(value, target, 3))
        value = grid.scatter("z", lambda target: chosen(value, target, 1))
        return grid.scatter("x", lambda target: chosen(value, target, 1))

    def scatter_rows(value, axes):
        count = value.shape[0]
        value = value.reshape(count, sizes["z"], sizes["x"], rows_in, sizes["y"], cols_in)
        dims = {"z": 1, "x": 2, "y": 4}
        for axis in axes:
            spot = dims.pop(axis)
            whole = value
            value = grid.scatter(axis, lambda target: chosen(whole, target, spot))
            dims = {name: at - (at > spot) for name, at in dims.items()}
        return value

    def scatter_cols(value, axes):
        count = value.shape[0]
        value = value.reshape(count, sizes["y"], cols_in, sizes["z"], sizes["x"], cols_out)
        dims = {"y": 1, "z": 3, "x": 4}
        for axis in axes:
            spot = dims.pop(axis)
            whole = value
            value = grid.scatter(axis, lambda target: chosen(whole, target, spot))
            dims = {name: at - (at > spot) for name, at in dims.items()}
        return value

    grad_head = scatter_head(grad_head)
    grad, gain_final, shift_final = norm_back(residual_three, gains[6], gains[7], grad_final)

    rows_grad = spread(grad)
    grad_active = jnp.einsum(
        "fd,bnd->bfn", rows_grad, weight_shrink, preferred_element_type=F32
    )
    grad_shrink = jnp.einsum("bfn,fd->bnd", active, rows_grad, preferred_element_type=F32)
    grad_upper = jax.vjp(exact_gelu, upper)[1](grad_active)[0].astype(BF16)
    grad_expand = jnp.einsum("fd,bfn->bdn", normed_three, grad_upper, preferred_element_type=F32)
    grad_normed = collect(
        jnp.einsum("bfn,bdn->fd", grad_upper, weight_expand, preferred_element_type=F32)
    )
    grad_shrink = scatter_cols(grad_shrink, ("y", "x", "z"))
    grad_expand = scatter_rows(grad_expand, ("x", "y", "z"))
    change, gain_three, shift_three = norm_back(residual_two, gains[4], gains[5], grad_normed)
    grad = grad + change

    rows_grad = spread(grad)
    grad_mixed = lax.dot_general(
        rows_grad, weight_out[1], (((1,), (1,)), ((), ())), preferred_element_type=F32
    ).astype(BF16)
    grad_cross_out = jnp.einsum("fn,fd->nd", cross_mixed, rows_grad, preferred_element_type=F32)
    grad_q, grad_k, grad_v = attend_back(*cross_parts, cross_total, heads_of(grad_mixed), False)
    grad_q = grad_q.astype(BF16).reshape(frames, -1)
    grad_kv = jnp.stack([grad_k, grad_v], 0).astype(BF16).reshape(2, memory.shape[0], -1)
    grad_cross_q = jnp.einsum("fd,fn->dn", normed_two, grad_q, preferred_element_type=F32)
    grad_cross_kv = jnp.einsum("sd,jsn->jdn", memory, grad_kv, preferred_element_type=F32)
    grad_normed = collect(
        jnp.einsum("fn,dn->fd", grad_q, weight_in[3], preferred_element_type=F32)
    )
    change, gain_two, shift_two = norm_back(residual_one, gains[2], gains[3], grad_normed)
    grad = grad + change

    rows_grad = spread(grad)
    grad_mixed = lax.dot_general(
        rows_grad, weight_out[0], (((1,), (1,)), ((), ())), preferred_element_type=F32
    ).astype(BF16)
    grad_self_out = jnp.einsum("fn,fd->nd", self_mixed, rows_grad, preferred_element_type=F32)
    grad_out = scatter_cols(jnp.stack([grad_self_out, grad_cross_out], 0), ("y", "x", "z"))
    grad_cross_in = scatter_rows(
        jnp.concatenate([grad_cross_q[None], grad_cross_kv], 0), ("x", "y", "z")
    )
    grad_q, grad_k, grad_v = attend_back(*self_parts, self_total, heads_of(grad_mixed), True)
    grad_triple = jnp.stack([grad_q, grad_k, grad_v], 0).astype(BF16).reshape(3, frames, -1)
    grad_normed = collect(
        jnp.einsum("jfn,jdn->fd", grad_triple, weight_in[:3], preferred_element_type=F32)
    )
    grad_self_in = jnp.einsum(
        "fd,jfn->jdn", normed_one, grad_triple, preferred_element_type=F32
    )
    grad_self_in = scatter_rows(grad_self_in, ("y", "x", "z"))
    change, gain_one, shift_one = norm_back(residual, gains[0], gains[1], grad_normed)
    grad = grad + change

    rows_grad = grad.astype(BF16)
    all_grad = jnp.zeros((clips, inner, own_frames, width), BF16)
    for piece, moved in grid.gather(rows_grad, ("y", "c")):
        all_grad = lax.dynamic_update_slice(
            all_grad, piece[None, None], (grid.source(moved, "y"), grid.source(moved, "c"), 0, 0)
        )
    grad_table = jnp.einsum("kyrfv,yrfd->kvd", hot, all_grad, preferred_element_type=F32)
    grad_table = grad_table.reshape(books, sizes["z"], sizes["x"], table_rows, width)
    grad_table = grid.scatter("x", lambda target, v=grad_table: chosen(v, target, 2))
    grad_table = grid.scatter("z", lambda target, v=grad_table: chosen(v, target, 1))

    norm_grads = [gain_one, shift_one, gain_two, shift_two, gain_three, shift_three]
    norm_grads = jnp.stack(norm_grads + [gain_final, shift_final], 0)
    loss_row = jnp.full((8, width), loss_local)
    summed = grid.total(jnp.concatenate([norm_grads, loss_row], 0), ("c", "y", "x", "z"))
    grad_norm, loss_sum = summed[:8], summed[8, 0]

    next_in = MOMENTUM * attend_in_momentum.transpose(1, 0, 2) + jnp.concatenate(
        [grad_self_in, grad_cross_in], 0
    )
    next_out = MOMENTUM * attend_out_momentum + grad_out
    turned_momentum = expand_momentum.reshape(rows_in, quarters, cols_in).transpose(1, 0, 2)
    next_expand = MOMENTUM * turned_momentum + grad_expand
    next_expand = next_expand.transpose(1, 0, 2).reshape(expand_weights.shape)
    next_shrink = MOMENTUM * shrink_momentum + grad_shrink.reshape(shrink_weights.shape)

    stack_rows = min(128, cols_in)
    data_blocks = jnp.concatenate(
        [next_out.reshape(-1, stack_rows, cols_out), next_shrink.reshape(-1, stack_rows, cols_out)],
        0,
    )
    tensor_grams = jnp.concatenate([folded_gram(next_in), folded_gram(next_expand[None])], 0)
    tensor_factor = newton(grid.total(tensor_grams, ("c", "y")))
    data_factor = newton(grid.total(folded_gram(data_blocks), ("x", "z")))
    ortho_in = orthogonal(tensor_factor[:members], next_in)
    ortho_expand = orthogonal(tensor_factor[members:], next_expand[None])[0]
    ortho_data = orthogonal(data_factor, data_blocks)
    count_out = next_out.size // (stack_rows * cols_out)
    ortho_out = ortho_data[:count_out].reshape(next_out.shape)
    ortho_shrink = ortho_data[count_out:].reshape(next_shrink.shape)
    attend_in_new = (turned_in * (1.0 - 0.5 * DECAY) - 0.5 * ortho_in).transpose(1, 0, 2)
    attend_out_new = attend_out * (1.0 - 1.0 * DECAY) - 1.0 * ortho_out
    expand_new = expand_weights * (1.0 - 0.5 * DECAY) - 0.5 * ortho_expand
    shrink_new = shrink_weights * (1.0 - 0.5 * DECAY) - 0.5 * ortho_shrink
    embed_new, embed_first_new, embed_second_new = adam(
        embed_table, embed_first, embed_second, grad_table, 0.1, DECAY
    )
    head_new, head_first_new, head_second_new = adam(
        head_table, head_first, head_second, grad_head, 0.03, DECAY
    )
    norm_new, norm_first_new, norm_second_new = adam(
        norm_params, norm_first, norm_second, grad_norm, 0.5, 0.0
    )
    return (
        loss_sum,
        token_count,
        attend_in_new,
        attend_out_new,
        expand_new,
        shrink_new,
        next_in.transpose(1, 0, 2),
        next_out,
        next_expand,
        next_shrink,
        embed_new,
        head_new,
        norm_new,
        embed_first_new,
        embed_second_new,
        head_first_new,
        head_second_new,
        norm_first_new,
        norm_second_new,
    )


def solution(mesh):
    n_dp, n_tensor = mesh.shape["dp"], mesh.shape["tensor"]
    sizes = {"z": n_dp // 2, "x": 2, "y": 2, "c": n_tensor // 2}
    cut = Mesh(mesh.devices.reshape(tuple(sizes.values())), tuple(sizes))
    dp, tensor = ("z", "x"), ("y", "c")
    table = P(None, dp + tensor, None)
    matrices = (P(dp, None, tensor), P(None, tensor, dp), P(dp, tensor), P(tensor, dp))
    return jax.shard_map(
        functools.partial(body, Grid(sizes)),
        mesh=cut,
        in_specs=(P(dp, tensor, None),) * 3
        + (P(), P(dp, None))
        + matrices * 2
        + (table, table, P())
        + (table,) * 4
        + (P(), P()),
        out_specs=(P(), P())
        + matrices * 2
        + (table, table, P())
        + (table,) * 4
        + (P(), P()),
        check_vma=False,
    )
```

time: 2830 us -> 1410 us (0.50)
  waiting for transfers between devices: 1930 us -> 504 us
  blocking collectives: 155 us -> 0 us
  local copies, waits for them, and re-layouts: 187 us -> 308 us
  starting transfers between devices: 3.8 us -> 109 us
  other arithmetic: 201 us -> 167 us
    reduce_scatter x10 -> x0, waiting for transfers between devices: 985 us -> none  [the longest x1 356 us: body(): lax.psum_scatter(grad_table, ('dp', 'tensor'), scatter_dimension=1, tiled...]
    ppermute x0 -> x139, waiting for transfers between devices: none -> 504 us  [the longest x124 482 us: rotate(): return lax.ppermute(value, axis, [(i, (i + 1) % size) for i in range(size)])]
    all_gather x12 -> x0, waiting for transfers between devices: 493 us -> none  [the longest x1 113 us: body(): lax.all_gather(embed_table.astype(jnp.bfloat16), ('dp', 'tensor'), axis=1...]
    psum x10 -> x0, waiting for transfers between devices: 392 us -> none  [the longest x5 256 us: data_total(): lax.psum(as_sent(grams), 'dp')]
    psum x7 -> x0, blocking collectives: 155 us -> none  [the longest x1 59.2 us: body(): lax.psum((loss_local, jnp.stack(grad_gains + [gain_final, shift_final], 0...]
    ppermute x0 -> x139, starting transfers between devices: none -> 109 us  [the longest x124 92.3 us: rotate(): return lax.ppermute(value, axis, [(i, (i + 1) % size) for i in range(size)])]
    dynamic_update_slice x0 -> x83, local copies, waits for them, and re-layouts: none -> 72 us  [the longest x15 17.9 us: body(): head = lax.dynamic_update_slice(head, piece, (0, place * table_rows, 0))]
    unnamed x36 -> x0, waiting for transfers between devices: 64.1 us -> none
  transfers between devices with their start and end apart: 34 -> 139, of which waited for: 30 -> 75; matrix products, arithmetic and copies ran while one was open for 18% -> 45% of each run, Pallas kernels for 0% -> 0%
where the time goes in v1:
time: 1410 us; the launch traced here: 1400 us
  waiting for transfers between devices  504 us (36%)
  local copies, waits for them, and re-layouts  308 us (22%)
  matrix products  299 us (21%)
  other arithmetic  167 us (12%)
  starting transfers between devices  109 us (8%)
    ppermute x124, waiting for transfers between devices, rotate(): return lax.ppermute(value, axis, [(i, (i + 1) % size) for i in range(size)])  482 us
    ppermute x124, starting transfers between devices, rotate(): return lax.ppermute(value, axis, [(i, (i + 1) % size) for i in range(size)])  92.3 us
    unnamed x354, local copies, waits for them, and re-layouts  54.3 us
    dynamic_slice x6, local copies, waits for them, and re-layouts, chosen(): return lax.dynamic_index_in_dim(array, index, axis, keepdims=False)  42.4 us
    dot_general x8, matrix products, scores_of(): jnp.einsum('qchd,kchd->chqk', part, key_rows, preferred_element_type=jnp....  31.3 us
    add x17, other arithmetic, scatter(): arrived.astype(F32)  30.4 us
  transfers between devices with their start and end apart: 139, of which 75 were waited for; matrix products, arithmetic and copies ran while one was open for 45% of the time, Pallas kernels for 0%

profile of v1, /device:TPU:0, one launch (start us, length us, event | category | flops | bytes accessed | tf_op | source)
XLA Modules:
  0.0 1397.7 jit_solution(10562774529746879042)
XLA Ops:
  7.1 14.1 %collective-permute-done.3 = bf16[4,64,1024]{2,1,0:T(8,128)(2,1)} collective-permute-done((bf16[4,64,1024]{2,1,0:T(8,128)(2,1)S(1)}, bf16[4,64,1024]{2,1,0:T(8,128)(2,1)}, u32[]{:S(2)}, u32[]{:S(2)}) %collective-permute-start.3) | collective-permute-done | bytes 524320 | tf_op jit(solution)/shard_map/ppermute | solution.py:140
  58.0 9.9 collective-permute-done.8
  68.8 7.7 collective-permute-done.9
  77.3 11.2 fusion.125
  101.6 6.9 collective-permute-done.44
  147.9 6.8 collective-permute-done.17
  173.2 6.8 collective-permute-done.52
  181.6 6.8 collective-permute-done.53
  190.0 6.8 collective-permute-done.54
  198.6 6.7 collective-permute-done.55
  207.0 6.8 collective-permute-done.56
  234.8 7.0 collective-permute-done.22
  251.1 7.6 collective-permute-done.25
  266.0 6.4 convert_bitcast_fusion
  279.8 32.3 %while.54 = (s32[]{:T(128)}, bf16[2,512,1,8,64]{1,4,3,2,0:T(8,128)(2,1)}, f32[2,1,8,512]{3,2,1,0:T(8,128)S(1)}, s32[2]{0:T(128)S(1)}, bf16[2,512,1,8,64]{1,4,3,2...) while((s32[]{:T(128)}, ...), condition=%wide.region_5.6_spmd, body=%wide.region_2.5_spmd.sunk | while | flops 1124856320 | bytes 64098480 | solution.py:76
  362.7 14.0 collective-permute-done.63
  396.8 6.1 collective-permute-done.67
  434.8 22.5 %fusion.79 = (f32[4,1024,512]{1,2,0:T(8,128)}, f32[4,512,1024]{2,1,0:T(8,128)S(1)}) fusion(bf16[4,1024,512]{2,1,0:T(8,128)(2,1)S(1)} %constant_dynamic-update-slice_fusion, bf16[1024,1024,1]{1,0,2:T(8,128)(2,1)S(1)} %bitcast.1074), kind=kOutput, calls=%fused_computation.114 | convolution fusion | flops 4424990720 | bytes 23068672 | tf_op jit(solution)/shard_map/fd,bdn->bfn/dot_general | solution.py:375
  457.3 11.7 fusion.119
  477.4 13.4 collective-permute-done.30
  492.5 9.6 collective-permute-done.31
  515.6 8.4 collective-permute-done.33
  530.5 11.3 collective-permute-done.34
  551.2 10.4 collective-permute-done.40
  562.4 10.4 collective-permute-done.41
  573.6 9.1 collective-permute-done.42
  583.7 12.1 bitcast_reduce_fusion
  633.4 17.1 %fusion.83 = f32[1024,1024,1]{1,0,2:T(8,128)S(1)} fusion(bf16[4,1024,1024]{2,1,0:T(8,128)(2,1)} %constant_dynamic-update-slice_fusion.32, f32[4,1024,1024]{2,1,0:T(8,128)} %copy-done.18, f32[4,1024]{1,0:T(4,128)S(1)} %get-tuple-element.519, f32[4,1024]{1,0:T(4,128)S(1)} %get-tuple-element.454, s32[4,1024]{1,0:T(4,128)S(1)} %bitcast.1096, s32[1024]{0:T(1024)S(1)} %fusion.251), kind=kOutput, calls=%fused_computation.118 | convolution fusion | flops 8615100416 | bytes 29413376 | tf_op jit(solution)/shard_map/kfv,kvd->fd/dot_general | solution.py:402
  652.7 20.9 %fusion.82 = bf16[4,512,1024]{2,1,0:T(8,128)(2,1)} fusion(f32[4,512,1024]{2,1,0:T(8,128)} %copy-done.47), kind=kLoop, calls=%fused_computation.117 | loop fusion | flops 136314880 | bytes 12582912 | tf_op jit(solution)/shard_map/convert_element_type | solution.py:376
  673.6 6.4 multiply_convert_fusion.2
  686.2 11.5 fusion.312
  708.3 11.7 fusion.90
  733.4 8.3 fusion.300
  741.7 6.7 convolution_bitcast_fusion.1
  748.3 12.1 reshape.965
  764.8 9.1 constant_dynamic-slice_fusion.4
  773.9 10.5 copy.245
  784.4 9.6 constant_dynamic-slice_fusion.3
  794.1 10.9 copy.194
  813.0 6.2 multiply_reduce_fusion.4
  822.6 17.0 %collective-permute-done.119 = bf16[4,256,4,2,128]{4,1,3,2,0:T(8,128)(2,1)} collective-permute-done((bf16[4,256,4,2,128]{4,1,3,2,0:T(8,128)(2,1)}, bf16[4,256,4,2,128]{4,1,3,2,0:T(8,128)(2,1)}, u32[]{:S(2)}, u32[]{:S(2)}) %collective-permute-start.119) | collective-permute-done | bytes 2097184 | tf_op jit(solution)/shard_map/ppermute | solution.py:140
  844.7 9.1 collective-permute-done.107
  888.7 6.6 concatenate.37
  895.3 7.3 copy.191
  933.2 24.9 %collective-permute-done.122 = bf16[4,256,128]{2,1,0:T(8,128)(2,1)S(1)} collective-permute-done((bf16[4,256,128]{2,1,0:T(8,128)(2,1)S(1)}, bf16[4,256,128]{2,1,0:T(8,128)(2,1)S(1)}, u32[]{:S(2)}, u32[]{:S(2)}) %collective-permute-start.122) | collective-permute-done | bytes 262176 | tf_op jit(solution)/shard_map/ppermute | solution.py:140
  981.7 12.0 collective-permute-done.103
  1022.0 82.4 %while.57 = (s32[]{:T(128)}, f32[1024,1,8,64]{0,3,2,1:T(8,128)}, f32[1024,1,8,64]{0,3,2,1:T(8,128)}, bf16[2,512,1,8,64]{1,4,3,2,0:T(8,128)(2,1)}, bf16[2,512,1,8...) while((s32[]{:T(128)}, f32[1024,1,8,64]{0,3,2,1:T(8,128)}, ...), condition=%wide.region_31.32_spmd.clone, body=%wide.region_29.31_spmd.clone.sunk | while | flops 2725507584 | bytes 212947344 | solution.py:116
  1027.6 10.9 multiply_reduce_fusion.19
  1038.5 9.4 multiply_convert_fusion.6
  1048.0 8.9 bitcast_add_fusion.51
  1068.4 10.9 multiply_reduce_fusion.19
  1079.3 9.4 multiply_convert_fusion.6
  1088.8 9.5 bitcast_add_fusion.51
  1125.9 8.6 convolution_bitcast_fusion.2
  1134.5 9.1 reshape.962
  1174.9 10.3 collective-permute-done.97
  1228.7 11.0 collective-permute-done.96
  1260.3 6.6 collective-permute-done.100
  1267.8 6.7 collective-permute-done.101
  1286.5 14.3 %fusion.77 = f32[4,512,1024,1,1]{2,1,4,0,3:T(8,128)S(1)} fusion(s32[4,2,2,512]{3,1,0,2:T(2,128)S(1)} %copy-done.151, bf16[2,2,512,1024]{3,2,0,1:T(8,128)(2,1)} %bitcast_dynamic-update-slice_fusion.2), kind=kOutput, calls=%fused_computation.110 | convolution fusion | flops 8594128896 | bytes 12615680 | tf_op jit(solution)/shard_map/kyrfv,yrfd->kvd/dot_general | solution.py:494
  1307.7 41.6 %collective-permute-done.130 = bf16[4,4,64,1024]{3,2,0,1:T(8,128)(2,1)S(1)} collective-permute-done((bf16[4,4,64,1024]{3,2,0,1:T(8,128)(2,1)S(1)}, bf16[4,4,64,1024]{3,2,0,1:T(8,128)(2,1)S(1)}, u32[]{:S(2)}, u32[]{:S(2)}) %collective-permute-start.130) | collective-permute-done | bytes 2097184 | tf_op jit(solution)/shard_map/ppermute | solution.py:140
  1352.2 13.5 collective-permute-done.131
  1367.7 12.6 collective-permute-done.132
  1383.8 10.3 collective-permute-done.133
  (1071 shorter events, 721.8 us)
Async XLA Ops:
  22.8 31.4 %collective-permute-start.6 = (bf16[4,64,1024]{2,1,0:T(8,128)(2,1)S(1)}, bf16[4,64,1024]{2,1,0:T(8,128)(2,1)}, u32[]{:S(2)}, u32[]{:S(2)}) collective-permute-start(bf16[4,64,1024]{2,1,0:T(8,128)(2,1)S(1)} %get-tuple-element.491), channel_id=1, source_target_pairs={{0,4},{4,0},{1,5},{5,1},{2,6},{6,2},{3,7},{7,3},{8,12},{12,8},{9,1... | collective-permute-start | bytes 1572872 | tf_op jit(solution)/shard_map/ppermute | solution.py:140
  28.9 97.0 %collective-permute-start.46 = (bf16[6,256,128]{2,1,0:T(8,128)(2,1)}, bf16[6,256,128]{2,1,0:T(8,128)(2,1)}, u32[]{:S(2)}, u32[]{:S(2)}) collective-permute-start(bf16[6,256,128]{2,1,0:T(8,128)(2,1)} %get-tuple-element.503), channel_id=1, source_target_pairs={{0,2},{2,0},{1,3},{3,1},{4,6},{6,4},{5,7},{7,5},{8,10},{10,8},{9,1... | collective-permute-start | bytes 1179656 | tf_op jit(solution)/shard_map/ppermute | solution.py:140
  43.1 24.8 %collective-permute-start.8 = (bf16[4,64,1024]{2,1,0:T(8,128)(2,1)}, bf16[4,64,1024]{2,1,0:T(8,128)(2,1)S(1)}, u32[]{:S(2)}, u32[]{:S(2)}) collective-permute-start(bf16[4,64,1024]{2,1,0:T(8,128)(2,1)} %collective-permute-done.4), channel_id=1, source_target_pairs={{0,4},{4,0},{1,5},{5,1},{2,6},{6,2},{3,7},{7,3},{8,12},{12,8},{9,1... | collective-permute-start | bytes 1572872 | tf_op jit(solution)/shard_map/ppermute | solution.py:140
  50.6 25.9 %collective-permute-start.9 = (bf16[4,64,1024]{2,1,0:T(8,128)(2,1)S(1)}, bf16[4,64,1024]{2,1,0:T(8,128)(2,1)S(1)}, u32[]{:S(2)}, u32[]{:S(2)}) collective-permute-start(bf16[4,64,1024]{2,1,0:T(8,128)(2,1)S(1)} %collective-permute-done.5), channel_id=1, source_target_pairs={{0,4},{4,0},{1,5},{5,1},{2,6},{6,2},{3,7},{7,3},{8,12},{12,8},{9,1... | collective-permute-start | bytes 1572872 | tf_op jit(solution)/shard_map/ppermute | solution.py:140
  54.3 39.9 %collective-permute-start.43 = (bf16[6,256,128]{2,1,0:T(8,128)(2,1)}, bf16[6,256,128]{2,1,0:T(8,128)(2,1)}, u32[]{:S(2)}, u32[]{:S(2)}) collective-permute-start(bf16[6,256,128]{2,1,0:T(8,128)(2,1)} %get-tuple-element.503), channel_id=1, source_target_pairs={{0,8},{8,16},{16,24},{24,0},{1,9},{9,17},{17,25},{25,1},{2,10},{10... | collective-permute-start | bytes 1179656 | tf_op jit(solution)/shard_map/ppermute | solution.py:140
  56.7 42.7 %collective-permute-start.12 = (bf16[6,128,256]{1,2,0:T(8,128)(2,1)S(1)}, bf16[6,128,256]{1,2,0:T(8,128)(2,1)S(1)}, u32[]{:S(2)}, u32[]{:S(2)}) collective-permute-start(bf16[6,128,256]{1,2,0:T(8,128)(2,1)S(1)} %bitcast.1083), channel_id=1, source_target_pairs={{0,8},{8,16},{16,24},{24,0},{1,9},{9,17},{17,25},{25,1},{2,10},{10... | collective-permute-start | bytes 1179656 | tf_op jit(solution)/shard_map/ppermute | solution.py:140
  93.5 62.8 %collective-permute-start.10 = (bf16[2,512,1024]{2,1,0:T(8,128)(2,1)}, bf16[2,512,1024]{2,1,0:T(8,128)(2,1)}, u32[]{:S(2)}, u32[]{:S(2)}) collective-permute-start(bf16[2,512,1024]{2,1,0:T(8,128)(2,1)} %fusion.135), channel_id=1, source_target_pairs={{0,1},{1,0},{2,3},{3,2},{4,5},{5,4},{6,7},{7,6},{8,9},{9,8},{10,11... | collective-permute-start | bytes 6291464 | tf_op jit(solution)/shard_map/ppermute | solution.py:140
  101.0 27.5 %collective-permute-start.47 = (bf16[6,256,128]{2,1,0:T(8,128)(2,1)}, bf16[6,256,128]{2,1,0:T(8,128)(2,1)S(1)}, u32[]{:S(2)}, u32[]{:S(2)}) collective-permute-start(bf16[6,256,128]{2,1,0:T(8,128)(2,1)} %collective-permute-done.43), channel_id=1, source_target_pairs={{0,2},{2,0},{1,3},{3,1},{4,6},{6,4},{5,7},{7,5},{8,10},{10,8},{9,1... | collective-permute-start | bytes 1179656 | tf_op jit(solution)/shard_map/ppermute | solution.py:140
  130.8 24.0 %collective-permute-start.17 = (bf16[6,128,256]{1,2,0:T(8,128)(2,1)}, bf16[6,128,256]{1,2,0:T(8,128)(2,1)S(1)}, u32[]{:S(2)}, u32[]{:S(2)}) collective-permute-start(bf16[6,128,256]{1,2,0:T(8,128)(2,1)} %collective-permute-done.13), channel_id=1, source_target_pairs={{0,4},{4,0},{1,5},{5,1},{2,6},{6,2},{3,7},{7,3},{8,12},{12,8},{9,1... | collective-permute-start | bytes 1179656 | tf_op jit(solution)/shard_map/ppermute | solution.py:140
  138.0 30.0 %collective-permute-start.50 = (bf16[6,256,128]{2,1,0:T(8,128)(2,1)}, bf16[6,256,128]{2,1,0:T(8,128)(2,1)S(1)}, u32[]{:S(2)}, u32[]{:S(2)}) collective-permute-start(bf16[6,256,128]{2,1,0:T(8,128)(2,1)} %get-tuple-element.503), channel_id=1, source_target_pairs={{0,4},{4,0},{1,5},{5,1},{2,6},{6,2},{3,7},{7,3},{8,12},{12,8},{9,1... | collective-permute-start | bytes 1179656 | tf_op jit(solution)/shard_map/ppermute | solution.py:140
  139.4 32.2 %collective-permute-start.51 = (bf16[6,256,128]{2,1,0:T(8,128)(2,1)}, bf16[6,256,128]{2,1,0:T(8,128)(2,1)S(1)}, u32[]{:S(2)}, u32[]{:S(2)}) collective-permute-start(bf16[6,256,128]{2,1,0:T(8,128)(2,1)} %collective-permute-done.43), channel_id=1, source_target_pairs={{0,4},{4,0},{1,5},{5,1},{2,6},{6,2},{3,7},{7,3},{8,12},{12,8},{9,1... | collective-permute-start | bytes 1179656 | tf_op jit(solution)/shard_map/ppermute | solution.py:140
  146.3 33.7 %collective-permute-start.52 = (bf16[6,256,128]{2,1,0:T(8,128)(2,1)}, bf16[6,256,128]{2,1,0:T(8,128)(2,1)S(1)}, u32[]{:S(2)}, u32[]{:S(2)}) collective-permute-start(bf16[6,256,128]{2,1,0:T(8,128)(2,1)} %collective-permute-done.44), channel_id=1, source_target_pairs={{0,4},{4,0},{1,5},{5,1},{2,6},{6,2},{3,7},{7,3},{8,12},{12,8},{9,1... | collective-permute-start | bytes 1179656 | tf_op jit(solution)/shard_map/ppermute | solution.py:140
  154.7 33.7 %collective-permute-start.53 = (bf16[6,256,128]{2,1,0:T(8,128)(2,1)S(1)}, bf16[6,256,128]{2,1,0:T(8,128)(2,1)S(1)}, u32[]{:S(2)}, u32[]{:S(2)}) collective-permute-start(bf16[6,256,128]{2,1,0:T(8,128)(2,1)S(1)} %collective-permute-done.45), channel_id=1, source_target_pairs={{0,4},{4,0},{1,5},{5,1},{2,6},{6,2},{3,7},{7,3},{8,12},{12,8},{9,1... | collective-permute-start | bytes 1179656 | tf_op jit(solution)/shard_map/ppermute | solution.py:140
  165.6 56.9 %collective-permute-start.11 = (bf16[512,1024]{1,0:T(8,128)(2,1)S(1)}, bf16[512,1024]{1,0:T(8,128)(2,1)S(1)}, u32[]{:S(2)}, u32[]{:S(2)}) collective-permute-start(bf16[512,1024]{1,0:T(8,128)(2,1)S(1)} %fusion.167), channel_id=1, source_target_pairs={{0,2},{2,0},{1,3},{3,1},{4,6},{6,4},{5,7},{7,5},{8,10},{10,8},{9,1... | collective-permute-start | bytes 3145736 | tf_op jit(solution)/shard_map/ppermute | solution.py:140
  168.0 28.9 %collective-permute-start.54 = (bf16[6,256,128]{2,1,0:T(8,128)(2,1)}, bf16[6,256,128]{2,1,0:T(8,128)(2,1)S(1)}, u32[]{:S(2)}, u32[]{:S(2)}) collective-permute-start(bf16[6,256,128]{2,1,0:T(8,128)(2,1)} %collective-permute-done.46), channel_id=1, source_target_pairs={{0,4},{4,0},{1,5},{5,1},{2,6},{6,2},{3,7},{7,3},{8,12},{12,8},{9,1... | collective-permute-start | bytes 1179656 | tf_op jit(solution)/shard_map/ppermute | solution.py:140
  171.6 33.7 %collective-permute-start.55 = (bf16[6,256,128]{2,1,0:T(8,128)(2,1)S(1)}, bf16[6,256,128]{2,1,0:T(8,128)(2,1)S(1)}, u32[]{:S(2)}, u32[]{:S(2)}) collective-permute-start(bf16[6,256,128]{2,1,0:T(8,128)(2,1)S(1)} %collective-permute-done.47), channel_id=1, source_target_pairs={{0,4},{4,0},{1,5},{5,1},{2,6},{6,2},{3,7},{7,3},{8,12},{12,8},{9,1... | collective-permute-start | bytes 1179656 | tf_op jit(solution)/shard_map/ppermute | solution.py:140
  180.0 33.7 %collective-permute-start.56 = (bf16[6,256,128]{2,1,0:T(8,128)(2,1)S(1)}, bf16[6,256,128]{2,1,0:T(8,128)(2,1)S(1)}, u32[]{:S(2)}, u32[]{:S(2)}) collective-permute-start(bf16[6,256,128]{2,1,0:T(8,128)(2,1)S(1)} %collective-permute-done.48), channel_id=1, source_target_pairs={{0,4},{4,0},{1,5},{5,1},{2,6},{6,2},{3,7},{7,3},{8,12},{12,8},{9,1... | collective-permute-start | bytes 1179656 | tf_op jit(solution)/shard_map/ppermute | solution.py:140
  188.5 32.6 %collective-permute-start.18 = (bf16[6,128,256]{1,2,0:T(8,128)(2,1)S(1)}, bf16[6,128,256]{1,2,0:T(8,128)(2,1)S(1)}, u32[]{:S(2)}, u32[]{:S(2)}) collective-permute-start(bf16[6,128,256]{1,2,0:T(8,128)(2,1)S(1)} %collective-permute-done.14), channel_id=1, source_target_pairs={{0,4},{4,0},{1,5},{5,1},{2,6},{6,2},{3,7},{7,3},{8,12},{12,8},{9,1... | collective-permute-start | bytes 1179656 | tf_op jit(solution)/shard_map/ppermute | solution.py:140
  196.9 28.9 %collective-permute-start.19 = (bf16[6,128,256]{1,2,0:T(8,128)(2,1)S(1)}, bf16[6,128,256]{1,2,0:T(8,128)(2,1)S(1)}, u32[]{:S(2)}, u32[]{:S(2)}) collective-permute-start(bf16[6,128,256]{1,2,0:T(8,128)(2,1)S(1)} %bitcast.1085), channel_id=1, source_target_pairs={{0,2},{2,0},{1,3},{3,1},{4,6},{6,4},{5,7},{7,5},{8,10},{10,8},{9,1... | collective-permute-start | bytes 1179656 | tf_op jit(solution)/shard_map/ppermute | solution.py:140
  205.3 37.9 %collective-permute-start.23 = (bf16[6,128,256]{1,2,0:T(8,128)(2,1)S(1)}, bf16[6,128,256]{1,2,0:T(8,128)(2,1)S(1)}, u32[]{:S(2)}, u32[]{:S(2)}) collective-permute-start(bf16[6,128,256]{1,2,0:T(8,128)(2,1)S(1)} %collective-permute-done.15), channel_id=1, source_target_pairs={{0,2},{2,0},{1,3},{3,1},{4,6},{6,4},{5,7},{7,5},{8,10},{10,8},{9,1... | collective-permute-start | bytes 1179656 | tf_op jit(solution)/shard_map/ppermute | solution.py:140
  225.8 40.1 %collective-permute-start.27 = (bf16[512,1024]{1,0:T(8,128)(2,1)S(1)}, bf16[512,1024]{1,0:T(8,128)(2,1)S(1)}, u32[]{:S(2)}, u32[]{:S(2)}) collective-permute-start(bf16[512,1024]{1,0:T(8,128)(2,1)S(1)} %get-tuple-element.487), channel_id=1, source_target_pairs={{0,1},{1,0},{2,3},{3,2},{4,5},{5,4},{6,7},{7,6},{8,9},{9,8},{10,11... | collective-permute-start | bytes 3145736 | tf_op jit(solution)/shard_map/ppermute | solution.py:140
  233.3 25.3 %collective-permute-start.25 = (bf16[6,128,256]{1,2,0:T(8,128)(2,1)S(1)}, bf16[6,128,256]{1,2,0:T(8,128)(2,1)S(1)}, u32[]{:S(2)}, u32[]{:S(2)}) collective-permute-start(bf16[6,128,256]{1,2,0:T(8,128)(2,1)S(1)} %collective-permute-done.17), channel_id=1, source_target_pairs={{0,2},{2,0},{1,3},{3,1},{4,6},{6,4},{5,7},{7,5},{8,10},{10,8},{9,1... | collective-permute-start | bytes 1179656 | tf_op jit(solution)/shard_map/ppermute | solution.py:140
  346.8 46.6 %collective-permute-start.60 = (f32[512,1024]{1,0:T(8,128)}, f32[512,1024]{1,0:T(8,128)}, u32[]{:S(2)}, u32[]{:S(2)}) collective-permute-start(f32[512,1024]{1,0:T(8,128)} %dynamic-slice_bitcast_fusion.7), channel_id=1, source_target_pairs={{0,1},{1,0},{2,3},{3,2},{4,5},{5,4},{6,7},{7,6},{8,9},{9,8},{10,11... | collective-permute-start | bytes 6291464 | tf_op jit(solution)/shard_map/ppermute | solution.py:140
  349.1 53.9 %collective-permute-start.68 = (bf16[4,128,256]{2,1,0:T(8,128)(2,1)}, bf16[4,128,256]{2,1,0:T(8,128)(2,1)}, u32[]{:S(2)}, u32[]{:S(2)}) collective-permute-start(bf16[4,128,256]{2,1,0:T(8,128)(2,1)} %bitcast.942), channel_id=1, source_target_pairs={{0,4},{4,0},{1,5},{5,1},{2,6},{6,2},{3,7},{7,3},{8,12},{12,8},{9,1... | collective-permute-start | bytes 786440 | tf_op jit(solution)/shard_map/ppermute | solution.py:140
  352.0 122.7 %collective-permute-start.29 = (bf16[4,64,1024]{2,1,0:T(8,128)(2,1)S(1)}, bf16[4,64,1024]{2,1,0:T(8,128)(2,1)}, u32[]{:S(2)}, u32[]{:S(2)}) collective-permute-start(bf16[4,64,1024]{2,1,0:T(8,128)(2,1)S(1)} %get-tuple-element.477), channel_id=1, source_target_pairs={{0,8},{8,16},{16,24},{24,0},{1,9},{9,17},{17,25},{25,1},{2,10},{10... | collective-permute-start | bytes 1572872 | tf_op jit(solution)/shard_map/ppermute | solution.py:140
  402.9 31.7 %collective-permute-start.76 = (bf16[512,1024]{1,0:T(8,128)(2,1)S(1)}, bf16[512,1024]{1,0:T(8,128)(2,1)S(1)}, u32[]{:S(2)}, u32[]{:S(2)}) collective-permute-start(bf16[512,1024]{1,0:T(8,128)(2,1)S(1)} %get-tuple-element.479), channel_id=1, source_target_pairs={{0,1},{1,0},{2,3},{3,2},{4,5},{5,4},{6,7},{7,6},{8,9},{9,8},{10,11... | collective-permute-start | bytes 3145736 | tf_op jit(solution)/shard_map/ppermute | solution.py:140
  423.4 50.6 %collective-permute-start.28 = (bf16[4,64,1024]{2,1,0:T(8,128)(2,1)S(1)}, bf16[4,64,1024]{2,1,0:T(8,128)(2,1)}, u32[]{:S(2)}, u32[]{:S(2)}) collective-permute-start(bf16[4,64,1024]{2,1,0:T(8,128)(2,1)S(1)} %get-tuple-element.477), channel_id=1, source_target_pairs={{0,4},{4,0},{1,5},{5,1},{2,6},{6,2},{3,7},{7,3},{8,12},{12,8},{9,1... | collective-permute-start | bytes 1572872 | tf_op jit(solution)/shard_map/ppermute | solution.py:140
  429.0 101.1 %collective-permute-start.35 = (bf16[4,64,1024]{2,1,0:T(8,128)(2,1)S(1)}, bf16[4,64,1024]{2,1,0:T(8,128)(2,1)}, u32[]{:S(2)}, u32[]{:S(2)}) collective-permute-start(bf16[4,64,1024]{2,1,0:T(8,128)(2,1)S(1)} %get-tuple-element.477), channel_id=1, source_target_pairs={{0,2},{2,0},{1,3},{3,1},{4,6},{6,4},{5,7},{7,5},{8,10},{10,8},{9,1... | collective-permute-start | bytes 1572872 | tf_op jit(solution)/shard_map/ppermute | solution.py:140
  472.6 53.9 %collective-permute-start.77 = (f32[512,1024]{1,0:T(8,128)}, f32[512,1024]{1,0:T(8,128)}, u32[]{:S(2)}, u32[]{:S(2)}) collective-permute-start(f32[512,1024]{1,0:T(8,128)} %dynamic-slice_bitcast_fusion.6), channel_id=1, source_target_pairs={{0,1},{1,0},{2,3},{3,2},{4,5},{5,4},{6,7},{7,6},{8,9},{9,8},{10,11... | collective-permute-start | bytes 6291464 | tf_op jit(solution)/shard_map/ppermute | solution.py:140
  474.7 27.4 %collective-permute-start.31 = (bf16[4,64,1024]{2,1,0:T(8,128)(2,1)}, bf16[4,64,1024]{2,1,0:T(8,128)(2,1)}, u32[]{:S(2)}, u32[]{:S(2)}) collective-permute-start(bf16[4,64,1024]{2,1,0:T(8,128)(2,1)} %collective-permute-done.29), channel_id=1, source_target_pairs={{0,8},{8,16},{16,24},{24,0},{1,9},{9,17},{17,25},{25,1},{2,10},{10... | collective-permute-start | bytes 1572872 | tf_op jit(solution)/shard_map/ppermute | solution.py:140
  490.9 51.9 %collective-permute-start.37 = (bf16[4,64,1024]{2,1,0:T(8,128)(2,1)}, bf16[4,64,1024]{2,1,0:T(8,128)(2,1)S(1)}, u32[]{:S(2)}, u32[]{:S(2)}) collective-permute-start(bf16[4,64,1024]{2,1,0:T(8,128)(2,1)} %collective-permute-done.29), channel_id=1, source_target_pairs={{0,2},{2,0},{1,3},{3,1},{4,6},{6,4},{5,7},{7,5},{8,10},{10,8},{9,1... | collective-permute-start | bytes 1572872 | tf_op jit(solution)/shard_map/ppermute | solution.py:140
  513.2 31.9 %collective-permute-start.36 = (bf16[4,64,1024]{2,1,0:T(8,128)(2,1)}, bf16[4,64,1024]{2,1,0:T(8,128)(2,1)S(1)}, u32[]{:S(2)}, u32[]{:S(2)}) collective-permute-start(bf16[4,64,1024]{2,1,0:T(8,128)(2,1)} %collective-permute-done.28), channel_id=1, source_target_pairs={{0,2},{2,0},{1,3},{3,1},{4,6},{6,4},{5,7},{7,5},{8,10},{10,8},{9,1... | collective-permute-start | bytes 1572872 | tf_op jit(solution)/shard_map/ppermute | solution.py:140
  541.9 41.7 %collective-permute-start.78 = (bf16[512,1024]{1,0:T(8,128)(2,1)S(1)}, bf16[512,1024]{1,0:T(8,128)(2,1)S(1)}, u32[]{:S(2)}, u32[]{:S(2)}) collective-permute-start(bf16[512,1024]{1,0:T(8,128)(2,1)S(1)} %get-tuple-element.473), channel_id=1, source_target_pairs={{0,1},{1,0},{2,3},{3,2},{4,5},{5,4},{6,7},{7,6},{8,9},{9,8},{10,11... | collective-permute-start | bytes 3145736 | tf_op jit(solution)/shard_map/ppermute | solution.py:140
  545.1 27.7 %collective-permute-start.41 = (bf16[4,64,1024]{2,1,0:T(8,128)(2,1)S(1)}, bf16[4,64,1024]{2,1,0:T(8,128)(2,1)S(1)}, u32[]{:S(2)}, u32[]{:S(2)}) collective-permute-start(bf16[4,64,1024]{2,1,0:T(8,128)(2,1)S(1)} %collective-permute-done.33), channel_id=1, source_target_pairs={{0,2},{2,0},{1,3},{3,1},{4,6},{6,4},{5,7},{7,5},{8,10},{10,8},{9,1... | collective-permute-start | bytes 1572872 | tf_op jit(solution)/shard_map/ppermute | solution.py:140
  547.5 35.3 %collective-permute-start.42 = (bf16[4,64,1024]{2,1,0:T(8,128)(2,1)S(1)}, bf16[4,64,1024]{2,1,0:T(8,128)(2,1)S(1)}, u32[]{:S(2)}, u32[]{:S(2)}) collective-permute-start(bf16[4,64,1024]{2,1,0:T(8,128)(2,1)S(1)} %collective-permute-done.34), channel_id=1, source_target_pairs={{0,2},{2,0},{1,3},{3,1},{4,6},{6,4},{5,7},{7,5},{8,10},{10,8},{9,1... | collective-permute-start | bytes 1572872 | tf_op jit(solution)/shard_map/ppermute | solution.py:140
  550.3 52.0 %collective-permute-start.80 = (f32[1,1]{1,0:T(1,128)}, f32[1,1]{1,0:T(1,128)}, u32[]{:S(2)}, u32[]{:S(2)}) collective-permute-start(f32[1,1]{1,0:T(1,128)} %bitcast.92), channel_id=1, source_target_pairs={{0,1},{1,0},{2,3},{3,2},{4,5},{5,4},{6,7},{7,6},{8,9},{9,8},{10,11... | collective-permute-start | bytes 20 | tf_op jit(solution)/shard_map/ppermute | solution.py:143
  601.6 31.2 %collective-permute-start.79 = (f32[3,4,1024]{2,1,0:T(4,128)S(1)}, f32[3,4,1024]{2,1,0:T(4,128)S(1)}, u32[]{:S(2)}, u32[]{:S(2)}) collective-permute-start(f32[3,4,1024]{2,1,0:T(4,128)S(1)} %pad_maximum_fusion.7), channel_id=1, source_target_pairs={{0,1},{1,0},{2,3},{3,2},{4,5},{5,4},{6,7},{7,6},{8,9},{9,8},{10,11... | collective-permute-start | bytes 147464 | tf_op jit(solution)/shard_map/ppermute | solution.py:140
  650.7 29.3 %collective-permute-start.85 = (f32[512,1024]{1,0:T(8,128)S(1)}, f32[512,1024]{1,0:T(8,128)S(1)}, u32[]{:S(2)}, u32[]{:S(2)}) collective-permute-start(f32[512,1024]{1,0:T(8,128)S(1)} %dynamic-slice_bitcast_fusion.5), channel_id=1, source_target_pairs={{0,1},{1,0},{2,3},{3,2},{4,5},{5,4},{6,7},{7,6},{8,9},{9,8},{10,11... | collective-permute-start | bytes 6291464 | tf_op jit(solution)/shard_map/ppermute | solution.py:140
  703.8 102.9 %collective-permute-start.134 = (bf16[4,4,2,64,1024]{4,3,2,1,0:T(8,128)(2,1)}, bf16[4,4,2,64,1024]{4,3,2,1,0:T(8,128)(2,1)}, u32[]{:S(2)}, u32[]{:S(2)}) collective-permute-start(bf16[4,4,2,64,1024]{4,3,2,1,0:T(8,128)(2,1)} %fusion.118), channel_id=1, source_target_pairs={{0,2},{2,0},{1,3},{3,1},{4,6},{6,4},{5,7},{7,5},{8,10},{10,8},{9,1... | collective-permute-start | bytes 12582920 | tf_op jit(solution)/shard_map/ppermute | solution.py:140
  733.3 79.7 %collective-permute-start.87 = (f32[512,1024]{1,0:T(8,128)}, f32[512,1024]{1,0:T(8,128)}, u32[]{:S(2)}, u32[]{:S(2)}) collective-permute-start(f32[512,1024]{1,0:T(8,128)} %dynamic-slice_bitcast_fusion.4), channel_id=1, source_target_pairs={{0,1},{1,0},{2,3},{3,2},{4,5},{5,4},{6,7},{7,6},{8,9},{9,8},{10,11... | collective-permute-start | bytes 6291464 | tf_op jit(solution)/shard_map/ppermute | solution.py:140
  764.3 75.3 %collective-permute-start.119 = (bf16[4,256,4,2,128]{4,1,3,2,0:T(8,128)(2,1)}, bf16[4,256,4,2,128]{4,1,3,2,0:T(8,128)(2,1)}, u32[]{:S(2)}, u32[]{:S(2)}) collective-permute-start(bf16[4,256,4,2,128]{4,1,3,2,0:T(8,128)(2,1)} %fusion.136), channel_id=1, source_target_pairs={{0,2},{2,0},{1,3},{3,1},{4,6},{6,4},{5,7},{7,5},{8,10},{10,8},{9,1... | collective-permute-start | bytes 6291464 | tf_op jit(solution)/shard_map/ppermute | solution.py:140
  805.0 48.8 %collective-permute-start.107 = (bf16[4,4,128,2,256]{4,2,0,1,3:T(8,128)(2,1)}, bf16[4,4,128,2,256]{4,2,0,1,3:T(8,128)(2,1)}, u32[]{:S(2)}, u32[]{:S(2)}) collective-permute-start(bf16[4,4,128,2,256]{4,2,0,1,3:T(8,128)(2,1)} %bitcast.1069), channel_id=1, source_target_pairs={{0,4},{4,0},{1,5},{5,1},{2,6},{6,2},{3,7},{7,3},{8,12},{12,8},{9,1... | collective-permute-start | bytes 6291464 | tf_op jit(solution)/shard_map/ppermute | solution.py:140
  812.8 46.1 %collective-permute-start.135 = (bf16[4,2,64,1024]{3,2,1,0:T(8,128)(2,1)S(1)}, bf16[4,2,64,1024]{3,2,1,0:T(8,128)(2,1)S(1)}, u32[]{:S(2)}, u32[]{:S(2)}) collective-permute-start(bf16[4,2,64,1024]{3,2,1,0:T(8,128)(2,1)S(1)} %fusion.170), channel_id=1, source_target_pairs={{0,8},{8,16},{16,24},{24,0},{1,9},{9,17},{17,25},{25,1},{2,10},{10... | collective-permute-start | bytes 3145736 | tf_op jit(solution)/shard_map/ppermute | solution.py:140
  822.6 37.7 %collective-permute-start.88 = (bf16[512,1024]{1,0:T(8,128)(2,1)S(1)}, bf16[512,1024]{1,0:T(8,128)(2,1)S(1)}, u32[]{:S(2)}, u32[]{:S(2)}) collective-permute-start(bf16[512,1024]{1,0:T(8,128)(2,1)S(1)} %get-tuple-element.462), channel_id=1, source_target_pairs={{0,1},{1,0},{2,3},{3,2},{4,5},{5,4},{6,7},{7,6},{8,9},{9,8},{10,11... | collective-permute-start | bytes 3145736 | tf_op jit(solution)/shard_map/ppermute | solution.py:140
  843.1 32.7 %collective-permute-start.120 = (bf16[4,256,4,128]{3,1,2,0:T(8,128)(2,1)}, bf16[4,256,4,128]{3,1,2,0:T(8,128)(2,1)}, u32[]{:S(2)}, u32[]{:S(2)}) collective-permute-start(bf16[4,256,4,128]{3,1,2,0:T(8,128)(2,1)} %fusion.169), channel_id=1, source_target_pairs={{0,4},{4,0},{1,5},{5,1},{2,6},{6,2},{3,7},{7,3},{8,12},{12,8},{9,1... | collective-permute-start | bytes 3145736 | tf_op jit(solution)/shard_map/ppermute | solution.py:140
  857.3 50.5 %collective-permute-start.108 = (bf16[4,4,128,256]{3,2,0,1:T(8,128)(2,1)}, bf16[4,4,128,256]{3,2,0,1:T(8,128)(2,1)}, u32[]{:S(2)}, u32[]{:S(2)}) collective-permute-start(bf16[4,4,128,256]{3,2,0,1:T(8,128)(2,1)} %fusion.168), channel_id=1, source_target_pairs={{0,2},{2,0},{1,3},{3,1},{4,6},{6,4},{5,7},{7,5},{8,10},{10,8},{9,1... | collective-permute-start | bytes 3145736 | tf_op jit(solution)/shard_map/ppermute | solution.py:140
  860.2 61.0 %collective-permute-start.136 = (bf16[4,2,64,1024]{3,2,1,0:T(8,128)(2,1)}, bf16[4,2,64,1024]{3,2,1,0:T(8,128)(2,1)}, u32[]{:S(2)}, u32[]{:S(2)}) collective-permute-start(bf16[4,2,64,1024]{3,2,1,0:T(8,128)(2,1)} %fusion.144), channel_id=1, source_target_pairs={{0,8},{8,16},{16,24},{24,0},{1,9},{9,17},{17,25},{25,1},{2,10},{10... | collective-permute-start | bytes 3145736 | tf_op jit(solution)/shard_map/ppermute | solution.py:140
  884.9 40.1 %collective-permute-start.121 = (bf16[4,256,128]{2,1,0:T(8,128)(2,1)S(1)}, bf16[4,256,128]{2,1,0:T(8,128)(2,1)S(1)}, u32[]{:S(2)}, u32[]{:S(2)}) collective-permute-start(bf16[4,256,128]{2,1,0:T(8,128)(2,1)S(1)} %fusion.209), channel_id=1, source_target_pairs={{0,8},{8,16},{16,24},{24,0},{1,9},{9,17},{17,25},{25,1},{2,10},{10... | collective-permute-start | bytes 786440 | tf_op jit(solution)/shard_map/ppermute | solution.py:140
  906.9 65.7 %collective-permute-start.102 = (bf16[3,4,128,2,256]{4,2,0,1,3:T(8,128)(2,1)}, bf16[3,4,128,2,256]{4,2,0,1,3:T(8,128)(2,1)}, u32[]{:S(2)}, u32[]{:S(2)}) collective-permute-start(bf16[3,4,128,2,256]{4,2,0,1,3:T(8,128)(2,1)} %fusion.148), channel_id=1, source_target_pairs={{0,4},{4,0},{1,5},{5,1},{2,6},{6,2},{3,7},{7,3},{8,12},{12,8},{9,1... | collective-permute-start | bytes 4718600 | tf_op jit(solution)/shard_map/ppermute | solution.py:140
  917.2 59.3 %collective-permute-start.89 = (f32[512,1024]{1,0:T(8,128)}, f32[512,1024]{1,0:T(8,128)}, u32[]{:S(2)}, u32[]{:S(2)}) collective-permute-start(f32[512,1024]{1,0:T(8,128)} %dynamic-slice_bitcast_fusion.3), channel_id=1, source_target_pairs={{0,1},{1,0},{2,3},{3,2},{4,5},{5,4},{6,7},{7,6},{8,9},{9,8},{10,11... | collective-permute-start | bytes 6291464 | tf_op jit(solution)/shard_map/ppermute | solution.py:140
  924.4 45.2 %collective-permute-start.137 = (bf16[4,2,64,1024]{3,2,1,0:T(8,128)(2,1)}, bf16[4,2,64,1024]{3,2,1,0:T(8,128)(2,1)}, u32[]{:S(2)}, u32[]{:S(2)}) collective-permute-start(bf16[4,2,64,1024]{3,2,1,0:T(8,128)(2,1)} %fusion.143), channel_id=1, source_target_pairs={{0,8},{8,16},{16,24},{24,0},{1,9},{9,17},{17,25},{25,1},{2,10},{10... | collective-permute-start | bytes 3145736 | tf_op jit(solution)/shard_map/ppermute | solution.py:140
  925.2 32.9 %collective-permute-start.122 = (bf16[4,256,128]{2,1,0:T(8,128)(2,1)S(1)}, bf16[4,256,128]{2,1,0:T(8,128)(2,1)S(1)}, u32[]{:S(2)}, u32[]{:S(2)}) collective-permute-start(bf16[4,256,128]{2,1,0:T(8,128)(2,1)S(1)} %fusion.198), channel_id=1, source_target_pairs={{0,8},{8,16},{16,24},{24,0},{1,9},{9,17},{17,25},{25,1},{2,10},{10... | collective-permute-start | bytes 786440 | tf_op jit(solution)/shard_map/ppermute | solution.py:140
  928.0 35.7 %collective-permute-start.111 = (bf16[4,128,256]{2,1,0:T(8,128)(2,1)S(1)}, bf16[4,128,256]{2,1,0:T(8,128)(2,1)S(1)}, u32[]{:S(2)}, u32[]{:S(2)}) collective-permute-start(bf16[4,128,256]{2,1,0:T(8,128)(2,1)S(1)} %fusion.200), channel_id=1, source_target_pairs={{0,8},{8,16},{16,24},{24,0},{1,9},{9,17},{17,25},{25,1},{2,10},{10... | collective-permute-start | bytes 786440 | tf_op jit(solution)/shard_map/ppermute | solution.py:140
  972.1 29.4 %collective-permute-start.138 = (bf16[4,64,1024]{2,1,0:T(8,128)(2,1)S(1)}, bf16[4,64,1024]{2,1,0:T(8,128)(2,1)S(1)}, u32[]{:S(2)}, u32[]{:S(2)}) collective-permute-start(bf16[4,64,1024]{2,1,0:T(8,128)(2,1)S(1)} %fusion.195), channel_id=1, source_target_pairs={{0,4},{4,0},{1,5},{5,1},{2,6},{6,2},{3,7},{7,3},{8,12},{12,8},{9,1... | collective-permute-start | bytes 1572872 | tf_op jit(solution)/shard_map/ppermute | solution.py:140
  981.7 28.0 %collective-permute-start.90 = (bf16[512,1024]{1,0:T(8,128)(2,1)S(1)}, bf16[512,1024]{1,0:T(8,128)(2,1)S(1)}, u32[]{:S(2)}, u32[]{:S(2)}) collective-permute-start(bf16[512,1024]{1,0:T(8,128)(2,1)S(1)} %get-tuple-element.457), channel_id=1, source_target_pairs={{0,1},{1,0},{2,3},{3,2},{4,5},{5,4},{6,7},{7,6},{8,9},{9,8},{10,11... | collective-permute-start | bytes 3145736 | tf_op jit(solution)/shard_map/ppermute | solution.py:140
  1009.7 154.2 %collective-permute-start.106 = (bf16[3,128,256]{2,1,0:T(8,128)(2,1)}, bf16[3,128,256]{2,1,0:T(8,128)(2,1)}, u32[]{:S(2)}, u32[]{:S(2)}) collective-permute-start(bf16[3,128,256]{2,1,0:T(8,128)(2,1)} %fusion.203), channel_id=1, source_target_pairs={{0,8},{8,16},{16,24},{24,0},{1,9},{9,17},{17,25},{25,1},{2,10},{10... | collective-permute-start | bytes 589832 | tf_op jit(solution)/shard_map/ppermute | solution.py:140
  1117.5 35.5 %collective-permute-start.114 = (bf16[2,256,4,2,128]{4,1,3,2,0:T(8,128)(2,1)}, bf16[2,256,4,2,128]{4,1,3,2,0:T(8,128)(2,1)}, u32[]{:S(2)}, u32[]{:S(2)}) collective-permute-start(bf16[2,256,4,2,128]{4,1,3,2,0:T(8,128)(2,1)} %fusion.171), channel_id=1, source_target_pairs={{0,2},{2,0},{1,3},{3,1},{4,6},{6,4},{5,7},{7,5},{8,10},{10,8},{9,1... | collective-permute-start | bytes 3145736 | tf_op jit(solution)/shard_map/ppermute | solution.py:140
  1152.6 32.5 %collective-permute-start.97 = (bf16[3,4,2,128,256]{4,3,0,1,2:T(8,128)(2,1)}, bf16[3,4,2,128,256]{4,3,0,1,2:T(8,128)(2,1)}, u32[]{:S(2)}, u32[]{:S(2)}) collective-permute-start(bf16[3,4,2,128,256]{4,3,0,1,2:T(8,128)(2,1)} %bitcast.1082), channel_id=1, source_target_pairs={{0,2},{2,0},{1,3},{3,1},{4,6},{6,4},{5,7},{7,5},{8,10},{10,8},{9,1... | collective-permute-start | bytes 4718600 | tf_op jit(solution)/shard_map/ppermute | solution.py:140
  1163.9 35.5 %collective-permute-start.91 = (f32[512,1024]{1,0:T(8,128)}, f32[512,1024]{1,0:T(8,128)}, u32[]{:S(2)}, u32[]{:S(2)}) collective-permute-start(f32[512,1024]{1,0:T(8,128)} %dynamic-slice_bitcast_fusion.2), channel_id=1, source_target_pairs={{0,1},{1,0},{2,3},{3,2},{4,5},{5,4},{6,7},{7,6},{8,9},{9,8},{10,11... | collective-permute-start | bytes 6291464 | tf_op jit(solution)/shard_map/ppermute | solution.py:140
  1190.5 33.5 %collective-permute-start.98 = (bf16[3,4,128,256]{3,2,0,1:T(8,128)(2,1)}, bf16[3,4,128,256]{3,2,0,1:T(8,128)(2,1)}, u32[]{:S(2)}, u32[]{:S(2)}) collective-permute-start(bf16[3,4,128,256]{3,2,0,1:T(8,128)(2,1)} %fusion.189), channel_id=1, source_target_pairs={{0,4},{4,0},{1,5},{5,1},{2,6},{6,2},{3,7},{7,3},{8,12},{12,8},{9,1... | collective-permute-start | bytes 2359304 | tf_op jit(solution)/shard_map/ppermute | solution.py:140
  1218.8 59.1 %collective-permute-start.127 = (bf16[512,1024]{1,0:T(8,128)(2,1)}, bf16[512,1024]{1,0:T(8,128)(2,1)}, u32[]{:S(2)}, u32[]{:S(2)}) collective-permute-start(bf16[512,1024]{1,0:T(8,128)(2,1)} %get-tuple-element.450), channel_id=1, source_target_pairs={{0,2},{2,0},{1,3},{3,1},{4,6},{6,4},{5,7},{7,5},{8,10},{10,8},{9,1... | collective-permute-start | bytes 3145736 | tf_op jit(solution)/shard_map/ppermute | solution.py:140
  1220.1 60.1 %collective-permute-start.128 = (bf16[512,1024]{1,0:T(8,128)(2,1)}, bf16[512,1024]{1,0:T(8,128)(2,1)}, u32[]{:S(2)}, u32[]{:S(2)}) collective-permute-start(bf16[512,1024]{1,0:T(8,128)(2,1)} %get-tuple-element.450), channel_id=1, source_target_pairs={{0,1},{1,0},{2,3},{3,2},{4,5},{5,4},{6,7},{7,6},{8,9},{9,8},{10,11... | collective-permute-start | bytes 3145736 | tf_op jit(solution)/shard_map/ppermute | solution.py:140
  1227.3 31.1 %collective-permute-start.99 = (bf16[3,128,256]{2,1,0:T(8,128)(2,1)}, bf16[3,128,256]{2,1,0:T(8,128)(2,1)}, u32[]{:S(2)}, u32[]{:S(2)}) collective-permute-start(bf16[3,128,256]{2,1,0:T(8,128)(2,1)} %fusion.213), channel_id=1, source_target_pairs={{0,8},{8,16},{16,24},{24,0},{1,9},{9,17},{17,25},{25,1},{2,10},{10... | collective-permute-start | bytes 589832 | tf_op jit(solution)/shard_map/ppermute | solution.py:140
  1301.2 48.1 %collective-permute-start.130 = (bf16[4,4,64,1024]{3,2,0,1:T(8,128)(2,1)S(1)}, bf16[4,4,64,1024]{3,2,0,1:T(8,128)(2,1)S(1)}, u32[]{:S(2)}, u32[]{:S(2)}) collective-permute-start(bf16[4,4,64,1024]{3,2,0,1:T(8,128)(2,1)S(1)} %fusion.137), channel_id=1, source_target_pairs={{0,4},{4,0},{1,5},{5,1},{2,6},{6,2},{3,7},{7,3},{8,12},{12,8},{9,1... | collective-permute-start | bytes 6291464 | tf_op jit(solution)/shard_map/ppermute | solution.py:140
  (270 other events, 3599.1 us)

commit v2 on v1

v2 whole, which is shorter than its diff:
```python
import functools
import math

import jax
import jax.numpy as jnp
from jax import lax
from jax.experimental import pallas as pl
from jax.experimental.pallas import tpu as pltpu
from jax.sharding import Mesh
from jax.sharding import PartitionSpec as P

HEAD_DIM = 64
MUON_ROWS = 32
STEP = 10

HIGHEST = lax.Precision.HIGHEST
NEWTON = (3.4445, -4.775, 2.0315)
BETA_ONE = 0.9
BETA_TWO = 0.95
ADAM_EPS = 1e-08
DECAY = 0.01
MOMENTUM = 0.95
BF16 = jnp.bfloat16
F32 = jnp.float32
LANES = 128
BUDGET = 8
BACK_BUDGET = 16
KERNEL_VMEM = 48 * 1024 * 1024


def layer_norm(values, gain, shift):
    centred = values - jnp.mean(values, -1, keepdims=True)
    variance = jnp.mean(centred * centred, -1, keepdims=True)
    return centred * lax.rsqrt(variance + 1e-05) * gain + shift


def norm_back(values, gain, shift, grad):
    result, backward = jax.vjp(layer_norm, values, gain, shift)
    return backward(grad)


def exact_gelu(values):
    return jax.nn.gelu(values, approximate=False)


def sinusoid(first, length, width):
    half = width // 2
    rates = jnp.exp(jnp.arange(half, dtype=jnp.float32) * (-math.log(10000.0) / half))
    places = (first + jnp.arange(length, dtype=jnp.int32)).astype(jnp.float32)
    angles = places[:, None] * rates[None, :]
    return jnp.concatenate([jnp.sin(angles), jnp.cos(angles)], -1)


def adam(weight, first, second, gradient, rate, decay):
    first = BETA_ONE * first + (1.0 - BETA_ONE) * gradient
    second = BETA_TWO * second + (1.0 - BETA_TWO) * gradient * gradient
    direction = (
        first / (1.0 - BETA_ONE**STEP) / (jnp.sqrt(second / (1.0 - BETA_TWO**STEP)) + ADAM_EPS)
    )
    return (weight - rate * (direction + decay * weight), first, second)


class Grid:
    def __init__(self, sizes):
        self.sizes = sizes

    def index(self, axis):
        return lax.axis_index(axis)

    def rotate(self, value, axis):
        size = self.sizes[axis]
        return lax.ppermute(value, axis, [(i, (i + 1) % size) for i in range(size)])

    def swap(self, value, axis, step=1):
        return lax.ppermute(value, axis, [(i, i ^ step) for i in range(self.sizes[axis])])

    def total(self, value, axes):
        for axis in axes:
            step = 1
            while step < self.sizes[axis]:
                value = value + lax.ppermute(
                    value, axis, [(i, i ^ step) for i in range(self.sizes[axis])]
                )
                step *= 2
        return value

    def ring(self, shard, axis):
        held = [shard]
        for _ in range(1, self.sizes[axis]):
            held.append(self.rotate(held[-1], axis))
        return [held[-r % self.sizes[axis]] for r in range(self.sizes[axis])]

    def ring_sum(self, parts, axis):
        size = self.sizes[axis]
        running = parts[size - 1]
        for step in range(1, size):
            arrived = self.rotate(running.astype(BF16), axis)
            running = arrived.astype(F32) + parts[size - 1 - step].astype(F32)
        return running

    def rounds(self, tasks, budget, early=None, pack=True):
        done, results, last, when = {}, {}, [], 0
        waiting = list(tasks)
        while waiting:
            used, picked = {}, []
            for name in waiting:
                axis, size, needs, between, first, _ = tasks[name]
                ready = when >= first and all(
                    done.get(need, when) + between < when for need in needs
                )
                load = used.get(axis, 0)
                if ready and (load == 0 or load + size <= budget):
                    used[axis] = load + size
                    picked.append(name)
            messages = {}
            for name in picked:
                value = tasks[name][-1](results)
                key = (tasks[name][0], value.shape[-1], None if pack else name)
                messages.setdefault(key, []).append((name, value))
            if messages:
                values = [
                    lists[0][1]
                    if len(lists) == 1
                    else jnp.concatenate([value.reshape(-1, key[1]) for _, value in lists], 0)
                    for key, lists in messages.items()
                ]
                held = last + (early or {}).get(when, [])
                tied = lax.optimization_barrier((values, held))[0]
                last = []
                for ((axis, _, _), lists), value in zip(messages.items(), tied):
                    arrived = self.rotate(value, axis) if axis == "z" else self.swap(value, axis)
                    last.append(arrived)
                    start = 0
                    for name, sent in lists:
                        results[name] = arrived
                        if len(lists) > 1:
                            rows = sent.size // sent.shape[-1]
                            results[name] = arrived[start : start + rows].reshape(sent.shape)
                            start += rows
                        done[name] = when
            waiting = [name for name in waiting if name not in picked]
            when += 1
        return results


def chosen(array, index, axis):
    return lax.dynamic_index_in_dim(array, index, axis, keepdims=False)


def move_blocks(array, order):
    rows, cols = array.shape
    count = order.shape[0]
    block = cols // count
    if block % LANES or rows % 16:
        return jnp.take(array.reshape(rows, count, block), order, axis=1).reshape(rows, cols)

    def kernel(order_ref, from_ref, to_ref):
        to_ref[...] = from_ref[...]

    return pl.pallas_call(
        kernel,
        grid_spec=pltpu.PrefetchScalarGridSpec(
            num_scalar_prefetch=1,
            grid=(count,),
            in_specs=[pl.BlockSpec((rows, block), lambda p, order: (0, order[p]))],
            out_specs=pl.BlockSpec((rows, block), lambda p, order: (0, p)),
        ),
        out_shape=jax.ShapeDtypeStruct(array.shape, array.dtype),
        cost_estimate=pl.CostEstimate(
            flops=0, bytes_accessed=2 * array.size * array.dtype.itemsize, transcendentals=0
        ),
    )(order, array)


def arranged(blocks, order):
    count, books, rows, cols = blocks.shape
    if rows % 16:
        return jnp.take(blocks, order, axis=0).transpose(1, 0, 2, 3)

    def kernel(order_ref, from_ref, to_ref):
        to_ref[...] = from_ref[...].reshape(to_ref.shape)

    return pl.pallas_call(
        kernel,
        grid_spec=pltpu.PrefetchScalarGridSpec(
            num_scalar_prefetch=1,
            grid=(count,),
            in_specs=[pl.BlockSpec((1, books, rows, cols), lambda p, order: (order[p], 0, 0, 0))],
            out_specs=pl.BlockSpec((books, 1, rows, cols), lambda p, order: (0, p, 0, 0)),
        ),
        out_shape=jax.ShapeDtypeStruct((books, count, rows, cols), blocks.dtype),
        cost_estimate=pl.CostEstimate(
            flops=0, bytes_accessed=2 * blocks.size * blocks.dtype.itemsize, transcendentals=0
        ),
    )(order, blocks)


def after(value, token):
    return lax.optimization_barrier((value, token))[0]


def contract(left, right, left_dim, right_dim):
    return lax.dot_general(
        left, right, (((left_dim,), (right_dim,)), ((), ())), preferred_element_type=F32
    )


def contract_rows(left, right):
    return contract(left, right, 1, 0)


def spans(frames, keys, causal):
    block = min(256 if causal else 512, frames)
    return [
        (first, block, min(keys, first + block) if causal else keys)
        for first in range(0, frames, block)
    ]


def softmax_down(query, key_rows, first, causal):
    scores = contract(key_rows, query, 1, 1) * 0.125
    if causal:
        key_at = lax.broadcasted_iota(jnp.int32, scores.shape, 0)
        query_at = first + lax.broadcasted_iota(jnp.int32, scores.shape, 1)
        scores = jnp.where(key_at <= query_at, scores, -jnp.inf)
    expo = jnp.exp(scores - jnp.max(scores, 0, keepdims=True))
    return expo * (1.0 / jnp.sum(expo, 0, keepdims=True))


def head_lanes(shape, head):
    lane = lax.broadcasted_iota(jnp.int32, shape, 1)
    return (lane // HEAD_DIM) == head


def attend_kernel(causal, query_ref, key_ref, value_ref, mixed_ref):
    frames, keys = query_ref.shape[0], key_ref.shape[0]
    turned = value_ref[...].astype(F32).T.astype(BF16)
    for first, block, last in spans(frames, keys, causal):
        query = query_ref[pl.ds(first, block), :]
        parts = []
        for head in range(LANES // HEAD_DIM):
            own = jnp.where(head_lanes(query.shape, head), query, jnp.zeros_like(query))
            probs = softmax_down(own, key_ref[pl.ds(0, last), :], first, causal).astype(BF16)
            parts.append(
                contract_rows(
                    turned[head * HEAD_DIM : (head + 1) * HEAD_DIM, :last],
                    probs,
                )
            )
        mixed_ref[pl.ds(first, block), :] = jnp.concatenate(parts, 0).T.astype(BF16)


def attend_back_kernel(
    causal,
    query_ref,
    key_ref,
    value_ref,
    grad_ref,
    grad_query_ref,
    grad_key_ref,
    grad_value_ref,
    key_sum,
    value_sum,
):
    frames, keys = query_ref.shape[0], key_ref.shape[0]
    turned = key_ref[...].astype(F32).T.astype(BF16)
    key_sum[...] = jnp.zeros_like(key_sum)
    value_sum[...] = jnp.zeros_like(value_sum)
    for first, block, last in spans(frames, keys, causal):
        query = query_ref[pl.ds(first, block), :]
        grad = grad_ref[pl.ds(first, block), :]
        parts = []
        for head in range(LANES // HEAD_DIM):
            lanes = head_lanes(query.shape, head)
            own = jnp.where(lanes, query, jnp.zeros_like(query))
            own_grad = jnp.where(lanes, grad, jnp.zeros_like(grad))
            probs = softmax_down(own, key_ref[pl.ds(0, last), :], first, causal)
            grad_probs = contract(value_ref[pl.ds(0, last), :], own_grad, 1, 1)
            product = probs * grad_probs
            grad_scores = (product - probs * jnp.sum(product, 0, keepdims=True)).astype(BF16)
            value_sum[pl.ds(0, last), :] += contract_rows(probs.astype(BF16), own_grad)
            key_sum[pl.ds(0, last), :] += contract_rows(grad_scores, own)
            parts.append(
                contract_rows(
                    turned[head * HEAD_DIM : (head + 1) * HEAD_DIM, :last],
                    grad_scores,
                )
            )
        grad_query_ref[pl.ds(first, block), :] = (jnp.concatenate(parts, 0).T * 0.125).astype(BF16)
    grad_key_ref[...] = (key_sum[...] * 0.125).astype(BF16)
    grad_value_ref[...] = value_sum[...].astype(BF16)


def attend(queries, keys, values, causal):
    frames, key_rows = queries[0].shape[0], keys[0].shape[0]
    count = queries[2]
    cost = 4 * frames * key_rows * LANES * count * 2

    def spec(rows, start):
        return pl.BlockSpec((rows, LANES), lambda p, start=start: (0, start + p))

    return pl.pallas_call(
        functools.partial(attend_kernel, causal),
        grid=(count,),
        in_specs=[
            spec(frames, queries[1]),
            spec(key_rows, keys[1]),
            spec(key_rows, values[1]),
        ],
        out_specs=spec(frames, 0),
        out_shape=jax.ShapeDtypeStruct((frames, count * LANES), BF16),
        compiler_params=pltpu.CompilerParams(vmem_limit_bytes=KERNEL_VMEM),
        cost_estimate=pl.CostEstimate(
            flops=cost, bytes_accessed=cost // 256, transcendentals=cost // 256
        ),
    )(queries[0], keys[0], values[0])


def attend_back(queries, keys, values, grad, causal):
    frames, key_rows = queries[0].shape[0], keys[0].shape[0]
    count = queries[2]
    cost = 10 * frames * key_rows * LANES * count * 2

    def spec(rows, start):
        return pl.BlockSpec((rows, LANES), lambda p, start=start: (0, start + p))

    wide = count * LANES
    return pl.pallas_call(
        functools.partial(attend_back_kernel, causal),
        grid=(count,),
        in_specs=[
            spec(frames, queries[1]),
            spec(key_rows, keys[1]),
            spec(key_rows, values[1]),
            spec(frames, 0),
        ],
        out_specs=[spec(frames, 0), spec(key_rows, 0), spec(key_rows, 0)],
        out_shape=[
            jax.ShapeDtypeStruct((frames, wide), BF16),
            jax.ShapeDtypeStruct((key_rows, wide), BF16),
            jax.ShapeDtypeStruct((key_rows, wide), BF16),
        ],
        scratch_shapes=[pltpu.VMEM((key_rows, LANES), F32), pltpu.VMEM((key_rows, LANES), F32)],
        compiler_params=pltpu.CompilerParams(vmem_limit_bytes=KERNEL_VMEM),
        cost_estimate=pl.CostEstimate(
            flops=cost, bytes_accessed=cost // 512, transcendentals=cost // 512
        ),
    )(queries[0], keys[0], values[0], grad)


def newton(grams):
    count, _, rows = grams.shape
    repeats = rows // MUON_ROWS
    band = jnp.arange(rows) // MUON_ROWS
    mask = band[:, None] == band[None, :]
    eye = jnp.eye(rows, dtype=F32)
    gram = jnp.where(mask, jnp.tile(grams, (1, repeats, 1)), 0.0)
    diagonal = jnp.sum(gram * eye, -1).reshape(count, repeats, MUON_ROWS)
    size = jnp.sqrt(jnp.sum(diagonal, -1, keepdims=True)) + 1e-07
    size = jnp.broadcast_to(size, diagonal.shape).reshape(count, rows, 1)
    gram = gram / (size * size)

    def times(left, right):
        return jnp.einsum("brs,bst->brt", left, right, precision=HIGHEST)

    factor = None
    for repeat in range(5):
        mixing = NEWTON[0] * eye + NEWTON[1] * gram + NEWTON[2] * times(gram, gram)
        factor = mixing if factor is None else times(mixing, factor)
        if repeat < 4:
            gram = times(mixing, times(gram, mixing))
    return factor / size


def folded_gram(part):
    count, rows, _ = part.shape
    gram = jnp.einsum("brc,bsc->brs", part, part, precision=HIGHEST)
    band = jnp.arange(rows) // MUON_ROWS
    gram = jnp.where(band[:, None] == band[None, :], gram, 0.0)
    return jnp.sum(gram.reshape(count, rows // MUON_ROWS, MUON_ROWS, rows), 1)


def orthogonal(factor, part):
    return jnp.einsum("brs,bsc->brc", factor, part, precision=HIGHEST)


def body(
    grid,
    codes_in,
    codes_out,
    pad_mask,
    text_table,
    text_index,
    attend_in,
    attend_out,
    expand_weights,
    shrink_weights,
    attend_in_momentum,
    attend_out_momentum,
    expand_momentum,
    shrink_momentum,
    embed_table,
    head_table,
    norm_params,
    embed_first,
    embed_second,
    head_first,
    head_second,
    norm_first,
    norm_second,
):
    sizes = grid.sizes
    at_z, at_x, at_y, at_c = (grid.index(axis) for axis in ("z", "x", "y", "c"))
    deep, inner = sizes["z"], sizes["c"]
    width = norm_params.shape[1]
    clips, frames_part, books = codes_in.shape
    frames = frames_part * 2 * inner
    own_frames = frames // inner
    rows_in, members, cols_in = attend_in.shape
    cols_out = attend_out.shape[2]
    table_rows = embed_table.shape[1]
    groups = deep * 2

    place = jnp.arange(groups)
    order_near = (place % deep + at_z) % deep * 2 + (place // deep + at_x) % 2
    order_true = (place % 2 + at_x) % 2 * deep + (place // 2 - at_z) % deep

    def near(array):
        return move_blocks(array, order_near)

    def true(array):
        return move_blocks(array, order_true)

    codes = jnp.stack([codes_in, codes_out, pad_mask], 0).transpose(0, 3, 1, 2)

    def placed(pieces, axis):
        full = jnp.zeros((len(pieces),) + pieces[0].shape, pieces[0].dtype)
        for step, piece in enumerate(pieces):
            full = lax.dynamic_update_index_in_dim(
                full, piece, (lax.axis_index(axis) + step) % len(pieces), 0
            )
        return full

    def all_along(piece, axis):
        size = sizes[axis]
        held = [piece]
        for _ in range(1, size):
            held.append(
                lax.ppermute(held[-1], axis, [(i, (i + 1) % size) for i in range(size)])
            )
        return placed([held[-step % size] for step in range(size)], axis)

    codes = all_along(all_along(codes, "c"), "y")
    codes = codes.transpose(2, 3, 4, 0, 1, 5).reshape(3, books, clips, frames)
    group_count = jnp.sum(codes[2])
    codes = chosen(codes, at_y, 2)
    next_codes, live = codes[1], codes[2].astype(F32)
    codes_own = codes[0]
    codes_other = lax.ppermute(
        jnp.concatenate([codes_own, jnp.full((books, frames), group_count)], 0),
        "x",
        [(0, 1), (1, 0)],
    )
    pair_count = (group_count + codes_other[books, 0]).astype(F32).reshape(1, 1)
    codes_other = codes_other[:books]

    turned_in = attend_in.transpose(1, 0, 2)
    turned_out = attend_out.transpose(0, 2, 1)

    def side_by_side(parts):
        return jnp.concatenate([part.astype(BF16) for part in parts], 1)

    shards = {
        "embed": embed_table.astype(BF16),
        "self": side_by_side(list(turned_in[:3]) + [turned_out[0]]),
        "cross": side_by_side(list(turned_in[3:]) + [turned_out[1]]),
        "expand": expand_weights.astype(BF16),
        "shrink": shrink_weights.T.astype(BF16),
    }
    routes = {"embed": "zy", "self": "zxy", "cross": "zxy", "expand": "zxy", "shrink": "zyx"}
    tasks = {}

    def piece(results, group, axis, step):
        return results[group + axis + str(step)] if step or axis != "z" else shards[group]

    def pair(results, group, axis, step):
        return jnp.concatenate(
            [piece(results, group, "z", step), piece(results, group, axis, step)], 0
        )

    for group, route in routes.items():
        weight = 4 if group == "embed" else 2
        for step in range(deep):
            name = group + "z" + str(step)
            needs = [name] if step else []
            if step:
                ahead = [group + "z" + str(step - 1)] if step > 1 else []
                tasks[name] = (
                    "z", weight, ahead, 0, 0, lambda r, g=group, k=step: piece(r, g, "z", k - 1)
                )
            first = group + route[1] + str(step)
            tasks[first] = (
                route[1], weight, needs, 0, 0, lambda r, g=group, k=step: piece(r, g, "z", k)
            )
            if len(route) > 2:
                tasks[group + route[2] + str(step)] = (
                    route[2],
                    2 * weight,
                    [first],
                    0,
                    0,
                    lambda r, g=group, k=step, a=route[1]: pair(r, g, a, k),
                )
        if group == "self":
            last = ["embedy" + str(step) for step in range(deep)]
            tasks["rows"] = ("x", 8, last, 0, 0, lambda r: embedded_of(codes_other, table_of(r)))

    z_place = (at_z - jnp.arange(deep)) % deep
    y_place = jnp.stack([at_y, 1 - at_y])
    table_ids = ((z_place * 2 + at_x) * 2)[:, None] + y_place[None, :]
    table_ids = ((table_ids * inner + at_c)[:, :, None] * table_rows + jnp.arange(table_rows)).reshape(
        -1
    )
    kept_table = []

    def table_of(results):
        if not kept_table:
            pieces = []
            for step in range(deep):
                pieces += [piece(results, "embed", "z", step), piece(results, "embed", "y", step)]
            kept_table.append(jnp.concatenate(pieces, 1))
        return kept_table[0]

    def hot(codes):
        return (codes[..., None] == table_ids).astype(BF16)

    def embedded_of(codes, table):
        rows = jnp.einsum("kfv,kvd->fd", hot(codes), table, preferred_element_type=F32)
        rows = rows.reshape(inner, own_frames, width)
        rows = grid.ring_sum(
            [chosen(rows, (at_c + step) % inner, 0) for step in range(inner)], "c"
        )
        return rows.astype(BF16)

    results = grid.rounds(tasks, BUDGET, {2: [codes_other]}, pack=False)
    own_part = embedded_of(codes_own, table_of(results)).astype(F32)
    embedded = own_part + results["rows"].astype(F32)
    residual = near(embedded + sinusoid(at_c * own_frames, own_frames, width))

    def both_of(group):
        halves = [[[None] * deep, [None] * deep], [[None] * deep, [None] * deep]]
        inside = routes[group][1]
        for step in range(deep):
            spot = -step % deep
            first = [piece(results, group, "z", step), piece(results, group, inside, step)]
            far = piece(results, group, routes[group][2], step)
            far = [far[:rows_in], far[rows_in:]]
            for at, block in enumerate(first):
                halves[0 if inside == "x" else at][at if inside == "x" else 0][spot] = block
            for at, block in enumerate(far):
                halves[1 if inside == "x" else at][at if inside == "x" else 1][spot] = block
        return [jnp.concatenate(half[0] + half[1], 0) for half in halves]

    weight_self, weight_cross = both_of("self"), both_of("cross")
    weight_expand, weight_shrink = both_of("expand"), both_of("shrink")
    head_shard = after(head_table.astype(BF16), results["embedy" + str(deep - 1)])
    head = lax.all_gather(head_shard, ("z", "x", "y"), axis=0)
    head_order = (order_near[:, None] * 2 + y_place[None, :]).reshape(-1)
    head = arranged(head, head_order).reshape(books, -1, width)
    head_ids = (head_order * inner + at_c)[:, None] * table_rows + jnp.arange(table_rows)
    head_ids = head_ids.reshape(-1)

    def spread(rows):
        return placed(grid.ring(rows.astype(BF16), "c"), "c").reshape(frames, width)

    def collect(partial_rows):
        parts = partial_rows.reshape(inner, own_frames, width)
        running = chosen(parts, (at_c + inner - 1) % inner, 0)
        for step in range(1, inner):
            arrived = grid.rotate(running, "c")
            running = arrived + chosen(parts, (at_c + inner - 1 - step) % inner, 0)
        return running

    def product(left, right):
        return contract(left, right, 1, 0)

    def across(left, right):
        return contract(left, right, 1, 1)

    def down(left, right):
        return contract(left, right, 0, 0)

    gains = jnp.take(norm_params.reshape(8, groups, -1), order_near, axis=1).reshape(8, width)
    memory = jnp.take(text_table, chosen(text_index, at_y, 0), axis=0)
    memory = near(memory)
    pairs = cols_in // LANES
    triple = 3 * cols_in

    normed_one = spread(layer_norm(residual, gains[0], gains[1]))
    self_parts, self_mixed, total = [], [], 0.0
    for weight in weight_self:
        heads = product(normed_one, weight[:, :triple]).astype(BF16)
        parts = [(heads, member * pairs, pairs) for member in range(3)]
        mixed = attend(*parts, True)
        total = total + across(mixed, weight[:, triple:])
        self_parts.append(parts)
        self_mixed.append(mixed)
    residual_one = residual + collect(total)

    normed_two = spread(layer_norm(residual_one, gains[2], gains[3]))
    cross_parts, cross_mixed, total = [], [], 0.0
    for weight in weight_cross:
        query = product(normed_two, weight[:, :cols_in]).astype(BF16)
        key_value = product(memory, weight[:, cols_in:triple]).astype(BF16)
        parts = [(query, 0, pairs), (key_value, 0, pairs), (key_value, pairs, pairs)]
        mixed = attend(*parts, False)
        total = total + across(mixed, weight[:, triple:])
        cross_parts.append(parts)
        cross_mixed.append(mixed)
    residual_two = after(residual_one + collect(total), head)

    normed_three = spread(layer_norm(residual_two, gains[4], gains[5]))
    uppers, actives, total = [], [], 0.0
    for up, back in zip(weight_expand, weight_shrink):
        upper = product(normed_three, up)
        active = exact_gelu(upper).astype(BF16)
        total = total + across(active, back)
        uppers.append(upper)
        actives.append(active)
    residual_three = true(residual_two + collect(total))

    token_count = grid.total(after(pair_count, residual_one), ("z",))[0, 0]
    final = spread(layer_norm(residual_three, norm_params[6], norm_params[7]))
    logits = jnp.einsum("fd,kvd->kfv", final, head, preferred_element_type=F32)
    is_target = head_ids[None, None, :] == next_codes[:, :, None]
    row_max = jnp.max(logits, -1)
    picked = jnp.sum(jnp.where(is_target, logits, 0.0), -1)
    row_sum = jnp.sum(jnp.exp(logits - row_max[..., None]), -1)
    stats = grid.ring(jnp.stack([row_max, row_sum, picked], 0), "c")
    top = stats[0][0]
    for stat in stats[1:]:
        top = jnp.maximum(top, stat[0])
    row_sum = sum(stat[1] * jnp.exp(stat[0] - top) for stat in stats)
    picked = sum(stat[2] for stat in stats)
    log_total = top + jnp.log(row_sum)
    loss_local = jnp.where(at_c == 0, jnp.sum((log_total - picked) * live), 0.0)
    grad_logits = (
        (jnp.exp(logits - log_total[..., None]) - is_target.astype(F32))
        * (live / token_count)[..., None]
    ).astype(BF16)
    grad_final = collect(
        jnp.einsum("kfv,kvd->fd", grad_logits, head, preferred_element_type=F32)
    )
    tasks, sums = {}, {}

    def add(name, axis, size, needs, value, between=0, first=0):
        tasks[name] = (axis, size, needs, between, first, lambda r: value(r).astype(BF16))

    def once(name, make):
        def get(results):
            if name not in sums:
                sums[name] = make(results)
            return sums[name]

        return get

    def add_ring(name, size, needs, parts):
        get = once(name + "0", lambda r: parts(r)[deep - 1])
        for step in range(1, deep):
            add(name + "z" + str(step), "z", size, needs, get)
            needs = [name + "z" + str(step)]
            get = once(
                name + str(step),
                lambda r, n=needs[0], k=step: r[n].astype(F32) + parts(r)[deep - 1 - k].astype(F32),
            )
        return get

    def add_rows(name, size, route, first, own, other):
        half = width // 2
        if route[0] == "y":
            add(name + "y", "y", 8 * size, [], lambda r: other, 0, first)
            whole = once(name + "sum", lambda r: own + r[name + "y"].astype(F32))
            add(name + "x", "x", 4 * size, [name + "y"], lambda r: whole(r)[half:])
            quarter = once(
                name + "part", lambda r: whole(r)[:half] + r[name + "x"].astype(F32)
            )
        else:
            far = jnp.concatenate([own[half:].astype(BF16), other[half:].astype(BF16)], 0)
            add(name + "x", "x", 8 * size, [], lambda r: far, 0, first)
            add(
                name + "y",
                "y",
                4 * size,
                [name + "x"],
                lambda r: other[:half] + r[name + "x"][half:].astype(F32),
            )
            quarter = once(
                name + "part",
                lambda r: own[:half]
                + r[name + "x"][:half].astype(F32)
                + r[name + "y"].astype(F32),
            )
        return add_ring(
            name,
            size,
            [name + route[1]],
            lambda r: [
                quarter(r)[step * rows_in : (step + 1) * rows_in] for step in range(deep)
            ],
        )

    def add_head(name, first, value):
        value = value.reshape(value.shape[0], 2, deep, 2, table_rows, width)
        add(name + "x", "x", 16, [], lambda r: value[:, 1], 0, first)
        nearer = once(name + "half", lambda r: value[:, 0] + r[name + "x"].astype(F32))
        last = add_ring(
            name, 4, [name + "x"], lambda r: [nearer(r)[:, step] for step in range(deep)]
        )
        add(name + "y", "y", 2, [name + "z" + str(deep - 1)], lambda r: last(r)[:, 1])
        return lambda r: last(r)[:, 0] + r[name + "y"].astype(F32)

    grad_head = [
        add_head(
            "head" + str(half),
            half,
            jnp.einsum(
                "kfv,fd->kvd",
                grad_logits[half * books // 2 : (half + 1) * books // 2],
                final,
                preferred_element_type=F32,
            ),
        )
        for half in range(2)
    ]

    grad, gain_final, shift_final = norm_back(
        residual_three, norm_params[6], norm_params[7], grad_final
    )
    grad = near(grad)

    rows_grad = spread(grad)
    grad_uppers, total = [], 0.0
    for up, back, upper in zip(weight_expand, weight_shrink, uppers):
        grad_active = product(rows_grad, back)
        grad_upper = jax.vjp(exact_gelu, upper)[1](grad_active)[0].astype(BF16)
        total = total + across(grad_upper, up)
        grad_uppers.append(grad_upper)
    grad_normed = collect(total)
    grad_expand = add_rows(
        "expand", 2, "yxz", 1, *(down(normed_three, part) for part in grad_uppers)
    )
    grad_shrink = add_rows("shrink", 2, "yxz", 2, *(down(rows_grad, active) for active in actives))
    change, gain_three, shift_three = norm_back(residual_two, gains[4], gains[5], grad_normed)
    grad = grad + change

    rows_grad = spread(grad)
    grads, total = [], 0.0
    for weight, parts, mixed in zip(weight_cross, cross_parts, cross_mixed):
        grad_mixed = product(rows_grad, weight[:, triple:]).astype(BF16)
        grad_q, grad_k, grad_v = attend_back(*parts, grad_mixed, False)
        total = total + across(grad_q, weight[:, :cols_in])
        grads.append(
            jnp.concatenate(
                [
                    down(normed_two, grad_q),
                    down(memory, grad_k),
                    down(memory, grad_v),
                    down(rows_grad, mixed),
                ],
                1,
            )
        )
    grad_normed = collect(total)
    grad_cross = add_rows("cross", 2, "xyz", 2, *grads)
    change, gain_two, shift_two = norm_back(residual_one, gains[2], gains[3], grad_normed)
    grad = grad + change

    rows_grad = spread(grad)
    grads, total = [], 0.0
    for weight, parts, mixed in zip(weight_self, self_parts, self_mixed):
        grad_mixed = product(rows_grad, weight[:, triple:]).astype(BF16)
        grad_heads = jnp.concatenate(attend_back(*parts, grad_mixed, True), 1)
        total = total + across(grad_heads, weight[:, :triple])
        grads.append(
            jnp.concatenate([down(normed_one, grad_heads), down(rows_grad, mixed)], 1)
        )
    grad_normed = collect(total)
    change, gain_one, shift_one = norm_back(residual, gains[0], gains[1], grad_normed)
    grad_self = add_rows("self", 2, "yxz", 4, *grads)
    grad = true(grad + change)

    rows_grad = grad.astype(BF16)

    def add_table():
        add("rows", "x", 8, [], lambda r: rows_grad, 0, 4)

        def spread_out(rows):
            return placed(grid.ring(rows, "c"), "c").reshape(frames, width)

        own_rows = spread_out(rows_grad)
        other_rows = once("rows", lambda r: spread_out(r["rows"]))
        halves = []
        for half in range(2):
            name = "table" + str(half)
            part = slice(half * books // 2, (half + 1) * books // 2)

            def value(r, part=part):
                result = 0.0
                for codes, rows in ((codes_own, own_rows), (codes_other, other_rows(r))):
                    result = result + jnp.einsum(
                        "kfv,fd->kvd", hot(codes[part]), rows, preferred_element_type=F32
                    )
                return result.reshape(-1, deep, 2, table_rows, width)

            value = once(name + "value", value)
            add(name + "y", "y", 8, ["rows"], lambda r, v=value: v(r)[:, :, 1], half)
            both = once(
                name + "both",
                lambda r, v=value, n=name: v(r)[:, :, 0] + r[n + "y"].astype(F32),
            )
            halves.append(
                add_ring(
                    name,
                    2,
                    [name + "y"],
                    lambda r, b=both: [b(r)[:, -step % deep] for step in range(deep)],
                )
            )
        return halves

    grad_table = add_table()
    ranks = ["rows", "self", "table", "cross", "expand", "shrink", "head"]
    tasks = {
        name: tasks[name]
        for rank in ranks
        for name in tasks
        if name.startswith(rank)
    }
    results = grid.rounds(tasks, BACK_BUDGET)
    grad_head = jnp.concatenate([part(results) for part in grad_head], 0)
    grad_table = jnp.concatenate([part(results) for part in grad_table], 0)
    grad_self, grad_cross = grad_self(results), grad_cross(results)
    grad_expand, grad_shrink = grad_expand(results), grad_shrink(results)

    norm_grads = [gain_one, shift_one, gain_two, shift_two, gain_three, shift_three]
    norm_grads = jnp.take(
        jnp.stack(norm_grads, 0).reshape(6, groups, -1), order_true, axis=1
    ).reshape(6, width)
    norm_grads = jnp.concatenate([norm_grads, gain_final[None], shift_final[None]], 0)
    loss_row = jnp.full((8, width), loss_local)
    norm_grads = after(jnp.concatenate([norm_grads, loss_row], 0), results["table1y"])
    summed = grid.total(norm_grads, ("c", "y", "x"))
    summed = grid.total(after(summed, grad_self), ("z",))
    grad_norm, loss_sum = summed[:8], summed[8, 0]

    def columns(array, first, count):
        return [
            array[:, (first + step) * cols_in : (first + step + 1) * cols_in]
            for step in range(count)
        ]

    grad_in = jnp.stack(columns(grad_self, 0, 3) + columns(grad_cross, 0, 3), 0)
    grad_out = jnp.stack([columns(grad_self, 3, 1)[0].T, columns(grad_cross, 3, 1)[0].T], 0)
    next_in = MOMENTUM * attend_in_momentum.transpose(1, 0, 2) + grad_in
    next_out = MOMENTUM * attend_out_momentum + grad_out
    next_expand = MOMENTUM * expand_momentum + grad_expand
    next_shrink = MOMENTUM * shrink_momentum + grad_shrink.T

    stack_rows = min(128, cols_in)
    data_blocks = jnp.concatenate(
        [next_out.reshape(-1, stack_rows, cols_out), next_shrink.reshape(-1, stack_rows, cols_out)],
        0,
    )
    tensor_grams = jnp.concatenate([folded_gram(next_in), folded_gram(next_expand[None])], 0)
    tensor_factor = newton(grid.total(tensor_grams, ("c", "y")))
    data_factor = newton(grid.total(folded_gram(data_blocks), ("x", "z")))
    ortho_in = orthogonal(tensor_factor[:members], next_in)
    ortho_expand = orthogonal(tensor_factor[members:], next_expand[None])[0]
    ortho_data = orthogonal(data_factor, data_blocks)
    count_out = next_out.size // (stack_rows * cols_out)
    ortho_out = ortho_data[:count_out].reshape(next_out.shape)
    ortho_shrink = ortho_data[count_out:].reshape(next_shrink.shape)
    attend_in_new = (turned_in * (1.0 - 0.5 * DECAY) - 0.5 * ortho_in).transpose(1, 0, 2)
    attend_out_new = attend_out * (1.0 - 1.0 * DECAY) - 1.0 * ortho_out
    expand_new = expand_weights * (1.0 - 0.5 * DECAY) - 0.5 * ortho_expand
    shrink_new = shrink_weights * (1.0 - 0.5 * DECAY) - 0.5 * ortho_shrink
    embed_new, embed_first_new, embed_second_new = adam(
        embed_table, embed_first, embed_second, grad_table, 0.1, DECAY
    )
    head_new, head_first_new, head_second_new = adam(
        head_table, head_first, head_second, grad_head, 0.03, DECAY
    )
    norm_new, norm_first_new, norm_second_new = adam(
        norm_params, norm_first, norm_second, grad_norm, 0.5, 0.0
    )
    return (
        loss_sum,
        token_count,
        attend_in_new,
        attend_out_new,
        expand_new,
        shrink_new,
        next_in.transpose(1, 0, 2),
        next_out,
        next_expand,
        next_shrink,
        embed_new,
        head_new,
        norm_new,
        embed_first_new,
        embed_second_new,
        head_first_new,
        head_second_new,
        norm_first_new,
        norm_second_new,
    )


def solution(mesh):
    n_dp, n_tensor = mesh.shape["dp"], mesh.shape["tensor"]
    sizes = {"z": n_dp // 2, "x": 2, "y": 2, "c": n_tensor // 2}
    cut = Mesh(mesh.devices.reshape(tuple(sizes.values())), tuple(sizes))
    dp, tensor = ("z", "x"), ("y", "c")
    table = P(None, dp + tensor, None)
    matrices = (P(dp, None, tensor), P(None, tensor, dp), P(dp, tensor), P(tensor, dp))
    return jax.shard_map(
        lambda *args: body(Grid(sizes), *args),
        mesh=cut,
        in_specs=(P(dp, tensor, None),) * 3
        + (P(), P(dp, None))
        + matrices * 2
        + (table, table, P())
        + (table,) * 4
        + (P(), P()),
        out_specs=(P(), P())
        + matrices * 2
        + (table, table, P())
        + (table,) * 4
        + (P(), P()),
        check_vma=False,
    )
```

time: 1410 us -> 1100 us (0.78)
  waiting for transfers between devices: 504 us -> 336 us
  local copies, waits for them, and re-layouts: 308 us -> 176 us
  Pallas kernels: 0 us -> 101 us
  matrix products: 299 us -> 199 us
  starting transfers between devices: 109 us -> 85.5 us
    ppermute x124 -> x43, waiting for transfers between devices: 482 us -> 82.2 us  [rotate(): return lax.ppermute(value, axis, [(i, (i + 1) % size) for i in range(size)])]
    ppermute x15 -> x49, waiting for transfers between devices: 21.4 us -> 232 us  [swap(): lax.ppermute(value, axis, [(i, i ^ step) for i in range(self.sizes[axis])])]
    pallas_call x0 -> x14, Pallas kernels: none -> 101 us  [the longest x4 32.9 us: attend_back(): pl.pallas_call(functools.partial(attend_back_kernel, causal), grid=(count...]
    dot_general x51 -> x50, matrix products: 236 us -> 140 us  [the longest x42 108 us: contract(): lax.dot_general(left, right, (((left_dim,), (right_dim,)), ((), ())), pre...]
    ppermute x124 -> x43, starting transfers between devices: 92.3 us -> 26.4 us  [rotate(): return lax.ppermute(value, axis, [(i, (i + 1) % size) for i in range(size)])]
    dynamic_update_slice x83 -> x14, local copies, waits for them, and re-layouts: 72 us -> 8.51 us  [placed(): lax.dynamic_update_index_in_dim(full, piece, (lax.axis_index(axis) + step...]
    dynamic_slice x10 -> x0, local copies, waits for them, and re-layouts: 44.7 us -> none  [the longest x6 42.4 us: chosen(): return lax.dynamic_index_in_dim(array, index, axis, keepdims=False)]
    unnamed x354 -> x577, local copies, waits for them, and re-layouts: 54.3 us -> 96.8 us
  transfers between devices with their start and end apart: 139 -> 108, of which waited for: 75 -> 46; matrix products, arithmetic and copies ran while one was open for 45% -> 32% of each run, Pallas kernels for 0% -> 8%
where the time goes in v2:
time: 1100 us; the launch traced here: 1090 us
  waiting for transfers between devices  336 us (31%)
  matrix products  199 us (18%)
  local copies, waits for them, and re-layouts  176 us (16%)
  other arithmetic  168 us (15%)
  Pallas kernels  101 us (9%)
  starting transfers between devices  85.5 us (8%)
  between operations  23.1 us (2%)
    ppermute x49, waiting for transfers between devices, swap(): lax.ppermute(value, axis, [(i, i ^ step) for i in range(self.sizes[axis])])  232 us
    dot_general x42, matrix products, contract(): lax.dot_general(left, right, (((left_dim,), (right_dim,)), ((), ())), pre...  108 us
    unnamed x577, local copies, waits for them, and re-layouts  96.8 us
    ppermute x43, waiting for transfers between devices, rotate(): return lax.ppermute(value, axis, [(i, (i + 1) % size) for i in range(size)])  82.2 us
    ppermute x49, starting transfers between devices, swap(): lax.ppermute(value, axis, [(i, i ^ step) for i in range(self.sizes[axis])])  49.7 us
    pallas_call x4, Pallas kernels, attend_back(): pl.pallas_call(functools.partial(attend_back_kernel, causal), grid=(count...  32.9 us
    pallas_call x5, Pallas kernels, move_blocks(): pl.pallas_call(kernel, grid_spec=pltpu.PrefetchScalarGridSpec(num_scalar_...  30.8 us
    ppermute x43, starting transfers between devices, rotate(): return lax.ppermute(value, axis, [(i, (i + 1) % size) for i in range(size)])  26.4 us
  transfers between devices with their start and end apart: 108, of which 46 were waited for; matrix products, arithmetic and copies ran while one was open for 32% of the time, Pallas kernels for 8%

profile of v2, /device:TPU:0, one launch (start us, length us, event | category | flops | bytes accessed | tf_op | source)
XLA Modules:
  0.0 1089.1 jit_solution(14296689876790367129)
XLA Ops:
  24.2 4.7 multiply_sine_fusion
  51.2 4.1 collective-permute-done.9
  58.9 4.8 shard_map.361
  82.9 7.6 collective-permute-done.14
  90.6 4.8 collective-permute-done.15
  103.5 11.8 %collective-permute-done.22 = bf16[128,1024]{0,1:T(8,128)(2,1)S(1)} collective-permute-done((bf16[128,1024]{0,1:T(8,128)(2,1)}, bf16[128,1024]{0,1:T(8,128)(2,1)S(1)}, u32[]{:S(2)}, u32[]{:S(2)}) %collective-permute-start.22) | collective-permute-done | bytes 262176 | tf_op jit(solution)/shard_map/ppermute | solution.py:72
  120.9 5.1 collective-permute-done.25
  131.8 4.1 collective-permute-done.28
  136.4 4.9 collective-permute-done.26
  141.4 4.6 fusion.14
  154.3 6.8 fusion.16
  162.6 8.8 collective-permute-done.36
  176.1 5.5 collective-permute-done.39
  182.4 4.8 collective-permute-done.34
  189.2 6.4 shard_map.357
  204.5 10.2 collective-permute-done.47
  217.7 5.6 collective-permute-done.42
  227.4 9.7 shard_map.360
  240.1 9.9 shard_map.359
  262.0 4.9 collective-permute-done.51
  270.0 4.0 collective-permute-done.48
  274.0 10.5 collective-permute-done.52
  292.3 7.0 collective-permute-done.53
  299.4 9.5 collective-permute-done.54
  313.8 4.3 collective-permute-done.55
  341.2 7.5 collective-permute-done.59
  348.7 8.2 collective-permute-done.60
  358.4 13.0 %shard_map.358 = bf16[4,16,64,1024]{3,2,1,0:T(8,128)(2,1)} custom-call(s32[16]{0:T(128)} %add.1104.order_ref, bf16[16,4,64,1024]{3,2,1,0:T(8,128)(2,1)} %bitcast.620), custom_call_target="tpu_custom_call" | custom-call | bytes 16777216 | tf_op jit(solution)/shard_map/pallas_call | solution.py:183
  378.7 12.3 %multiply_convert_fusion = (bf16[1024,1024]{1,0:T(8,128)(2,1)S(1)}, f32[1024,1024]{1,0:T(8,128)}, f32[1024,1024]{1,0:T(8,128)}) fusion(bf16[1024,1024]{1,0:T(8,128)(2,1)S(1)} %bitcast.656, bf16[1024,1024]{1,0:T(8,128)(2,1)S(1)} %copy-done.203), kind=kOutput, calls=%fused_computation.46 | convolution fusion | flops 2215641088 | bytes 14680064 | tf_op jit(solution)/shard_map/dot_general | solution.py:203
  391.0 12.4 %multiply_convert_fusion.1 = (bf16[1024,1024]{1,0:T(8,128)(2,1)S(1)}, f32[1024,1024]{1,0:T(8,128)}, f32[1024,1024]{1,0:T(8,128)}) fusion(bf16[1024,1024]{1,0:T(8,128)(2,1)S(1)} %bitcast.657, bf16[1024,1024]{1,0:T(8,128)(2,1)S(1)} %copy-done.205), kind=kOutput, calls=%fused_computation.59 | convolution fusion | flops 2215641088 | bytes 14680064 | tf_op jit(solution)/shard_map/dot_general | solution.py:203
  403.4 4.7 fusion.223
  417.0 6.5 shard_map.364
  435.7 12.1 %bitcast_reduce_fusion = (f32[4,1024]{1,0:T(4,128)S(1)}, f32[4,1024,1024]{2,1,0:T(8,128)S(1)}) fusion(bf16[4,1024,1024]{2,1,0:T(8,128)(2,1)} %bitcast.621, bf16[1024,1024,1]{1,0,2:T(8,128)(2,1)} %bitcast.660), kind=kOutput, calls=%fused_computation.11 | convolution fusion | flops 8594124800 | bytes 27279360 | tf_op jit(solution)/shard_map/fd,kvd->kfv/dot_general | solution.py:634
  447.8 4.5 fusion.5
  467.9 8.1 fusion.10
  476.1 12.8 %fusion.46 = f32[2,512,1024]{2,1,0:T(8,128)} fusion(bf16[4,1024,1024,1]{2,1,0,3:T(8,128)(2,1)} %bitcast.622, bf16[4,128,2,8,512]{4,3,2,1,0:T(8,128)(2,1)S(1)} %bitcast.623), kind=kOutput, calls=%fused_computation.90 | convolution fusion | flops 8589934592 | bytes 20971520 | tf_op jit(solution)/shard_map/kfv,kvd->fd/dot_general | solution.py:652
  493.6 4.7 fusion.3
  498.3 4.6 fusion.216
  509.5 6.8 shard_map.365
  520.1 6.4 fusion.235
  529.6 5.8 add_convert_fusion
  537.9 7.2 add_convert_fusion.1
  550.5 4.6 fusion.22
  559.0 17.4 %collective-permute-done.74 = bf16[2,4,2,64,1024]{4,3,2,1,0:T(8,128)(2,1)S(1)} collective-permute-done((bf16[2,4,2,64,1024]{4,3,2,1,0:T(8,128)(2,1)}, bf16[2,4,2,64,1024]{4,3,2,1,0:T(8,128)(2,1)S(1)}, u32[]{:S(2)}, u32[]{:S(2)}) %collective-permute-start.74) | collective-permute-done | bytes 2097184 | tf_op jit(solution)/shard_map/ppermute | solution.py:75
  599.1 29.9 %collective-permute-done.76 = bf16[2,4,2,64,1024]{4,3,0,2,1:T(8,128)(2,1)} collective-permute-done((bf16[2,4,2,64,1024]{4,3,0,2,1:T(8,128)(2,1)}, bf16[2,4,2,64,1024]{4,3,0,2,1:T(8,128)(2,1)}, u32[]{:S(2)}, u32[]{:S(2)}) %collective-permute-start.76) | collective-permute-done | bytes 2097184 | tf_op jit(solution)/shard_map/ppermute | solution.py:75
  666.3 7.4 convert_add_fusion.1
  682.4 10.0 collective-permute-done.80
  703.1 19.0 %collective-permute-done.79 = bf16[1024,1024]{0,1:T(8,128)(2,1)} collective-permute-done((bf16[1024,1024]{0,1:T(8,128)(2,1)}, bf16[1024,1024]{0,1:T(8,128)(2,1)}, u32[]{:S(2)}, u32[]{:S(2)}) %collective-permute-start.79) | collective-permute-done | bytes 2097184 | tf_op jit(solution)/shard_map/ppermute | solution.py:75
  722.1 4.1 convert_add_fusion
  739.0 12.8 %shard_map.369 = (bf16[1024,256]{1,0:T(8,128)(2,1)S(1)}, bf16[1024,256]{1,0:T(8,128)(2,1)S(1)}, bf16[1024,256]{1,0:T(8,128)(2,1)S(1)}) custom-call(bf16[1024,768]{1,0:T(8,128)(2,1)S(1)} %copy-done.19, bf16[1024,768]{1,0:T(8,128)(2,1)S(1)} %copy-done.19, bf16[1024,768]{1,0:T(8,128)(2,1)S(1)} %copy-done.19, ...), custom_call_target="tpu_custom_call" | custom-call | flops 5368709120 | bytes 10485760 | tf_op jit(solution)/shard_map/pallas_call | solution.py:328
  757.8 13.5 %shard_map.368 = (bf16[1024,256]{1,0:T(8,128)(2,1)S(1)}, bf16[1024,256]{1,0:T(8,128)(2,1)S(1)}, bf16[1024,256]{1,0:T(8,128)(2,1)S(1)}) custom-call(bf16[1024,768]{1,0:T(8,128)(2,1)S(1)} %copy-done.17, bf16[1024,768]{1,0:T(8,128)(2,1)S(1)} %copy-done.17, bf16[1024,768]{1,0:T(8,128)(2,1)S(1)} %copy-done.17, ...), custom_call_target="tpu_custom_call" | custom-call | flops 5368709120 | bytes 10485760 | tf_op jit(solution)/shard_map/pallas_call | solution.py:328
  772.9 4.5 convolution_add_fusion.3
  807.2 6.3 shard_map.370
  825.0 14.9 %collective-permute-done.86 = bf16[512,1024]{1,0:T(8,128)(2,1)} collective-permute-done((bf16[512,1024]{1,0:T(8,128)(2,1)S(1)}, bf16[512,1024]{1,0:T(8,128)(2,1)}, u32[]{:S(2)}, u32[]{:S(2)}) %collective-permute-start.86) | collective-permute-done | bytes 1048608 | tf_op jit(solution)/shard_map/ppermute | solution.py:75
  843.1 9.3 collective-permute-done.88
  859.5 6.9 collective-permute-done.84
  887.5 14.4 %collective-permute-done.89 = bf16[512,1024]{0,1:T(8,128)(2,1)S(1)} collective-permute-done((bf16[512,1024]{0,1:T(8,128)(2,1)S(1)}, bf16[512,1024]{0,1:T(8,128)(2,1)S(1)}, u32[]{:S(2)}, u32[]{:S(2)}) %collective-permute-start.89) | collective-permute-done | bytes 1048608 | tf_op jit(solution)/shard_map/ppermute | solution.py:75
  903.2 10.9 %collective-permute-done.90 = bf16[768,1024]{1,0:T(8,128)(2,1)S(1)} collective-permute-done((bf16[768,1024]{1,0:T(8,128)(2,1)S(1)}, bf16[768,1024]{1,0:T(8,128)(2,1)S(1)}, u32[]{:S(2)}, u32[]{:S(2)}) %collective-permute-start.90) | collective-permute-done | bytes 1572896 | tf_op jit(solution)/shard_map/ppermute | solution.py:75
  933.8 13.4 %collective-permute-done.92 = bf16[2,4,64,1024]{3,2,0,1:T(8,128)(2,1)} collective-permute-done((bf16[2,4,64,1024]{3,2,0,1:T(8,128)(2,1)}, bf16[2,4,64,1024]{3,2,0,1:T(8,128)(2,1)}, u32[]{:S(2)}, u32[]{:S(2)}) %collective-permute-start.92) | collective-permute-done | bytes 1048608 | tf_op jit(solution)/shard_map/ppermute | solution.py:75
  951.8 4.2 collective-permute-done.96
  971.8 7.2 collective-permute-done.97
  991.0 9.8 collective-permute-done.98
  1025.7 4.2 collective-permute-done.100
  1054.0 7.7 collective-permute-done.105
  (1131 shorter events, 531.5 us)
Async XLA Ops:
  7.2 351.2 %all-gather.3.cloned.1.call-start = ((), (), s32[]{:S(2)}) async-start(), calls=%async_computation | async-start | bytes 8912896 | tf_op jit(solution)/shard_map/all_gather | solution.py:567
  13.1 42.2 %collective-permute-start.3 = (bf16[4,64,1024]{2,1,0:T(8,128)(2,1)}, bf16[4,64,1024]{2,1,0:T(8,128)(2,1)}, u32[]{:S(2)}, u32[]{:S(2)}) collective-permute-start(bf16[4,64,1024]{2,1,0:T(8,128)(2,1)} %get-tuple-element.108), channel_id=1, source_target_pairs={{0,8},{8,16},{16,24},{24,0},{1,9},{9,17},{17,25},{25,1},{2,10},{10... | collective-permute-start | bytes 1572872 | tf_op jit(solution)/shard_map/ppermute | solution.py:72
  16.1 24.0 %collective-permute-start.4 = (bf16[128,1024]{0,1:T(8,128)(2,1)}, bf16[128,1024]{0,1:T(8,128)(2,1)S(1)}, u32[]{:S(2)}, u32[]{:S(2)}) collective-permute-start(bf16[128,1024]{0,1:T(8,128)(2,1)} %get-tuple-element.111), channel_id=1, source_target_pairs={{0,4},{4,0},{1,5},{5,1},{2,6},{6,2},{3,7},{7,3},{8,12},{12,8},{9,1... | collective-permute-start | bytes 786440 | tf_op jit(solution)/shard_map/ppermute | solution.py:75
  17.6 24.1 %collective-permute-start.5 = (bf16[128,1024]{0,1:T(8,128)(2,1)}, bf16[128,1024]{0,1:T(8,128)(2,1)S(1)}, u32[]{:S(2)}, u32[]{:S(2)}) collective-permute-start(bf16[128,1024]{0,1:T(8,128)(2,1)} %get-tuple-element.111), channel_id=1, source_target_pairs={{0,8},{8,16},{16,24},{24,0},{1,9},{9,17},{17,25},{25,1},{2,10},{10... | collective-permute-start | bytes 786440 | tf_op jit(solution)/shard_map/ppermute | solution.py:72
  19.2 23.1 %collective-permute-start.7 = (bf16[128,1024]{0,1:T(8,128)(2,1)}, bf16[128,1024]{0,1:T(8,128)(2,1)S(1)}, u32[]{:S(2)}, u32[]{:S(2)}) collective-permute-start(bf16[128,1024]{0,1:T(8,128)(2,1)} %get-tuple-element.134), channel_id=1, source_target_pairs={{0,2},{2,0},{1,3},{3,1},{4,6},{6,4},{5,7},{7,5},{8,10},{10,8},{9,1... | collective-permute-start | bytes 786440 | tf_op jit(solution)/shard_map/ppermute | solution.py:75
  55.3 19.5 %collective-permute-start.12 = (bf16[128,1024]{0,1:T(8,128)(2,1)S(1)}, bf16[128,1024]{0,1:T(8,128)(2,1)S(1)}, u32[]{:S(2)}, u32[]{:S(2)}) collective-permute-start(bf16[128,1024]{0,1:T(8,128)(2,1)S(1)} %collective-permute-done.5), channel_id=1, source_target_pairs={{0,4},{4,0},{1,5},{5,1},{2,6},{6,2},{3,7},{7,3},{8,12},{12,8},{9,1... | collective-permute-start | bytes 786440 | tf_op jit(solution)/shard_map/ppermute | solution.py:75
  55.9 19.4 %collective-permute-start.13 = (bf16[128,1024]{0,1:T(8,128)(2,1)S(1)}, bf16[128,1024]{0,1:T(8,128)(2,1)}, u32[]{:S(2)}, u32[]{:S(2)}) collective-permute-start(bf16[128,1024]{0,1:T(8,128)(2,1)S(1)} %collective-permute-done.5), channel_id=1, source_target_pairs={{0,8},{8,16},{16,24},{24,0},{1,9},{9,17},{17,25},{25,1},{2,10},{10... | collective-permute-start | bytes 786440 | tf_op jit(solution)/shard_map/ppermute | solution.py:72
  71.8 18.7 %collective-permute-start.11 = (bf16[4,64,1024]{2,1,0:T(8,128)(2,1)}, bf16[4,64,1024]{2,1,0:T(8,128)(2,1)S(1)}, u32[]{:S(2)}, u32[]{:S(2)}) collective-permute-start(bf16[4,64,1024]{2,1,0:T(8,128)(2,1)} %collective-permute-done.3), channel_id=1, source_target_pairs={{0,8},{8,16},{16,24},{24,0},{1,9},{9,17},{17,25},{25,1},{2,10},{10... | collective-permute-start | bytes 1572872 | tf_op jit(solution)/shard_map/ppermute | solution.py:72
  74.8 20.5 %collective-permute-start.15 = (bf16[256,1024]{0,1:T(8,128)(2,1)}, bf16[256,1024]{0,1:T(8,128)(2,1)S(1)}, u32[]{:S(2)}, u32[]{:S(2)}) collective-permute-start(bf16[256,1024]{0,1:T(8,128)(2,1)} %pad_maximum_fusion.17), channel_id=1, source_target_pairs={{0,2},{2,0},{1,3},{3,1},{4,6},{6,4},{5,7},{7,5},{8,10},{10,8},{9,1... | collective-permute-start | bytes 1572872 | tf_op jit(solution)/shard_map/ppermute | solution.py:75
  75.3 20.0 %collective-permute-start.17 = (bf16[256,1024]{0,1:T(8,128)(2,1)S(1)}, bf16[256,1024]{0,1:T(8,128)(2,1)S(1)}, u32[]{:S(2)}, u32[]{:S(2)}) collective-permute-start(bf16[256,1024]{0,1:T(8,128)(2,1)S(1)} %copy-done.158), channel_id=1, source_target_pairs={{0,4},{4,0},{1,5},{5,1},{2,6},{6,2},{3,7},{7,3},{8,12},{12,8},{9,1... | collective-permute-start | bytes 1572872 | tf_op jit(solution)/shard_map/ppermute | solution.py:75
  95.3 31.5 %collective-permute-start.20 = (bf16[4,64,1024]{2,1,0:T(8,128)(2,1)S(1)}, bf16[4,64,1024]{2,1,0:T(8,128)(2,1)S(1)}, u32[]{:S(2)}, u32[]{:S(2)}) collective-permute-start(bf16[4,64,1024]{2,1,0:T(8,128)(2,1)S(1)} %collective-permute-done.11), channel_id=1, source_target_pairs={{0,8},{8,16},{16,24},{24,0},{1,9},{9,17},{17,25},{25,1},{2,10},{10... | collective-permute-start | bytes 1572872 | tf_op jit(solution)/shard_map/ppermute | solution.py:72
  97.0 22.0 %collective-permute-start.21 = (bf16[128,1024]{0,1:T(8,128)(2,1)}, bf16[128,1024]{0,1:T(8,128)(2,1)S(1)}, u32[]{:S(2)}, u32[]{:S(2)}) collective-permute-start(bf16[128,1024]{0,1:T(8,128)(2,1)} %collective-permute-done.13), channel_id=1, source_target_pairs={{0,4},{4,0},{1,5},{5,1},{2,6},{6,2},{3,7},{7,3},{8,12},{12,8},{9,1... | collective-permute-start | bytes 786440 | tf_op jit(solution)/shard_map/ppermute | solution.py:75
  99.0 19.1 %collective-permute-start.23 = (bf16[128,1024]{0,1:T(8,128)(2,1)S(1)}, bf16[128,1024]{0,1:T(8,128)(2,1)S(1)}, u32[]{:S(2)}, u32[]{:S(2)}) collective-permute-start(bf16[128,1024]{0,1:T(8,128)(2,1)S(1)} %collective-permute-done.14), channel_id=1, source_target_pairs={{0,8},{8,16},{16,24},{24,0},{1,9},{9,17},{17,25},{25,1},{2,10},{10... | collective-permute-start | bytes 786440 | tf_op jit(solution)/shard_map/ppermute | solution.py:72
  99.7 27.2 %collective-permute-start.19 = (bf16[4,64,1024]{2,1,0:T(8,128)(2,1)S(1)}, bf16[4,64,1024]{2,1,0:T(8,128)(2,1)S(1)}, u32[]{:S(2)}, u32[]{:S(2)}) collective-permute-start(bf16[4,64,1024]{2,1,0:T(8,128)(2,1)S(1)} %collective-permute-done.11), channel_id=1, source_target_pairs={{0,2},{2,0},{1,3},{3,1},{4,6},{6,4},{5,7},{7,5},{8,10},{10,8},{9,1... | collective-permute-start | bytes 1572872 | tf_op jit(solution)/shard_map/ppermute | solution.py:75
  130.1 22.6 %collective-permute-start.30 = (bf16[128,1024]{1,0:T(8,128)(2,1)}, bf16[128,1024]{1,0:T(8,128)(2,1)S(1)}, u32[]{:S(2)}, u32[]{:S(2)}) collective-permute-start(bf16[128,1024]{1,0:T(8,128)(2,1)} %get-tuple-element.133), channel_id=1, source_target_pairs={{0,8},{8,16},{16,24},{24,0},{1,9},{9,17},{17,25},{25,1},{2,10},{10... | collective-permute-start | bytes 786440 | tf_op jit(solution)/shard_map/ppermute | solution.py:72
  130.1 22.5 %collective-permute-start.31 = (bf16[128,1024]{0,1:T(8,128)(2,1)}, bf16[128,1024]{0,1:T(8,128)(2,1)S(1)}, u32[]{:S(2)}, u32[]{:S(2)}) collective-permute-start(bf16[128,1024]{0,1:T(8,128)(2,1)} %get-tuple-element.134), channel_id=1, source_target_pairs={{0,8},{8,16},{16,24},{24,0},{1,9},{9,17},{17,25},{25,1},{2,10},{10... | collective-permute-start | bytes 786440 | tf_op jit(solution)/shard_map/ppermute | solution.py:72
  131.7 21.0 %collective-permute-start.32 = (bf16[256,1024]{0,1:T(8,128)(2,1)}, bf16[256,1024]{0,1:T(8,128)(2,1)}, u32[]{:S(2)}, u32[]{:S(2)}) collective-permute-start(bf16[256,1024]{0,1:T(8,128)(2,1)} %pad_maximum_fusion.20), channel_id=1, source_target_pairs={{0,2},{2,0},{1,3},{3,1},{4,6},{6,4},{5,7},{7,5},{8,10},{10,8},{9,1... | collective-permute-start | bytes 1572872 | tf_op jit(solution)/shard_map/ppermute | solution.py:75
  161.3 21.0 %collective-permute-start.27 = (bf16[512,1024]{1,0:T(8,128)(2,1)S(1)}, bf16[512,1024]{1,0:T(8,128)(2,1)S(1)}, u32[]{:S(2)}, u32[]{:S(2)}) collective-permute-start(bf16[512,1024]{1,0:T(8,128)(2,1)S(1)} %fusion.94), channel_id=1, source_target_pairs={{0,1},{1,0},{2,3},{3,2},{4,5},{5,4},{6,7},{7,6},{8,9},{9,8},{10,11... | collective-permute-start | bytes 3145736 | tf_op jit(solution)/shard_map/ppermute | solution.py:72
  161.4 25.7 %collective-permute-start.34 = (bf16[512,1024]{1,0:T(8,128)(2,1)S(1)}, bf16[512,1024]{1,0:T(8,128)(2,1)S(1)}, u32[]{:S(2)}, u32[]{:S(2)}) collective-permute-start(bf16[512,1024]{1,0:T(8,128)(2,1)S(1)} %fusion.58), channel_id=1, source_target_pairs={{0,4},{4,0},{1,5},{5,1},{2,6},{6,2},{3,7},{7,3},{8,12},{12,8},{9,1... | collective-permute-start | bytes 3145736 | tf_op jit(solution)/shard_map/ppermute | solution.py:75
  162.2 19.4 %collective-permute-start.39 = (bf16[256,1024]{0,1:T(8,128)(2,1)S(1)}, bf16[256,1024]{0,1:T(8,128)(2,1)S(1)}, u32[]{:S(2)}, u32[]{:S(2)}) collective-permute-start(bf16[256,1024]{0,1:T(8,128)(2,1)S(1)} %copy-done.146), channel_id=1, source_target_pairs={{0,2},{2,0},{1,3},{3,1},{4,6},{6,4},{5,7},{7,5},{8,10},{10,8},{9,1... | collective-permute-start | bytes 1572872 | tf_op jit(solution)/shard_map/ppermute | solution.py:75
  162.6 36.6 %collective-permute-start.40 = (bf16[128,1024]{1,0:T(8,128)(2,1)S(1)}, bf16[128,1024]{1,0:T(8,128)(2,1)}, u32[]{:S(2)}, u32[]{:S(2)}) collective-permute-start(bf16[128,1024]{1,0:T(8,128)(2,1)S(1)} %collective-permute-done.30), channel_id=1, source_target_pairs={{0,8},{8,16},{16,24},{24,0},{1,9},{9,17},{17,25},{25,1},{2,10},{10... | collective-permute-start | bytes 786440 | tf_op jit(solution)/shard_map/ppermute | solution.py:72
  171.3 27.8 %collective-permute-start.41 = (bf16[128,1024]{0,1:T(8,128)(2,1)S(1)}, bf16[128,1024]{0,1:T(8,128)(2,1)S(1)}, u32[]{:S(2)}, u32[]{:S(2)}) collective-permute-start(bf16[128,1024]{0,1:T(8,128)(2,1)S(1)} %collective-permute-done.31), channel_id=1, source_target_pairs={{0,8},{8,16},{16,24},{24,0},{1,9},{9,17},{17,25},{25,1},{2,10},{10... | collective-permute-start | bytes 786440 | tf_op jit(solution)/shard_map/ppermute | solution.py:72
  199.0 26.3 %collective-permute-start.35 = (bf16[512,1024]{1,0:T(8,128)(2,1)S(1)}, bf16[512,1024]{1,0:T(8,128)(2,1)S(1)}, u32[]{:S(2)}, u32[]{:S(2)}) collective-permute-start(bf16[512,1024]{1,0:T(8,128)(2,1)S(1)} %get-tuple-element.338), channel_id=1, source_target_pairs={{0,1},{1,0},{2,3},{3,2},{4,5},{5,4},{6,7},{7,6},{8,9},{9,8},{10,11... | collective-permute-start | bytes 3145736 | tf_op jit(solution)/shard_map/ppermute | solution.py:72
  201.3 21.9 %collective-permute-start.42 = (bf16[128,1024]{1,0:T(8,128)(2,1)}, bf16[128,1024]{1,0:T(8,128)(2,1)S(1)}, u32[]{:S(2)}, u32[]{:S(2)}) collective-permute-start(bf16[128,1024]{1,0:T(8,128)(2,1)} %collective-permute-done.40), channel_id=1, source_target_pairs={{0,8},{8,16},{16,24},{24,0},{1,9},{9,17},{17,25},{25,1},{2,10},{10... | collective-permute-start | bytes 786440 | tf_op jit(solution)/shard_map/ppermute | solution.py:72
  202.5 53.4 %collective-permute-start.43 = (bf16[256,1024]{0,1:T(8,128)(2,1)S(1)}, bf16[256,1024]{0,1:T(8,128)(2,1)}, u32[]{:S(2)}, u32[]{:S(2)}) collective-permute-start(bf16[256,1024]{0,1:T(8,128)(2,1)S(1)} %copy-done.145), channel_id=1, source_target_pairs={{0,2},{2,0},{1,3},{3,1},{4,6},{6,4},{5,7},{7,5},{8,10},{10,8},{9,1... | collective-permute-start | bytes 1572872 | tf_op jit(solution)/shard_map/ppermute | solution.py:75
  204.0 51.9 %collective-permute-start.44 = (bf16[256,1024]{0,1:T(8,128)(2,1)}, bf16[256,1024]{0,1:T(8,128)(2,1)}, u32[]{:S(2)}, u32[]{:S(2)}) collective-permute-start(bf16[256,1024]{0,1:T(8,128)(2,1)} %pad_maximum_fusion.26), channel_id=1, source_target_pairs={{0,2},{2,0},{1,3},{3,1},{4,6},{6,4},{5,7},{7,5},{8,10},{10,8},{9,1... | collective-permute-start | bytes 1572872 | tf_op jit(solution)/shard_map/ppermute | solution.py:75
  223.2 32.6 %collective-permute-start.46 = (bf16[128,1024]{1,0:T(8,128)(2,1)}, bf16[128,1024]{1,0:T(8,128)(2,1)S(1)}, u32[]{:S(2)}, u32[]{:S(2)}) collective-permute-start(bf16[128,1024]{1,0:T(8,128)(2,1)} %collective-permute-done.40), channel_id=1, source_target_pairs={{0,4},{4,0},{1,5},{5,1},{2,6},{6,2},{3,7},{7,3},{8,12},{12,8},{9,1... | collective-permute-start | bytes 786440 | tf_op jit(solution)/shard_map/ppermute | solution.py:75
  254.0 35.5 %collective-permute-start.37 = (f32[512,1024]{1,0:T(8,128)S(1)}, f32[512,1024]{1,0:T(8,128)S(1)}, u32[]{:S(2)}, u32[]{:S(2)}) collective-permute-start(f32[512,1024]{1,0:T(8,128)S(1)} %dynamic-slice_bitcast_fusion.6), channel_id=1, source_target_pairs={{0,1},{1,0},{2,3},{3,2},{4,5},{5,4},{6,7},{7,6},{8,9},{9,8},{10,11... | collective-permute-start | bytes 6291464 | tf_op jit(solution)/shard_map/ppermute | solution.py:72
  260.6 23.9 %collective-permute-start.52 = (bf16[256,1024]{1,0:T(8,128)(2,1)S(1)}, bf16[256,1024]{1,0:T(8,128)(2,1)S(1)}, u32[]{:S(2)}, u32[]{:S(2)}) collective-permute-start(bf16[256,1024]{1,0:T(8,128)(2,1)S(1)} %copy-done.144), channel_id=1, source_target_pairs={{0,2},{2,0},{1,3},{3,1},{4,6},{6,4},{5,7},{7,5},{8,10},{10,8},{9,1... | collective-permute-start | bytes 1572872 | tf_op jit(solution)/shard_map/ppermute | solution.py:75
  285.8 23.1 %collective-permute-start.54 = (bf16[256,1024]{1,0:T(8,128)(2,1)S(1)}, bf16[256,1024]{1,0:T(8,128)(2,1)S(1)}, u32[]{:S(2)}, u32[]{:S(2)}) collective-permute-start(bf16[256,1024]{1,0:T(8,128)(2,1)S(1)} %pad_maximum_fusion.29), channel_id=1, source_target_pairs={{0,2},{2,0},{1,3},{3,1},{4,6},{6,4},{5,7},{7,5},{8,10},{10,8},{9,1... | collective-permute-start | bytes 1572872 | tf_op jit(solution)/shard_map/ppermute | solution.py:75
  291.2 27.0 %collective-permute-start.38 = (bf16[512,1024]{1,0:T(8,128)(2,1)S(1)}, bf16[512,1024]{1,0:T(8,128)(2,1)S(1)}, u32[]{:S(2)}, u32[]{:S(2)}) collective-permute-start(bf16[512,1024]{1,0:T(8,128)(2,1)S(1)} %get-tuple-element.334), channel_id=1, source_target_pairs={{0,1},{1,0},{2,3},{3,2},{4,5},{5,4},{6,7},{7,6},{8,9},{9,8},{10,11... | collective-permute-start | bytes 3145736 | tf_op jit(solution)/shard_map/ppermute | solution.py:72
  311.7 20.7 %collective-permute-start.57 = (bf16[256,1024]{1,0:T(8,128)(2,1)}, bf16[256,1024]{1,0:T(8,128)(2,1)S(1)}, u32[]{:S(2)}, u32[]{:S(2)}) collective-permute-start(bf16[256,1024]{1,0:T(8,128)(2,1)} %pad_maximum_fusion.27), channel_id=1, source_target_pairs={{0,2},{2,0},{1,3},{3,1},{4,6},{6,4},{5,7},{7,5},{8,10},{10,8},{9,1... | collective-permute-start | bytes 1572872 | tf_op jit(solution)/shard_map/ppermute | solution.py:75
  312.5 19.9 %collective-permute-start.56 = (bf16[128,1024]{0,1:T(8,128)(2,1)S(1)}, bf16[128,1024]{0,1:T(8,128)(2,1)S(1)}, u32[]{:S(2)}, u32[]{:S(2)}) collective-permute-start(bf16[128,1024]{0,1:T(8,128)(2,1)S(1)} %collective-permute-done.41), channel_id=1, source_target_pairs={{0,2},{2,0},{1,3},{3,1},{4,6},{6,4},{5,7},{7,5},{8,10},{10,8},{9,1... | collective-permute-start | bytes 786440 | tf_op jit(solution)/shard_map/ppermute | solution.py:75
  328.8 28.9 %collective-permute-start.49 = (f32[512,1024]{1,0:T(8,128)S(1)}, f32[512,1024]{1,0:T(8,128)S(1)}, u32[]{:S(2)}, u32[]{:S(2)}) collective-permute-start(f32[512,1024]{1,0:T(8,128)S(1)} %dynamic-slice_bitcast_fusion.5), channel_id=1, source_target_pairs={{0,1},{1,0},{2,3},{3,2},{4,5},{5,4},{6,7},{7,6},{8,9},{9,8},{10,11... | collective-permute-start | bytes 6291464 | tf_op jit(solution)/shard_map/ppermute | solution.py:72
  334.5 22.4 %collective-permute-start.60 = (bf16[256,1024]{0,1:T(8,128)(2,1)S(1)}, bf16[256,1024]{0,1:T(8,128)(2,1)S(1)}, u32[]{:S(2)}, u32[]{:S(2)}) collective-permute-start(bf16[256,1024]{0,1:T(8,128)(2,1)S(1)} %pad_maximum_fusion.31), channel_id=1, source_target_pairs={{0,4},{4,0},{1,5},{5,1},{2,6},{6,2},{3,7},{7,3},{8,12},{12,8},{9,1... | collective-permute-start | bytes 1572872 | tf_op jit(solution)/shard_map/ppermute | solution.py:75
  528.2 48.3 %collective-permute-start.74 = (bf16[2,4,2,64,1024]{4,3,2,1,0:T(8,128)(2,1)}, bf16[2,4,2,64,1024]{4,3,2,1,0:T(8,128)(2,1)S(1)}, u32[]{:S(2)}, u32[]{:S(2)}) collective-permute-start(bf16[2,4,2,64,1024]{4,3,2,1,0:T(8,128)(2,1)} %fusion.49), channel_id=1, source_target_pairs={{0,4},{4,0},{1,5},{5,1},{2,6},{6,2},{3,7},{7,3},{8,12},{12,8},{9,1... | collective-permute-start | bytes 6291464 | tf_op jit(solution)/shard_map/ppermute | solution.py:75
  549.0 33.8 %collective-permute-start.69 = (f32[512,1024]{1,0:T(8,128)}, f32[512,1024]{1,0:T(8,128)}, u32[]{:S(2)}, u32[]{:S(2)}) collective-permute-start(f32[512,1024]{1,0:T(8,128)} %dynamic-slice_bitcast_fusion.2), channel_id=1, source_target_pairs={{0,1},{1,0},{2,3},{3,2},{4,5},{5,4},{6,7},{7,6},{8,9},{9,8},{10,11... | collective-permute-start | bytes 6291464 | tf_op jit(solution)/shard_map/ppermute | solution.py:72
  581.4 47.6 %collective-permute-start.76 = (bf16[2,4,2,64,1024]{4,3,0,2,1:T(8,128)(2,1)}, bf16[2,4,2,64,1024]{4,3,0,2,1:T(8,128)(2,1)}, u32[]{:S(2)}, u32[]{:S(2)}) collective-permute-start(bf16[2,4,2,64,1024]{4,3,0,2,1:T(8,128)(2,1)} %fusion.50), channel_id=1, source_target_pairs={{0,4},{4,0},{1,5},{5,1},{2,6},{6,2},{3,7},{7,3},{8,12},{12,8},{9,1... | collective-permute-start | bytes 6291464 | tf_op jit(solution)/shard_map/ppermute | solution.py:75
  588.4 49.7 %collective-permute-start.70 = (bf16[512,1024]{1,0:T(8,128)(2,1)}, bf16[512,1024]{1,0:T(8,128)(2,1)}, u32[]{:S(2)}, u32[]{:S(2)}) collective-permute-start(bf16[512,1024]{1,0:T(8,128)(2,1)} %get-tuple-element.312), channel_id=1, source_target_pairs={{0,1},{1,0},{2,3},{3,2},{4,5},{5,4},{6,7},{7,6},{8,9},{9,8},{10,11... | collective-permute-start | bytes 3145736 | tf_op jit(solution)/shard_map/ppermute | solution.py:72
  593.8 70.9 %collective-permute-start.77 = (bf16[1024,1024]{0,1:T(8,128)(2,1)}, bf16[1024,1024]{0,1:T(8,128)(2,1)}, u32[]{:S(2)}, u32[]{:S(2)}) collective-permute-start(bf16[1024,1024]{0,1:T(8,128)(2,1)} %convolution_convert_fusion), channel_id=1, source_target_pairs={{0,2},{2,0},{1,3},{3,1},{4,6},{6,4},{5,7},{7,5},{8,10},{10,8},{9,1... | collective-permute-start | bytes 6291464 | tf_op jit(solution)/shard_map/ppermute | solution.py:75
  653.1 41.4 %collective-permute-start.71 = (f32[512,1024]{1,0:T(8,128)}, f32[512,1024]{1,0:T(8,128)}, u32[]{:S(2)}, u32[]{:S(2)}) collective-permute-start(f32[512,1024]{1,0:T(8,128)} %dynamic-slice_bitcast_fusion.1), channel_id=1, source_target_pairs={{0,1},{1,0},{2,3},{3,2},{4,5},{5,4},{6,7},{7,6},{8,9},{9,8},{10,11... | collective-permute-start | bytes 6291464 | tf_op jit(solution)/shard_map/ppermute | solution.py:72
  664.7 27.8 %collective-permute-start.80 = (bf16[512,1024]{0,1:T(8,128)(2,1)}, bf16[512,1024]{0,1:T(8,128)(2,1)}, u32[]{:S(2)}, u32[]{:S(2)}) collective-permute-start(bf16[512,1024]{0,1:T(8,128)(2,1)} %pad_maximum_fusion.7), channel_id=1, source_target_pairs={{0,8},{8,16},{16,24},{24,0},{1,9},{9,17},{17,25},{25,1},{2,10},{10... | collective-permute-start | bytes 3145736 | tf_op jit(solution)/shard_map/ppermute | solution.py:72
  673.7 48.4 %collective-permute-start.79 = (bf16[1024,1024]{0,1:T(8,128)(2,1)}, bf16[1024,1024]{0,1:T(8,128)(2,1)}, u32[]{:S(2)}, u32[]{:S(2)}) collective-permute-start(bf16[1024,1024]{0,1:T(8,128)(2,1)} %convolution_convert_fusion.1), channel_id=1, source_target_pairs={{0,2},{2,0},{1,3},{3,1},{4,6},{6,4},{5,7},{7,5},{8,10},{10,8},{9,1... | collective-permute-start | bytes 6291464 | tf_op jit(solution)/shard_map/ppermute | solution.py:75
  681.2 49.9 %collective-permute-start.78 = (bf16[1024,1024]{0,1:T(8,128)(2,1)}, bf16[1024,1024]{0,1:T(8,128)(2,1)S(1)}, u32[]{:S(2)}, u32[]{:S(2)}) collective-permute-start(bf16[1024,1024]{0,1:T(8,128)(2,1)} %pad_maximum_fusion.3), channel_id=1, source_target_pairs={{0,4},{4,0},{1,5},{5,1},{2,6},{6,2},{3,7},{7,3},{8,12},{12,8},{9,1... | collective-permute-start | bytes 6291464 | tf_op jit(solution)/shard_map/ppermute | solution.py:75
  703.0 32.2 %collective-permute-start.72 = (bf16[512,1024]{1,0:T(8,128)(2,1)S(1)}, bf16[512,1024]{1,0:T(8,128)(2,1)S(1)}, u32[]{:S(2)}, u32[]{:S(2)}) collective-permute-start(bf16[512,1024]{1,0:T(8,128)(2,1)S(1)} %get-tuple-element.306), channel_id=1, source_target_pairs={{0,1},{1,0},{2,3},{3,2},{4,5},{5,4},{6,7},{7,6},{8,9},{9,8},{10,11... | collective-permute-start | bytes 3145736 | tf_op jit(solution)/shard_map/ppermute | solution.py:72
  732.9 51.0 %collective-permute-start.83 = (bf16[512,1024]{0,1:T(8,128)(2,1)S(1)}, bf16[512,1024]{0,1:T(8,128)(2,1)S(1)}, u32[]{:S(2)}, u32[]{:S(2)}) collective-permute-start(bf16[512,1024]{0,1:T(8,128)(2,1)S(1)} %pad_maximum_fusion.8), channel_id=1, source_target_pairs={{0,8},{8,16},{16,24},{24,0},{1,9},{9,17},{17,25},{25,1},{2,10},{10... | collective-permute-start | bytes 3145736 | tf_op jit(solution)/shard_map/ppermute | solution.py:72
  733.2 60.8 %collective-permute-start.82 = (bf16[1024,1024]{0,1:T(8,128)(2,1)}, bf16[1024,1024]{0,1:T(8,128)(2,1)}, u32[]{:S(2)}, u32[]{:S(2)}) collective-permute-start(bf16[1024,1024]{0,1:T(8,128)(2,1)} %pad_maximum_fusion.4), channel_id=1, source_target_pairs={{0,4},{4,0},{1,5},{5,1},{2,6},{6,2},{3,7},{7,3},{8,12},{12,8},{9,1... | collective-permute-start | bytes 6291464 | tf_op jit(solution)/shard_map/ppermute | solution.py:75
  734.5 46.1 %collective-permute-start.81 = (bf16[512,1024]{0,1:T(8,128)(2,1)S(1)}, bf16[512,1024]{0,1:T(8,128)(2,1)S(1)}, u32[]{:S(2)}, u32[]{:S(2)}) collective-permute-start(bf16[512,1024]{0,1:T(8,128)(2,1)S(1)} %fusion.52), channel_id=1, source_target_pairs={{0,2},{2,0},{1,3},{3,1},{4,6},{6,4},{5,7},{7,5},{8,10},{10,8},{9,1... | collective-permute-start | bytes 3145736 | tf_op jit(solution)/shard_map/ppermute | solution.py:75
  780.6 19.5 %collective-permute-start.73 = (f32[512,1024]{1,0:T(8,128)}, f32[512,1024]{1,0:T(8,128)}, u32[]{:S(2)}, u32[]{:S(2)}) collective-permute-start(f32[512,1024]{1,0:T(8,128)} %dynamic-slice_bitcast_fusion), channel_id=1, source_target_pairs={{0,1},{1,0},{2,3},{3,2},{4,5},{5,4},{6,7},{7,6},{8,9},{9,8},{10,11... | collective-permute-start | bytes 6291464 | tf_op jit(solution)/shard_map/ppermute | solution.py:72
  815.4 24.5 %collective-permute-start.86 = (bf16[512,1024]{1,0:T(8,128)(2,1)S(1)}, bf16[512,1024]{1,0:T(8,128)(2,1)}, u32[]{:S(2)}, u32[]{:S(2)}) collective-permute-start(bf16[512,1024]{1,0:T(8,128)(2,1)S(1)} %get-tuple-element.185), channel_id=1, source_target_pairs={{0,4},{4,0},{1,5},{5,1},{2,6},{6,2},{3,7},{7,3},{8,12},{12,8},{9,1... | collective-permute-start | bytes 3145736 | tf_op jit(solution)/shard_map/ppermute | solution.py:75
  818.0 23.5 %collective-permute-start.85 = (bf16[512,1024]{1,0:T(8,128)(2,1)S(1)}, bf16[512,1024]{1,0:T(8,128)(2,1)S(1)}, u32[]{:S(2)}, u32[]{:S(2)}) collective-permute-start(bf16[512,1024]{1,0:T(8,128)(2,1)S(1)} %get-tuple-element.185), channel_id=1, source_target_pairs={{0,1},{1,0},{2,3},{3,2},{4,5},{5,4},{6,7},{7,6},{8,9},{9,8},{10,11... | collective-permute-start | bytes 3145736 | tf_op jit(solution)/shard_map/ppermute | solution.py:72
  818.0 48.4 %collective-permute-start.84 = (bf16[1024,1024]{0,1:T(8,128)(2,1)}, bf16[1024,1024]{0,1:T(8,128)(2,1)}, u32[]{:S(2)}, u32[]{:S(2)}) collective-permute-start(bf16[1024,1024]{0,1:T(8,128)(2,1)} %pad_maximum_fusion.2), channel_id=1, source_target_pairs={{0,2},{2,0},{1,3},{3,1},{4,6},{6,4},{5,7},{7,5},{8,10},{10,8},{9,1... | collective-permute-start | bytes 6291464 | tf_op jit(solution)/shard_map/ppermute | solution.py:75
  819.4 33.1 %collective-permute-start.88 = (bf16[640,1024]{0,1:T(8,128)(2,1)S(1)}, bf16[640,1024]{0,1:T(8,128)(2,1)S(1)}, u32[]{:S(2)}, u32[]{:S(2)}) collective-permute-start(bf16[640,1024]{0,1:T(8,128)(2,1)S(1)} %copy-done.109), channel_id=1, source_target_pairs={{0,8},{8,16},{16,24},{24,0},{1,9},{9,17},{17,25},{25,1},{2,10},{10... | collective-permute-start | bytes 3932168 | tf_op jit(solution)/shard_map/ppermute | solution.py:72
  839.9 29.3 %collective-permute-start.87 = (bf16[512,1024]{1,0:T(8,128)(2,1)}, bf16[512,1024]{1,0:T(8,128)(2,1)}, u32[]{:S(2)}, u32[]{:S(2)}) collective-permute-start(bf16[512,1024]{1,0:T(8,128)(2,1)} %collective-permute-done.86), channel_id=1, source_target_pairs={{0,1},{1,0},{2,3},{3,2},{4,5},{5,4},{6,7},{7,6},{8,9},{9,8},{10,11... | collective-permute-start | bytes 3145736 | tf_op jit(solution)/shard_map/ppermute | solution.py:72
  877.1 24.9 %collective-permute-start.89 = (bf16[512,1024]{0,1:T(8,128)(2,1)S(1)}, bf16[512,1024]{0,1:T(8,128)(2,1)S(1)}, u32[]{:S(2)}, u32[]{:S(2)}) collective-permute-start(bf16[512,1024]{0,1:T(8,128)(2,1)S(1)} %slice.1126), channel_id=1, source_target_pairs={{0,4},{4,0},{1,5},{5,1},{2,6},{6,2},{3,7},{7,3},{8,12},{12,8},{9,1... | collective-permute-start | bytes 3145736 | tf_op jit(solution)/shard_map/ppermute | solution.py:75
  878.4 35.7 %collective-permute-start.90 = (bf16[768,1024]{1,0:T(8,128)(2,1)S(1)}, bf16[768,1024]{1,0:T(8,128)(2,1)S(1)}, u32[]{:S(2)}, u32[]{:S(2)}) collective-permute-start(bf16[768,1024]{1,0:T(8,128)(2,1)S(1)} %pad_maximum_fusion.5), channel_id=1, source_target_pairs={{0,2},{2,0},{1,3},{3,1},{4,6},{6,4},{5,7},{7,5},{8,10},{10,8},{9,1... | collective-permute-start | bytes 4718600 | tf_op jit(solution)/shard_map/ppermute | solution.py:75
  879.8 37.9 %collective-permute-start.91 = (bf16[384,1024]{0,1:T(8,128)(2,1)S(1)}, bf16[384,1024]{0,1:T(8,128)(2,1)}, u32[]{:S(2)}, u32[]{:S(2)}) collective-permute-start(bf16[384,1024]{0,1:T(8,128)(2,1)S(1)} %pad_maximum_fusion.11), channel_id=1, source_target_pairs={{0,8},{8,16},{16,24},{24,0},{1,9},{9,17},{17,25},{25,1},{2,10},{10... | collective-permute-start | bytes 2359304 | tf_op jit(solution)/shard_map/ppermute | solution.py:72
  923.4 23.9 %collective-permute-start.92 = (bf16[2,4,64,1024]{3,2,0,1:T(8,128)(2,1)}, bf16[2,4,64,1024]{3,2,0,1:T(8,128)(2,1)}, u32[]{:S(2)}, u32[]{:S(2)}) collective-permute-start(bf16[2,4,64,1024]{3,2,0,1:T(8,128)(2,1)} %fusion.96), channel_id=1, source_target_pairs={{0,2},{2,0},{1,3},{3,1},{4,6},{6,4},{5,7},{7,5},{8,10},{10,8},{9,1... | collective-permute-start | bytes 3145736 | tf_op jit(solution)/shard_map/ppermute | solution.py:75
  924.7 31.2 %collective-permute-start.96 = (bf16[640,1024]{0,1:T(8,128)(2,1)}, bf16[640,1024]{0,1:T(8,128)(2,1)}, u32[]{:S(2)}, u32[]{:S(2)}) collective-permute-start(bf16[640,1024]{0,1:T(8,128)(2,1)} %fusion.143), channel_id=1, source_target_pairs={{0,8},{8,16},{16,24},{24,0},{1,9},{9,17},{17,25},{25,1},{2,10},{10... | collective-permute-start | bytes 3932168 | tf_op jit(solution)/shard_map/ppermute | solution.py:72
  960.0 19.1 %collective-permute-start.97 = (bf16[384,1024]{0,1:T(8,128)(2,1)}, bf16[384,1024]{0,1:T(8,128)(2,1)}, u32[]{:S(2)}, u32[]{:S(2)}) collective-permute-start(bf16[384,1024]{0,1:T(8,128)(2,1)} %pad_maximum_fusion.12), channel_id=1, source_target_pairs={{0,8},{8,16},{16,24},{24,0},{1,9},{9,17},{17,25},{25,1},{2,10},{10... | collective-permute-start | bytes 2359304 | tf_op jit(solution)/shard_map/ppermute | solution.py:72
  981.8 18.9 %collective-permute-start.98 = (bf16[384,1024]{0,1:T(8,128)(2,1)}, bf16[384,1024]{0,1:T(8,128)(2,1)}, u32[]{:S(2)}, u32[]{:S(2)}) collective-permute-start(bf16[384,1024]{0,1:T(8,128)(2,1)} %pad_maximum_fusion.13), channel_id=1, source_target_pairs={{0,8},{8,16},{16,24},{24,0},{1,9},{9,17},{17,25},{25,1},{2,10},{10... | collective-permute-start | bytes 2359304 | tf_op jit(solution)/shard_map/ppermute | solution.py:72
  1002.0 21.0 %collective-permute-start.99 = (f32[16,1024]{1,0:T(8,128)}, f32[16,1024]{1,0:T(8,128)}, u32[]{:S(2)}, u32[]{:S(2)}) collective-permute-start(f32[16,1024]{1,0:T(8,128)} %add.1186), channel_id=1, source_target_pairs={{0,8},{8,0},{16,24},{24,16},{1,9},{9,1},{17,25},{25,17},{2,10},{10... | collective-permute-start | bytes 196616 | tf_op jit(solution)/shard_map/ppermute | solution.py:81
  1009.6 22.3 %collective-permute-start.103 = (f32[12,32,128]{2,1,0:T(8,128)}, f32[12,32,128]{2,1,0:T(8,128)}, u32[]{:S(2)}, u32[]{:S(2)}) collective-permute-start(f32[12,32,128]{2,1,0:T(8,128)} %reduce_sum.349), channel_id=1, source_target_pairs={{0,4},{4,0},{1,5},{5,1},{2,6},{6,2},{3,7},{7,3},{8,12},{12,8},{9,1... | collective-permute-start | bytes 589832 | tf_op jit(solution)/shard_map/ppermute | solution.py:81
  1015.3 32.3 %collective-permute-start.106 = (bf16[2,64,1024]{2,1,0:T(8,128)(2,1)}, bf16[2,64,1024]{2,1,0:T(8,128)(2,1)}, u32[]{:S(2)}, u32[]{:S(2)}) collective-permute-start(bf16[2,64,1024]{2,1,0:T(8,128)(2,1)} %fusion.110), channel_id=1, source_target_pairs={{0,8},{8,16},{16,24},{24,0},{1,9},{9,17},{17,25},{25,1},{2,10},{10... | collective-permute-start | bytes 786440 | tf_op jit(solution)/shard_map/ppermute | solution.py:72
  (298 other events, 2169.6 us)
Sparse Core Ops, SparseCore 0:
  150.8 130.1 all-gather.2

commit v3 on v2

--- a/solution.py
+++ b/solution.py
@@ -67,9 +67,9 @@
     def index(self, axis):
         return lax.axis_index(axis)
 
-    def rotate(self, value, axis):
+    def rotate(self, value, axis, step=1):
         size = self.sizes[axis]
-        return lax.ppermute(value, axis, [(i, (i + 1) % size) for i in range(size)])
+        return lax.ppermute(value, axis, [(i, (i + step) % size) for i in range(size)])
 
     def swap(self, value, axis, step=1):
         return lax.ppermute(value, axis, [(i, i ^ step) for i in range(self.sizes[axis])])
@@ -99,7 +99,17 @@
         return running
 
     def rounds(self, tasks, budget, early=None, pack=True):
-        done, results, last, when = {}, {}, [], 0
+        done, results, last, sent, when = {}, {}, [], [], 0
+
+        def unpack(lists, arrived):
+            start = 0
+            for name, value in lists:
+                results[name] = arrived
+                if len(lists) > 1:
+                    rows = value.size // value.shape[-1]
+                    results[name] = arrived[start : start + rows].reshape(value.shape)
+                    start += rows
+
         waiting = list(tasks)
         while waiting:
             used, picked = {}, []
@@ -108,14 +118,19 @@
                 ready = when >= first and all(
                     done.get(need, when) + between < when for need in needs
                 )
-                load = used.get(axis, 0)
+                load = used.get(axis[0], 0)
                 if ready and (load == 0 or load + size <= budget):
-                    used[axis] = load + size
+                    used[axis[0]] = load + size
                     picked.append(name)
+            tokens = (early or {}).get(when)
+            if tokens and last:
+                last = lax.optimization_barrier((last, tokens))[0]
+                for (_, lists), arrived in zip(sent, last):
+                    unpack(lists, arrived)
             messages = {}
             for name in picked:
                 value = tasks[name][-1](results)
-                key = (tasks[name][0], value.shape[-1], None if pack else name)
+                key = (tasks[name][0], value.shape[-1], value.dtype if pack else name)
                 messages.setdefault(key, []).append((name, value))
             if messages:
                 values = [
@@ -124,19 +139,15 @@
                     else jnp.concatenate([value.reshape(-1, key[1]) for _, value in lists], 0)
                     for key, lists in messages.items()
                 ]
-                held = last + (early or {}).get(when, [])
-                tied = lax.optimization_barrier((values, held))[0]
-                last = []
-                for ((axis, _, _), lists), value in zip(messages.items(), tied):
-                    arrived = self.rotate(value, axis) if axis == "z" else self.swap(value, axis)
-                    last.append(arrived)
-                    start = 0
-                    for name, sent in lists:
-                        results[name] = arrived
-                        if len(lists) > 1:
-                            rows = sent.size // sent.shape[-1]
-                            results[name] = arrived[start : start + rows].reshape(sent.shape)
-                            start += rows
+                tied = lax.optimization_barrier((values, last))[0]
+                last, sent = [], list(messages.items())
+                for ((axis, _, _), lists), value in zip(sent, tied):
+                    if axis[0] == "z":
+                        last.append(self.rotate(value, "z", int(axis[1:] or 1)))
+                    else:
+                        last.append(self.swap(value, axis))
+                    unpack(lists, last[-1])
+                    for name, _ in lists:
                         done[name] = when
             waiting = [name for name in waiting if name not in picked]
             when += 1
@@ -155,15 +166,18 @@
         return jnp.take(array.reshape(rows, count, block), order, axis=1).reshape(rows, cols)
 
     def kernel(order_ref, from_ref, to_ref):
-        to_ref[...] = from_ref[...]
-
+        for p in range(count):
+            start = pl.multiple_of(order_ref[p] * block, LANES)
+            to_ref[:, p * block : (p + 1) * block] = from_ref[:, pl.ds(start, block)]
+
+    step = min(rows, 128)
     return pl.pallas_call(
         kernel,
         grid_spec=pltpu.PrefetchScalarGridSpec(
             num_scalar_prefetch=1,
-            grid=(count,),
-            in_specs=[pl.BlockSpec((rows, block), lambda p, order: (0, order[p]))],
-            out_specs=pl.BlockSpec((rows, block), lambda p, order: (0, p)),
+            grid=(rows // step,),
+            in_specs=[pl.BlockSpec((step, cols), lambda p, order: (p, 0))],
+            out_specs=pl.BlockSpec((step, cols), lambda p, order: (p, 0)),
         ),
         out_shape=jax.ShapeDtypeStruct(array.shape, array.dtype),
         cost_estimate=pl.CostEstimate(
@@ -450,19 +464,28 @@
             )
         return placed([held[-step % size] for step in range(size)], axis)
 
-    codes = all_along(all_along(codes, "c"), "y")
-    codes = codes.transpose(2, 3, 4, 0, 1, 5).reshape(3, books, clips, frames)
-    group_count = jnp.sum(codes[2])
-    codes = chosen(codes, at_y, 2)
-    next_codes, live = codes[1], codes[2].astype(F32)
-    codes_own = codes[0]
-    codes_other = lax.ppermute(
-        jnp.concatenate([codes_own, jnp.full((books, frames), group_count)], 0),
-        "x",
-        [(0, 1), (1, 0)],
-    )
-    pair_count = (group_count + codes_other[books, 0]).astype(F32).reshape(1, 1)
-    codes_other = codes_other[:books]
+    codes = all_along(codes, "c")
+
+    def once(kept, name, make):
+        def get(results):
+            if name not in kept:
+                kept[name] = make(results)
+            return kept[name]
+
+        return get
+
+    made = {}
+
+    def clip_codes(results):
+        both = placed([codes, results["codesy"]], "y")
+        both = both.transpose(2, 3, 4, 0, 1, 5).reshape(3, books, clips, frames)
+        return chosen(both, at_y, 2), jnp.sum(both[2]), chosen(both[0], 1 - at_y, 1)
+
+    clip_codes = once(made, "codes", clip_codes)
+
+    def codes_sent(results):
+        own, count, _ = clip_codes(results)
+        return jnp.concatenate([own[0], jnp.full((books, frames), count)], 0)
 
     turned_in = attend_in.transpose(1, 0, 2)
     turned_out = attend_out.transpose(0, 2, 1)
@@ -470,50 +493,100 @@
     def side_by_side(parts):
         return jnp.concatenate([part.astype(BF16) for part in parts], 1)
 
+    hidden = expand_weights.shape[1]
+    shard_rows = [books * table_rows, rows_in, rows_in]
     shards = {
-        "embed": embed_table.astype(BF16),
-        "self": side_by_side(list(turned_in[:3]) + [turned_out[0]]),
-        "cross": side_by_side(list(turned_in[3:]) + [turned_out[1]]),
-        "expand": expand_weights.astype(BF16),
-        "shrink": shrink_weights.T.astype(BF16),
+        "first": jnp.concatenate(
+            [embed_table.astype(BF16).reshape(-1, width)]
+            + [
+                side_by_side(parts).reshape(-1, width)
+                for parts in (
+                    list(turned_in[:3]) + [turned_out[0]],
+                    list(turned_in[3:]) + [turned_out[1]],
+                )
+            ],
+            0,
+        ),
+        "feed": jnp.concatenate(
+            [part.astype(BF16).reshape(-1, width) for part in (expand_weights, shrink_weights.T)], 0
+        ),
     }
-    routes = {"embed": "zy", "self": "zxy", "cross": "zxy", "expand": "zxy", "shrink": "zyx"}
+    attend_rows = (shards["first"].shape[0] - books * table_rows) // 2
+    starts = {"embed": 0, "self": books * table_rows, "cross": books * table_rows + attend_rows}
     tasks = {}
 
-    def piece(results, group, axis, step):
-        return results[group + axis + str(step)] if step or axis != "z" else shards[group]
-
-    def pair(results, group, axis, step):
-        return jnp.concatenate(
-            [piece(results, group, "z", step), piece(results, group, axis, step)], 0
-        )
-
-    for group, route in routes.items():
-        weight = 4 if group == "embed" else 2
-        for step in range(deep):
-            name = group + "z" + str(step)
-            needs = [name] if step else []
-            if step:
-                ahead = [group + "z" + str(step - 1)] if step > 1 else []
-                tasks[name] = (
-                    "z", weight, ahead, 0, 0, lambda r, g=group, k=step: piece(r, g, "z", k - 1)
-                )
-            first = group + route[1] + str(step)
-            tasks[first] = (
-                route[1], weight, needs, 0, 0, lambda r, g=group, k=step: piece(r, g, "z", k)
-            )
-            if len(route) > 2:
-                tasks[group + route[2] + str(step)] = (
-                    route[2],
-                    2 * weight,
-                    [first],
-                    0,
-                    0,
-                    lambda r, g=group, k=step, a=route[1]: pair(r, g, a, k),
-                )
-        if group == "self":
-            last = ["embedy" + str(step) for step in range(deep)]
-            tasks["rows"] = ("x", 8, last, 0, 0, lambda r: embedded_of(codes_other, table_of(r)))
+    def arrived(results, group, step):
+        return results[group + "z" + str(step)] if step else shards[group]
+
+    def embed_piece(results, axis, step):
+        if axis == "y":
+            return results["embedy" + str(step)]
+        rows = arrived(results, "first", step)[: starts["self"]]
+        return rows.reshape(books, table_rows, width)
+
+    def attend_piece(results, axis, step, part=None):
+        if axis == "x":
+            rows = results["attendx" + str(step)]
+        else:
+            rows = arrived(results, "first", step)[starts["self"] :]
+        if part is not None:
+            rows = rows[part * attend_rows : (part + 1) * attend_rows]
+        return rows
+
+    def near_part(results, part):
+        order = [-spot % deep for spot in range(deep)]
+        blocks = [
+            attend_piece(results, axis, step, part).reshape(rows_in, -1)
+            for axis in ("z", "x")
+            for step in order
+        ]
+        return jnp.concatenate(blocks, 0)
+
+    def add_ring_of(group, size, first):
+        for step in range(1, deep):
+            ahead = [group + "z" + str(step - 1)] if step > 1 else []
+            tasks[group + "z" + str(step)] = (
+                "z", size, ahead, 0, first, lambda r, k=step: arrived(r, group, k - 1)
+            )
+
+    add_ring_of("first", 8, 0)
+    for step in range(deep):
+        needs = ["firstz" + str(step)] if step else []
+        tasks["embedy" + str(step)] = (
+            "y", 4, needs, 0, 0, lambda r, k=step: embed_piece(r, "z", k)
+        )
+        tasks["attendx" + str(step)] = (
+            "x", 4, needs, 0, 0, lambda r, k=step: attend_piece(r, "z", k)
+        )
+        tasks["selfy" + str(step)] = (
+            "y", 4, ["attendx" + str(step)], 0, 0,
+            lambda r, k=step: jnp.concatenate(
+                [attend_piece(r, "z", k, 0), attend_piece(r, "x", k, 0)], 0
+            ),
+        )
+    tasks["codesy"] = ("y", 0, [], 0, 1, lambda r: codes)
+    tasks["codesx"] = ("x", 0, ["codesy"], 0, 2, codes_sent)
+
+    def pair_count(results):
+        count = clip_codes(results)[1] + results["codesx"][books, 0]
+        return jnp.full((8, LANES), count)
+
+    for step in range(1, deep):
+        ahead = "codesx" if step == 1 else "countz" + str(step - 1)
+        tasks["countz" + str(step)] = (
+            "z", 0, [ahead], 0, 0,
+            lambda r, k=step: pair_count(r) if k == 1 else r["countz" + str(k - 1)],
+        )
+
+    add_ring_of("feed", 4, deep - 1)
+    tasks["rows"] = (
+        "x", 8, ["embedy" + str(step) for step in range(deep)] + ["codesx"], 0, deep + 1,
+        lambda r: embedded_of(r["codesx"][:books], table_of(r)),
+    )
+    tasks["crossy"] = (
+        "y", 16, ["attendx" + str(step) for step in range(deep)], 0, deep + 1,
+        lambda r: near_part(r, 1),
+    )
 
     z_place = (at_z - jnp.arange(deep)) % deep
     y_place = jnp.stack([at_y, 1 - at_y])
@@ -521,13 +594,16 @@
     table_ids = ((table_ids * inner + at_c)[:, :, None] * table_rows + jnp.arange(table_rows)).reshape(
         -1
     )
+    beside_ids = ((z_place * 2)[:, None] + jnp.stack([at_x, 1 - at_x])[None, :]) * 2 + at_y
+    beside_ids = (beside_ids * inner + at_c)[:, :, None] * table_rows + jnp.arange(table_rows)
+    beside_ids = beside_ids.reshape(-1)
     kept_table = []
 
     def table_of(results):
         if not kept_table:
             pieces = []
             for step in range(deep):
-                pieces += [piece(results, "embed", "z", step), piece(results, "embed", "y", step)]
+                pieces += [embed_piece(results, "z", step), embed_piece(results, "y", step)]
             kept_table.append(jnp.concatenate(pieces, 1))
         return kept_table[0]
 
@@ -542,27 +618,59 @@
         )
         return rows.astype(BF16)
 
-    results = grid.rounds(tasks, BUDGET, {2: [codes_other]}, pack=False)
+    results = grid.rounds(tasks, BUDGET, pack=False)
+    clip, _, codes_beside = clip_codes(results)
+    codes_own, next_codes, live = clip[0], clip[1], clip[2].astype(F32)
+    codes_other = results["codesx"][:books]
+    token_count = pair_count(results)[0, 0]
+    for step in range(1, deep):
+        token_count = token_count + results["countz" + str(step)][0, 0]
+    token_count = token_count.astype(F32)
     own_part = embedded_of(codes_own, table_of(results)).astype(F32)
     embedded = own_part + results["rows"].astype(F32)
     residual = near(embedded + sinusoid(at_c * own_frames, own_frames, width))
-
-    def both_of(group):
-        halves = [[[None] * deep, [None] * deep], [[None] * deep, [None] * deep]]
-        inside = routes[group][1]
-        for step in range(deep):
-            spot = -step % deep
-            first = [piece(results, group, "z", step), piece(results, group, inside, step)]
-            far = piece(results, group, routes[group][2], step)
-            far = [far[:rows_in], far[rows_in:]]
-            for at, block in enumerate(first):
-                halves[0 if inside == "x" else at][at if inside == "x" else 0][spot] = block
-            for at, block in enumerate(far):
-                halves[1 if inside == "x" else at][at if inside == "x" else 1][spot] = block
-        return [jnp.concatenate(half[0] + half[1], 0) for half in halves]
-
-    weight_self, weight_cross = both_of("self"), both_of("cross")
-    weight_expand, weight_shrink = both_of("expand"), both_of("shrink")
+    residual = after(
+        residual, (results["crossy"], results["feedz" + str(deep - 1)], token_count)
+    )
+
+    far_self = [results["selfy" + str(-spot % deep)] for spot in range(deep)]
+    far_self = [
+        part[half * attend_rows : (half + 1) * attend_rows].reshape(rows_in, -1)
+        for half in range(2)
+        for part in far_self
+    ]
+    weight_self = [near_part(results, 0), jnp.concatenate(far_self, 0)]
+    weight_cross = [near_part(results, 1), results["crossy"]]
+
+    feed_rows = shards["feed"].shape[0] // 2
+    halves = [
+        jnp.concatenate(
+            [
+                arrived(results, "feed", -spot % deep)[part * feed_rows : (part + 1) * feed_rows]
+                for spot in range(deep)
+            ],
+            0,
+        )
+        for part in range(2)
+    ]
+    up_half, back_half = after(halves, residual)
+    up_far, back_far = grid.swap(up_half, "x"), grid.swap(back_half, "y")
+
+    def feed_second(token):
+        rows = up_half.shape[0]
+        near_up, far_back = after((up_far, back_far), token)
+        up = jnp.concatenate([up_half, near_up], 0)
+        back = jnp.concatenate([back_half, far_back], 0)
+        up_other, back_other = grid.swap(up, "y"), grid.swap(back, "x")
+        backs = [
+            jnp.concatenate([back_half, back_other[:rows]], 0),
+            jnp.concatenate([far_back, back_other[rows:]], 0),
+        ]
+        ups = [up, up_other]
+        return [
+            [matrix.reshape(width, hidden) for matrix in pair] for pair in (ups, backs)
+        ]
+
     head_shard = after(head_table.astype(BF16), results["embedy" + str(deep - 1)])
     head = lax.all_gather(head_shard, ("z", "x", "y"), axis=0)
     head_order = (order_near[:, None] * 2 + y_place[None, :]).reshape(-1)
@@ -605,7 +713,8 @@
         total = total + across(mixed, weight[:, triple:])
         self_parts.append(parts)
         self_mixed.append(mixed)
-    residual_one = residual + collect(total)
+    weight_expand, weight_shrink = feed_second(self_mixed[1])
+    residual_one = residual + collect(after(total, (up_far, back_far)))
 
     normed_two = spread(layer_norm(residual_one, gains[2], gains[3]))
     cross_parts, cross_mixed, total = [], [], 0.0
@@ -617,7 +726,9 @@
         total = total + across(mixed, weight[:, triple:])
         cross_parts.append(parts)
         cross_mixed.append(mixed)
-    residual_two = after(residual_one + collect(total), head)
+    residual_two = after(
+        residual_one + collect(total), (head, weight_expand[1], weight_shrink[1])
+    )
 
     normed_three = spread(layer_norm(residual_two, gains[4], gains[5]))
     uppers, actives, total = [], [], 0.0
@@ -629,7 +740,6 @@
         actives.append(active)
     residual_three = true(residual_two + collect(total))
 
-    token_count = grid.total(after(pair_count, residual_one), ("z",))[0, 0]
     final = spread(layer_norm(residual_three, norm_params[6], norm_params[7]))
     logits = jnp.einsum("fd,kvd->kfv", final, head, preferred_element_type=F32)
     is_target = head_ids[None, None, :] == next_codes[:, :, None]
@@ -656,20 +766,27 @@
     def add(name, axis, size, needs, value, between=0, first=0):
         tasks[name] = (axis, size, needs, between, first, lambda r: value(r).astype(BF16))
 
-    def once(name, make):
-        def get(results):
-            if name not in sums:
-                sums[name] = make(results)
-            return sums[name]
-
-        return get
-
-    def add_ring(name, size, needs, parts):
-        get = once(name + "0", lambda r: parts(r)[deep - 1])
+    def add_ring(name, size, needs, parts, direct=False):
+        if direct:
+            for step in range(1, deep):
+                add(
+                    name + "z" + str(step), "z" + str(step), size, needs,
+                    lambda r, k=step: parts(r)[k],
+                )
+            return once(
+                sums,
+                name + "far",
+                lambda r: sum(
+                    (r[name + "z" + str(step)].astype(F32) for step in range(1, deep)),
+                    parts(r)[0].astype(F32),
+                ),
+            )
+        get = once(sums, name + "0", lambda r: parts(r)[deep - 1])
         for step in range(1, deep):
             add(name + "z" + str(step), "z", size, needs, get)
             needs = [name + "z" + str(step)]
             get = once(
+                sums,
                 name + str(step),
                 lambda r, n=needs[0], k=step: r[n].astype(F32) + parts(r)[deep - 1 - k].astype(F32),
             )
@@ -679,9 +796,10 @@
         half = width // 2
         if route[0] == "y":
             add(name + "y", "y", 8 * size, [], lambda r: other, 0, first)
-            whole = once(name + "sum", lambda r: own + r[name + "y"].astype(F32))
+            whole = once(sums, name + "sum", lambda r: own + r[name + "y"].astype(F32))
             add(name + "x", "x", 4 * size, [name + "y"], lambda r: whole(r)[half:])
             quarter = once(
+                sums,
                 name + "part", lambda r: whole(r)[:half] + r[name + "x"].astype(F32)
             )
         else:
@@ -695,34 +813,56 @@
                 lambda r: other[:half] + r[name + "x"][half:].astype(F32),
             )
             quarter = once(
+                sums,
                 name + "part",
                 lambda r: own[:half]
                 + r[name + "x"][:half].astype(F32)
                 + r[name + "y"].astype(F32),
             )
+        return quarter, [name + route[1]]
+
+    def add_rest(name, size, parts, direct=False):
+        whole = once(
+            sums,
+            name + "whole",
+            lambda r: jnp.concatenate([quarter(r) for quarter, _ in parts], 1)
+            if len(parts) > 1
+            else parts[0][0](r),
+        )
         return add_ring(
             name,
             size,
-            [name + route[1]],
+            [need for _, needs in parts for need in needs],
             lambda r: [
-                quarter(r)[step * rows_in : (step + 1) * rows_in] for step in range(deep)
+                whole(r)[step * rows_in : (step + 1) * rows_in] for step in range(deep)
             ],
-        )
-
-    def add_head(name, first, value):
+            direct,
+        )
+
+    def add_head(name, route, value):
         value = value.reshape(value.shape[0], 2, deep, 2, table_rows, width)
-        add(name + "x", "x", 16, [], lambda r: value[:, 1], 0, first)
-        nearer = once(name + "half", lambda r: value[:, 0] + r[name + "x"].astype(F32))
+        own, far = (value[:, 0], value[:, 1]) if route == "x" else (
+            value[:, :, :, 0], value[:, :, :, 1]
+        )
+        add(name + route, route, 16, [], lambda r: far)
+        nearer = once(sums, name + "half", lambda r: own + r[name + route].astype(F32))
+        depth = 1 if route == "x" else 2
         last = add_ring(
-            name, 4, [name + "x"], lambda r: [nearer(r)[:, step] for step in range(deep)]
-        )
-        add(name + "y", "y", 2, [name + "z" + str(deep - 1)], lambda r: last(r)[:, 1])
-        return lambda r: last(r)[:, 0] + r[name + "y"].astype(F32)
+            name,
+            4,
+            [name + route],
+            lambda r: [
+                lax.index_in_dim(nearer(r), step, depth, keepdims=False) for step in range(deep)
+            ],
+        )
+        final_axis = "y" if route == "x" else "x"
+        add(name + final_axis, final_axis, 2, [name + "z" + str(deep - 1)], lambda r: last(r)[:, 1])
+        return lambda r: last(r)[:, 0] + r[name + final_axis].astype(F32)
 
     grad_head = [
         add_head(
             "head" + str(half),
-            half,
+            "xy"[half],
             jnp.einsum(
                 "kfv,fd->kvd",
                 grad_logits[half * books // 2 : (half + 1) * books // 2],
@@ -746,10 +886,13 @@
         total = total + across(grad_upper, up)
         grad_uppers.append(grad_upper)
     grad_normed = collect(total)
-    grad_expand = add_rows(
-        "expand", 2, "yxz", 1, *(down(normed_three, part) for part in grad_uppers)
-    )
-    grad_shrink = add_rows("shrink", 2, "yxz", 2, *(down(rows_grad, active) for active in actives))
+    grad_expand = add_rest(
+        "expand",
+        2,
+        [add_rows("expand", 2, "yxz", 1, *(down(normed_three, part) for part in grad_uppers))],
+    )
+    grads_shrink = [down(rows_grad, active) for active in actives]
+    grad_shrink = add_rest("shrink", 2, [add_rows("shrink", 2, "xyz", 1, *grads_shrink)])
     change, gain_three, shift_three = norm_back(residual_two, gains[4], gains[5], grad_normed)
     grad = grad + change
 
@@ -771,7 +914,16 @@
             )
         )
     grad_normed = collect(total)
-    grad_cross = add_rows("cross", 2, "xyz", 2, *grads)
+    cut = grads[0].shape[1] // 2
+    grad_cross = add_rest(
+        "cross",
+        2,
+        [
+            add_rows("cross0", 1, "yxz", 2, grads[0][:, :cut], grads[1][:, :cut]),
+            add_rows("cross1", 1, "xyz", 2, grads[0][:, cut:], grads[1][:, cut:]),
+        ],
+    )
+    early = {1: [rows_grad]}
     change, gain_two, shift_two = norm_back(residual_one, gains[2], gains[3], grad_normed)
     grad = grad + change
 
@@ -780,77 +932,101 @@
     for weight, parts, mixed in zip(weight_self, self_parts, self_mixed):
         grad_mixed = product(rows_grad, weight[:, triple:]).astype(BF16)
         grad_heads = jnp.concatenate(attend_back(*parts, grad_mixed, True), 1)
+        early[2] = [grad_heads]
         total = total + across(grad_heads, weight[:, :triple])
         grads.append(
             jnp.concatenate([down(normed_one, grad_heads), down(rows_grad, mixed)], 1)
         )
     grad_normed = collect(total)
     change, gain_one, shift_one = norm_back(residual, gains[0], gains[1], grad_normed)
-    grad_self = add_rows("self", 2, "yxz", 4, *grads)
+    cut = grads[0].shape[1] // 2
+    grad_self = add_rest(
+        "self",
+        2,
+        [
+            add_rows("self0", 1, "yxz", 3, grads[0][:, :cut], grads[1][:, :cut]),
+            add_rows("self1", 1, "xyz", 3, grads[0][:, cut:], grads[1][:, cut:]),
+        ],
+        True,
+    )
     grad = true(grad + change)
 
     rows_grad = grad.astype(BF16)
+    early[3] = [rows_grad]
 
     def add_table():
-        add("rows", "x", 8, [], lambda r: rows_grad, 0, 4)
-
         def spread_out(rows):
             return placed(grid.ring(rows, "c"), "c").reshape(frames, width)
 
         own_rows = spread_out(rows_grad)
-        other_rows = once("rows", lambda r: spread_out(r["rows"]))
+        beside = [("x", "y", codes_other, table_ids), ("y", "x", codes_beside, beside_ids)]
         halves = []
-        for half in range(2):
+        for half, (across_axis, sum_axis, codes_far, ids) in enumerate(beside):
             name = "table" + str(half)
             part = slice(half * books // 2, (half + 1) * books // 2)
-
-            def value(r, part=part):
+            add("rows" + str(half), across_axis, 8, [], lambda r: rows_grad, 0, 4)
+            far_rows = once(
+                sums, "rows" + str(half), lambda r, k=half: spread_out(r["rows" + str(k)])
+            )
+
+            def value(r, part=part, far_rows=far_rows, codes_far=codes_far, ids=ids):
                 result = 0.0
-                for codes, rows in ((codes_own, own_rows), (codes_other, other_rows(r))):
+                for codes, rows in ((codes_own, own_rows), (codes_far, far_rows(r))):
+                    places = (codes[part][..., None] == ids).astype(BF16)
                     result = result + jnp.einsum(
-                        "kfv,fd->kvd", hot(codes[part]), rows, preferred_element_type=F32
+                        "kfv,fd->kvd", places, rows, preferred_element_type=F32
                     )
                 return result.reshape(-1, deep, 2, table_rows, width)
 
-            value = once(name + "value", value)
-            add(name + "y", "y", 8, ["rows"], lambda r, v=value: v(r)[:, :, 1], half)
+            value = once(sums, name + "value", value)
+            add(
+                name + sum_axis, sum_axis, 8, ["rows" + str(half)],
+                lambda r, v=value: v(r)[:, :, 1],
+            )
             both = once(
+                sums,
                 name + "both",
-                lambda r, v=value, n=name: v(r)[:, :, 0] + r[n + "y"].astype(F32),
+                lambda r, v=value, n=name + sum_axis: v(r)[:, :, 0] + r[n].astype(F32),
             )
             halves.append(
                 add_ring(
                     name,
                     2,
-                    [name + "y"],
+                    [name + sum_axis],
                     lambda r, b=both: [b(r)[:, -step % deep] for step in range(deep)],
+                    True,
                 )
             )
         return halves
 
     grad_table = add_table()
-    ranks = ["rows", "self", "table", "cross", "expand", "shrink", "head"]
+    norm_grads = [gain_one, shift_one, gain_two, shift_two, gain_three, shift_three]
+    norm_grads = jnp.take(
+        jnp.stack(norm_grads, 0).reshape(6, groups, -1), order_true, axis=1
+    ).reshape(6, width)
+    norm_grads = jnp.concatenate([norm_grads, gain_final[None], shift_final[None]], 0)
+    loss_row = jnp.full((8, width), loss_local)
+    norm_own = grid.total(jnp.concatenate([norm_grads, loss_row], 0), ("c",))
+    tasks["normy"] = ("y", 0, [], 0, 3, lambda r: norm_own)
+    tasks["normx"] = ("x", 0, ["normy"], 0, 4, lambda r: norm_own + r["normy"])
+    norm_plane = once(sums, "norm", lambda r: norm_own + r["normy"] + r["normx"])
+    for step in range(1, deep):
+        tasks["normz" + str(step)] = ("z" + str(step), 0, ["normx"], 0, 0, norm_plane)
+    ranks = ["self", "rows", "table", "cross", "expand", "shrink", "head", "norm"]
     tasks = {
         name: tasks[name]
         for rank in ranks
         for name in tasks
         if name.startswith(rank)
     }
-    results = grid.rounds(tasks, BACK_BUDGET)
+    results = grid.rounds(tasks, BACK_BUDGET, early)
     grad_head = jnp.concatenate([part(results) for part in grad_head], 0)
     grad_table = jnp.concatenate([part(results) for part in grad_table], 0)
     grad_self, grad_cross = grad_self(results), grad_cross(results)
     grad_expand, grad_shrink = grad_expand(results), grad_shrink(results)
-
-    norm_grads = [gain_one, shift_one, gain_two, shift_two, gain_three, shift_three]
-    norm_grads = jnp.take(
-        jnp.stack(norm_grads, 0).reshape(6, groups, -1), order_true, axis=1
-    ).reshape(6, width)
-    norm_grads = jnp.concatenate([norm_grads, gain_final[None], shift_final[None]], 0)
-    loss_row = jnp.full((8, width), loss_local)
-    norm_grads = after(jnp.concatenate([norm_grads, loss_row], 0), results["table1y"])
-    summed = grid.total(norm_grads, ("c", "y", "x"))
-    summed = grid.total(after(summed, grad_self), ("z",))
+    summed = norm_plane(results)
+    for step in range(1, deep):
+        summed = summed + results["normz" + str(step)]
     grad_norm, loss_sum = summed[:8], summed[8, 0]
 
     def columns(array, first, count):
@@ -859,27 +1035,41 @@
             for step in range(count)
         ]
 
-    grad_in = jnp.stack(columns(grad_self, 0, 3) + columns(grad_cross, 0, 3), 0)
-    grad_out = jnp.stack([columns(grad_self, 3, 1)[0].T, columns(grad_cross, 3, 1)[0].T], 0)
-    next_in = MOMENTUM * attend_in_momentum.transpose(1, 0, 2) + grad_in
-    next_out = MOMENTUM * attend_out_momentum + grad_out
+    stack_rows = min(128, cols_in)
+    momentum_in = attend_in_momentum.transpose(1, 0, 2)
+
+    def muon(tensor_parts, data_parts):
+        tensor_factor = newton(
+            grid.total(jnp.concatenate([folded_gram(part) for part in tensor_parts], 0), ("c", "y"))
+        )
+        blocks = [part.reshape(-1, stack_rows, cols_out) for part in data_parts]
+        blocks = jnp.concatenate(blocks, 0)
+        grams = grid.total(folded_gram(blocks), ("x", "z"))
+        ortho = orthogonal(newton(grams), blocks)
+        tensor_out, data_out, start = [], [], 0
+        for part in tensor_parts:
+            count = part.shape[0]
+            tensor_out.append(orthogonal(tensor_factor[start : start + count], part))
+            start += count
+        start = 0
+        for part in data_parts:
+            count = part.size // (stack_rows * cols_out)
+            data_out.append(ortho[start : start + count].reshape(part.shape))
+            start += count
+        return tensor_out, data_out
+
+    next_cross = MOMENTUM * momentum_in[3:] + jnp.stack(columns(grad_cross, 0, 3), 0)
     next_expand = MOMENTUM * expand_momentum + grad_expand
     next_shrink = MOMENTUM * shrink_momentum + grad_shrink.T
-
-    stack_rows = min(128, cols_in)
-    data_blocks = jnp.concatenate(
-        [next_out.reshape(-1, stack_rows, cols_out), next_shrink.reshape(-1, stack_rows, cols_out)],
-        0,
-    )
-    tensor_grams = jnp.concatenate([folded_gram(next_in), folded_gram(next_expand[None])], 0)
-    tensor_factor = newton(grid.total(tensor_grams, ("c", "y")))
-    data_factor = newton(grid.total(folded_gram(data_blocks), ("x", "z")))
-    ortho_in = orthogonal(tensor_factor[:members], next_in)
-    ortho_expand = orthogonal(tensor_factor[members:], next_expand[None])[0]
-    ortho_data = orthogonal(data_factor, data_blocks)
-    count_out = next_out.size // (stack_rows * cols_out)
-    ortho_out = ortho_data[:count_out].reshape(next_out.shape)
-    ortho_shrink = ortho_data[count_out:].reshape(next_shrink.shape)
+    next_out_cross = MOMENTUM * attend_out_momentum[1] + columns(grad_cross, 3, 1)[0].T
+    next_self = MOMENTUM * momentum_in[:3] + jnp.stack(columns(grad_self, 0, 3), 0)
+    next_out_self = MOMENTUM * attend_out_momentum[0] + columns(grad_self, 3, 1)[0].T
+    next_in = jnp.concatenate([next_self, next_cross], 0)
+    next_out = jnp.stack([next_out_self, next_out_cross], 0)
+    (ortho_in, ortho_expand), (ortho_out, ortho_shrink) = muon(
+        [next_in, next_expand[None]], [next_out, next_shrink]
+    )
+    ortho_expand = ortho_expand[0]
     attend_in_new = (turned_in * (1.0 - 0.5 * DECAY) - 0.5 * ortho_in).transpose(1, 0, 2)
     attend_out_new = attend_out * (1.0 - 1.0 * DECAY) - 1.0 * ortho_out
     expand_new = expand_weights * (1.0 - 0.5 * DECAY) - 0.5 * ortho_expand

time: 1100 us -> 1020 us (0.927)
  waiting for transfers between devices: 336 us -> 273 us
  matrix products: 199 us -> 212 us
  other arithmetic: 168 us -> 155 us
    ppermute x49 -> x38, waiting for transfers between devices: 232 us -> 166 us  [swap(): lax.ppermute(value, axis, [(i, i ^ step) for i in range(self.sizes[axis])])]
    slice x17 -> x46, local copies, waits for them, and re-layouts: 6.08 us -> 28.4 us  [the longest x3 5.27 us: attend_piece(): rows = arrived(results, 'first', step)[starts['self']:]]
    ppermute x44, waiting for transfers between devices: 82.2 us -> 97.4 us  [rotate(): lax.ppermute(value, axis, [(i, (i + step) % size) for i in range(size)])]
    dot_general x42, matrix products: 108 us -> 122 us  [contract(): lax.dot_general(left, right, (((left_dim,), (right_dim,)), ((), ())), pre...]
    ppermute x44, starting transfers between devices: 27 us -> 39.7 us  [rotate(): lax.ppermute(value, axis, [(i, (i + step) % size) for i in range(size)])]
    ppermute x49 -> x38, starting transfers between devices: 49.7 us -> 38.4 us  [swap(): lax.ppermute(value, axis, [(i, i ^ step) for i in range(self.sizes[axis])])]
    unnamed x577 -> x488, local copies, waits for them, and re-layouts: 96.8 us -> 91.6 us
  transfers between devices with their start and end apart: 108 -> 90, of which waited for: 46 -> 35; matrix products, arithmetic and copies ran while one was open for 32% -> 33% of each run, Pallas kernels for 8% -> 8%
where the time goes in v3:
time: 1020 us; the launch traced here: 1010 us
  waiting for transfers between devices  273 us (27%)
  matrix products  212 us (21%)
  local copies, waits for them, and re-layouts  168 us (16%)
  other arithmetic  155 us (15%)
  Pallas kernels  90.7 us (9%)
  starting transfers between devices  90.2 us (9%)
  between operations  23.5 us (2%)
    ppermute x38, waiting for transfers between devices, swap(): lax.ppermute(value, axis, [(i, i ^ step) for i in range(self.sizes[axis])])  166 us
    dot_general x42, matrix products, contract(): lax.dot_general(left, right, (((left_dim,), (right_dim,)), ((), ())), pre...  122 us
    ppermute x44, waiting for transfers between devices, rotate(): lax.ppermute(value, axis, [(i, (i + step) % size) for i in range(size)])  97.4 us
    unnamed x488, local copies, waits for them, and re-layouts  91.6 us
    ppermute x44, starting transfers between devices, rotate(): lax.ppermute(value, axis, [(i, (i + step) % size) for i in range(size)])  39.7 us
    ppermute x38, starting transfers between devices, swap(): lax.ppermute(value, axis, [(i, i ^ step) for i in range(self.sizes[axis])])  38.4 us
    pallas_call x4, Pallas kernels, attend_back(): pl.pallas_call(functools.partial(attend_back_kernel, causal), grid=(count...  32.6 us
    dot_general x34, matrix products, times(): return jnp.einsum('brs,bst->brt', left, right, precision=HIGHEST)  25.6 us
  transfers between devices with their start and end apart: 90, of which 35 were waited for; matrix products, arithmetic and copies ran while one was open for 33% of the time, Pallas kernels for 8%

profile of v3, /device:TPU:0, one launch (start us, length us, event | category | flops | bytes accessed | tf_op | source)
XLA Modules:
  0.0 1012.5 jit_solution(16387795324487270862)
XLA Ops:
  26.7 3.8 collective-permute-done.2
  32.1 12.9 %collective-permute-done.1 = bf16[512,1024]{0,1:T(8,128)(2,1)S(1)} collective-permute-done((bf16[512,1024]{0,1:T(8,128)(2,1)}, bf16[512,1024]{0,1:T(8,128)(2,1)S(1)}, u32[]{:S(2)}, u32[]{:S(2)}) %collective-permute-start.1) | collective-permute-done | bytes 1048608 | tf_op jit(solution)/shard_map/ppermute | solution.py:72
  55.1 7.7 collective-permute-done.7
  64.4 8.3 collective-permute-done.6
  78.9 3.7 multiply_sine_fusion
  130.2 6.7 fusion.14
  153.0 3.3 fusion.59
  156.4 6.0 collective-permute-done.20
  164.0 4.6 fusion.16
  189.1 17.0 %collective-permute-done.27 = s32[8,128]{1,0:T(8,128)S(1)} collective-permute-done((s32[8,128]{1,0:T(8,128)S(1)}, s32[8,128]{1,0:T(8,128)S(1)}, u32[]{:S(2)}, u32[]{:S(2)}) %collective-permute-start.27) | collective-permute-done | bytes 4128 | tf_op jit(solution)/shard_map/ppermute | solution.py:72
  207.2 8.2 collective-permute-done.24
  215.4 4.3 maximum_add_fusion.from_ref
  219.7 4.6 shard_map.357
  240.6 9.7 shard_map.360
  250.4 9.9 shard_map.359
  262.8 16.7 %collective-permute-done.29 = bf16[512,1024]{0,1:T(8,128)(2,1)} collective-permute-done((bf16[512,1024]{0,1:T(8,128)(2,1)S(1)}, bf16[512,1024]{0,1:T(8,128)(2,1)}, u32[]{:S(2)}, u32[]{:S(2)}) %collective-permute-start.29) | collective-permute-done | bytes 1048608 | tf_op jit(solution)/shard_map/ppermute | solution.py:75
  279.7 4.1 collective-permute-done.31
  321.7 3.5 fusion.57
  325.2 12.5 %shard_map.358 = bf16[4,16,64,1024]{3,2,1,0:T(8,128)(2,1)} custom-call(s32[16]{0:T(128)} %add.1206.order_ref, bf16[16,4,64,1024]{3,2,1,0:T(8,128)(2,1)} %bitcast.633), custom_call_target="tpu_custom_call" | custom-call | bytes 16777216 | tf_op jit(solution)/shard_map/pallas_call | solution.py:197
  337.8 26.0 %collective-permute-done.34 = bf16[1024,1024]{0,1:T(8,128)(2,1)} collective-permute-done((bf16[1024,1024]{0,1:T(8,128)(2,1)}, bf16[1024,1024]{0,1:T(8,128)(2,1)}, u32[]{:S(2)}, u32[]{:S(2)}) %collective-permute-start.34) | collective-permute-done | bytes 2097184 | tf_op jit(solution)/shard_map/ppermute | solution.py:75
  370.0 15.0 %multiply_convert_fusion.1 = (bf16[1024,1024]{1,0:T(8,128)(2,1)S(1)}, f32[1024,1024]{1,0:T(8,128)}, f32[1024,1024]{1,0:T(8,128)}) fusion(bf16[1024,1024]{1,0:T(8,128)(2,1)S(1)} %bitcast.674, bf16[1024,1024]{0,1:T(8,128)(2,1)} %constant_dynamic-update-slice_fusion.15), kind=kOutput, calls=%fused_computation.59 | convolution fusion | flops 2215641088 | bytes 14680064 | tf_op jit(solution)/shard_map/dot_general | solution.py:217
  385.0 14.9 %multiply_convert_fusion = (bf16[1024,1024]{1,0:T(8,128)(2,1)S(1)}, f32[1024,1024]{1,0:T(8,128)}, f32[1024,1024]{1,0:T(8,128)}) fusion(bf16[1024,1024]{1,0:T(8,128)(2,1)S(1)} %bitcast.675, bf16[1024,1024]{0,1:T(8,128)(2,1)} %collective-permute-done.34), kind=kOutput, calls=%fused_computation.46 | convolution fusion | flops 2215641088 | bytes 14680064 | tf_op jit(solution)/shard_map/dot_general | solution.py:217
  399.9 4.3 fusion.236
  404.3 3.5 convolution_add_fusion.5
  414.3 4.5 shard_map.364
  431.0 12.2 %bitcast_reduce_fusion = (f32[4,1024]{1,0:T(4,128)S(1)}, f32[4,1024,1024]{2,1,0:T(8,128)S(1)}) fusion(bf16[4,1024,1024]{2,1,0:T(8,128)(2,1)} %bitcast.634, bf16[1024,1024,1]{1,0,2:T(8,128)(2,1)} %bitcast.678), kind=kOutput, calls=%fused_computation.11 | convolution fusion | flops 8594124800 | bytes 27279360 | tf_op jit(solution)/shard_map/fd,kvd->kfv/dot_general | solution.py:744
  443.3 4.5 fusion.5
  449.7 6.1 fusion.10
  455.8 13.1 %fusion.46 = f32[2,512,1024]{2,1,0:T(8,128)S(1)} fusion(bf16[4,1024,1024,1]{2,1,0,3:T(8,128)(2,1)} %bitcast.635, bf16[4,128,2,8,512]{4,3,2,1,0:T(8,128)(2,1)} %bitcast.636), kind=kOutput, calls=%fused_computation.101 | convolution fusion | flops 8589934592 | bytes 20971520 | tf_op jit(solution)/shard_map/kfv,kvd->fd/dot_general | solution.py:762
  472.3 8.3 fusion.3
  480.6 4.6 fusion.256
  486.3 3.2 multiply_reduce_fusion.1
  491.8 4.5 shard_map.365
  500.1 6.3 fusion.285
  508.4 8.5 add_convert_fusion.1
  516.9 5.4 add_convert_fusion
  522.3 4.7 fusion.277
  527.0 4.0 convolution_add_fusion.4
  536.8 4.7 fusion.22
  541.5 3.2 copy-done.49
  548.9 5.0 fusion.283
  569.0 3.7 convolution_convert_fusion
  581.8 3.5 shard_map.367
  590.9 3.6 collective-permute-done.48
  597.5 3.7 fusion.20
  630.0 13.0 %shard_map.369 = (bf16[1024,256]{1,0:T(8,128)(2,1)S(1)}, bf16[1024,256]{1,0:T(8,128)(2,1)S(1)}, bf16[1024,256]{1,0:T(8,128)(2,1)S(1)}) custom-call(bf16[1024,768]{1,0:T(8,128)(2,1)S(1)} %copy-done.21, bf16[1024,768]{1,0:T(8,128)(2,1)S(1)} %copy-done.21, bf16[1024,768]{1,0:T(8,128)(2,1)S(1)} %copy-done.21, ...), custom_call_target="tpu_custom_call" | custom-call | flops 5368709120 | bytes 10485760 | tf_op jit(solution)/shard_map/pallas_call | solution.py:342
  644.2 3.7 fusion.75
  647.9 13.0 %shard_map.368 = (bf16[1024,256]{1,0:T(8,128)(2,1)S(1)}, bf16[1024,256]{1,0:T(8,128)(2,1)S(1)}, bf16[1024,256]{1,0:T(8,128)(2,1)S(1)}) custom-call(bf16[1024,768]{1,0:T(8,128)(2,1)S(1)} %copy-done.19, bf16[1024,768]{1,0:T(8,128)(2,1)S(1)} %copy-done.19, bf16[1024,768]{1,0:T(8,128)(2,1)S(1)} %copy-done.19, ...), custom_call_target="tpu_custom_call" | custom-call | flops 5368709120 | bytes 10485760 | tf_op jit(solution)/shard_map/pallas_call | solution.py:342
  661.1 4.0 convolution_add_fusion.3
  667.3 4.0 convert_add_fusion
  698.2 4.7 shard_map.370
  707.0 21.7 %collective-permute-done.55 = bf16[512,1024]{1,0:T(8,128)(2,1)} collective-permute-done((bf16[512,1024]{1,0:T(8,128)(2,1)}, bf16[512,1024]{1,0:T(8,128)(2,1)}, u32[]{:S(2)}, u32[]{:S(2)}) %collective-permute-start.55) | collective-permute-done | bytes 1048608 | tf_op jit(solution)/shard_map/ppermute | solution.py:75
  747.9 33.7 %collective-permute-done.58 = f32[16,1024]{1,0:T(8,128)S(1)} collective-permute-done((f32[16,1024]{1,0:T(8,128)S(1)}, f32[16,1024]{1,0:T(8,128)S(1)}, u32[]{:S(2)}, u32[]{:S(2)}) %collective-permute-start.58) | collective-permute-done | bytes 65568 | tf_op jit(solution)/shard_map/ppermute | solution.py:75
  813.0 6.5 collective-permute-done.63
  819.8 7.6 collective-permute-done.70
  827.8 7.6 collective-permute-done.68
  835.5 8.6 collective-permute-done.66
  870.5 22.1 %collective-permute-done.74 = bf16[128,1024]{1,0:T(8,128)(2,1)S(1)} collective-permute-done((bf16[128,1024]{1,0:T(8,128)(2,1)S(1)}, bf16[128,1024]{1,0:T(8,128)(2,1)S(1)}, u32[]{:S(2)}, u32[]{:S(2)}) %collective-permute-start.74) | collective-permute-done | bytes 262176 | tf_op jit(solution)/shard_map/ppermute | solution.py:72
  893.6 8.6 collective-permute-done.75
  905.9 8.5 collective-permute-done.78
  938.3 3.5 collective-permute-done.83
  957.5 3.7 collective-permute-done.87
  967.0 9.3 collective-permute-start.85
  978.5 6.6 collective-permute-done.85
  (1025 shorter events, 470.1 us)
Async XLA Ops:
  7.2 318.0 %all-gather.3.cloned.1.call-start = ((), (), s32[]{:S(2)}) async-start(), calls=%async_computation | async-start | bytes 8912896 | tf_op jit(solution)/shard_map/all_gather | solution.py:675
  8.7 16.5 %collective-permute-start = (s32[3,4,2,256]{3,1,2,0:T(4,128)}, s32[3,4,2,256]{3,1,2,0:T(4,128)}, u32[]{:S(2)}, u32[]{:S(2)}) collective-permute-start(s32[3,4,2,256]{3,1,2,0:T(4,128)} %get-tuple-element.462), channel_id=1, source_target_pairs={{0,1},{1,0},{2,3},{3,2},{4,5},{5,4},{6,7},{7,6},{8,9},{9,8},{10,11... | collective-permute-start | bytes 73736 | tf_op jit(solution)/shard_map/ppermute | solution.py:463
  15.2 15.3 %collective-permute-start.2 = (bf16[256,1024]{0,1:T(8,128)(2,1)}, bf16[256,1024]{0,1:T(8,128)(2,1)S(1)}, u32[]{:S(2)}, u32[]{:S(2)}) collective-permute-start(bf16[256,1024]{0,1:T(8,128)(2,1)} %maximum_maximum_fusion.1), channel_id=1, source_target_pairs={{0,4},{4,0},{1,5},{5,1},{2,6},{6,2},{3,7},{7,3},{8,12},{12,8},{9,1... | collective-permute-start | bytes 1572872 | tf_op jit(solution)/shard_map/ppermute | solution.py:75
  17.6 27.4 %collective-permute-start.1 = (bf16[512,1024]{0,1:T(8,128)(2,1)}, bf16[512,1024]{0,1:T(8,128)(2,1)S(1)}, u32[]{:S(2)}, u32[]{:S(2)}) collective-permute-start(bf16[512,1024]{0,1:T(8,128)(2,1)} %maximum_maximum_fusion), channel_id=1, source_target_pairs={{0,8},{8,16},{16,24},{24,0},{1,9},{9,17},{17,25},{25,1},{2,10},{10... | collective-permute-start | bytes 3145736 | tf_op jit(solution)/shard_map/ppermute | solution.py:72
  19.2 27.0 %collective-permute-start.3 = (bf16[4,64,1024]{2,1,0:T(8,128)(2,1)}, bf16[4,64,1024]{2,1,0:T(8,128)(2,1)}, u32[]{:S(2)}, u32[]{:S(2)}) collective-permute-start(bf16[4,64,1024]{2,1,0:T(8,128)(2,1)} %get-tuple-element.109), channel_id=1, source_target_pairs={{0,2},{2,0},{1,3},{3,1},{4,6},{6,4},{5,7},{7,5},{8,10},{10,8},{9,1... | collective-permute-start | bytes 1572872 | tf_op jit(solution)/shard_map/ppermute | solution.py:75
  46.2 26.5 %collective-permute-start.6 = (bf16[512,1024]{0,1:T(8,128)(2,1)S(1)}, bf16[512,1024]{0,1:T(8,128)(2,1)}, u32[]{:S(2)}, u32[]{:S(2)}) collective-permute-start(bf16[512,1024]{0,1:T(8,128)(2,1)S(1)} %collective-permute-done.1), channel_id=1, source_target_pairs={{0,8},{8,16},{16,24},{24,0},{1,9},{9,17},{17,25},{25,1},{2,10},{10... | collective-permute-start | bytes 3145736 | tf_op jit(solution)/shard_map/ppermute | solution.py:72
  50.1 25.7 %collective-permute-start.5 = (bf16[4,64,1024]{2,1,0:T(8,128)(2,1)S(1)}, bf16[4,64,1024]{2,1,0:T(8,128)(2,1)}, u32[]{:S(2)}, u32[]{:S(2)}) collective-permute-start(bf16[4,64,1024]{2,1,0:T(8,128)(2,1)S(1)} %bitcast.693), channel_id=1, source_target_pairs={{0,2},{2,0},{1,3},{3,1},{4,6},{6,4},{5,7},{7,5},{8,10},{10,8},{9,1... | collective-permute-start | bytes 1572872 | tf_op jit(solution)/shard_map/ppermute | solution.py:75
  50.6 25.2 %collective-permute-start.8 = (bf16[256,1024]{0,1:T(8,128)(2,1)}, bf16[256,1024]{0,1:T(8,128)(2,1)}, u32[]{:S(2)}, u32[]{:S(2)}) collective-permute-start(bf16[256,1024]{0,1:T(8,128)(2,1)} %pad_maximum_fusion.34), channel_id=1, source_target_pairs={{0,2},{2,0},{1,3},{3,1},{4,6},{6,4},{5,7},{7,5},{8,10},{10,8},{9,1... | collective-permute-start | bytes 1572872 | tf_op jit(solution)/shard_map/ppermute | solution.py:75
  75.8 25.7 %collective-permute-start.10 = (bf16[512,1024]{0,1:T(8,128)(2,1)}, bf16[512,1024]{0,1:T(8,128)(2,1)}, u32[]{:S(2)}, u32[]{:S(2)}) collective-permute-start(bf16[512,1024]{0,1:T(8,128)(2,1)} %collective-permute-done.6), channel_id=1, source_target_pairs={{0,8},{8,16},{16,24},{24,0},{1,9},{9,17},{17,25},{25,1},{2,10},{10... | collective-permute-start | bytes 3145736 | tf_op jit(solution)/shard_map/ppermute | solution.py:72
  82.6 15.2 %collective-permute-start.11 = (bf16[256,1024]{0,1:T(8,128)(2,1)}, bf16[256,1024]{0,1:T(8,128)(2,1)}, u32[]{:S(2)}, u32[]{:S(2)}) collective-permute-start(bf16[256,1024]{0,1:T(8,128)(2,1)} %get-tuple-element.117), channel_id=1, source_target_pairs={{0,4},{4,0},{1,5},{5,1},{2,6},{6,2},{3,7},{7,3},{8,12},{12,8},{9,1... | collective-permute-start | bytes 1572872 | tf_op jit(solution)/shard_map/ppermute | solution.py:75
  91.0 20.8 %collective-permute-start.13 = (bf16[256,1024]{0,1:T(8,128)(2,1)}, bf16[256,1024]{0,1:T(8,128)(2,1)}, u32[]{:S(2)}, u32[]{:S(2)}) collective-permute-start(bf16[256,1024]{0,1:T(8,128)(2,1)} %pad_maximum_fusion.35), channel_id=1, source_target_pairs={{0,2},{2,0},{1,3},{3,1},{4,6},{6,4},{5,7},{7,5},{8,10},{10,8},{9,1... | collective-permute-start | bytes 1572872 | tf_op jit(solution)/shard_map/ppermute | solution.py:75
  92.5 22.0 %collective-permute-start.9 = (bf16[4,64,1024]{2,1,0:T(8,128)(2,1)}, bf16[4,64,1024]{2,1,0:T(8,128)(2,1)}, u32[]{:S(2)}, u32[]{:S(2)}) collective-permute-start(bf16[4,64,1024]{2,1,0:T(8,128)(2,1)} %bitcast.25), channel_id=1, source_target_pairs={{0,2},{2,0},{1,3},{3,1},{4,6},{6,4},{5,7},{7,5},{8,10},{10,8},{9,1... | collective-permute-start | bytes 1572872 | tf_op jit(solution)/shard_map/ppermute | solution.py:75
  114.5 14.9 %collective-permute-start.14 = (bf16[4,64,1024]{2,1,0:T(8,128)(2,1)S(1)}, bf16[4,64,1024]{2,1,0:T(8,128)(2,1)S(1)}, u32[]{:S(2)}, u32[]{:S(2)}) collective-permute-start(bf16[4,64,1024]{2,1,0:T(8,128)(2,1)S(1)} %bitcast.695), channel_id=1, source_target_pairs={{0,2},{2,0},{1,3},{3,1},{4,6},{6,4},{5,7},{7,5},{8,10},{10,8},{9,1... | collective-permute-start | bytes 1572872 | tf_op jit(solution)/shard_map/ppermute | solution.py:75
  119.8 22.2 %collective-permute-start.16 = (bf16[256,1024]{0,1:T(8,128)(2,1)}, bf16[256,1024]{0,1:T(8,128)(2,1)}, u32[]{:S(2)}, u32[]{:S(2)}) collective-permute-start(bf16[256,1024]{0,1:T(8,128)(2,1)} %get-tuple-element.121), channel_id=1, source_target_pairs={{0,4},{4,0},{1,5},{5,1},{2,6},{6,2},{3,7},{7,3},{8,12},{12,8},{9,1... | collective-permute-start | bytes 1572872 | tf_op jit(solution)/shard_map/ppermute | solution.py:75
  120.4 24.6 %collective-permute-start.18 = (bf16[256,1024]{0,1:T(8,128)(2,1)}, bf16[256,1024]{0,1:T(8,128)(2,1)}, u32[]{:S(2)}, u32[]{:S(2)}) collective-permute-start(bf16[256,1024]{0,1:T(8,128)(2,1)} %pad_maximum_fusion.37), channel_id=1, source_target_pairs={{0,8},{8,16},{16,24},{24,0},{1,9},{9,17},{17,25},{25,1},{2,10},{10... | collective-permute-start | bytes 1572872 | tf_op jit(solution)/shard_map/ppermute | solution.py:72
  121.6 23.3 %collective-permute-start.19 = (bf16[256,1024]{0,1:T(8,128)(2,1)}, bf16[256,1024]{0,1:T(8,128)(2,1)}, u32[]{:S(2)}, u32[]{:S(2)}) collective-permute-start(bf16[256,1024]{0,1:T(8,128)(2,1)} %pad_maximum_fusion.36), channel_id=1, source_target_pairs={{0,2},{2,0},{1,3},{3,1},{4,6},{6,4},{5,7},{7,5},{8,10},{10,8},{9,1... | collective-permute-start | bytes 1572872 | tf_op jit(solution)/shard_map/ppermute | solution.py:75
  122.3 18.6 %collective-permute-start.17 = (s32[8,128]{1,0:T(8,128)S(1)}, s32[8,128]{1,0:T(8,128)S(1)}, u32[]{:S(2)}, u32[]{:S(2)}) collective-permute-start(s32[8,128]{1,0:T(8,128)S(1)} %broadcast_in_dim.275), channel_id=1, source_target_pairs={{0,8},{8,16},{16,24},{24,0},{1,9},{9,17},{17,25},{25,1},{2,10},{10... | collective-permute-start | bytes 12296 | tf_op jit(solution)/shard_map/ppermute | solution.py:72
  144.9 17.5 %collective-permute-start.21 = (bf16[256,1024]{0,1:T(8,128)(2,1)}, bf16[256,1024]{0,1:T(8,128)(2,1)}, u32[]{:S(2)}, u32[]{:S(2)}) collective-permute-start(bf16[256,1024]{0,1:T(8,128)(2,1)} %collective-permute-done.18), channel_id=1, source_target_pairs={{0,8},{8,16},{16,24},{24,0},{1,9},{9,17},{17,25},{25,1},{2,10},{10... | collective-permute-start | bytes 1572872 | tf_op jit(solution)/shard_map/ppermute | solution.py:72
  146.3 16.5 %collective-permute-start.23 = (bf16[256,1024]{0,1:T(8,128)(2,1)}, bf16[256,1024]{0,1:T(8,128)(2,1)}, u32[]{:S(2)}, u32[]{:S(2)}) collective-permute-start(bf16[256,1024]{0,1:T(8,128)(2,1)} %pad_maximum_fusion.38), channel_id=1, source_target_pairs={{0,2},{2,0},{1,3},{3,1},{4,6},{6,4},{5,7},{7,5},{8,10},{10,8},{9,1... | collective-permute-start | bytes 1572872 | tf_op jit(solution)/shard_map/ppermute | solution.py:75
  146.8 15.6 %collective-permute-start.20 = (s32[8,128]{1,0:T(8,128)S(1)}, s32[8,128]{1,0:T(8,128)S(1)}, u32[]{:S(2)}, u32[]{:S(2)}) collective-permute-start(s32[8,128]{1,0:T(8,128)S(1)} %collective-permute-done.17), channel_id=1, source_target_pairs={{0,8},{8,16},{16,24},{24,0},{1,9},{9,17},{17,25},{25,1},{2,10},{10... | collective-permute-start | bytes 12296 | tf_op jit(solution)/shard_map/ppermute | solution.py:72
  162.8 61.5 %collective-permute-start.25 = (bf16[1024,1024]{0,1:T(8,128)(2,1)}, bf16[1024,1024]{0,1:T(8,128)(2,1)}, u32[]{:S(2)}, u32[]{:S(2)}) collective-permute-start(bf16[1024,1024]{0,1:T(8,128)(2,1)} %get-tuple-element.129), channel_id=1, source_target_pairs={{0,2},{2,0},{1,3},{3,1},{4,6},{6,4},{5,7},{7,5},{8,10},{10,8},{9,1... | collective-permute-start | bytes 6291464 | tf_op jit(solution)/shard_map/ppermute | solution.py:75
  171.6 35.6 %collective-permute-start.15 = (bf16[512,1024]{1,0:T(8,128)(2,1)}, bf16[512,1024]{1,0:T(8,128)(2,1)}, u32[]{:S(2)}, u32[]{:S(2)}) collective-permute-start(bf16[512,1024]{1,0:T(8,128)(2,1)} %fusion.96), channel_id=1, source_target_pairs={{0,1},{1,0},{2,3},{3,2},{4,5},{5,4},{6,7},{7,6},{8,9},{9,8},{10,11... | collective-permute-start | bytes 3145736 | tf_op jit(solution)/shard_map/ppermute | solution.py:72
  174.6 40.9 %collective-permute-start.24 = (bf16[512,1024]{1,0:T(8,128)(2,1)}, bf16[512,1024]{1,0:T(8,128)(2,1)}, u32[]{:S(2)}, u32[]{:S(2)}) collective-permute-start(bf16[512,1024]{1,0:T(8,128)(2,1)} %fusion.59), channel_id=1, source_target_pairs={{0,4},{4,0},{1,5},{5,1},{2,6},{6,2},{3,7},{7,3},{8,12},{12,8},{9,1... | collective-permute-start | bytes 3145736 | tf_op jit(solution)/shard_map/ppermute | solution.py:75
  182.2 42.0 %collective-permute-start.26 = (bf16[256,1024]{0,1:T(8,128)(2,1)}, bf16[256,1024]{0,1:T(8,128)(2,1)}, u32[]{:S(2)}, u32[]{:S(2)}) collective-permute-start(bf16[256,1024]{0,1:T(8,128)(2,1)} %collective-permute-done.21), channel_id=1, source_target_pairs={{0,8},{8,16},{16,24},{24,0},{1,9},{9,17},{17,25},{25,1},{2,10},{10... | collective-permute-start | bytes 1572872 | tf_op jit(solution)/shard_map/ppermute | solution.py:72
  185.0 21.1 %collective-permute-start.27 = (s32[8,128]{1,0:T(8,128)S(1)}, s32[8,128]{1,0:T(8,128)S(1)}, u32[]{:S(2)}, u32[]{:S(2)}) collective-permute-start(s32[8,128]{1,0:T(8,128)S(1)} %collective-permute-done.20), channel_id=1, source_target_pairs={{0,8},{8,16},{16,24},{24,0},{1,9},{9,17},{17,25},{25,1},{2,10},{10... | collective-permute-start | bytes 12296 | tf_op jit(solution)/shard_map/ppermute | solution.py:72
  235.7 43.8 %collective-permute-start.29 = (bf16[512,1024]{0,1:T(8,128)(2,1)S(1)}, bf16[512,1024]{0,1:T(8,128)(2,1)}, u32[]{:S(2)}, u32[]{:S(2)}) collective-permute-start(bf16[512,1024]{0,1:T(8,128)(2,1)S(1)} %pad_maximum_fusion.18), channel_id=1, source_target_pairs={{0,4},{4,0},{1,5},{5,1},{2,6},{6,2},{3,7},{7,3},{8,12},{12,8},{9,1... | collective-permute-start | bytes 3145736 | tf_op jit(solution)/shard_map/ppermute | solution.py:75
  235.7 43.8 %collective-permute-start.30 = (bf16[512,1024]{0,1:T(8,128)(2,1)}, bf16[512,1024]{0,1:T(8,128)(2,1)}, u32[]{:S(2)}, u32[]{:S(2)}) collective-permute-start(bf16[512,1024]{0,1:T(8,128)(2,1)} %pad_maximum_fusion.19), channel_id=1, source_target_pairs={{0,2},{2,0},{1,3},{3,1},{4,6},{6,4},{5,7},{7,5},{8,10},{10,8},{9,1... | collective-permute-start | bytes 3145736 | tf_op jit(solution)/shard_map/ppermute | solution.py:75
  315.8 48.0 %collective-permute-start.34 = (bf16[1024,1024]{0,1:T(8,128)(2,1)}, bf16[1024,1024]{0,1:T(8,128)(2,1)}, u32[]{:S(2)}, u32[]{:S(2)}) collective-permute-start(bf16[1024,1024]{0,1:T(8,128)(2,1)} %constant_dynamic-update-slice_fusion.15), channel_id=1, source_target_pairs={{0,2},{2,0},{1,3},{3,1},{4,6},{6,4},{5,7},{7,5},{8,10},{10,8},{9,1... | collective-permute-start | bytes 6291464 | tf_op jit(solution)/shard_map/ppermute | solution.py:75
  320.4 47.7 %collective-permute-start.35 = (bf16[1024,1024]{0,1:T(8,128)(2,1)}, bf16[1024,1024]{0,1:T(8,128)(2,1)}, u32[]{:S(2)}, u32[]{:S(2)}) collective-permute-start(bf16[1024,1024]{0,1:T(8,128)(2,1)} %pad_maximum_fusion.2), channel_id=1, source_target_pairs={{0,4},{4,0},{1,5},{5,1},{2,6},{6,2},{3,7},{7,3},{8,12},{12,8},{9,1... | collective-permute-start | bytes 6291464 | tf_op jit(solution)/shard_map/ppermute | solution.py:75
  533.8 22.1 %collective-permute-start.42 = (f32[512,1024]{1,0:T(8,128)}, f32[512,1024]{1,0:T(8,128)}, u32[]{:S(2)}, u32[]{:S(2)}) collective-permute-start(f32[512,1024]{1,0:T(8,128)} %dynamic-slice_bitcast_fusion.2), channel_id=1, source_target_pairs={{0,1},{1,0},{2,3},{3,2},{4,5},{5,4},{6,7},{7,6},{8,9},{9,8},{10,11... | collective-permute-start | bytes 6291464 | tf_op jit(solution)/shard_map/ppermute | solution.py:72
  546.3 48.2 %collective-permute-start.48 = (bf16[2,4,2,64,1024]{4,3,2,1,0:T(8,128)(2,1)}, bf16[2,4,2,64,1024]{4,3,2,1,0:T(8,128)(2,1)}, u32[]{:S(2)}, u32[]{:S(2)}) collective-permute-start(bf16[2,4,2,64,1024]{4,3,2,1,0:T(8,128)(2,1)} %fusion.50), channel_id=1, source_target_pairs={{0,4},{4,0},{1,5},{5,1},{2,6},{6,2},{3,7},{7,3},{8,12},{12,8},{9,1... | collective-permute-start | bytes 6291464 | tf_op jit(solution)/shard_map/ppermute | solution.py:75
  546.8 47.9 %collective-permute-start.49 = (bf16[2,2,4,64,1024]{4,3,0,1,2:T(8,128)(2,1)}, bf16[2,2,4,64,1024]{4,3,0,1,2:T(8,128)(2,1)}, u32[]{:S(2)}, u32[]{:S(2)}) collective-permute-start(bf16[2,2,4,64,1024]{4,3,0,1,2:T(8,128)(2,1)} %fusion.51), channel_id=1, source_target_pairs={{0,2},{2,0},{1,3},{3,1},{4,6},{6,4},{5,7},{7,5},{8,10},{10,8},{9,1... | collective-permute-start | bytes 6291464 | tf_op jit(solution)/shard_map/ppermute | solution.py:75
  590.9 21.3 %collective-permute-start.44 = (f32[512,1024]{1,0:T(8,128)}, f32[512,1024]{1,0:T(8,128)}, u32[]{:S(2)}, u32[]{:S(2)}) collective-permute-start(f32[512,1024]{1,0:T(8,128)} %dynamic-slice_bitcast_fusion.1), channel_id=1, source_target_pairs={{0,1},{1,0},{2,3},{3,2},{4,5},{5,4},{6,7},{7,6},{8,9},{9,8},{10,11... | collective-permute-start | bytes 6291464 | tf_op jit(solution)/shard_map/ppermute | solution.py:72
  602.4 63.4 %collective-permute-start.50 = (bf16[1024,1024]{1,0:T(8,128)(2,1)}, bf16[1024,1024]{1,0:T(8,128)(2,1)}, u32[]{:S(2)}, u32[]{:S(2)}) collective-permute-start(bf16[1024,1024]{1,0:T(8,128)(2,1)} %convolution_convert_fusion), channel_id=1, source_target_pairs={{0,2},{2,0},{1,3},{3,1},{4,6},{6,4},{5,7},{7,5},{8,10},{10,8},{9,1... | collective-permute-start | bytes 6291464 | tf_op jit(solution)/shard_map/ppermute | solution.py:75
  603.8 62.1 %collective-permute-start.51 = (bf16[1024,1024]{1,0:T(8,128)(2,1)}, bf16[1024,1024]{1,0:T(8,128)(2,1)}, u32[]{:S(2)}, u32[]{:S(2)}) collective-permute-start(bf16[1024,1024]{1,0:T(8,128)(2,1)} %pad_maximum_fusion.4), channel_id=1, source_target_pairs={{0,4},{4,0},{1,5},{5,1},{2,6},{6,2},{3,7},{7,3},{8,12},{12,8},{9,1... | collective-permute-start | bytes 6291464 | tf_op jit(solution)/shard_map/ppermute | solution.py:75
  604.5 61.3 %collective-permute-start.52 = (bf16[512,1024]{1,0:T(8,128)(2,1)}, bf16[512,1024]{1,0:T(8,128)(2,1)}, u32[]{:S(2)}, u32[]{:S(2)}) collective-permute-start(bf16[512,1024]{1,0:T(8,128)(2,1)} %pad_maximum_fusion.22), channel_id=1, source_target_pairs={{0,8},{8,16},{16,24},{24,0},{1,9},{9,17},{17,25},{25,1},{2,10},{10... | collective-permute-start | bytes 3145736 | tf_op jit(solution)/shard_map/ppermute | solution.py:72
  665.2 27.9 %collective-permute-start.46 = (f32[512,1024]{1,0:T(8,128)S(1)}, f32[512,1024]{1,0:T(8,128)S(1)}, u32[]{:S(2)}, u32[]{:S(2)}) collective-permute-start(f32[512,1024]{1,0:T(8,128)S(1)} %dynamic-slice_bitcast_fusion), channel_id=1, source_target_pairs={{0,1},{1,0},{2,3},{3,2},{4,5},{5,4},{6,7},{7,6},{8,9},{9,8},{10,11... | collective-permute-start | bytes 6291464 | tf_op jit(solution)/shard_map/ppermute | solution.py:72
  679.2 27.2 %collective-permute-start.53 = (bf16[1024,512]{1,0:T(8,128)(2,1)}, bf16[1024,512]{1,0:T(8,128)(2,1)}, u32[]{:S(2)}, u32[]{:S(2)}) collective-permute-start(bf16[1024,512]{1,0:T(8,128)(2,1)} %pad_maximum_fusion.20), channel_id=1, source_target_pairs={{0,2},{2,0},{1,3},{3,1},{4,6},{6,4},{5,7},{7,5},{8,10},{10,8},{9,1... | collective-permute-start | bytes 3145736 | tf_op jit(solution)/shard_map/ppermute | solution.py:75
  680.7 26.3 %collective-permute-start.54 = (bf16[1024,512]{1,0:T(8,128)(2,1)}, bf16[1024,512]{1,0:T(8,128)(2,1)}, u32[]{:S(2)}, u32[]{:S(2)}) collective-permute-start(bf16[1024,512]{1,0:T(8,128)(2,1)} %pad_maximum_fusion.21), channel_id=1, source_target_pairs={{0,4},{4,0},{1,5},{5,1},{2,6},{6,2},{3,7},{7,3},{8,12},{12,8},{9,1... | collective-permute-start | bytes 3145736 | tf_op jit(solution)/shard_map/ppermute | solution.py:75
  681.2 47.5 %collective-permute-start.55 = (bf16[512,1024]{1,0:T(8,128)(2,1)}, bf16[512,1024]{1,0:T(8,128)(2,1)}, u32[]{:S(2)}, u32[]{:S(2)}) collective-permute-start(bf16[512,1024]{1,0:T(8,128)(2,1)} %slice.1361), channel_id=1, source_target_pairs={{0,4},{4,0},{1,5},{5,1},{2,6},{6,2},{3,7},{7,3},{8,12},{12,8},{9,1... | collective-permute-start | bytes 3145736 | tf_op jit(solution)/shard_map/ppermute | solution.py:75
  682.7 46.0 %collective-permute-start.56 = (bf16[512,1024]{1,0:T(8,128)(2,1)}, bf16[512,1024]{1,0:T(8,128)(2,1)}, u32[]{:S(2)}, u32[]{:S(2)}) collective-permute-start(bf16[512,1024]{1,0:T(8,128)(2,1)} %fusion.55), channel_id=1, source_target_pairs={{0,2},{2,0},{1,3},{3,1},{4,6},{6,4},{5,7},{7,5},{8,10},{10,8},{9,1... | collective-permute-start | bytes 3145736 | tf_op jit(solution)/shard_map/ppermute | solution.py:75
  693.1 35.6 %collective-permute-start.57 = (bf16[512,1024]{1,0:T(8,128)(2,1)}, bf16[512,1024]{1,0:T(8,128)(2,1)}, u32[]{:S(2)}, u32[]{:S(2)}) collective-permute-start(bf16[512,1024]{1,0:T(8,128)(2,1)} %pad_maximum_fusion.23), channel_id=1, source_target_pairs={{0,8},{8,16},{16,24},{24,0},{1,9},{9,17},{17,25},{25,1},{2,10},{10... | collective-permute-start | bytes 3145736 | tf_op jit(solution)/shard_map/ppermute | solution.py:72
  706.4 34.3 %collective-permute-start.47 = (f32[16,1024]{1,0:T(8,128)S(1)}, f32[16,1024]{1,0:T(8,128)S(1)}, u32[]{:S(2)}, u32[]{:S(2)}) collective-permute-start(f32[16,1024]{1,0:T(8,128)S(1)} %maximum_maximum_fusion.2), channel_id=1, source_target_pairs={{0,1},{1,0},{2,3},{3,2},{4,5},{5,4},{6,7},{7,6},{8,9},{9,8},{10,11... | collective-permute-start | bytes 196616 | tf_op jit(solution)/shard_map/ppermute | solution.py:81
  740.8 41.4 %collective-permute-start.61 = (bf16[768,1024]{1,0:T(8,128)(2,1)S(1)}, bf16[768,1024]{1,0:T(8,128)(2,1)S(1)}, u32[]{:S(2)}, u32[]{:S(2)}) collective-permute-start(bf16[768,1024]{1,0:T(8,128)(2,1)S(1)} %pad_maximum_fusion.7), channel_id=1, source_target_pairs={{0,8},{8,16},{16,24},{24,0},{1,9},{9,17},{17,25},{25,1},{2,10},{10... | collective-permute-start | bytes 4718600 | tf_op jit(solution)/shard_map/ppermute | solution.py:72
  743.7 41.9 %collective-permute-start.60 = (bf16[1536,512]{1,0:T(8,128)(2,1)S(1)}, bf16[1536,512]{1,0:T(8,128)(2,1)S(1)}, u32[]{:S(2)}, u32[]{:S(2)}) collective-permute-start(bf16[1536,512]{1,0:T(8,128)(2,1)S(1)} %pad_maximum_fusion.6), channel_id=1, source_target_pairs={{0,4},{4,0},{1,5},{5,1},{2,6},{6,2},{3,7},{7,3},{8,12},{12,8},{9,1... | collective-permute-start | bytes 4718600 | tf_op jit(solution)/shard_map/ppermute | solution.py:75
  745.1 42.0 %collective-permute-start.59 = (bf16[1536,512]{1,0:T(8,128)(2,1)S(1)}, bf16[1536,512]{1,0:T(8,128)(2,1)S(1)}, u32[]{:S(2)}, u32[]{:S(2)}) collective-permute-start(bf16[1536,512]{1,0:T(8,128)(2,1)S(1)} %pad_maximum_fusion.5), channel_id=1, source_target_pairs={{0,2},{2,0},{1,3},{3,1},{4,6},{6,4},{5,7},{7,5},{8,10},{10,8},{9,1... | collective-permute-start | bytes 4718600 | tf_op jit(solution)/shard_map/ppermute | solution.py:75
  746.5 35.1 %collective-permute-start.58 = (f32[16,1024]{1,0:T(8,128)S(1)}, f32[16,1024]{1,0:T(8,128)S(1)}, u32[]{:S(2)}, u32[]{:S(2)}) collective-permute-start(f32[16,1024]{1,0:T(8,128)S(1)} %fusion.234), channel_id=1, source_target_pairs={{0,2},{2,0},{1,3},{3,1},{4,6},{6,4},{5,7},{7,5},{8,10},{10,8},{9,1... | collective-permute-start | bytes 196616 | tf_op jit(solution)/shard_map/ppermute | solution.py:75
  747.9 57.2 %collective-permute-start.65 = (bf16[512,1024]{1,0:T(8,128)(2,1)}, bf16[512,1024]{1,0:T(8,128)(2,1)}, u32[]{:S(2)}, u32[]{:S(2)}) collective-permute-start(bf16[512,1024]{1,0:T(8,128)(2,1)} %get-tuple-element.318), channel_id=1, source_target_pairs={{0,1},{1,0},{2,3},{3,2},{4,5},{5,4},{6,7},{7,6},{8,9},{9,8},{10,11... | collective-permute-start | bytes 3145736 | tf_op jit(solution)/shard_map/ppermute | solution.py:72
  795.3 15.8 %collective-permute-start.64 = (bf16[512,512]{1,0:T(8,128)(2,1)}, bf16[512,512]{1,0:T(8,128)(2,1)}, u32[]{:S(2)}, u32[]{:S(2)}) collective-permute-start(bf16[512,512]{1,0:T(8,128)(2,1)} %get-tuple-element.178), channel_id=1, source_target_pairs={{0,2},{2,0},{1,3},{3,1},{4,6},{6,4},{5,7},{7,5},{8,10},{10,8},{9,1... | collective-permute-start | bytes 1572872 | tf_op jit(solution)/shard_map/ppermute | solution.py:75
  803.7 15.8 %collective-permute-start.63 = (bf16[512,512]{1,0:T(8,128)(2,1)}, bf16[512,512]{1,0:T(8,128)(2,1)S(1)}, u32[]{:S(2)}, u32[]{:S(2)}) collective-permute-start(bf16[512,512]{1,0:T(8,128)(2,1)} %slice.1365), channel_id=1, source_target_pairs={{0,4},{4,0},{1,5},{5,1},{2,6},{6,2},{3,7},{7,3},{8,12},{12,8},{9,1... | collective-permute-start | bytes 1572872 | tf_op jit(solution)/shard_map/ppermute | solution.py:75
  807.3 28.1 %collective-permute-start.68 = (bf16[640,1024]{1,0:T(8,128)(2,1)}, bf16[640,1024]{1,0:T(8,128)(2,1)S(1)}, u32[]{:S(2)}, u32[]{:S(2)}) collective-permute-start(bf16[640,1024]{1,0:T(8,128)(2,1)} %get-tuple-element.180), channel_id=1, source_target_pairs={{0,2},{2,0},{1,3},{3,1},{4,6},{6,4},{5,7},{7,5},{8,10},{10,8},{9,1... | collective-permute-start | bytes 3932168 | tf_op jit(solution)/shard_map/ppermute | solution.py:75
  808.0 36.2 %collective-permute-start.66 = (bf16[640,1024]{1,0:T(8,128)(2,1)S(1)}, bf16[640,1024]{1,0:T(8,128)(2,1)S(1)}, u32[]{:S(2)}, u32[]{:S(2)}) collective-permute-start(bf16[640,1024]{1,0:T(8,128)(2,1)S(1)} %copy-done.118), channel_id=1, source_target_pairs={{0,4},{4,0},{1,5},{5,1},{2,6},{6,2},{3,7},{7,3},{8,12},{12,8},{9,1... | collective-permute-start | bytes 3932168 | tf_op jit(solution)/shard_map/ppermute | solution.py:75
  809.4 18.0 %collective-permute-start.70 = (bf16[384,1024]{1,0:T(8,128)(2,1)S(1)}, bf16[384,1024]{1,0:T(8,128)(2,1)S(1)}, u32[]{:S(2)}, u32[]{:S(2)}) collective-permute-start(bf16[384,1024]{1,0:T(8,128)(2,1)S(1)} %pad_maximum_fusion.26), channel_id=1, source_target_pairs={{0,8},{8,16},{16,24},{24,0},{1,9},{9,17},{17,25},{25,1},{2,10},{10... | collective-permute-start | bytes 2359304 | tf_op jit(solution)/shard_map/ppermute | solution.py:72
  863.4 40.6 %collective-permute-start.77 = (bf16[2,4,64,1024]{3,2,0,1:T(8,128)(2,1)S(1)}, bf16[2,4,64,1024]{3,2,0,1:T(8,128)(2,1)S(1)}, u32[]{:S(2)}, u32[]{:S(2)}) collective-permute-start(bf16[2,4,64,1024]{3,2,0,1:T(8,128)(2,1)S(1)} %fusion.103), channel_id=1, source_target_pairs={{0,2},{2,0},{1,3},{3,1},{4,6},{6,4},{5,7},{7,5},{8,10},{10,8},{9,1... | collective-permute-start | bytes 3145736 | tf_op jit(solution)/shard_map/ppermute | solution.py:75
  864.6 38.5 %collective-permute-start.79 = (bf16[384,1024]{1,0:T(8,128)(2,1)S(1)}, bf16[384,1024]{1,0:T(8,128)(2,1)S(1)}, u32[]{:S(2)}, u32[]{:S(2)}) collective-permute-start(bf16[384,1024]{1,0:T(8,128)(2,1)S(1)} %pad_maximum_fusion.27), channel_id=1, source_target_pairs={{0,8},{8,16},{16,24},{24,0},{1,9},{9,17},{17,25},{25,1},{2,10},{10... | collective-permute-start | bytes 2359304 | tf_op jit(solution)/shard_map/ppermute | solution.py:72
  864.8 27.7 %collective-permute-start.74 = (bf16[128,1024]{1,0:T(8,128)(2,1)S(1)}, bf16[128,1024]{1,0:T(8,128)(2,1)S(1)}, u32[]{:S(2)}, u32[]{:S(2)}) collective-permute-start(bf16[128,1024]{1,0:T(8,128)(2,1)S(1)} %get-tuple-element.185), channel_id=1, source_target_pairs={{0,8},{8,16},{16,24},{24,0},{1,9},{9,17},{17,25},{25,1},{2,10},{10... | collective-permute-start | bytes 786440 | tf_op jit(solution)/shard_map/ppermute | solution.py:72
  866.4 35.8 %collective-permute-start.75 = (bf16[128,1024]{1,0:T(8,128)(2,1)S(1)}, bf16[128,1024]{1,0:T(8,128)(2,1)S(1)}, u32[]{:S(2)}, u32[]{:S(2)}) collective-permute-start(bf16[128,1024]{1,0:T(8,128)(2,1)S(1)} %get-tuple-element.186), channel_id=1, source_target_pairs={{0,16},{8,24},{16,0},{24,8},{1,17},{9,25},{17,1},{25,9},{2,18},{10... | collective-permute-start | bytes 786440 | tf_op jit(solution)/shard_map/ppermute | solution.py:72
  869.0 33.2 %collective-permute-start.76 = (bf16[128,1024]{1,0:T(8,128)(2,1)S(1)}, bf16[128,1024]{1,0:T(8,128)(2,1)S(1)}, u32[]{:S(2)}, u32[]{:S(2)}) collective-permute-start(bf16[128,1024]{1,0:T(8,128)(2,1)S(1)} %get-tuple-element.187), channel_id=1, source_target_pairs={{0,24},{8,0},{16,8},{24,16},{1,25},{9,1},{17,9},{25,17},{2,26},{10... | collective-permute-start | bytes 786440 | tf_op jit(solution)/shard_map/ppermute | solution.py:72
  892.6 21.8 %collective-permute-start.78 = (bf16[2,4,64,1024]{3,2,0,1:T(8,128)(2,1)S(1)}, bf16[2,4,64,1024]{3,2,0,1:T(8,128)(2,1)S(1)}, u32[]{:S(2)}, u32[]{:S(2)}) collective-permute-start(bf16[2,4,64,1024]{3,2,0,1:T(8,128)(2,1)S(1)} %fusion.104), channel_id=1, source_target_pairs={{0,4},{4,0},{1,5},{5,1},{2,6},{6,2},{3,7},{7,3},{8,12},{12,8},{9,1... | collective-permute-start | bytes 3145736 | tf_op jit(solution)/shard_map/ppermute | solution.py:75
  924.5 31.9 %collective-permute-start.86 = (bf16[256,1024]{1,0:T(8,128)(2,1)}, bf16[256,1024]{1,0:T(8,128)(2,1)}, u32[]{:S(2)}, u32[]{:S(2)}) collective-permute-start(bf16[256,1024]{1,0:T(8,128)(2,1)} %pad_maximum_fusion.39), channel_id=1, source_target_pairs={{0,8},{8,16},{16,24},{24,0},{1,9},{9,17},{17,25},{25,1},{2,10},{10... | collective-permute-start | bytes 1572872 | tf_op jit(solution)/shard_map/ppermute | solution.py:72
  927.0 34.2 %collective-permute-start.87 = (bf16[256,1024]{1,0:T(8,128)(2,1)}, bf16[256,1024]{1,0:T(8,128)(2,1)}, u32[]{:S(2)}, u32[]{:S(2)}) collective-permute-start(bf16[256,1024]{1,0:T(8,128)(2,1)} %pad_maximum_fusion.40), channel_id=1, source_target_pairs={{0,16},{8,24},{16,0},{24,8},{1,17},{9,25},{17,1},{25,9},{2,18},{10... | collective-permute-start | bytes 1572872 | tf_op jit(solution)/shard_map/ppermute | solution.py:72
  927.3 35.0 %collective-permute-start.88 = (bf16[256,1024]{1,0:T(8,128)(2,1)}, bf16[256,1024]{1,0:T(8,128)(2,1)}, u32[]{:S(2)}, u32[]{:S(2)}) collective-permute-start(bf16[256,1024]{1,0:T(8,128)(2,1)} %pad_maximum_fusion.41), channel_id=1, source_target_pairs={{0,24},{8,0},{16,8},{24,16},{1,25},{9,1},{17,9},{25,17},{2,26},{10... | collective-permute-start | bytes 1572872 | tf_op jit(solution)/shard_map/ppermute | solution.py:72
  942.5 23.4 %collective-permute-start.84 = (f32[12,32,128]{2,1,0:T(8,128)}, f32[12,32,128]{2,1,0:T(8,128)}, u32[]{:S(2)}, u32[]{:S(2)}) collective-permute-start(f32[12,32,128]{2,1,0:T(8,128)} %add.1334), channel_id=1, source_target_pairs={{0,8},{8,0},{16,24},{24,16},{1,9},{9,1},{17,25},{25,17},{2,10},{10... | collective-permute-start | bytes 589832 | tf_op jit(solution)/shard_map/ppermute | solution.py:81
  967.0 18.1 %collective-permute-start.85 = (f32[12,32,128]{2,1,0:T(8,128)S(1)}, f32[12,32,128]{2,1,0:T(8,128)S(1)}, u32[]{:S(2)}, u32[]{:S(2)}) collective-permute-start(f32[12,32,128]{2,1,0:T(8,128)S(1)} %add.1335), channel_id=1, source_target_pairs={{0,16},{8,24},{16,0},{24,8},{1,17},{9,25},{17,1},{25,9},{2,18},{10... | collective-permute-start | bytes 589832 | tf_op jit(solution)/shard_map/ppermute | solution.py:81
  (255 other events, 2960.1 us)
Sparse Core Ops, SparseCore 0:
  149.3 144.0 all-gather.2

commit v4 on v3

--- a/solution.py
+++ b/solution.py
@@ -26,6 +26,7 @@
 BUDGET = 8
 BACK_BUDGET = 16
 KERNEL_VMEM = 48 * 1024 * 1024
+LIGHT = pl.CostEstimate(flops=1024, bytes_accessed=1024, transcendentals=0)
 
 
 def layer_norm(values, gain, shift):
@@ -39,8 +40,15 @@
     return backward(grad)
 
 
-def exact_gelu(values):
-    return jax.nn.gelu(values, approximate=False)
+def gelu_and_slope(values):
+    falling = jnp.exp(-0.5 * values * values)
+    near = 1.0 / (1.0 + (0.3275911 * math.sqrt(0.5)) * jnp.abs(values))
+    series = 1.061405429
+    for weight in (-1.453152027, 1.421413741, -0.284496736, 0.254829592):
+        series = series * near + weight
+    tail = 0.5 * series * near * falling
+    below = jnp.where(values >= 0.0, 1.0 - tail, tail)
+    return values * below, below + values * falling * (1.0 / math.sqrt(2.0 * math.pi))
 
 
 def sinusoid(first, length, width):
@@ -180,32 +188,33 @@
             out_specs=pl.BlockSpec((step, cols), lambda p, order: (p, 0)),
         ),
         out_shape=jax.ShapeDtypeStruct(array.shape, array.dtype),
-        cost_estimate=pl.CostEstimate(
-            flops=0, bytes_accessed=2 * array.size * array.dtype.itemsize, transcendentals=0
-        ),
+        cost_estimate=LIGHT,
     )(order, array)
 
 
 def arranged(blocks, order):
     count, books, rows, cols = blocks.shape
+    half = books // 2
     if rows % 16:
-        return jnp.take(blocks, order, axis=0).transpose(1, 0, 2, 3)
-
-    def kernel(order_ref, from_ref, to_ref):
-        to_ref[...] = from_ref[...].reshape(to_ref.shape)
-
+        whole = jnp.take(blocks, order, axis=0).transpose(1, 0, 2, 3)
+        return whole[:half], whole[half:]
+
+    def kernel(order_ref, from_ref, first_ref, second_ref):
+        first_ref[...] = from_ref[:, :half].reshape(first_ref.shape)
+        second_ref[...] = from_ref[:, half:].reshape(second_ref.shape)
+
+    result = jax.ShapeDtypeStruct((half, count, rows, cols), blocks.dtype)
+    spec = pl.BlockSpec((half, 1, rows, cols), lambda p, order: (0, p, 0, 0))
     return pl.pallas_call(
         kernel,
         grid_spec=pltpu.PrefetchScalarGridSpec(
             num_scalar_prefetch=1,
             grid=(count,),
             in_specs=[pl.BlockSpec((1, books, rows, cols), lambda p, order: (order[p], 0, 0, 0))],
-            out_specs=pl.BlockSpec((books, 1, rows, cols), lambda p, order: (0, p, 0, 0)),
+            out_specs=[spec, spec],
         ),
-        out_shape=jax.ShapeDtypeStruct((books, count, rows, cols), blocks.dtype),
-        cost_estimate=pl.CostEstimate(
-            flops=0, bytes_accessed=2 * blocks.size * blocks.dtype.itemsize, transcendentals=0
-        ),
+        out_shape=[result, result],
+        cost_estimate=LIGHT,
     )(order, blocks)
 
 
@@ -308,7 +317,6 @@
 def attend(queries, keys, values, causal):
     frames, key_rows = queries[0].shape[0], keys[0].shape[0]
     count = queries[2]
-    cost = 4 * frames * key_rows * LANES * count * 2
 
     def spec(rows, start):
         return pl.BlockSpec((rows, LANES), lambda p, start=start: (0, start + p))
@@ -324,16 +332,13 @@
         out_specs=spec(frames, 0),
         out_shape=jax.ShapeDtypeStruct((frames, count * LANES), BF16),
         compiler_params=pltpu.CompilerParams(vmem_limit_bytes=KERNEL_VMEM),
-        cost_estimate=pl.CostEstimate(
-            flops=cost, bytes_accessed=cost // 256, transcendentals=cost // 256
-        ),
+        cost_estimate=LIGHT,
     )(queries[0], keys[0], values[0])
 
 
 def attend_back(queries, keys, values, grad, causal):
     frames, key_rows = queries[0].shape[0], keys[0].shape[0]
     count = queries[2]
-    cost = 10 * frames * key_rows * LANES * count * 2
 
     def spec(rows, start):
         return pl.BlockSpec((rows, LANES), lambda p, start=start: (0, start + p))
@@ -356,9 +361,7 @@
         ],
         scratch_shapes=[pltpu.VMEM((key_rows, LANES), F32), pltpu.VMEM((key_rows, LANES), F32)],
         compiler_params=pltpu.CompilerParams(vmem_limit_bytes=KERNEL_VMEM),
-        cost_estimate=pl.CostEstimate(
-            flops=cost, bytes_accessed=cost // 512, transcendentals=cost // 512
-        ),
+        cost_estimate=LIGHT,
     )(queries[0], keys[0], values[0], grad)
 
 
@@ -571,13 +574,19 @@
         count = clip_codes(results)[1] + results["codesx"][books, 0]
         return jnp.full((8, LANES), count)
 
-    for step in range(1, deep):
-        ahead = "codesx" if step == 1 else "countz" + str(step - 1)
-        tasks["countz" + str(step)] = (
-            "z", 0, [ahead], 0, 0,
-            lambda r, k=step: pair_count(r) if k == 1 else r["countz" + str(k - 1)],
-        )
-
+    steps = [1 << power for power in range((deep - 1).bit_length())]
+
+    def counted(results, known):
+        count = pair_count(results)
+        for step in steps[:known]:
+            count = count + results["count" + str(step)]
+        return count
+
+    for at, step in enumerate(steps):
+        ahead = "count" + str(steps[at - 1]) if at else "codesx"
+        tasks["count" + str(step)] = (
+            "z" + str(step), 0, [ahead], 0, 0, lambda r, k=at: counted(r, k)
+        )
     add_ring_of("feed", 4, deep - 1)
     tasks["rows"] = (
         "x", 8, ["embedy" + str(step) for step in range(deep)] + ["codesx"], 0, deep + 1,
@@ -622,16 +631,11 @@
     clip, _, codes_beside = clip_codes(results)
     codes_own, next_codes, live = clip[0], clip[1], clip[2].astype(F32)
     codes_other = results["codesx"][:books]
-    token_count = pair_count(results)[0, 0]
-    for step in range(1, deep):
-        token_count = token_count + results["countz" + str(step)][0, 0]
-    token_count = token_count.astype(F32)
+    token_count = counted(results, len(steps))[0, 0].astype(F32)
     own_part = embedded_of(codes_own, table_of(results)).astype(F32)
     embedded = own_part + results["rows"].astype(F32)
     residual = near(embedded + sinusoid(at_c * own_frames, own_frames, width))
-    residual = after(
-        residual, (results["crossy"], results["feedz" + str(deep - 1)], token_count)
-    )
+    residual = after(residual, token_count)
 
     far_self = [results["selfy" + str(-spot % deep)] for spot in range(deep)]
     far_self = [
@@ -671,10 +675,10 @@
             [matrix.reshape(width, hidden) for matrix in pair] for pair in (ups, backs)
         ]
 
-    head_shard = after(head_table.astype(BF16), results["embedy" + str(deep - 1)])
+    head_shard = after(head_table.astype(BF16), results["rows"])
     head = lax.all_gather(head_shard, ("z", "x", "y"), axis=0)
     head_order = (order_near[:, None] * 2 + y_place[None, :]).reshape(-1)
-    head = arranged(head, head_order).reshape(books, -1, width)
+    head = [part.reshape(books // 2, -1, width) for part in arranged(head, head_order)]
     head_ids = (head_order * inner + at_c)[:, None] * table_rows + jnp.arange(table_rows)
     head_ids = head_ids.reshape(-1)
 
@@ -713,8 +717,8 @@
         total = total + across(mixed, weight[:, triple:])
         self_parts.append(parts)
         self_mixed.append(mixed)
-    weight_expand, weight_shrink = feed_second(self_mixed[1])
-    residual_one = residual + collect(after(total, (up_far, back_far)))
+    total = after(total, (results["crossy"], results["feedz" + str(deep - 1)]))
+    residual_one = residual + collect(total)
 
     normed_two = spread(layer_norm(residual_one, gains[2], gains[3]))
     cross_parts, cross_mixed, total = [], [], 0.0
@@ -726,27 +730,35 @@
         total = total + across(mixed, weight[:, triple:])
         cross_parts.append(parts)
         cross_mixed.append(mixed)
+    weight_expand, weight_shrink = feed_second(cross_mixed[0])
+    total = after(total, (up_far, back_far))
     residual_two = after(
         residual_one + collect(total), (head, weight_expand[1], weight_shrink[1])
     )
 
     normed_three = spread(layer_norm(residual_two, gains[4], gains[5]))
-    uppers, actives, total = [], [], 0.0
+    slopes, actives, total = [], [], 0.0
     for up, back in zip(weight_expand, weight_shrink):
-        upper = product(normed_three, up)
-        active = exact_gelu(upper).astype(BF16)
+        active, slope = gelu_and_slope(product(normed_three, up))
+        active, slope = lax.optimization_barrier((active.astype(BF16), slope))
         total = total + across(active, back)
-        uppers.append(upper)
+        slopes.append(slope)
         actives.append(active)
     residual_three = true(residual_two + collect(total))
 
     final = spread(layer_norm(residual_three, norm_params[6], norm_params[7]))
-    logits = jnp.einsum("fd,kvd->kfv", final, head, preferred_element_type=F32)
-    is_target = head_ids[None, None, :] == next_codes[:, :, None]
-    row_max = jnp.max(logits, -1)
-    picked = jnp.sum(jnp.where(is_target, logits, 0.0), -1)
-    row_sum = jnp.sum(jnp.exp(logits - row_max[..., None]), -1)
-    stats = grid.ring(jnp.stack([row_max, row_sum, picked], 0), "c")
+    logits, targets, stats = [], [], []
+    for half, part in enumerate(head):
+        wanted = next_codes[half * books // 2 : (half + 1) * books // 2]
+        values = jnp.einsum("fd,kvd->kfv", final, part, preferred_element_type=F32)
+        is_target = head_ids[None, None, :] == wanted[:, :, None]
+        row_max = jnp.max(values, -1)
+        picked = jnp.sum(jnp.where(is_target, values, 0.0), -1)
+        row_sum = jnp.sum(jnp.exp(values - row_max[..., None]), -1)
+        logits.append(values)
+        targets.append(is_target)
+        stats.append(jnp.stack([row_max, row_sum, picked], 0))
+    stats = grid.ring(jnp.concatenate(stats, 1), "c")
     top = stats[0][0]
     for stat in stats[1:]:
         top = jnp.maximum(top, stat[0])
@@ -754,12 +766,18 @@
     picked = sum(stat[2] for stat in stats)
     log_total = top + jnp.log(row_sum)
     loss_local = jnp.where(at_c == 0, jnp.sum((log_total - picked) * live), 0.0)
-    grad_logits = (
-        (jnp.exp(logits - log_total[..., None]) - is_target.astype(F32))
-        * (live / token_count)[..., None]
-    ).astype(BF16)
+    share = live / token_count
+    grad_logits = []
+    for half in range(2):
+        part = slice(half * books // 2, (half + 1) * books // 2)
+        grad_part = jnp.exp(logits[half] - log_total[part][..., None]) - targets[half].astype(F32)
+        grad_logits.append((grad_part * share[part][..., None]).astype(BF16))
+    grad_logits = lax.optimization_barrier(grad_logits)
     grad_final = collect(
-        jnp.einsum("kfv,kvd->fd", grad_logits, head, preferred_element_type=F32)
+        sum(
+            jnp.einsum("kfv,kvd->fd", values, part, preferred_element_type=F32)
+            for values, part in zip(grad_logits, head)
+        )
     )
     tasks, sums = {}, {}
 
@@ -865,7 +883,7 @@
             "xy"[half],
             jnp.einsum(
                 "kfv,fd->kvd",
-                grad_logits[half * books // 2 : (half + 1) * books // 2],
+                grad_logits[half],
                 final,
                 preferred_element_type=F32,
             ),
@@ -880,9 +898,9 @@
 
     rows_grad = spread(grad)
     grad_uppers, total = [], 0.0
-    for up, back, upper in zip(weight_expand, weight_shrink, uppers):
+    for up, back, slope in zip(weight_expand, weight_shrink, slopes):
         grad_active = product(rows_grad, back)
-        grad_upper = jax.vjp(exact_gelu, upper)[1](grad_active)[0].astype(BF16)
+        grad_upper = (slope * grad_active).astype(BF16)
         total = total + across(grad_upper, up)
         grad_uppers.append(grad_upper)
     grad_normed = collect(total)

time: 1020 us -> 975 us (0.956)
  local copies, waits for them, and re-layouts: 168 us -> 145 us
  matrix products: 212 us -> 190 us
  waiting for transfers between devices: 273 us -> 292 us
  other arithmetic: 155 us -> 137 us
    ppermute x38, waiting for transfers between devices: 166 us -> 201 us  [swap(): lax.ppermute(value, axis, [(i, i ^ step) for i in range(self.sizes[axis])])]
    dot_general x42, matrix products: 122 us -> 96.8 us  [contract(): lax.dot_general(left, right, (((left_dim,), (right_dim,)), ((), ())), pre...]
    unnamed x488 -> x481, local copies, waits for them, and re-layouts: 91.6 us -> 74.8 us
    ppermute x44 -> x43, waiting for transfers between devices: 97.4 us -> 80.7 us  [rotate(): lax.ppermute(value, axis, [(i, (i + step) % size) for i in range(size)])]
    ppermute x44 -> x43, starting transfers between devices: 39.7 us -> 31.7 us  [rotate(): lax.ppermute(value, axis, [(i, (i + step) % size) for i in range(size)])]
    dot_general x4 -> x6, matrix products: 36.3 us -> 37.1 us  [the longest x2 13.9 us: body(): jnp.einsum('kfv,kvd->fd', values, part, preferred_element_type=F32)]
  transfers between devices with their start and end apart: 90 -> 89, of which waited for: 35 -> 37; matrix products, arithmetic and copies ran while one was open for 33% -> 32% of each run, Pallas kernels for 8% -> 8%
where the time goes in v4:
time: 975 us; the launch traced here: 964 us
  waiting for transfers between devices  292 us (30%)
  matrix products  190 us (19%)
  local copies, waits for them, and re-layouts  145 us (15%)
  other arithmetic  137 us (14%)
  Pallas kernels  90.9 us (9%)
  starting transfers between devices  87.8 us (9%)
  between operations  22.6 us (2%)
    ppermute x38, waiting for transfers between devices, swap(): lax.ppermute(value, axis, [(i, i ^ step) for i in range(self.sizes[axis])])  201 us
    dot_general x42, matrix products, contract(): lax.dot_general(left, right, (((left_dim,), (right_dim,)), ((), ())), pre...  96.8 us
    ppermute x43, waiting for transfers between devices, rotate(): lax.ppermute(value, axis, [(i, (i + step) % size) for i in range(size)])  80.7 us
    unnamed x481, local copies, waits for them, and re-layouts  74.8 us
    ppermute x38, starting transfers between devices, swap(): lax.ppermute(value, axis, [(i, i ^ step) for i in range(self.sizes[axis])])  43.5 us
    pallas_call x4, Pallas kernels, attend_back(): pl.pallas_call(functools.partial(attend_back_kernel, causal), grid=(count...  32.4 us
    ppermute x43, starting transfers between devices, rotate(): lax.ppermute(value, axis, [(i, (i + step) % size) for i in range(size)])  31.7 us
    dot_general x34, matrix products, times(): return jnp.einsum('brs,bst->brt', left, right, precision=HIGHEST)  25.6 us
  transfers between devices with their start and end apart: 89, of which 37 were waited for; matrix products, arithmetic and copies ran while one was open for 32% of the time, Pallas kernels for 8%

profile of v4, /device:TPU:0, one launch (start us, length us, event | category | flops | bytes accessed | tf_op | source)
XLA Modules:
  0.0 964.3 jit_solution(1035858880004838211)
XLA Ops:
  11.2 3.0 collective-permute-start.1
  23.0 6.1 collective-permute-done.2
  30.2 9.4 collective-permute-done.1
  61.2 6.4 collective-permute-done.6
  92.0 4.0 collective-permute-done.10
  109.4 10.0 %collective-permute-done.14 = bf16[4,64,1024]{2,1,0:T(8,128)(2,1)S(1)} collective-permute-done((bf16[4,64,1024]{2,1,0:T(8,128)(2,1)S(1)}, bf16[4,64,1024]{2,1,0:T(8,128)(2,1)S(1)}, u32[]{:S(2)}, u32[]{:S(2)}) %collective-permute-start.14) | collective-permute-done | bytes 524320 | tf_op jit(solution)/shard_map/ppermute | solution.py:83
  120.2 6.7 fusion.14
  135.0 5.8 collective-permute-done.23
  140.8 4.0 collective-permute-done.20
  149.7 21.6 %collective-permute-done.24 = bf16[512,1024]{1,0:T(8,128)(2,1)S(1)} collective-permute-done((bf16[512,1024]{1,0:T(8,128)(2,1)}, bf16[512,1024]{1,0:T(8,128)(2,1)S(1)}, u32[]{:S(2)}, u32[]{:S(2)}) %collective-permute-start.24) | collective-permute-done | bytes 1048608 | tf_op jit(solution)/shard_map/ppermute | solution.py:83
  171.3 6.7 fusion.16
  178.3 3.7 multiply_sine_fusion
  188.5 4.9 shard_map.357
  205.8 4.0 convolution_convert_fusion.1.query_ref.key_ref.value_ref
  210.4 9.7 %shard_map.360 = bf16[1024,256]{1,0:T(8,128)(2,1)S(1)} custom-call(bf16[1024,768]{1,0:T(8,128)(2,1)S(1)} %convolution_convert_fusion.1.query_ref.key_ref.value_ref, bf16[1024,768]{1,0:T(8,128)(2,1)S(1)} %convolution_convert_fusion.1.query_ref.key_ref.value_ref, bf16[1024,768]{1,0:T(8,128)(2,1)S(1)} %convolution_convert_fusion.1.query_ref.key_ref.value_ref), custom_call_target="tpu_custom_call" | custom-call | flops 1024 | bytes 1024 | tf_op jit(solution)/shard_map/pallas_call | solution.py:324
  224.1 9.9 %shard_map.359 = bf16[1024,256]{1,0:T(8,128)(2,1)S(1)} custom-call(bf16[1024,768]{1,0:T(8,128)(2,1)S(1)} %convolution_convert_fusion.2.query_ref.key_ref.value_ref, bf16[1024,768]{1,0:T(8,128)(2,1)S(1)} %convolution_convert_fusion.2.query_ref.key_ref.value_ref, bf16[1024,768]{1,0:T(8,128)(2,1)S(1)} %convolution_convert_fusion.2.query_ref.key_ref.value_ref), custom_call_target="tpu_custom_call" | custom-call | flops 1024 | bytes 1024 | tf_op jit(solution)/shard_map/pallas_call | solution.py:324
  236.0 27.6 %collective-permute-done.26 = bf16[1024,1024]{0,1:T(8,128)(2,1)} collective-permute-done((bf16[1024,1024]{0,1:T(8,128)(2,1)S(1)}, bf16[1024,1024]{0,1:T(8,128)(2,1)}, u32[]{:S(2)}, u32[]{:S(2)}) %collective-permute-start.26) | collective-permute-done | bytes 2097184 | tf_op jit(solution)/shard_map/ppermute | solution.py:83
  292.5 10.4 %collective-permute-done.30 = bf16[512,1024]{0,1:T(8,128)(2,1)S(1)} collective-permute-done((bf16[512,1024]{0,1:T(8,128)(2,1)S(1)}, bf16[512,1024]{0,1:T(8,128)(2,1)S(1)}, u32[]{:S(2)}, u32[]{:S(2)}) %collective-permute-start.30) | collective-permute-done | bytes 1048608 | tf_op jit(solution)/shard_map/ppermute | solution.py:83
  311.9 3.5 fusion.52
  315.5 12.6 %shard_map.358 = (bf16[2,16,64,1024]{3,2,1,0:T(8,128)(2,1)}, bf16[2,16,64,1024]{3,2,1,0:T(8,128)(2,1)}) custom-call(s32[16]{0:T(128)} %add.1238.order_ref, bf16[16,4,64,1024]{3,2,1,0:T(8,128)(2,1)} %bitcast.646), custom_call_target="tpu_custom_call" | custom-call | flops 1024 | bytes 1024 | tf_op jit(solution)/shard_map/pallas_call | solution.py:208
  328.0 27.7 %collective-permute-done.33 = bf16[1024,1024]{0,1:T(8,128)(2,1)} collective-permute-done((bf16[1024,1024]{0,1:T(8,128)(2,1)}, bf16[1024,1024]{0,1:T(8,128)(2,1)}, u32[]{:S(2)}, u32[]{:S(2)}) %collective-permute-start.33) | collective-permute-done | bytes 2097184 | tf_op jit(solution)/shard_map/ppermute | solution.py:83
  359.9 9.5 fusion.22
  369.5 9.5 fusion.27
  384.8 3.5 collective-permute-done.36
  390.2 4.6 shard_map.364
  407.0 7.6 bitcast_reduce_fusion.1
  414.6 4.6 bitcast_reduce_fusion
  419.2 4.5 fusion.12
  425.7 5.9 fusion.7
  431.6 9.3 fusion.270
  440.9 4.6 bitcast_add_fusion
  453.7 4.7 shard_map.365
  462.2 6.4 fusion.279
  478.1 4.7 fusion.271
  482.8 4.0 convolution_add_fusion.4
  492.7 4.6 fusion.30
  497.2 3.2 copy-done.49
  506.1 4.8 fusion.277
  510.9 3.9 multiply_reduce_fusion.2
  521.7 3.9 convolution_convert_fusion
  532.3 3.1 shard_map.366
  535.5 3.1 shard_map.367
  543.0 6.7 collective-permute-done.47
  553.8 3.7 fusion.28
  585.7 13.2 %shard_map.369 = (bf16[1024,256]{1,0:T(8,128)(2,1)S(1)}, bf16[1024,256]{1,0:T(8,128)(2,1)S(1)}, bf16[1024,256]{1,0:T(8,128)(2,1)S(1)}) custom-call(bf16[1024,768]{1,0:T(8,128)(2,1)S(1)} %copy-done.3, bf16[1024,768]{1,0:T(8,128)(2,1)S(1)} %copy-done.3, bf16[1024,768]{1,0:T(8,128)(2,1)S(1)} %copy-done.3, bf16[1024,256]{1,0:T(8,128)(2,1)S(1)} %convolution_convert_fusion.4.grad_ref), custom_call_target="tpu_custom_call" | custom-call | flops 1024 | bytes 1024 | tf_op jit(solution)/shard_map/pallas_call | solution.py:347
  598.9 13.0 %shard_map.368 = (bf16[1024,256]{1,0:T(8,128)(2,1)S(1)}, bf16[1024,256]{1,0:T(8,128)(2,1)S(1)}, bf16[1024,256]{1,0:T(8,128)(2,1)S(1)}) custom-call(bf16[1024,768]{1,0:T(8,128)(2,1)S(1)} %copy-done.5, bf16[1024,768]{1,0:T(8,128)(2,1)S(1)} %copy-done.5, bf16[1024,768]{1,0:T(8,128)(2,1)S(1)} %copy-done.5, bf16[1024,256]{1,0:T(8,128)(2,1)S(1)} %convolution_convert_fusion.5.grad_ref), custom_call_target="tpu_custom_call" | custom-call | flops 1024 | bytes 1024 | tf_op jit(solution)/shard_map/pallas_call | solution.py:347
  612.1 3.2 fusion.70
  620.9 4.0 convert_add_fusion
  630.1 2.8 fusion.50
  651.0 4.7 shard_map.370
  659.7 21.8 %collective-permute-done.54 = bf16[512,1024]{1,0:T(8,128)(2,1)} collective-permute-done((bf16[512,1024]{1,0:T(8,128)(2,1)}, bf16[512,1024]{1,0:T(8,128)(2,1)}, u32[]{:S(2)}, u32[]{:S(2)}) %collective-permute-start.54) | collective-permute-done | bytes 1048608 | tf_op jit(solution)/shard_map/ppermute | solution.py:83
  700.9 31.1 %collective-permute-done.57 = f32[16,1024]{1,0:T(8,128)S(1)} collective-permute-done((f32[16,1024]{1,0:T(8,128)S(1)}, f32[16,1024]{1,0:T(8,128)S(1)}, u32[]{:S(2)}, u32[]{:S(2)}) %collective-permute-start.57) | collective-permute-done | bytes 65568 | tf_op jit(solution)/shard_map/ppermute | solution.py:83
  743.1 3.1 pad_maximum_fusion.11
  764.1 6.3 collective-permute-done.62
  770.9 8.0 collective-permute-done.69
  779.2 7.4 collective-permute-done.67
  786.8 9.1 collective-permute-done.65
  821.7 21.8 %collective-permute-done.73 = bf16[128,1024]{1,0:T(8,128)(2,1)S(1)} collective-permute-done((bf16[128,1024]{1,0:T(8,128)(2,1)S(1)}, bf16[128,1024]{1,0:T(8,128)(2,1)S(1)}, u32[]{:S(2)}, u32[]{:S(2)}) %collective-permute-start.73) | collective-permute-done | bytes 262176 | tf_op jit(solution)/shard_map/ppermute | solution.py:80
  844.5 8.6 collective-permute-done.74
  856.8 8.5 collective-permute-done.77
  889.7 3.0 collective-permute-done.82
  908.5 3.4 collective-permute-done.86
  917.8 9.6 collective-permute-start.84
  929.7 7.0 collective-permute-done.84
  (1019 shorter events, 433.7 us)
Async XLA Ops:
  7.2 308.2 %all-gather.3.cloned.1.call-start = ((), (), s32[]{:S(2)}) async-start(), calls=%async_computation | async-start | bytes 8912896 | tf_op jit(solution)/shard_map/all_gather | solution.py:679
  11.2 28.4 %collective-permute-start.1 = (bf16[512,1024]{0,1:T(8,128)(2,1)}, bf16[512,1024]{0,1:T(8,128)(2,1)S(1)}, u32[]{:S(2)}, u32[]{:S(2)}) collective-permute-start(bf16[512,1024]{0,1:T(8,128)(2,1)} %maximum_maximum_fusion), channel_id=1, source_target_pairs={{0,8},{8,16},{16,24},{24,0},{1,9},{9,17},{17,25},{25,1},{2,10},{10... | collective-permute-start | bytes 3145736 | tf_op jit(solution)/shard_map/ppermute | solution.py:80
  14.8 14.3 %collective-permute-start.2 = (bf16[256,1024]{0,1:T(8,128)(2,1)S(1)}, bf16[256,1024]{0,1:T(8,128)(2,1)S(1)}, u32[]{:S(2)}, u32[]{:S(2)}) collective-permute-start(bf16[256,1024]{0,1:T(8,128)(2,1)S(1)} %maximum_maximum_fusion.1), channel_id=1, source_target_pairs={{0,4},{4,0},{1,5},{5,1},{2,6},{6,2},{3,7},{7,3},{8,12},{12,8},{9,1... | collective-permute-start | bytes 1572872 | tf_op jit(solution)/shard_map/ppermute | solution.py:83
  16.3 25.1 %collective-permute-start.3 = (bf16[4,64,1024]{2,1,0:T(8,128)(2,1)S(1)}, bf16[4,64,1024]{2,1,0:T(8,128)(2,1)}, u32[]{:S(2)}, u32[]{:S(2)}) collective-permute-start(bf16[4,64,1024]{2,1,0:T(8,128)(2,1)S(1)} %get-tuple-element.117), channel_id=1, source_target_pairs={{0,2},{2,0},{1,3},{3,1},{4,6},{6,4},{5,7},{7,5},{8,10},{10,8},{9,1... | collective-permute-start | bytes 1572872 | tf_op jit(solution)/shard_map/ppermute | solution.py:83
  41.5 26.1 %collective-permute-start.6 = (bf16[512,1024]{0,1:T(8,128)(2,1)S(1)}, bf16[512,1024]{0,1:T(8,128)(2,1)S(1)}, u32[]{:S(2)}, u32[]{:S(2)}) collective-permute-start(bf16[512,1024]{0,1:T(8,128)(2,1)S(1)} %collective-permute-done.1), channel_id=1, source_target_pairs={{0,8},{8,16},{16,24},{24,0},{1,9},{9,17},{17,25},{25,1},{2,10},{10... | collective-permute-start | bytes 3145736 | tf_op jit(solution)/shard_map/ppermute | solution.py:80
  45.8 12.8 %collective-permute-start.7 = (bf16[256,1024]{0,1:T(8,128)(2,1)}, bf16[256,1024]{0,1:T(8,128)(2,1)S(1)}, u32[]{:S(2)}, u32[]{:S(2)}) collective-permute-start(bf16[256,1024]{0,1:T(8,128)(2,1)} %get-tuple-element.121), channel_id=1, source_target_pairs={{0,4},{4,0},{1,5},{5,1},{2,6},{6,2},{3,7},{7,3},{8,12},{12,8},{9,1... | collective-permute-start | bytes 1572872 | tf_op jit(solution)/shard_map/ppermute | solution.py:83
  47.3 23.4 %collective-permute-start.5 = (bf16[4,64,1024]{2,1,0:T(8,128)(2,1)}, bf16[4,64,1024]{2,1,0:T(8,128)(2,1)}, u32[]{:S(2)}, u32[]{:S(2)}) collective-permute-start(bf16[4,64,1024]{2,1,0:T(8,128)(2,1)} %bitcast.19), channel_id=1, source_target_pairs={{0,2},{2,0},{1,3},{3,1},{4,6},{6,4},{5,7},{7,5},{8,10},{10,8},{9,1... | collective-permute-start | bytes 1572872 | tf_op jit(solution)/shard_map/ppermute | solution.py:83
  47.8 23.3 %collective-permute-start.8 = (bf16[256,1024]{0,1:T(8,128)(2,1)}, bf16[256,1024]{0,1:T(8,128)(2,1)}, u32[]{:S(2)}, u32[]{:S(2)}) collective-permute-start(bf16[256,1024]{0,1:T(8,128)(2,1)} %pad_maximum_fusion.32), channel_id=1, source_target_pairs={{0,2},{2,0},{1,3},{3,1},{4,6},{6,4},{5,7},{7,5},{8,10},{10,8},{9,1... | collective-permute-start | bytes 1572872 | tf_op jit(solution)/shard_map/ppermute | solution.py:83
  71.1 24.9 %collective-permute-start.10 = (bf16[512,1024]{0,1:T(8,128)(2,1)S(1)}, bf16[512,1024]{0,1:T(8,128)(2,1)}, u32[]{:S(2)}, u32[]{:S(2)}) collective-permute-start(bf16[512,1024]{0,1:T(8,128)(2,1)S(1)} %collective-permute-done.6), channel_id=1, source_target_pairs={{0,8},{8,16},{16,24},{24,0},{1,9},{9,17},{17,25},{25,1},{2,10},{10... | collective-permute-start | bytes 3145736 | tf_op jit(solution)/shard_map/ppermute | solution.py:80
  75.1 13.8 %collective-permute-start.11 = (bf16[256,1024]{0,1:T(8,128)(2,1)}, bf16[256,1024]{0,1:T(8,128)(2,1)}, u32[]{:S(2)}, u32[]{:S(2)}) collective-permute-start(bf16[256,1024]{0,1:T(8,128)(2,1)} %get-tuple-element.125), channel_id=1, source_target_pairs={{0,4},{4,0},{1,5},{5,1},{2,6},{6,2},{3,7},{7,3},{8,12},{12,8},{9,1... | collective-permute-start | bytes 1572872 | tf_op jit(solution)/shard_map/ppermute | solution.py:83
  75.7 14.4 %collective-permute-start.9 = (bf16[4,64,1024]{2,1,0:T(8,128)(2,1)}, bf16[4,64,1024]{2,1,0:T(8,128)(2,1)}, u32[]{:S(2)}, u32[]{:S(2)}) collective-permute-start(bf16[4,64,1024]{2,1,0:T(8,128)(2,1)} %bitcast.705), channel_id=1, source_target_pairs={{0,2},{2,0},{1,3},{3,1},{4,6},{6,4},{5,7},{7,5},{8,10},{10,8},{9,1... | collective-permute-start | bytes 1572872 | tf_op jit(solution)/shard_map/ppermute | solution.py:83
  84.3 19.1 %collective-permute-start.13 = (bf16[256,1024]{0,1:T(8,128)(2,1)}, bf16[256,1024]{0,1:T(8,128)(2,1)}, u32[]{:S(2)}, u32[]{:S(2)}) collective-permute-start(bf16[256,1024]{0,1:T(8,128)(2,1)} %pad_maximum_fusion.33), channel_id=1, source_target_pairs={{0,2},{2,0},{1,3},{3,1},{4,6},{6,4},{5,7},{7,5},{8,10},{10,8},{9,1... | collective-permute-start | bytes 1572872 | tf_op jit(solution)/shard_map/ppermute | solution.py:83
  103.5 23.8 %collective-permute-start.16 = (bf16[256,1024]{0,1:T(8,128)(2,1)S(1)}, bf16[256,1024]{0,1:T(8,128)(2,1)S(1)}, u32[]{:S(2)}, u32[]{:S(2)}) collective-permute-start(bf16[256,1024]{0,1:T(8,128)(2,1)S(1)} %copy-done.153), channel_id=1, source_target_pairs={{0,4},{4,0},{1,5},{5,1},{2,6},{6,2},{3,7},{7,3},{8,12},{12,8},{9,1... | collective-permute-start | bytes 1572872 | tf_op jit(solution)/shard_map/ppermute | solution.py:83
  104.5 14.9 %collective-permute-start.14 = (bf16[4,64,1024]{2,1,0:T(8,128)(2,1)S(1)}, bf16[4,64,1024]{2,1,0:T(8,128)(2,1)S(1)}, u32[]{:S(2)}, u32[]{:S(2)}) collective-permute-start(bf16[4,64,1024]{2,1,0:T(8,128)(2,1)S(1)} %bitcast.707), channel_id=1, source_target_pairs={{0,2},{2,0},{1,3},{3,1},{4,6},{6,4},{5,7},{7,5},{8,10},{10,8},{9,1... | collective-permute-start | bytes 1572872 | tf_op jit(solution)/shard_map/ppermute | solution.py:83
  106.9 20.3 %collective-permute-start.17 = (s32[8,128]{1,0:T(8,128)S(1)}, s32[8,128]{1,0:T(8,128)S(1)}, u32[]{:S(2)}, u32[]{:S(2)}) collective-permute-start(s32[8,128]{1,0:T(8,128)S(1)} %broadcast_in_dim.282), channel_id=1, source_target_pairs={{0,8},{8,16},{16,24},{24,0},{1,9},{9,17},{17,25},{25,1},{2,10},{10... | collective-permute-start | bytes 12296 | tf_op jit(solution)/shard_map/ppermute | solution.py:80
  106.9 21.4 %collective-permute-start.18 = (bf16[256,1024]{0,1:T(8,128)(2,1)S(1)}, bf16[256,1024]{0,1:T(8,128)(2,1)S(1)}, u32[]{:S(2)}, u32[]{:S(2)}) collective-permute-start(bf16[256,1024]{0,1:T(8,128)(2,1)S(1)} %copy-done.148), channel_id=1, source_target_pairs={{0,8},{8,16},{16,24},{24,0},{1,9},{9,17},{17,25},{25,1},{2,10},{10... | collective-permute-start | bytes 1572872 | tf_op jit(solution)/shard_map/ppermute | solution.py:80
  106.9 21.4 %collective-permute-start.19 = (bf16[256,1024]{0,1:T(8,128)(2,1)S(1)}, bf16[256,1024]{0,1:T(8,128)(2,1)S(1)}, u32[]{:S(2)}, u32[]{:S(2)}) collective-permute-start(bf16[256,1024]{0,1:T(8,128)(2,1)S(1)} %pad_maximum_fusion.34), channel_id=1, source_target_pairs={{0,2},{2,0},{1,3},{3,1},{4,6},{6,4},{5,7},{7,5},{8,10},{10,8},{9,1... | collective-permute-start | bytes 1572872 | tf_op jit(solution)/shard_map/ppermute | solution.py:83
  128.4 16.5 %collective-permute-start.20 = (bf16[256,1024]{0,1:T(8,128)(2,1)S(1)}, bf16[256,1024]{0,1:T(8,128)(2,1)S(1)}, u32[]{:S(2)}, u32[]{:S(2)}) collective-permute-start(bf16[256,1024]{0,1:T(8,128)(2,1)S(1)} %collective-permute-done.18), channel_id=1, source_target_pairs={{0,8},{8,16},{16,24},{24,0},{1,9},{9,17},{17,25},{25,1},{2,10},{10... | collective-permute-start | bytes 1572872 | tf_op jit(solution)/shard_map/ppermute | solution.py:80
  128.6 16.2 %collective-permute-start.22 = (bf16[256,1024]{0,1:T(8,128)(2,1)S(1)}, bf16[256,1024]{0,1:T(8,128)(2,1)S(1)}, u32[]{:S(2)}, u32[]{:S(2)}) collective-permute-start(bf16[256,1024]{0,1:T(8,128)(2,1)S(1)} %pad_maximum_fusion.36), channel_id=1, source_target_pairs={{0,2},{2,0},{1,3},{3,1},{4,6},{6,4},{5,7},{7,5},{8,10},{10,8},{9,1... | collective-permute-start | bytes 1572872 | tf_op jit(solution)/shard_map/ppermute | solution.py:83
  130.2 10.6 %collective-permute-start.23 = (s32[8,128]{1,0:T(8,128)S(1)}, s32[8,128]{1,0:T(8,128)S(1)}, u32[]{:S(2)}, u32[]{:S(2)}) collective-permute-start(s32[8,128]{1,0:T(8,128)S(1)} %broadcast_add_fusion.2), channel_id=1, source_target_pairs={{0,16},{8,24},{16,0},{24,8},{1,17},{9,25},{17,1},{25,9},{2,18},{10... | collective-permute-start | bytes 12296 | tf_op jit(solution)/shard_map/ppermute | solution.py:80
  146.4 24.9 %collective-permute-start.24 = (bf16[512,1024]{1,0:T(8,128)(2,1)}, bf16[512,1024]{1,0:T(8,128)(2,1)S(1)}, u32[]{:S(2)}, u32[]{:S(2)}) collective-permute-start(bf16[512,1024]{1,0:T(8,128)(2,1)} %fusion.54), channel_id=1, source_target_pairs={{0,4},{4,0},{1,5},{5,1},{2,6},{6,2},{3,7},{7,3},{8,12},{12,8},{9,1... | collective-permute-start | bytes 3145736 | tf_op jit(solution)/shard_map/ppermute | solution.py:83
  202.6 61.0 %collective-permute-start.26 = (bf16[1024,1024]{0,1:T(8,128)(2,1)S(1)}, bf16[1024,1024]{0,1:T(8,128)(2,1)}, u32[]{:S(2)}, u32[]{:S(2)}) collective-permute-start(bf16[1024,1024]{0,1:T(8,128)(2,1)S(1)} %copy-done.134), channel_id=1, source_target_pairs={{0,2},{2,0},{1,3},{3,1},{4,6},{6,4},{5,7},{7,5},{8,10},{10,8},{9,1... | collective-permute-start | bytes 6291464 | tf_op jit(solution)/shard_map/ppermute | solution.py:83
  209.8 26.2 %collective-permute-start.27 = (bf16[256,1024]{0,1:T(8,128)(2,1)S(1)}, bf16[256,1024]{0,1:T(8,128)(2,1)}, u32[]{:S(2)}, u32[]{:S(2)}) collective-permute-start(bf16[256,1024]{0,1:T(8,128)(2,1)S(1)} %copy-done.143), channel_id=1, source_target_pairs={{0,8},{8,16},{16,24},{24,0},{1,9},{9,17},{17,25},{25,1},{2,10},{10... | collective-permute-start | bytes 1572872 | tf_op jit(solution)/shard_map/ppermute | solution.py:80
  277.3 25.6 %collective-permute-start.30 = (bf16[512,1024]{0,1:T(8,128)(2,1)S(1)}, bf16[512,1024]{0,1:T(8,128)(2,1)S(1)}, u32[]{:S(2)}, u32[]{:S(2)}) collective-permute-start(bf16[512,1024]{0,1:T(8,128)(2,1)S(1)} %pad_maximum_fusion.16), channel_id=1, source_target_pairs={{0,4},{4,0},{1,5},{5,1},{2,6},{6,2},{3,7},{7,3},{8,12},{12,8},{9,1... | collective-permute-start | bytes 3145736 | tf_op jit(solution)/shard_map/ppermute | solution.py:83
  278.8 26.2 %collective-permute-start.31 = (bf16[512,1024]{0,1:T(8,128)(2,1)S(1)}, bf16[512,1024]{0,1:T(8,128)(2,1)S(1)}, u32[]{:S(2)}, u32[]{:S(2)}) collective-permute-start(bf16[512,1024]{0,1:T(8,128)(2,1)S(1)} %pad_maximum_fusion.17), channel_id=1, source_target_pairs={{0,2},{2,0},{1,3},{3,1},{4,6},{6,4},{5,7},{7,5},{8,10},{10,8},{9,1... | collective-permute-start | bytes 3145736 | tf_op jit(solution)/shard_map/ppermute | solution.py:83
  307.5 48.3 %collective-permute-start.33 = (bf16[1024,1024]{0,1:T(8,128)(2,1)}, bf16[1024,1024]{0,1:T(8,128)(2,1)}, u32[]{:S(2)}, u32[]{:S(2)}) collective-permute-start(bf16[1024,1024]{0,1:T(8,128)(2,1)} %constant_dynamic-update-slice_fusion.15), channel_id=1, source_target_pairs={{0,2},{2,0},{1,3},{3,1},{4,6},{6,4},{5,7},{7,5},{8,10},{10,8},{9,1... | collective-permute-start | bytes 6291464 | tf_op jit(solution)/shard_map/ppermute | solution.py:83
  309.5 48.0 %collective-permute-start.34 = (bf16[1024,1024]{0,1:T(8,128)(2,1)}, bf16[1024,1024]{0,1:T(8,128)(2,1)}, u32[]{:S(2)}, u32[]{:S(2)}) collective-permute-start(bf16[1024,1024]{0,1:T(8,128)(2,1)} %pad_maximum_fusion.2), channel_id=1, source_target_pairs={{0,4},{4,0},{1,5},{5,1},{2,6},{6,2},{3,7},{7,3},{8,12},{12,8},{9,1... | collective-permute-start | bytes 6291464 | tf_op jit(solution)/shard_map/ppermute | solution.py:83
  489.6 21.2 %collective-permute-start.41 = (f32[512,1024]{1,0:T(8,128)}, f32[512,1024]{1,0:T(8,128)}, u32[]{:S(2)}, u32[]{:S(2)}) collective-permute-start(f32[512,1024]{1,0:T(8,128)} %dynamic-slice_bitcast_fusion.2), channel_id=1, source_target_pairs={{0,1},{1,0},{2,3},{3,2},{4,5},{5,4},{6,7},{7,6},{8,9},{9,8},{10,11... | collective-permute-start | bytes 6291464 | tf_op jit(solution)/shard_map/ppermute | solution.py:80
  502.1 47.6 %collective-permute-start.47 = (bf16[2,4,2,64,1024]{4,3,2,1,0:T(8,128)(2,1)}, bf16[2,4,2,64,1024]{4,3,2,1,0:T(8,128)(2,1)}, u32[]{:S(2)}, u32[]{:S(2)}) collective-permute-start(bf16[2,4,2,64,1024]{4,3,2,1,0:T(8,128)(2,1)} %fusion.45), channel_id=1, source_target_pairs={{0,4},{4,0},{1,5},{5,1},{2,6},{6,2},{3,7},{7,3},{8,12},{12,8},{9,1... | collective-permute-start | bytes 6291464 | tf_op jit(solution)/shard_map/ppermute | solution.py:83
  503.8 47.3 %collective-permute-start.48 = (bf16[2,2,4,64,1024]{4,3,0,1,2:T(8,128)(2,1)}, bf16[2,2,4,64,1024]{4,3,0,1,2:T(8,128)(2,1)}, u32[]{:S(2)}, u32[]{:S(2)}) collective-permute-start(bf16[2,2,4,64,1024]{4,3,0,1,2:T(8,128)(2,1)} %fusion.46), channel_id=1, source_target_pairs={{0,2},{2,0},{1,3},{3,1},{4,6},{6,4},{5,7},{7,5},{8,10},{10,8},{9,1... | collective-permute-start | bytes 6291464 | tf_op jit(solution)/shard_map/ppermute | solution.py:83
  543.0 25.6 %collective-permute-start.43 = (f32[512,1024]{1,0:T(8,128)}, f32[512,1024]{1,0:T(8,128)}, u32[]{:S(2)}, u32[]{:S(2)}) collective-permute-start(f32[512,1024]{1,0:T(8,128)} %dynamic-slice_bitcast_fusion.1), channel_id=1, source_target_pairs={{0,1},{1,0},{2,3},{3,2},{4,5},{5,4},{6,7},{7,6},{8,9},{9,8},{10,11... | collective-permute-start | bytes 6291464 | tf_op jit(solution)/shard_map/ppermute | solution.py:80
  558.7 60.8 %collective-permute-start.49 = (bf16[1024,1024]{1,0:T(8,128)(2,1)}, bf16[1024,1024]{1,0:T(8,128)(2,1)}, u32[]{:S(2)}, u32[]{:S(2)}) collective-permute-start(bf16[1024,1024]{1,0:T(8,128)(2,1)} %convolution_convert_fusion), channel_id=1, source_target_pairs={{0,2},{2,0},{1,3},{3,1},{4,6},{6,4},{5,7},{7,5},{8,10},{10,8},{9,1... | collective-permute-start | bytes 6291464 | tf_op jit(solution)/shard_map/ppermute | solution.py:83
  560.2 59.3 %collective-permute-start.50 = (bf16[1024,1024]{1,0:T(8,128)(2,1)}, bf16[1024,1024]{1,0:T(8,128)(2,1)}, u32[]{:S(2)}, u32[]{:S(2)}) collective-permute-start(bf16[1024,1024]{1,0:T(8,128)(2,1)} %pad_maximum_fusion.4), channel_id=1, source_target_pairs={{0,4},{4,0},{1,5},{5,1},{2,6},{6,2},{3,7},{7,3},{8,12},{12,8},{9,1... | collective-permute-start | bytes 6291464 | tf_op jit(solution)/shard_map/ppermute | solution.py:83
  560.8 58.7 %collective-permute-start.51 = (bf16[512,1024]{1,0:T(8,128)(2,1)}, bf16[512,1024]{1,0:T(8,128)(2,1)}, u32[]{:S(2)}, u32[]{:S(2)}) collective-permute-start(bf16[512,1024]{1,0:T(8,128)(2,1)} %pad_maximum_fusion.20), channel_id=1, source_target_pairs={{0,8},{8,16},{16,24},{24,0},{1,9},{9,17},{17,25},{25,1},{2,10},{10... | collective-permute-start | bytes 3145736 | tf_op jit(solution)/shard_map/ppermute | solution.py:80
  619.0 25.1 %collective-permute-start.45 = (f32[512,1024]{1,0:T(8,128)S(1)}, f32[512,1024]{1,0:T(8,128)S(1)}, u32[]{:S(2)}, u32[]{:S(2)}) collective-permute-start(f32[512,1024]{1,0:T(8,128)S(1)} %dynamic-slice_bitcast_fusion), channel_id=1, source_target_pairs={{0,1},{1,0},{2,3},{3,2},{4,5},{5,4},{6,7},{7,6},{8,9},{9,8},{10,11... | collective-permute-start | bytes 6291464 | tf_op jit(solution)/shard_map/ppermute | solution.py:80
  632.9 26.4 %collective-permute-start.52 = (bf16[1024,512]{1,0:T(8,128)(2,1)}, bf16[1024,512]{1,0:T(8,128)(2,1)}, u32[]{:S(2)}, u32[]{:S(2)}) collective-permute-start(bf16[1024,512]{1,0:T(8,128)(2,1)} %pad_maximum_fusion.18), channel_id=1, source_target_pairs={{0,2},{2,0},{1,3},{3,1},{4,6},{6,4},{5,7},{7,5},{8,10},{10,8},{9,1... | collective-permute-start | bytes 3145736 | tf_op jit(solution)/shard_map/ppermute | solution.py:83
  633.4 26.3 %collective-permute-start.53 = (bf16[1024,512]{1,0:T(8,128)(2,1)}, bf16[1024,512]{1,0:T(8,128)(2,1)}, u32[]{:S(2)}, u32[]{:S(2)}) collective-permute-start(bf16[1024,512]{1,0:T(8,128)(2,1)} %pad_maximum_fusion.19), channel_id=1, source_target_pairs={{0,4},{4,0},{1,5},{5,1},{2,6},{6,2},{3,7},{7,3},{8,12},{12,8},{9,1... | collective-permute-start | bytes 3145736 | tf_op jit(solution)/shard_map/ppermute | solution.py:83
  634.9 46.6 %collective-permute-start.54 = (bf16[512,1024]{1,0:T(8,128)(2,1)}, bf16[512,1024]{1,0:T(8,128)(2,1)}, u32[]{:S(2)}, u32[]{:S(2)}) collective-permute-start(bf16[512,1024]{1,0:T(8,128)(2,1)} %slice.1397), channel_id=1, source_target_pairs={{0,4},{4,0},{1,5},{5,1},{2,6},{6,2},{3,7},{7,3},{8,12},{12,8},{9,1... | collective-permute-start | bytes 3145736 | tf_op jit(solution)/shard_map/ppermute | solution.py:83
  635.4 46.0 %collective-permute-start.55 = (bf16[512,1024]{1,0:T(8,128)(2,1)}, bf16[512,1024]{1,0:T(8,128)(2,1)}, u32[]{:S(2)}, u32[]{:S(2)}) collective-permute-start(bf16[512,1024]{1,0:T(8,128)(2,1)} %fusion.50), channel_id=1, source_target_pairs={{0,2},{2,0},{1,3},{3,1},{4,6},{6,4},{5,7},{7,5},{8,10},{10,8},{9,1... | collective-permute-start | bytes 3145736 | tf_op jit(solution)/shard_map/ppermute | solution.py:83
  644.1 37.4 %collective-permute-start.56 = (bf16[512,1024]{1,0:T(8,128)(2,1)}, bf16[512,1024]{1,0:T(8,128)(2,1)}, u32[]{:S(2)}, u32[]{:S(2)}) collective-permute-start(bf16[512,1024]{1,0:T(8,128)(2,1)} %pad_maximum_fusion.21), channel_id=1, source_target_pairs={{0,8},{8,16},{16,24},{24,0},{1,9},{9,17},{17,25},{25,1},{2,10},{10... | collective-permute-start | bytes 3145736 | tf_op jit(solution)/shard_map/ppermute | solution.py:80
  659.2 34.2 %collective-permute-start.46 = (f32[16,1024]{1,0:T(8,128)S(1)}, f32[16,1024]{1,0:T(8,128)S(1)}, u32[]{:S(2)}, u32[]{:S(2)}) collective-permute-start(f32[16,1024]{1,0:T(8,128)S(1)} %maximum_maximum_fusion.2), channel_id=1, source_target_pairs={{0,1},{1,0},{2,3},{3,2},{4,5},{5,4},{6,7},{7,6},{8,9},{9,8},{10,11... | collective-permute-start | bytes 196616 | tf_op jit(solution)/shard_map/ppermute | solution.py:89
  693.6 39.0 %collective-permute-start.60 = (bf16[768,1024]{1,0:T(8,128)(2,1)S(1)}, bf16[768,1024]{1,0:T(8,128)(2,1)S(1)}, u32[]{:S(2)}, u32[]{:S(2)}) collective-permute-start(bf16[768,1024]{1,0:T(8,128)(2,1)S(1)} %pad_maximum_fusion.7), channel_id=1, source_target_pairs={{0,8},{8,16},{16,24},{24,0},{1,9},{9,17},{17,25},{25,1},{2,10},{10... | collective-permute-start | bytes 4718600 | tf_op jit(solution)/shard_map/ppermute | solution.py:80
  695.0 37.6 %collective-permute-start.58 = (bf16[1536,512]{1,0:T(8,128)(2,1)S(1)}, bf16[1536,512]{1,0:T(8,128)(2,1)S(1)}, u32[]{:S(2)}, u32[]{:S(2)}) collective-permute-start(bf16[1536,512]{1,0:T(8,128)(2,1)S(1)} %pad_maximum_fusion.5), channel_id=1, source_target_pairs={{0,2},{2,0},{1,3},{3,1},{4,6},{6,4},{5,7},{7,5},{8,10},{10,8},{9,1... | collective-permute-start | bytes 4718600 | tf_op jit(solution)/shard_map/ppermute | solution.py:83
  698.7 33.2 %collective-permute-start.57 = (f32[16,1024]{1,0:T(8,128)S(1)}, f32[16,1024]{1,0:T(8,128)S(1)}, u32[]{:S(2)}, u32[]{:S(2)}) collective-permute-start(f32[16,1024]{1,0:T(8,128)S(1)} %fusion.228), channel_id=1, source_target_pairs={{0,2},{2,0},{1,3},{3,1},{4,6},{6,4},{5,7},{7,5},{8,10},{10,8},{9,1... | collective-permute-start | bytes 196616 | tf_op jit(solution)/shard_map/ppermute | solution.py:83
  699.2 38.4 %collective-permute-start.59 = (bf16[1536,512]{1,0:T(8,128)(2,1)S(1)}, bf16[1536,512]{1,0:T(8,128)(2,1)S(1)}, u32[]{:S(2)}, u32[]{:S(2)}) collective-permute-start(bf16[1536,512]{1,0:T(8,128)(2,1)S(1)} %pad_maximum_fusion.6), channel_id=1, source_target_pairs={{0,4},{4,0},{1,5},{5,1},{2,6},{6,2},{3,7},{7,3},{8,12},{12,8},{9,1... | collective-permute-start | bytes 4718600 | tf_op jit(solution)/shard_map/ppermute | solution.py:83
  700.8 55.1 %collective-permute-start.64 = (bf16[512,1024]{1,0:T(8,128)(2,1)}, bf16[512,1024]{1,0:T(8,128)(2,1)}, u32[]{:S(2)}, u32[]{:S(2)}) collective-permute-start(bf16[512,1024]{1,0:T(8,128)(2,1)} %get-tuple-element.336), channel_id=1, source_target_pairs={{0,1},{1,0},{2,3},{3,2},{4,5},{5,4},{6,7},{7,6},{8,9},{9,8},{10,11... | collective-permute-start | bytes 3145736 | tf_op jit(solution)/shard_map/ppermute | solution.py:80
  746.2 16.0 %collective-permute-start.63 = (bf16[512,512]{1,0:T(8,128)(2,1)}, bf16[512,512]{1,0:T(8,128)(2,1)}, u32[]{:S(2)}, u32[]{:S(2)}) collective-permute-start(bf16[512,512]{1,0:T(8,128)(2,1)} %get-tuple-element.194), channel_id=1, source_target_pairs={{0,2},{2,0},{1,3},{3,1},{4,6},{6,4},{5,7},{7,5},{8,10},{10,8},{9,1... | collective-permute-start | bytes 1572872 | tf_op jit(solution)/shard_map/ppermute | solution.py:83
  755.4 15.1 %collective-permute-start.62 = (bf16[512,512]{1,0:T(8,128)(2,1)}, bf16[512,512]{1,0:T(8,128)(2,1)S(1)}, u32[]{:S(2)}, u32[]{:S(2)}) collective-permute-start(bf16[512,512]{1,0:T(8,128)(2,1)} %slice.1401), channel_id=1, source_target_pairs={{0,4},{4,0},{1,5},{5,1},{2,6},{6,2},{3,7},{7,3},{8,12},{12,8},{9,1... | collective-permute-start | bytes 1572872 | tf_op jit(solution)/shard_map/ppermute | solution.py:83
  758.3 28.3 %collective-permute-start.67 = (bf16[640,1024]{1,0:T(8,128)(2,1)}, bf16[640,1024]{1,0:T(8,128)(2,1)S(1)}, u32[]{:S(2)}, u32[]{:S(2)}) collective-permute-start(bf16[640,1024]{1,0:T(8,128)(2,1)} %get-tuple-element.196), channel_id=1, source_target_pairs={{0,2},{2,0},{1,3},{3,1},{4,6},{6,4},{5,7},{7,5},{8,10},{10,8},{9,1... | collective-permute-start | bytes 3932168 | tf_op jit(solution)/shard_map/ppermute | solution.py:83
  758.9 37.0 %collective-permute-start.65 = (bf16[640,1024]{1,0:T(8,128)(2,1)S(1)}, bf16[640,1024]{1,0:T(8,128)(2,1)S(1)}, u32[]{:S(2)}, u32[]{:S(2)}) collective-permute-start(bf16[640,1024]{1,0:T(8,128)(2,1)S(1)} %copy-done.113), channel_id=1, source_target_pairs={{0,4},{4,0},{1,5},{5,1},{2,6},{6,2},{3,7},{7,3},{8,12},{12,8},{9,1... | collective-permute-start | bytes 3932168 | tf_op jit(solution)/shard_map/ppermute | solution.py:83
  760.4 18.5 %collective-permute-start.69 = (bf16[384,1024]{1,0:T(8,128)(2,1)S(1)}, bf16[384,1024]{1,0:T(8,128)(2,1)S(1)}, u32[]{:S(2)}, u32[]{:S(2)}) collective-permute-start(bf16[384,1024]{1,0:T(8,128)(2,1)S(1)} %pad_maximum_fusion.24), channel_id=1, source_target_pairs={{0,8},{8,16},{16,24},{24,0},{1,9},{9,17},{17,25},{25,1},{2,10},{10... | collective-permute-start | bytes 2359304 | tf_op jit(solution)/shard_map/ppermute | solution.py:80
  786.7 10.3 %collective-permute-start.68 = (bf16[512,1024]{1,0:T(8,128)(2,1)S(1)}, bf16[512,1024]{1,0:T(8,128)(2,1)S(1)}, u32[]{:S(2)}, u32[]{:S(2)}) collective-permute-start(bf16[512,1024]{1,0:T(8,128)(2,1)S(1)} %slice.1049), channel_id=1, source_target_pairs={{0,1},{1,0},{2,3},{3,2},{4,5},{5,4},{6,7},{7,6},{8,9},{9,8},{10,11... | collective-permute-start | bytes 3145736 | tf_op jit(solution)/shard_map/ppermute | solution.py:80
  814.8 40.1 %collective-permute-start.76 = (bf16[2,4,64,1024]{3,2,0,1:T(8,128)(2,1)S(1)}, bf16[2,4,64,1024]{3,2,0,1:T(8,128)(2,1)S(1)}, u32[]{:S(2)}, u32[]{:S(2)}) collective-permute-start(bf16[2,4,64,1024]{3,2,0,1:T(8,128)(2,1)S(1)} %fusion.97), channel_id=1, source_target_pairs={{0,2},{2,0},{1,3},{3,1},{4,6},{6,4},{5,7},{7,5},{8,10},{10,8},{9,1... | collective-permute-start | bytes 3145736 | tf_op jit(solution)/shard_map/ppermute | solution.py:83
  815.5 38.5 %collective-permute-start.78 = (bf16[384,1024]{1,0:T(8,128)(2,1)S(1)}, bf16[384,1024]{1,0:T(8,128)(2,1)S(1)}, u32[]{:S(2)}, u32[]{:S(2)}) collective-permute-start(bf16[384,1024]{1,0:T(8,128)(2,1)S(1)} %pad_maximum_fusion.25), channel_id=1, source_target_pairs={{0,8},{8,16},{16,24},{24,0},{1,9},{9,17},{17,25},{25,1},{2,10},{10... | collective-permute-start | bytes 2359304 | tf_op jit(solution)/shard_map/ppermute | solution.py:80
  816.1 27.4 %collective-permute-start.73 = (bf16[128,1024]{1,0:T(8,128)(2,1)S(1)}, bf16[128,1024]{1,0:T(8,128)(2,1)S(1)}, u32[]{:S(2)}, u32[]{:S(2)}) collective-permute-start(bf16[128,1024]{1,0:T(8,128)(2,1)S(1)} %get-tuple-element.201), channel_id=1, source_target_pairs={{0,8},{8,16},{16,24},{24,0},{1,9},{9,17},{17,25},{25,1},{2,10},{10... | collective-permute-start | bytes 786440 | tf_op jit(solution)/shard_map/ppermute | solution.py:80
  817.6 35.5 %collective-permute-start.74 = (bf16[128,1024]{1,0:T(8,128)(2,1)S(1)}, bf16[128,1024]{1,0:T(8,128)(2,1)S(1)}, u32[]{:S(2)}, u32[]{:S(2)}) collective-permute-start(bf16[128,1024]{1,0:T(8,128)(2,1)S(1)} %get-tuple-element.202), channel_id=1, source_target_pairs={{0,16},{8,24},{16,0},{24,8},{1,17},{9,25},{17,1},{25,9},{2,18},{10... | collective-permute-start | bytes 786440 | tf_op jit(solution)/shard_map/ppermute | solution.py:80
  819.9 33.2 %collective-permute-start.75 = (bf16[128,1024]{1,0:T(8,128)(2,1)S(1)}, bf16[128,1024]{1,0:T(8,128)(2,1)S(1)}, u32[]{:S(2)}, u32[]{:S(2)}) collective-permute-start(bf16[128,1024]{1,0:T(8,128)(2,1)S(1)} %get-tuple-element.203), channel_id=1, source_target_pairs={{0,24},{8,0},{16,8},{24,16},{1,25},{9,1},{17,9},{25,17},{2,26},{10... | collective-permute-start | bytes 786440 | tf_op jit(solution)/shard_map/ppermute | solution.py:80
  843.5 21.8 %collective-permute-start.77 = (bf16[2,4,64,1024]{3,2,0,1:T(8,128)(2,1)S(1)}, bf16[2,4,64,1024]{3,2,0,1:T(8,128)(2,1)S(1)}, u32[]{:S(2)}, u32[]{:S(2)}) collective-permute-start(bf16[2,4,64,1024]{3,2,0,1:T(8,128)(2,1)S(1)} %fusion.98), channel_id=1, source_target_pairs={{0,4},{4,0},{1,5},{5,1},{2,6},{6,2},{3,7},{7,3},{8,12},{12,8},{9,1... | collective-permute-start | bytes 3145736 | tf_op jit(solution)/shard_map/ppermute | solution.py:83
  869.6 11.1 %collective-permute-start.79 = (bf16[128,1024]{1,0:T(8,128)(2,1)}, bf16[128,1024]{1,0:T(8,128)(2,1)S(1)}, u32[]{:S(2)}, u32[]{:S(2)}) collective-permute-start(bf16[128,1024]{1,0:T(8,128)(2,1)} %get-tuple-element.207), channel_id=1, source_target_pairs={{0,8},{8,16},{16,24},{24,0},{1,9},{9,17},{17,25},{25,1},{2,10},{10... | collective-permute-start | bytes 786440 | tf_op jit(solution)/shard_map/ppermute | solution.py:80
  875.7 31.8 %collective-permute-start.85 = (bf16[256,1024]{1,0:T(8,128)(2,1)}, bf16[256,1024]{1,0:T(8,128)(2,1)}, u32[]{:S(2)}, u32[]{:S(2)}) collective-permute-start(bf16[256,1024]{1,0:T(8,128)(2,1)} %pad_maximum_fusion.37), channel_id=1, source_target_pairs={{0,8},{8,16},{16,24},{24,0},{1,9},{9,17},{17,25},{25,1},{2,10},{10... | collective-permute-start | bytes 1572872 | tf_op jit(solution)/shard_map/ppermute | solution.py:80
  878.2 33.8 %collective-permute-start.86 = (bf16[256,1024]{1,0:T(8,128)(2,1)}, bf16[256,1024]{1,0:T(8,128)(2,1)}, u32[]{:S(2)}, u32[]{:S(2)}) collective-permute-start(bf16[256,1024]{1,0:T(8,128)(2,1)} %pad_maximum_fusion.38), channel_id=1, source_target_pairs={{0,16},{8,24},{16,0},{24,8},{1,17},{9,25},{17,1},{25,9},{2,18},{10... | collective-permute-start | bytes 1572872 | tf_op jit(solution)/shard_map/ppermute | solution.py:80
  878.2 34.9 %collective-permute-start.87 = (bf16[256,1024]{1,0:T(8,128)(2,1)}, bf16[256,1024]{1,0:T(8,128)(2,1)}, u32[]{:S(2)}, u32[]{:S(2)}) collective-permute-start(bf16[256,1024]{1,0:T(8,128)(2,1)} %pad_maximum_fusion.39), channel_id=1, source_target_pairs={{0,24},{8,0},{16,8},{24,16},{1,25},{9,1},{17,9},{25,17},{2,26},{10... | collective-permute-start | bytes 1572872 | tf_op jit(solution)/shard_map/ppermute | solution.py:80
  893.4 23.3 %collective-permute-start.83 = (f32[12,32,128]{2,1,0:T(8,128)}, f32[12,32,128]{2,1,0:T(8,128)}, u32[]{:S(2)}, u32[]{:S(2)}) collective-permute-start(f32[12,32,128]{2,1,0:T(8,128)} %add.1380), channel_id=1, source_target_pairs={{0,8},{8,0},{16,24},{24,16},{1,9},{9,1},{17,25},{25,17},{2,10},{10... | collective-permute-start | bytes 589832 | tf_op jit(solution)/shard_map/ppermute | solution.py:89
  917.8 18.9 %collective-permute-start.84 = (f32[12,32,128]{2,1,0:T(8,128)S(1)}, f32[12,32,128]{2,1,0:T(8,128)S(1)}, u32[]{:S(2)}, u32[]{:S(2)}) collective-permute-start(f32[12,32,128]{2,1,0:T(8,128)S(1)} %add.1381), channel_id=1, source_target_pairs={{0,16},{8,24},{16,0},{24,8},{1,17},{9,25},{17,1},{25,9},{2,18},{10... | collective-permute-start | bytes 589832 | tf_op jit(solution)/shard_map/ppermute | solution.py:89
  (251 other events, 2403.6 us)
Sparse Core Ops, SparseCore 0:
  171.4 131.2 all-gather.2

commit v5 on v4

--- a/solution.py
+++ b/solution.py
@@ -240,14 +240,16 @@
     ]
 
 
-def softmax_down(query, key_rows, first, causal):
-    scores = contract(key_rows, query, 1, 1) * 0.125
-    if causal:
-        key_at = lax.broadcasted_iota(jnp.int32, scores.shape, 0)
-        query_at = first + lax.broadcasted_iota(jnp.int32, scores.shape, 1)
-        scores = jnp.where(key_at <= query_at, scores, -jnp.inf)
-    expo = jnp.exp(scores - jnp.max(scores, 0, keepdims=True))
-    return expo * (1.0 / jnp.sum(expo, 0, keepdims=True))
+def scores_down(query, key_ref, first, last, causal):
+    if not causal:
+        return contract(key_ref[pl.ds(0, last), :], query, 1, 1)
+    edge = contract(key_ref[pl.ds(first, last - first), :], query, 1, 1)
+    key_at = lax.broadcasted_iota(jnp.int32, edge.shape, 0)
+    query_at = lax.broadcasted_iota(jnp.int32, edge.shape, 1)
+    edge = jnp.where(key_at <= query_at, edge, -jnp.inf)
+    if first == 0:
+        return edge
+    return jnp.concatenate([contract(key_ref[pl.ds(0, first), :], query, 1, 1), edge], 0)
 
 
 def head_lanes(shape, head):
@@ -255,19 +257,23 @@
     return (lane // HEAD_DIM) == head
 
 
-def attend_kernel(causal, query_ref, key_ref, value_ref, mixed_ref):
+def attend_kernel(causal, query_ref, key_ref, value_ref, mixed_ref, total_ref):
     frames, keys = query_ref.shape[0], key_ref.shape[0]
     turned = value_ref[...].astype(F32).T.astype(BF16)
     for first, block, last in spans(frames, keys, causal):
-        query = query_ref[pl.ds(first, block), :]
+        query = query_ref[pl.ds(first, block), :] * jnp.asarray(0.125, BF16)
         parts = []
         for head in range(LANES // HEAD_DIM):
             own = jnp.where(head_lanes(query.shape, head), query, jnp.zeros_like(query))
-            probs = softmax_down(own, key_ref[pl.ds(0, last), :], first, causal).astype(BF16)
+            scores = scores_down(own, key_ref, first, last, causal)
+            top = jnp.max(scores, 0, keepdims=True)
+            expo = jnp.exp(scores - top)
+            total = jnp.sum(expo, 0, keepdims=True)
+            total_ref[0, head : head + 1, pl.ds(first, block)] = top + jnp.log(total)
             parts.append(
                 contract_rows(
                     turned[head * HEAD_DIM : (head + 1) * HEAD_DIM, :last],
-                    probs,
+                    (expo * (1.0 / total)).astype(BF16),
                 )
             )
         mixed_ref[pl.ds(first, block), :] = jnp.concatenate(parts, 0).T.astype(BF16)
@@ -278,6 +284,8 @@
     query_ref,
     key_ref,
     value_ref,
+    mixed_ref,
+    total_ref,
     grad_ref,
     grad_query_ref,
     grad_key_ref,
@@ -290,17 +298,19 @@
     key_sum[...] = jnp.zeros_like(key_sum)
     value_sum[...] = jnp.zeros_like(value_sum)
     for first, block, last in spans(frames, keys, causal):
-        query = query_ref[pl.ds(first, block), :]
+        query = query_ref[pl.ds(first, block), :] * jnp.asarray(0.125, BF16)
         grad = grad_ref[pl.ds(first, block), :]
+        shared = (grad.astype(F32) * mixed_ref[pl.ds(first, block), :].astype(F32)).T
         parts = []
         for head in range(LANES // HEAD_DIM):
             lanes = head_lanes(query.shape, head)
             own = jnp.where(lanes, query, jnp.zeros_like(query))
             own_grad = jnp.where(lanes, grad, jnp.zeros_like(grad))
-            probs = softmax_down(own, key_ref[pl.ds(0, last), :], first, causal)
+            scores = scores_down(own, key_ref, first, last, causal)
+            probs = jnp.exp(scores - total_ref[0, head : head + 1, pl.ds(first, block)])
             grad_probs = contract(value_ref[pl.ds(0, last), :], own_grad, 1, 1)
-            product = probs * grad_probs
-            grad_scores = (product - probs * jnp.sum(product, 0, keepdims=True)).astype(BF16)
+            mean = jnp.sum(shared[head * HEAD_DIM : (head + 1) * HEAD_DIM], 0, keepdims=True)
+            grad_scores = (probs * (grad_probs - mean)).astype(BF16)
             value_sum[pl.ds(0, last), :] += contract_rows(probs.astype(BF16), own_grad)
             key_sum[pl.ds(0, last), :] += contract_rows(grad_scores, own)
             parts.append(
@@ -310,7 +320,7 @@
                 )
             )
         grad_query_ref[pl.ds(first, block), :] = (jnp.concatenate(parts, 0).T * 0.125).astype(BF16)
-    grad_key_ref[...] = (key_sum[...] * 0.125).astype(BF16)
+    grad_key_ref[...] = key_sum[...].astype(BF16)
     grad_value_ref[...] = value_sum[...].astype(BF16)
 
 
@@ -329,14 +339,17 @@
             spec(key_rows, keys[1]),
             spec(key_rows, values[1]),
         ],
-        out_specs=spec(frames, 0),
-        out_shape=jax.ShapeDtypeStruct((frames, count * LANES), BF16),
+        out_specs=[spec(frames, 0), pl.BlockSpec((1, 2, frames), lambda p: (p, 0, 0))],
+        out_shape=[
+            jax.ShapeDtypeStruct((frames, count * LANES), BF16),
+            jax.ShapeDtypeStruct((count, 2, frames), F32),
+        ],
         compiler_params=pltpu.CompilerParams(vmem_limit_bytes=KERNEL_VMEM),
         cost_estimate=LIGHT,
     )(queries[0], keys[0], values[0])
 
 
-def attend_back(queries, keys, values, grad, causal):
+def attend_back(queries, keys, values, mixed, total, grad, causal):
     frames, key_rows = queries[0].shape[0], keys[0].shape[0]
     count = queries[2]
 
@@ -351,6 +364,8 @@
             spec(frames, queries[1]),
             spec(key_rows, keys[1]),
             spec(key_rows, values[1]),
+            spec(frames, 0),
+            pl.BlockSpec((1, 2, frames), lambda p: (p, 0, 0)),
             spec(frames, 0),
         ],
         out_specs=[spec(frames, 0), spec(key_rows, 0), spec(key_rows, 0)],
@@ -362,7 +377,7 @@
         scratch_shapes=[pltpu.VMEM((key_rows, LANES), F32), pltpu.VMEM((key_rows, LANES), F32)],
         compiler_params=pltpu.CompilerParams(vmem_limit_bytes=KERNEL_VMEM),
         cost_estimate=LIGHT,
-    )(queries[0], keys[0], values[0], grad)
+    )(queries[0], keys[0], values[0], mixed, total, grad)
 
 
 def newton(grams):
@@ -713,9 +728,9 @@
     for weight in weight_self:
         heads = product(normed_one, weight[:, :triple]).astype(BF16)
         parts = [(heads, member * pairs, pairs) for member in range(3)]
-        mixed = attend(*parts, True)
+        mixed, log_sums = attend(*parts, True)
         total = total + across(mixed, weight[:, triple:])
-        self_parts.append(parts)
+        self_parts.append(parts + [mixed, log_sums])
         self_mixed.append(mixed)
     total = after(total, (results["crossy"], results["feedz" + str(deep - 1)]))
     residual_one = residual + collect(total)
@@ -726,9 +741,9 @@
         query = product(normed_two, weight[:, :cols_in]).astype(BF16)
         key_value = product(memory, weight[:, cols_in:triple]).astype(BF16)
         parts = [(query, 0, pairs), (key_value, 0, pairs), (key_value, pairs, pairs)]
-        mixed = attend(*parts, False)
+        mixed, log_sums = attend(*parts, False)
         total = total + across(mixed, weight[:, triple:])
-        cross_parts.append(parts)
+        cross_parts.append(parts + [mixed, log_sums])
         cross_mixed.append(mixed)
     weight_expand, weight_shrink = feed_second(cross_mixed[0])
     total = after(total, (up_far, back_far))

time: 975 us -> 972 us (level)
  Pallas kernels: 90.9 us -> 78.7 us
  waiting for transfers between devices: 292 us -> 304 us
    pallas_call x4, Pallas kernels: 32.4 us -> 22.6 us  [attend_back(): pl.pallas_call(functools.partial(attend_back_kernel, causal), grid=(count...]
    unnamed x481 -> x465, local copies, waits for them, and re-layouts: 74.8 us -> 70.6 us
  transfers between devices with their start and end apart: 89 -> 89, of which waited for: 37 -> 35; matrix products, arithmetic and copies ran while one was open for 32% -> 32% of each run, Pallas kernels for 8% -> 7%
where the time goes in v5:
time: 972 us; the launch traced here: 961 us
  waiting for transfers between devices  304 us (31%)
  matrix products  194 us (20%)
  local copies, waits for them, and re-layouts  138 us (14%)
  other arithmetic  138 us (14%)
  starting transfers between devices  86.8 us (9%)
  Pallas kernels  78.7 us (8%)
  between operations  22.6 us (2%)
    ppermute x38, waiting for transfers between devices, swap(): lax.ppermute(value, axis, [(i, i ^ step) for i in range(self.sizes[axis])])  210 us
    dot_general x42, matrix products, contract(): lax.dot_general(left, right, (((left_dim,), (right_dim,)), ((), ())), pre...  101 us
    ppermute x43, waiting for transfers between devices, rotate(): lax.ppermute(value, axis, [(i, (i + step) % size) for i in range(size)])  83.4 us
    unnamed x465, local copies, waits for them, and re-layouts  70.6 us
    ppermute x38, starting transfers between devices, swap(): lax.ppermute(value, axis, [(i, i ^ step) for i in range(self.sizes[axis])])  42.9 us
    ppermute x43, starting transfers between devices, rotate(): lax.ppermute(value, axis, [(i, (i + step) % size) for i in range(size)])  31.5 us
    dot_general x34, matrix products, times(): return jnp.einsum('brs,bst->brt', left, right, precision=HIGHEST)  25.6 us
    pallas_call x4, Pallas kernels, attend_back(): pl.pallas_call(functools.partial(attend_back_kernel, causal), grid=(count...  22.6 us
  transfers between devices with their start and end apart: 89, of which 35 were waited for; matrix products, arithmetic and copies ran while one was open for 32% of the time, Pallas kernels for 7%

profile of v5, /device:TPU:0, one launch (start us, length us, event | category | flops | bytes accessed | tf_op | source)
XLA Modules:
  0.0 961.0 jit_solution(17627591055403723731)
XLA Ops:
  11.2 3.0 collective-permute-start.1
  20.0 9.3 collective-permute-done.2
  30.2 9.5 collective-permute-done.1
  60.5 7.2 collective-permute-done.6
  92.6 3.5 collective-permute-done.10
  109.4 10.1 %collective-permute-done.14 = bf16[4,64,1024]{2,1,0:T(8,128)(2,1)S(1)} collective-permute-done((bf16[4,64,1024]{2,1,0:T(8,128)(2,1)S(1)}, bf16[4,64,1024]{2,1,0:T(8,128)(2,1)S(1)}, u32[]{:S(2)}, u32[]{:S(2)}) %collective-permute-start.14) | collective-permute-done | bytes 524320 | tf_op jit(solution)/shard_map/ppermute | solution.py:83
  120.3 6.7 fusion.14
  135.3 5.7 collective-permute-done.23
  140.9 4.1 collective-permute-done.20
  149.0 21.7 %collective-permute-done.24 = bf16[512,1024]{1,0:T(8,128)(2,1)S(1)} collective-permute-done((bf16[512,1024]{1,0:T(8,128)(2,1)}, bf16[512,1024]{1,0:T(8,128)(2,1)S(1)}, u32[]{:S(2)}, u32[]{:S(2)}) %collective-permute-start.24) | collective-permute-done | bytes 1048608 | tf_op jit(solution)/shard_map/ppermute | solution.py:83
  170.8 6.7 fusion.16
  177.8 3.7 multiply_sine_fusion
  187.9 5.0 shard_map.357
  205.2 4.0 convolution_convert_fusion.1.query_ref.key_ref.value_ref
  209.5 8.6 shard_map.360
  222.2 8.8 shard_map.358
  232.9 3.0 collective-permute-done.27
  235.9 27.6 %collective-permute-done.26 = bf16[1024,1024]{0,1:T(8,128)(2,1)S(1)} collective-permute-done((bf16[1024,1024]{0,1:T(8,128)(2,1)S(1)}, bf16[1024,1024]{0,1:T(8,128)(2,1)S(1)}, u32[]{:S(2)}, u32[]{:S(2)}) %collective-permute-start.26) | collective-permute-done | bytes 2097184 | tf_op jit(solution)/shard_map/ppermute | solution.py:83
  291.8 12.2 %collective-permute-done.30 = bf16[512,1024]{0,1:T(8,128)(2,1)} collective-permute-done((bf16[512,1024]{0,1:T(8,128)(2,1)S(1)}, bf16[512,1024]{0,1:T(8,128)(2,1)}, u32[]{:S(2)}, u32[]{:S(2)}) %collective-permute-start.30) | collective-permute-done | bytes 1048608 | tf_op jit(solution)/shard_map/ppermute | solution.py:83
  314.2 3.5 fusion.52
  317.8 12.6 %shard_map.359 = (bf16[2,16,64,1024]{3,2,1,0:T(8,128)(2,1)}, bf16[2,16,64,1024]{3,2,1,0:T(8,128)(2,1)}) custom-call(s32[16]{0:T(128)} %add.1238.order_ref, bf16[16,4,64,1024]{3,2,1,0:T(8,128)(2,1)} %bitcast.646), custom_call_target="tpu_custom_call" | custom-call | flops 1024 | bytes 1024 | tf_op jit(solution)/shard_map/pallas_call | solution.py:208
  330.4 26.7 %collective-permute-done.33 = bf16[1024,1024]{0,1:T(8,128)(2,1)} collective-permute-done((bf16[1024,1024]{0,1:T(8,128)(2,1)}, bf16[1024,1024]{0,1:T(8,128)(2,1)}, u32[]{:S(2)}, u32[]{:S(2)}) %collective-permute-start.33) | collective-permute-done | bytes 2097184 | tf_op jit(solution)/shard_map/ppermute | solution.py:83
  362.0 10.1 %fusion.22 = (f32[1024,1024]{1,0:T(8,128)}, bf16[1024,1024]{1,0:T(8,128)(2,1)S(1)}) fusion(bf16[1024,1024]{1,0:T(8,128)(2,1)S(1)} %bitcast.683, bf16[1024,1024]{0,1:T(8,128)(2,1)} %constant_dynamic-update-slice_fusion.15), kind=kOutput, calls=%fused_computation.39 | convolution fusion | flops 2173698048 | bytes 10485760 | tf_op jit(solution)/shard_map/dot_general | solution.py:226
  372.2 9.5 fusion.27
  381.6 4.3 fusion.230
  389.2 3.6 collective-permute-done.36
  394.8 4.5 shard_map.364
  411.5 7.6 bitcast_reduce_fusion.1
  419.2 4.6 bitcast_reduce_fusion
  423.8 4.5 fusion.12
  430.3 5.9 fusion.7
  436.1 9.3 fusion.270
  445.5 4.6 bitcast_add_fusion
  458.2 4.7 shard_map.365
  466.7 6.4 fusion.279
  479.9 4.4 multiply_convert_fusion
  484.3 4.7 fusion.271
  489.0 4.0 convolution_add_fusion.4
  498.8 4.6 fusion.30
  503.4 3.2 copy-done.49
  511.9 4.8 fusion.277
  516.7 3.9 multiply_reduce_fusion.2
  527.6 3.9 convolution_convert_fusion
  546.1 10.3 %collective-permute-done.47 = bf16[2,4,2,64,1024]{4,3,2,1,0:T(8,128)(2,1)} collective-permute-done((bf16[2,4,2,64,1024]{4,3,2,1,0:T(8,128)(2,1)}, bf16[2,4,2,64,1024]{4,3,2,1,0:T(8,128)(2,1)}, u32[]{:S(2)}, u32[]{:S(2)}) %collective-permute-start.47) | collective-permute-done | bytes 2097184 | tf_op jit(solution)/shard_map/ppermute | solution.py:83
  560.2 5.0 fusion.28
  591.8 8.6 shard_map.369
  600.4 8.4 shard_map.368
  608.9 3.2 fusion.70
  617.8 4.1 convert_add_fusion
  647.9 4.6 shard_map.370
  656.6 21.8 %collective-permute-done.54 = bf16[512,1024]{1,0:T(8,128)(2,1)} collective-permute-done((bf16[512,1024]{1,0:T(8,128)(2,1)}, bf16[512,1024]{1,0:T(8,128)(2,1)}, u32[]{:S(2)}, u32[]{:S(2)}) %collective-permute-start.54) | collective-permute-done | bytes 1048608 | tf_op jit(solution)/shard_map/ppermute | solution.py:83
  697.7 31.2 %collective-permute-done.57 = f32[16,1024]{1,0:T(8,128)S(1)} collective-permute-done((f32[16,1024]{1,0:T(8,128)S(1)}, f32[16,1024]{1,0:T(8,128)S(1)}, u32[]{:S(2)}, u32[]{:S(2)}) %collective-permute-start.57) | collective-permute-done | bytes 65568 | tf_op jit(solution)/shard_map/ppermute | solution.py:83
  740.0 3.2 pad_maximum_fusion.11
  761.0 6.4 collective-permute-done.62
  767.8 7.9 collective-permute-done.69
  776.0 7.6 collective-permute-done.67
  783.8 9.0 collective-permute-done.65
  818.6 21.8 %collective-permute-done.73 = bf16[128,1024]{1,0:T(8,128)(2,1)S(1)} collective-permute-done((bf16[128,1024]{1,0:T(8,128)(2,1)S(1)}, bf16[128,1024]{1,0:T(8,128)(2,1)S(1)}, u32[]{:S(2)}, u32[]{:S(2)}) %collective-permute-start.73) | collective-permute-done | bytes 262176 | tf_op jit(solution)/shard_map/ppermute | solution.py:80
  841.4 8.6 collective-permute-done.74
  853.7 8.5 collective-permute-done.77
  886.6 3.0 collective-permute-done.82
  905.5 3.5 collective-permute-done.86
  914.7 9.5 collective-permute-start.84
  926.5 6.9 collective-permute-done.84
  (1002 shorter events, 429.5 us)
Async XLA Ops:
  7.2 310.6 %all-gather.3.cloned.1.call-start = ((), (), s32[]{:S(2)}) async-start(), calls=%async_computation | async-start | bytes 8912896 | tf_op jit(solution)/shard_map/all_gather | solution.py:694
  11.2 28.4 %collective-permute-start.1 = (bf16[512,1024]{0,1:T(8,128)(2,1)}, bf16[512,1024]{0,1:T(8,128)(2,1)S(1)}, u32[]{:S(2)}, u32[]{:S(2)}) collective-permute-start(bf16[512,1024]{0,1:T(8,128)(2,1)} %maximum_maximum_fusion), channel_id=1, source_target_pairs={{0,8},{8,16},{16,24},{24,0},{1,9},{9,17},{17,25},{25,1},{2,10},{10... | collective-permute-start | bytes 3145736 | tf_op jit(solution)/shard_map/ppermute | solution.py:80
  14.9 14.3 %collective-permute-start.2 = (bf16[256,1024]{0,1:T(8,128)(2,1)S(1)}, bf16[256,1024]{0,1:T(8,128)(2,1)S(1)}, u32[]{:S(2)}, u32[]{:S(2)}) collective-permute-start(bf16[256,1024]{0,1:T(8,128)(2,1)S(1)} %maximum_maximum_fusion.1), channel_id=1, source_target_pairs={{0,4},{4,0},{1,5},{5,1},{2,6},{6,2},{3,7},{7,3},{8,12},{12,8},{9,1... | collective-permute-start | bytes 1572872 | tf_op jit(solution)/shard_map/ppermute | solution.py:83
  16.4 25.1 %collective-permute-start.3 = (bf16[4,64,1024]{2,1,0:T(8,128)(2,1)S(1)}, bf16[4,64,1024]{2,1,0:T(8,128)(2,1)}, u32[]{:S(2)}, u32[]{:S(2)}) collective-permute-start(bf16[4,64,1024]{2,1,0:T(8,128)(2,1)S(1)} %get-tuple-element.125), channel_id=1, source_target_pairs={{0,2},{2,0},{1,3},{3,1},{4,6},{6,4},{5,7},{7,5},{8,10},{10,8},{9,1... | collective-permute-start | bytes 1572872 | tf_op jit(solution)/shard_map/ppermute | solution.py:83
  41.5 26.1 %collective-permute-start.6 = (bf16[512,1024]{0,1:T(8,128)(2,1)S(1)}, bf16[512,1024]{0,1:T(8,128)(2,1)S(1)}, u32[]{:S(2)}, u32[]{:S(2)}) collective-permute-start(bf16[512,1024]{0,1:T(8,128)(2,1)S(1)} %collective-permute-done.1), channel_id=1, source_target_pairs={{0,8},{8,16},{16,24},{24,0},{1,9},{9,17},{17,25},{25,1},{2,10},{10... | collective-permute-start | bytes 3145736 | tf_op jit(solution)/shard_map/ppermute | solution.py:80
  45.0 12.8 %collective-permute-start.7 = (bf16[256,1024]{0,1:T(8,128)(2,1)}, bf16[256,1024]{0,1:T(8,128)(2,1)S(1)}, u32[]{:S(2)}, u32[]{:S(2)}) collective-permute-start(bf16[256,1024]{0,1:T(8,128)(2,1)} %get-tuple-element.129), channel_id=1, source_target_pairs={{0,4},{4,0},{1,5},{5,1},{2,6},{6,2},{3,7},{7,3},{8,12},{12,8},{9,1... | collective-permute-start | bytes 1572872 | tf_op jit(solution)/shard_map/ppermute | solution.py:83
  46.5 24.2 %collective-permute-start.5 = (bf16[4,64,1024]{2,1,0:T(8,128)(2,1)}, bf16[4,64,1024]{2,1,0:T(8,128)(2,1)}, u32[]{:S(2)}, u32[]{:S(2)}) collective-permute-start(bf16[4,64,1024]{2,1,0:T(8,128)(2,1)} %bitcast.19), channel_id=1, source_target_pairs={{0,2},{2,0},{1,3},{3,1},{4,6},{6,4},{5,7},{7,5},{8,10},{10,8},{9,1... | collective-permute-start | bytes 1572872 | tf_op jit(solution)/shard_map/ppermute | solution.py:83
  47.0 23.7 %collective-permute-start.8 = (bf16[256,1024]{0,1:T(8,128)(2,1)}, bf16[256,1024]{0,1:T(8,128)(2,1)}, u32[]{:S(2)}, u32[]{:S(2)}) collective-permute-start(bf16[256,1024]{0,1:T(8,128)(2,1)} %pad_maximum_fusion.32), channel_id=1, source_target_pairs={{0,2},{2,0},{1,3},{3,1},{4,6},{6,4},{5,7},{7,5},{8,10},{10,8},{9,1... | collective-permute-start | bytes 1572872 | tf_op jit(solution)/shard_map/ppermute | solution.py:83
  70.8 25.3 %collective-permute-start.10 = (bf16[512,1024]{0,1:T(8,128)(2,1)S(1)}, bf16[512,1024]{0,1:T(8,128)(2,1)}, u32[]{:S(2)}, u32[]{:S(2)}) collective-permute-start(bf16[512,1024]{0,1:T(8,128)(2,1)S(1)} %collective-permute-done.6), channel_id=1, source_target_pairs={{0,8},{8,16},{16,24},{24,0},{1,9},{9,17},{17,25},{25,1},{2,10},{10... | collective-permute-start | bytes 3145736 | tf_op jit(solution)/shard_map/ppermute | solution.py:80
  74.4 15.3 %collective-permute-start.11 = (bf16[256,1024]{0,1:T(8,128)(2,1)}, bf16[256,1024]{0,1:T(8,128)(2,1)}, u32[]{:S(2)}, u32[]{:S(2)}) collective-permute-start(bf16[256,1024]{0,1:T(8,128)(2,1)} %get-tuple-element.133), channel_id=1, source_target_pairs={{0,4},{4,0},{1,5},{5,1},{2,6},{6,2},{3,7},{7,3},{8,12},{12,8},{9,1... | collective-permute-start | bytes 1572872 | tf_op jit(solution)/shard_map/ppermute | solution.py:83
  75.1 15.6 %collective-permute-start.9 = (bf16[4,64,1024]{2,1,0:T(8,128)(2,1)}, bf16[4,64,1024]{2,1,0:T(8,128)(2,1)}, u32[]{:S(2)}, u32[]{:S(2)}) collective-permute-start(bf16[4,64,1024]{2,1,0:T(8,128)(2,1)} %bitcast.703), channel_id=1, source_target_pairs={{0,2},{2,0},{1,3},{3,1},{4,6},{6,4},{5,7},{7,5},{8,10},{10,8},{9,1... | collective-permute-start | bytes 1572872 | tf_op jit(solution)/shard_map/ppermute | solution.py:83
  84.5 19.0 %collective-permute-start.13 = (bf16[256,1024]{0,1:T(8,128)(2,1)}, bf16[256,1024]{0,1:T(8,128)(2,1)}, u32[]{:S(2)}, u32[]{:S(2)}) collective-permute-start(bf16[256,1024]{0,1:T(8,128)(2,1)} %pad_maximum_fusion.33), channel_id=1, source_target_pairs={{0,2},{2,0},{1,3},{3,1},{4,6},{6,4},{5,7},{7,5},{8,10},{10,8},{9,1... | collective-permute-start | bytes 1572872 | tf_op jit(solution)/shard_map/ppermute | solution.py:83
  103.6 23.8 %collective-permute-start.16 = (bf16[256,1024]{0,1:T(8,128)(2,1)S(1)}, bf16[256,1024]{0,1:T(8,128)(2,1)S(1)}, u32[]{:S(2)}, u32[]{:S(2)}) collective-permute-start(bf16[256,1024]{0,1:T(8,128)(2,1)S(1)} %copy-done.149), channel_id=1, source_target_pairs={{0,4},{4,0},{1,5},{5,1},{2,6},{6,2},{3,7},{7,3},{8,12},{12,8},{9,1... | collective-permute-start | bytes 1572872 | tf_op jit(solution)/shard_map/ppermute | solution.py:83
  104.6 14.9 %collective-permute-start.14 = (bf16[4,64,1024]{2,1,0:T(8,128)(2,1)S(1)}, bf16[4,64,1024]{2,1,0:T(8,128)(2,1)S(1)}, u32[]{:S(2)}, u32[]{:S(2)}) collective-permute-start(bf16[4,64,1024]{2,1,0:T(8,128)(2,1)S(1)} %bitcast.705), channel_id=1, source_target_pairs={{0,2},{2,0},{1,3},{3,1},{4,6},{6,4},{5,7},{7,5},{8,10},{10,8},{9,1... | collective-permute-start | bytes 1572872 | tf_op jit(solution)/shard_map/ppermute | solution.py:83
  107.0 20.3 %collective-permute-start.17 = (s32[8,128]{1,0:T(8,128)S(1)}, s32[8,128]{1,0:T(8,128)S(1)}, u32[]{:S(2)}, u32[]{:S(2)}) collective-permute-start(s32[8,128]{1,0:T(8,128)S(1)} %broadcast_in_dim.282), channel_id=1, source_target_pairs={{0,8},{8,16},{16,24},{24,0},{1,9},{9,17},{17,25},{25,1},{2,10},{10... | collective-permute-start | bytes 12296 | tf_op jit(solution)/shard_map/ppermute | solution.py:80
  107.0 21.4 %collective-permute-start.18 = (bf16[256,1024]{0,1:T(8,128)(2,1)S(1)}, bf16[256,1024]{0,1:T(8,128)(2,1)S(1)}, u32[]{:S(2)}, u32[]{:S(2)}) collective-permute-start(bf16[256,1024]{0,1:T(8,128)(2,1)S(1)} %copy-done.144), channel_id=1, source_target_pairs={{0,8},{8,16},{16,24},{24,0},{1,9},{9,17},{17,25},{25,1},{2,10},{10... | collective-permute-start | bytes 1572872 | tf_op jit(solution)/shard_map/ppermute | solution.py:80
  107.0 21.4 %collective-permute-start.19 = (bf16[256,1024]{0,1:T(8,128)(2,1)S(1)}, bf16[256,1024]{0,1:T(8,128)(2,1)S(1)}, u32[]{:S(2)}, u32[]{:S(2)}) collective-permute-start(bf16[256,1024]{0,1:T(8,128)(2,1)S(1)} %pad_maximum_fusion.34), channel_id=1, source_target_pairs={{0,2},{2,0},{1,3},{3,1},{4,6},{6,4},{5,7},{7,5},{8,10},{10,8},{9,1... | collective-permute-start | bytes 1572872 | tf_op jit(solution)/shard_map/ppermute | solution.py:83
  128.5 16.6 %collective-permute-start.20 = (bf16[256,1024]{0,1:T(8,128)(2,1)S(1)}, bf16[256,1024]{0,1:T(8,128)(2,1)}, u32[]{:S(2)}, u32[]{:S(2)}) collective-permute-start(bf16[256,1024]{0,1:T(8,128)(2,1)S(1)} %collective-permute-done.18), channel_id=1, source_target_pairs={{0,8},{8,16},{16,24},{24,0},{1,9},{9,17},{17,25},{25,1},{2,10},{10... | collective-permute-start | bytes 1572872 | tf_op jit(solution)/shard_map/ppermute | solution.py:80
  128.7 16.3 %collective-permute-start.22 = (bf16[256,1024]{0,1:T(8,128)(2,1)S(1)}, bf16[256,1024]{0,1:T(8,128)(2,1)S(1)}, u32[]{:S(2)}, u32[]{:S(2)}) collective-permute-start(bf16[256,1024]{0,1:T(8,128)(2,1)S(1)} %pad_maximum_fusion.36), channel_id=1, source_target_pairs={{0,2},{2,0},{1,3},{3,1},{4,6},{6,4},{5,7},{7,5},{8,10},{10,8},{9,1... | collective-permute-start | bytes 1572872 | tf_op jit(solution)/shard_map/ppermute | solution.py:83
  130.3 10.6 %collective-permute-start.23 = (s32[8,128]{1,0:T(8,128)S(1)}, s32[8,128]{1,0:T(8,128)S(1)}, u32[]{:S(2)}, u32[]{:S(2)}) collective-permute-start(s32[8,128]{1,0:T(8,128)S(1)} %broadcast_add_fusion.2), channel_id=1, source_target_pairs={{0,16},{8,24},{16,0},{24,8},{1,17},{9,25},{17,1},{25,9},{2,18},{10... | collective-permute-start | bytes 12296 | tf_op jit(solution)/shard_map/ppermute | solution.py:80
  145.9 24.9 %collective-permute-start.24 = (bf16[512,1024]{1,0:T(8,128)(2,1)}, bf16[512,1024]{1,0:T(8,128)(2,1)S(1)}, u32[]{:S(2)}, u32[]{:S(2)}) collective-permute-start(bf16[512,1024]{1,0:T(8,128)(2,1)} %fusion.54), channel_id=1, source_target_pairs={{0,4},{4,0},{1,5},{5,1},{2,6},{6,2},{3,7},{7,3},{8,12},{12,8},{9,1... | collective-permute-start | bytes 3145736 | tf_op jit(solution)/shard_map/ppermute | solution.py:83
  201.9 61.6 %collective-permute-start.26 = (bf16[1024,1024]{0,1:T(8,128)(2,1)S(1)}, bf16[1024,1024]{0,1:T(8,128)(2,1)S(1)}, u32[]{:S(2)}, u32[]{:S(2)}) collective-permute-start(bf16[1024,1024]{0,1:T(8,128)(2,1)S(1)} %copy-done.132), channel_id=1, source_target_pairs={{0,2},{2,0},{1,3},{3,1},{4,6},{6,4},{5,7},{7,5},{8,10},{10,8},{9,1... | collective-permute-start | bytes 6291464 | tf_op jit(solution)/shard_map/ppermute | solution.py:83
  209.2 26.7 %collective-permute-start.27 = (bf16[256,1024]{0,1:T(8,128)(2,1)}, bf16[256,1024]{0,1:T(8,128)(2,1)}, u32[]{:S(2)}, u32[]{:S(2)}) collective-permute-start(bf16[256,1024]{0,1:T(8,128)(2,1)} %collective-permute-done.20), channel_id=1, source_target_pairs={{0,8},{8,16},{16,24},{24,0},{1,9},{9,17},{17,25},{25,1},{2,10},{10... | collective-permute-start | bytes 1572872 | tf_op jit(solution)/shard_map/ppermute | solution.py:80
  278.4 25.5 %collective-permute-start.30 = (bf16[512,1024]{0,1:T(8,128)(2,1)S(1)}, bf16[512,1024]{0,1:T(8,128)(2,1)}, u32[]{:S(2)}, u32[]{:S(2)}) collective-permute-start(bf16[512,1024]{0,1:T(8,128)(2,1)S(1)} %pad_maximum_fusion.16), channel_id=1, source_target_pairs={{0,4},{4,0},{1,5},{5,1},{2,6},{6,2},{3,7},{7,3},{8,12},{12,8},{9,1... | collective-permute-start | bytes 3145736 | tf_op jit(solution)/shard_map/ppermute | solution.py:83
  280.0 25.2 %collective-permute-start.31 = (bf16[512,1024]{0,1:T(8,128)(2,1)S(1)}, bf16[512,1024]{0,1:T(8,128)(2,1)}, u32[]{:S(2)}, u32[]{:S(2)}) collective-permute-start(bf16[512,1024]{0,1:T(8,128)(2,1)S(1)} %pad_maximum_fusion.17), channel_id=1, source_target_pairs={{0,2},{2,0},{1,3},{3,1},{4,6},{6,4},{5,7},{7,5},{8,10},{10,8},{9,1... | collective-permute-start | bytes 3145736 | tf_op jit(solution)/shard_map/ppermute | solution.py:83
  308.8 48.3 %collective-permute-start.33 = (bf16[1024,1024]{0,1:T(8,128)(2,1)}, bf16[1024,1024]{0,1:T(8,128)(2,1)}, u32[]{:S(2)}, u32[]{:S(2)}) collective-permute-start(bf16[1024,1024]{0,1:T(8,128)(2,1)} %constant_dynamic-update-slice_fusion.15), channel_id=1, source_target_pairs={{0,2},{2,0},{1,3},{3,1},{4,6},{6,4},{5,7},{7,5},{8,10},{10,8},{9,1... | collective-permute-start | bytes 6291464 | tf_op jit(solution)/shard_map/ppermute | solution.py:83
  312.1 48.1 %collective-permute-start.34 = (bf16[1024,1024]{0,1:T(8,128)(2,1)}, bf16[1024,1024]{0,1:T(8,128)(2,1)}, u32[]{:S(2)}, u32[]{:S(2)}) collective-permute-start(bf16[1024,1024]{0,1:T(8,128)(2,1)} %pad_maximum_fusion.2), channel_id=1, source_target_pairs={{0,4},{4,0},{1,5},{5,1},{2,6},{6,2},{3,7},{7,3},{8,12},{12,8},{9,1... | collective-permute-start | bytes 6291464 | tf_op jit(solution)/shard_map/ppermute | solution.py:83
  495.8 20.9 %collective-permute-start.41 = (f32[512,1024]{1,0:T(8,128)}, f32[512,1024]{1,0:T(8,128)}, u32[]{:S(2)}, u32[]{:S(2)}) collective-permute-start(f32[512,1024]{1,0:T(8,128)} %dynamic-slice_bitcast_fusion.2), channel_id=1, source_target_pairs={{0,1},{1,0},{2,3},{3,2},{4,5},{5,4},{6,7},{7,6},{8,9},{9,8},{10,11... | collective-permute-start | bytes 6291464 | tf_op jit(solution)/shard_map/ppermute | solution.py:80
  508.3 48.1 %collective-permute-start.47 = (bf16[2,4,2,64,1024]{4,3,2,1,0:T(8,128)(2,1)}, bf16[2,4,2,64,1024]{4,3,2,1,0:T(8,128)(2,1)}, u32[]{:S(2)}, u32[]{:S(2)}) collective-permute-start(bf16[2,4,2,64,1024]{4,3,2,1,0:T(8,128)(2,1)} %fusion.45), channel_id=1, source_target_pairs={{0,4},{4,0},{1,5},{5,1},{2,6},{6,2},{3,7},{7,3},{8,12},{12,8},{9,1... | collective-permute-start | bytes 6291464 | tf_op jit(solution)/shard_map/ppermute | solution.py:83
  509.7 47.8 %collective-permute-start.48 = (bf16[2,2,4,64,1024]{4,3,0,1,2:T(8,128)(2,1)}, bf16[2,2,4,64,1024]{4,3,0,1,2:T(8,128)(2,1)}, u32[]{:S(2)}, u32[]{:S(2)}) collective-permute-start(bf16[2,2,4,64,1024]{4,3,0,1,2:T(8,128)(2,1)} %fusion.46), channel_id=1, source_target_pairs={{0,2},{2,0},{1,3},{3,1},{4,6},{6,4},{5,7},{7,5},{8,10},{10,8},{9,1... | collective-permute-start | bytes 6291464 | tf_op jit(solution)/shard_map/ppermute | solution.py:83
  546.0 30.6 %collective-permute-start.43 = (f32[512,1024]{1,0:T(8,128)S(1)}, f32[512,1024]{1,0:T(8,128)S(1)}, u32[]{:S(2)}, u32[]{:S(2)}) collective-permute-start(f32[512,1024]{1,0:T(8,128)S(1)} %dynamic-slice_bitcast_fusion.1), channel_id=1, source_target_pairs={{0,1},{1,0},{2,3},{3,2},{4,5},{5,4},{6,7},{7,6},{8,9},{9,8},{10,11... | collective-permute-start | bytes 6291464 | tf_op jit(solution)/shard_map/ppermute | solution.py:80
  566.4 49.9 %collective-permute-start.49 = (bf16[1024,1024]{1,0:T(8,128)(2,1)}, bf16[1024,1024]{1,0:T(8,128)(2,1)}, u32[]{:S(2)}, u32[]{:S(2)}) collective-permute-start(bf16[1024,1024]{1,0:T(8,128)(2,1)} %convolution_convert_fusion), channel_id=1, source_target_pairs={{0,2},{2,0},{1,3},{3,1},{4,6},{6,4},{5,7},{7,5},{8,10},{10,8},{9,1... | collective-permute-start | bytes 6291464 | tf_op jit(solution)/shard_map/ppermute | solution.py:83
  567.8 48.5 %collective-permute-start.50 = (bf16[1024,1024]{1,0:T(8,128)(2,1)}, bf16[1024,1024]{1,0:T(8,128)(2,1)}, u32[]{:S(2)}, u32[]{:S(2)}) collective-permute-start(bf16[1024,1024]{1,0:T(8,128)(2,1)} %pad_maximum_fusion.4), channel_id=1, source_target_pairs={{0,4},{4,0},{1,5},{5,1},{2,6},{6,2},{3,7},{7,3},{8,12},{12,8},{9,1... | collective-permute-start | bytes 6291464 | tf_op jit(solution)/shard_map/ppermute | solution.py:83
  568.5 47.8 %collective-permute-start.51 = (bf16[512,1024]{1,0:T(8,128)(2,1)}, bf16[512,1024]{1,0:T(8,128)(2,1)}, u32[]{:S(2)}, u32[]{:S(2)}) collective-permute-start(bf16[512,1024]{1,0:T(8,128)(2,1)} %pad_maximum_fusion.20), channel_id=1, source_target_pairs={{0,8},{8,16},{16,24},{24,0},{1,9},{9,17},{17,25},{25,1},{2,10},{10... | collective-permute-start | bytes 3145736 | tf_op jit(solution)/shard_map/ppermute | solution.py:80
  615.7 25.2 %collective-permute-start.45 = (f32[512,1024]{1,0:T(8,128)S(1)}, f32[512,1024]{1,0:T(8,128)S(1)}, u32[]{:S(2)}, u32[]{:S(2)}) collective-permute-start(f32[512,1024]{1,0:T(8,128)S(1)} %dynamic-slice_bitcast_fusion), channel_id=1, source_target_pairs={{0,1},{1,0},{2,3},{3,2},{4,5},{5,4},{6,7},{7,6},{8,9},{9,8},{10,11... | collective-permute-start | bytes 6291464 | tf_op jit(solution)/shard_map/ppermute | solution.py:80
  629.7 26.3 %collective-permute-start.52 = (bf16[1024,512]{1,0:T(8,128)(2,1)}, bf16[1024,512]{1,0:T(8,128)(2,1)}, u32[]{:S(2)}, u32[]{:S(2)}) collective-permute-start(bf16[1024,512]{1,0:T(8,128)(2,1)} %pad_maximum_fusion.18), channel_id=1, source_target_pairs={{0,2},{2,0},{1,3},{3,1},{4,6},{6,4},{5,7},{7,5},{8,10},{10,8},{9,1... | collective-permute-start | bytes 3145736 | tf_op jit(solution)/shard_map/ppermute | solution.py:83
  630.3 26.3 %collective-permute-start.53 = (bf16[1024,512]{1,0:T(8,128)(2,1)}, bf16[1024,512]{1,0:T(8,128)(2,1)}, u32[]{:S(2)}, u32[]{:S(2)}) collective-permute-start(bf16[1024,512]{1,0:T(8,128)(2,1)} %pad_maximum_fusion.19), channel_id=1, source_target_pairs={{0,4},{4,0},{1,5},{5,1},{2,6},{6,2},{3,7},{7,3},{8,12},{12,8},{9,1... | collective-permute-start | bytes 3145736 | tf_op jit(solution)/shard_map/ppermute | solution.py:83
  631.7 46.6 %collective-permute-start.54 = (bf16[512,1024]{1,0:T(8,128)(2,1)}, bf16[512,1024]{1,0:T(8,128)(2,1)}, u32[]{:S(2)}, u32[]{:S(2)}) collective-permute-start(bf16[512,1024]{1,0:T(8,128)(2,1)} %slice.1397), channel_id=1, source_target_pairs={{0,4},{4,0},{1,5},{5,1},{2,6},{6,2},{3,7},{7,3},{8,12},{12,8},{9,1... | collective-permute-start | bytes 3145736 | tf_op jit(solution)/shard_map/ppermute | solution.py:83
  632.3 46.0 %collective-permute-start.55 = (bf16[512,1024]{1,0:T(8,128)(2,1)}, bf16[512,1024]{1,0:T(8,128)(2,1)}, u32[]{:S(2)}, u32[]{:S(2)}) collective-permute-start(bf16[512,1024]{1,0:T(8,128)(2,1)} %fusion.50), channel_id=1, source_target_pairs={{0,2},{2,0},{1,3},{3,1},{4,6},{6,4},{5,7},{7,5},{8,10},{10,8},{9,1... | collective-permute-start | bytes 3145736 | tf_op jit(solution)/shard_map/ppermute | solution.py:83
  640.9 37.4 %collective-permute-start.56 = (bf16[512,1024]{1,0:T(8,128)(2,1)}, bf16[512,1024]{1,0:T(8,128)(2,1)}, u32[]{:S(2)}, u32[]{:S(2)}) collective-permute-start(bf16[512,1024]{1,0:T(8,128)(2,1)} %pad_maximum_fusion.21), channel_id=1, source_target_pairs={{0,8},{8,16},{16,24},{24,0},{1,9},{9,17},{17,25},{25,1},{2,10},{10... | collective-permute-start | bytes 3145736 | tf_op jit(solution)/shard_map/ppermute | solution.py:80
  656.1 34.3 %collective-permute-start.46 = (f32[16,1024]{1,0:T(8,128)S(1)}, f32[16,1024]{1,0:T(8,128)S(1)}, u32[]{:S(2)}, u32[]{:S(2)}) collective-permute-start(f32[16,1024]{1,0:T(8,128)S(1)} %maximum_maximum_fusion.2), channel_id=1, source_target_pairs={{0,1},{1,0},{2,3},{3,2},{4,5},{5,4},{6,7},{7,6},{8,9},{9,8},{10,11... | collective-permute-start | bytes 196616 | tf_op jit(solution)/shard_map/ppermute | solution.py:89
  690.4 39.1 %collective-permute-start.60 = (bf16[768,1024]{1,0:T(8,128)(2,1)S(1)}, bf16[768,1024]{1,0:T(8,128)(2,1)S(1)}, u32[]{:S(2)}, u32[]{:S(2)}) collective-permute-start(bf16[768,1024]{1,0:T(8,128)(2,1)S(1)} %pad_maximum_fusion.7), channel_id=1, source_target_pairs={{0,8},{8,16},{16,24},{24,0},{1,9},{9,17},{17,25},{25,1},{2,10},{10... | collective-permute-start | bytes 4718600 | tf_op jit(solution)/shard_map/ppermute | solution.py:80
  692.0 37.6 %collective-permute-start.58 = (bf16[1536,512]{1,0:T(8,128)(2,1)S(1)}, bf16[1536,512]{1,0:T(8,128)(2,1)S(1)}, u32[]{:S(2)}, u32[]{:S(2)}) collective-permute-start(bf16[1536,512]{1,0:T(8,128)(2,1)S(1)} %pad_maximum_fusion.5), channel_id=1, source_target_pairs={{0,2},{2,0},{1,3},{3,1},{4,6},{6,4},{5,7},{7,5},{8,10},{10,8},{9,1... | collective-permute-start | bytes 4718600 | tf_op jit(solution)/shard_map/ppermute | solution.py:83
  695.6 33.2 %collective-permute-start.57 = (f32[16,1024]{1,0:T(8,128)S(1)}, f32[16,1024]{1,0:T(8,128)S(1)}, u32[]{:S(2)}, u32[]{:S(2)}) collective-permute-start(f32[16,1024]{1,0:T(8,128)S(1)} %fusion.228), channel_id=1, source_target_pairs={{0,2},{2,0},{1,3},{3,1},{4,6},{6,4},{5,7},{7,5},{8,10},{10,8},{9,1... | collective-permute-start | bytes 196616 | tf_op jit(solution)/shard_map/ppermute | solution.py:83
  696.2 38.3 %collective-permute-start.59 = (bf16[1536,512]{1,0:T(8,128)(2,1)S(1)}, bf16[1536,512]{1,0:T(8,128)(2,1)S(1)}, u32[]{:S(2)}, u32[]{:S(2)}) collective-permute-start(bf16[1536,512]{1,0:T(8,128)(2,1)S(1)} %pad_maximum_fusion.6), channel_id=1, source_target_pairs={{0,4},{4,0},{1,5},{5,1},{2,6},{6,2},{3,7},{7,3},{8,12},{12,8},{9,1... | collective-permute-start | bytes 4718600 | tf_op jit(solution)/shard_map/ppermute | solution.py:83
  697.7 55.3 %collective-permute-start.64 = (bf16[512,1024]{1,0:T(8,128)(2,1)}, bf16[512,1024]{1,0:T(8,128)(2,1)}, u32[]{:S(2)}, u32[]{:S(2)}) collective-permute-start(bf16[512,1024]{1,0:T(8,128)(2,1)} %get-tuple-element.352), channel_id=1, source_target_pairs={{0,1},{1,0},{2,3},{3,2},{4,5},{5,4},{6,7},{7,6},{8,9},{9,8},{10,11... | collective-permute-start | bytes 3145736 | tf_op jit(solution)/shard_map/ppermute | solution.py:80
  743.3 15.9 %collective-permute-start.63 = (bf16[512,512]{1,0:T(8,128)(2,1)}, bf16[512,512]{1,0:T(8,128)(2,1)}, u32[]{:S(2)}, u32[]{:S(2)}) collective-permute-start(bf16[512,512]{1,0:T(8,128)(2,1)} %get-tuple-element.210), channel_id=1, source_target_pairs={{0,2},{2,0},{1,3},{3,1},{4,6},{6,4},{5,7},{7,5},{8,10},{10,8},{9,1... | collective-permute-start | bytes 1572872 | tf_op jit(solution)/shard_map/ppermute | solution.py:83
  752.3 15.1 %collective-permute-start.62 = (bf16[512,512]{1,0:T(8,128)(2,1)}, bf16[512,512]{1,0:T(8,128)(2,1)S(1)}, u32[]{:S(2)}, u32[]{:S(2)}) collective-permute-start(bf16[512,512]{1,0:T(8,128)(2,1)} %slice.1401), channel_id=1, source_target_pairs={{0,4},{4,0},{1,5},{5,1},{2,6},{6,2},{3,7},{7,3},{8,12},{12,8},{9,1... | collective-permute-start | bytes 1572872 | tf_op jit(solution)/shard_map/ppermute | solution.py:83
  755.2 28.4 %collective-permute-start.67 = (bf16[640,1024]{1,0:T(8,128)(2,1)}, bf16[640,1024]{1,0:T(8,128)(2,1)S(1)}, u32[]{:S(2)}, u32[]{:S(2)}) collective-permute-start(bf16[640,1024]{1,0:T(8,128)(2,1)} %get-tuple-element.212), channel_id=1, source_target_pairs={{0,2},{2,0},{1,3},{3,1},{4,6},{6,4},{5,7},{7,5},{8,10},{10,8},{9,1... | collective-permute-start | bytes 3932168 | tf_op jit(solution)/shard_map/ppermute | solution.py:83
  755.8 36.9 %collective-permute-start.65 = (bf16[640,1024]{1,0:T(8,128)(2,1)S(1)}, bf16[640,1024]{1,0:T(8,128)(2,1)S(1)}, u32[]{:S(2)}, u32[]{:S(2)}) collective-permute-start(bf16[640,1024]{1,0:T(8,128)(2,1)S(1)} %copy-done.113), channel_id=1, source_target_pairs={{0,4},{4,0},{1,5},{5,1},{2,6},{6,2},{3,7},{7,3},{8,12},{12,8},{9,1... | collective-permute-start | bytes 3932168 | tf_op jit(solution)/shard_map/ppermute | solution.py:83
  757.2 18.5 %collective-permute-start.69 = (bf16[384,1024]{1,0:T(8,128)(2,1)S(1)}, bf16[384,1024]{1,0:T(8,128)(2,1)S(1)}, u32[]{:S(2)}, u32[]{:S(2)}) collective-permute-start(bf16[384,1024]{1,0:T(8,128)(2,1)S(1)} %pad_maximum_fusion.24), channel_id=1, source_target_pairs={{0,8},{8,16},{16,24},{24,0},{1,9},{9,17},{17,25},{25,1},{2,10},{10... | collective-permute-start | bytes 2359304 | tf_op jit(solution)/shard_map/ppermute | solution.py:80
  783.7 10.2 %collective-permute-start.68 = (bf16[512,1024]{1,0:T(8,128)(2,1)S(1)}, bf16[512,1024]{1,0:T(8,128)(2,1)S(1)}, u32[]{:S(2)}, u32[]{:S(2)}) collective-permute-start(bf16[512,1024]{1,0:T(8,128)(2,1)S(1)} %slice.1049), channel_id=1, source_target_pairs={{0,1},{1,0},{2,3},{3,2},{4,5},{5,4},{6,7},{7,6},{8,9},{9,8},{10,11... | collective-permute-start | bytes 3145736 | tf_op jit(solution)/shard_map/ppermute | solution.py:80
  811.7 40.1 %collective-permute-start.76 = (bf16[2,4,64,1024]{3,2,0,1:T(8,128)(2,1)S(1)}, bf16[2,4,64,1024]{3,2,0,1:T(8,128)(2,1)S(1)}, u32[]{:S(2)}, u32[]{:S(2)}) collective-permute-start(bf16[2,4,64,1024]{3,2,0,1:T(8,128)(2,1)S(1)} %fusion.97), channel_id=1, source_target_pairs={{0,2},{2,0},{1,3},{3,1},{4,6},{6,4},{5,7},{7,5},{8,10},{10,8},{9,1... | collective-permute-start | bytes 3145736 | tf_op jit(solution)/shard_map/ppermute | solution.py:83
  812.4 38.5 %collective-permute-start.78 = (bf16[384,1024]{1,0:T(8,128)(2,1)S(1)}, bf16[384,1024]{1,0:T(8,128)(2,1)S(1)}, u32[]{:S(2)}, u32[]{:S(2)}) collective-permute-start(bf16[384,1024]{1,0:T(8,128)(2,1)S(1)} %pad_maximum_fusion.25), channel_id=1, source_target_pairs={{0,8},{8,16},{16,24},{24,0},{1,9},{9,17},{17,25},{25,1},{2,10},{10... | collective-permute-start | bytes 2359304 | tf_op jit(solution)/shard_map/ppermute | solution.py:80
  812.9 27.5 %collective-permute-start.73 = (bf16[128,1024]{1,0:T(8,128)(2,1)S(1)}, bf16[128,1024]{1,0:T(8,128)(2,1)S(1)}, u32[]{:S(2)}, u32[]{:S(2)}) collective-permute-start(bf16[128,1024]{1,0:T(8,128)(2,1)S(1)} %get-tuple-element.217), channel_id=1, source_target_pairs={{0,8},{8,16},{16,24},{24,0},{1,9},{9,17},{17,25},{25,1},{2,10},{10... | collective-permute-start | bytes 786440 | tf_op jit(solution)/shard_map/ppermute | solution.py:80
  814.5 35.5 %collective-permute-start.74 = (bf16[128,1024]{1,0:T(8,128)(2,1)S(1)}, bf16[128,1024]{1,0:T(8,128)(2,1)S(1)}, u32[]{:S(2)}, u32[]{:S(2)}) collective-permute-start(bf16[128,1024]{1,0:T(8,128)(2,1)S(1)} %get-tuple-element.218), channel_id=1, source_target_pairs={{0,16},{8,24},{16,0},{24,8},{1,17},{9,25},{17,1},{25,9},{2,18},{10... | collective-permute-start | bytes 786440 | tf_op jit(solution)/shard_map/ppermute | solution.py:80
  816.8 33.2 %collective-permute-start.75 = (bf16[128,1024]{1,0:T(8,128)(2,1)S(1)}, bf16[128,1024]{1,0:T(8,128)(2,1)S(1)}, u32[]{:S(2)}, u32[]{:S(2)}) collective-permute-start(bf16[128,1024]{1,0:T(8,128)(2,1)S(1)} %get-tuple-element.219), channel_id=1, source_target_pairs={{0,24},{8,0},{16,8},{24,16},{1,25},{9,1},{17,9},{25,17},{2,26},{10... | collective-permute-start | bytes 786440 | tf_op jit(solution)/shard_map/ppermute | solution.py:80
  840.4 21.8 %collective-permute-start.77 = (bf16[2,4,64,1024]{3,2,0,1:T(8,128)(2,1)S(1)}, bf16[2,4,64,1024]{3,2,0,1:T(8,128)(2,1)S(1)}, u32[]{:S(2)}, u32[]{:S(2)}) collective-permute-start(bf16[2,4,64,1024]{3,2,0,1:T(8,128)(2,1)S(1)} %fusion.98), channel_id=1, source_target_pairs={{0,4},{4,0},{1,5},{5,1},{2,6},{6,2},{3,7},{7,3},{8,12},{12,8},{9,1... | collective-permute-start | bytes 3145736 | tf_op jit(solution)/shard_map/ppermute | solution.py:83
  866.6 11.1 %collective-permute-start.79 = (bf16[128,1024]{1,0:T(8,128)(2,1)}, bf16[128,1024]{1,0:T(8,128)(2,1)S(1)}, u32[]{:S(2)}, u32[]{:S(2)}) collective-permute-start(bf16[128,1024]{1,0:T(8,128)(2,1)} %get-tuple-element.223), channel_id=1, source_target_pairs={{0,8},{8,16},{16,24},{24,0},{1,9},{9,17},{17,25},{25,1},{2,10},{10... | collective-permute-start | bytes 786440 | tf_op jit(solution)/shard_map/ppermute | solution.py:80
  872.6 31.8 %collective-permute-start.85 = (bf16[256,1024]{1,0:T(8,128)(2,1)}, bf16[256,1024]{1,0:T(8,128)(2,1)}, u32[]{:S(2)}, u32[]{:S(2)}) collective-permute-start(bf16[256,1024]{1,0:T(8,128)(2,1)} %pad_maximum_fusion.37), channel_id=1, source_target_pairs={{0,8},{8,16},{16,24},{24,0},{1,9},{9,17},{17,25},{25,1},{2,10},{10... | collective-permute-start | bytes 1572872 | tf_op jit(solution)/shard_map/ppermute | solution.py:80
  875.1 33.8 %collective-permute-start.86 = (bf16[256,1024]{1,0:T(8,128)(2,1)}, bf16[256,1024]{1,0:T(8,128)(2,1)}, u32[]{:S(2)}, u32[]{:S(2)}) collective-permute-start(bf16[256,1024]{1,0:T(8,128)(2,1)} %pad_maximum_fusion.38), channel_id=1, source_target_pairs={{0,16},{8,24},{16,0},{24,8},{1,17},{9,25},{17,1},{25,9},{2,18},{10... | collective-permute-start | bytes 1572872 | tf_op jit(solution)/shard_map/ppermute | solution.py:80
  875.1 34.9 %collective-permute-start.87 = (bf16[256,1024]{1,0:T(8,128)(2,1)}, bf16[256,1024]{1,0:T(8,128)(2,1)}, u32[]{:S(2)}, u32[]{:S(2)}) collective-permute-start(bf16[256,1024]{1,0:T(8,128)(2,1)} %pad_maximum_fusion.39), channel_id=1, source_target_pairs={{0,24},{8,0},{16,8},{24,16},{1,25},{9,1},{17,9},{25,17},{2,26},{10... | collective-permute-start | bytes 1572872 | tf_op jit(solution)/shard_map/ppermute | solution.py:80
  890.3 23.3 %collective-permute-start.83 = (f32[12,32,128]{2,1,0:T(8,128)}, f32[12,32,128]{2,1,0:T(8,128)}, u32[]{:S(2)}, u32[]{:S(2)}) collective-permute-start(f32[12,32,128]{2,1,0:T(8,128)} %add.1380), channel_id=1, source_target_pairs={{0,8},{8,0},{16,24},{24,16},{1,9},{9,1},{17,25},{25,17},{2,10},{10... | collective-permute-start | bytes 589832 | tf_op jit(solution)/shard_map/ppermute | solution.py:89
  914.7 18.7 %collective-permute-start.84 = (f32[12,32,128]{2,1,0:T(8,128)S(1)}, f32[12,32,128]{2,1,0:T(8,128)S(1)}, u32[]{:S(2)}, u32[]{:S(2)}) collective-permute-start(f32[12,32,128]{2,1,0:T(8,128)S(1)} %add.1381), channel_id=1, source_target_pairs={{0,16},{8,24},{16,0},{24,8},{1,17},{9,25},{17,1},{25,9},{2,18},{10... | collective-permute-start | bytes 589832 | tf_op jit(solution)/shard_map/ppermute | solution.py:89
  (243 other events, 2377.2 us)
Sparse Core Ops, SparseCore 0:
  170.9 131.2 all-gather.2

commit v6 on v5

--- a/solution.py
+++ b/solution.py
@@ -178,7 +178,7 @@
             start = pl.multiple_of(order_ref[p] * block, LANES)
             to_ref[:, p * block : (p + 1) * block] = from_ref[:, pl.ds(start, block)]
 
-    step = min(rows, 128)
+    step = min(rows, 256)
     return pl.pallas_call(
         kernel,
         grid_spec=pltpu.PrefetchScalarGridSpec(
@@ -759,9 +759,9 @@
         total = total + across(active, back)
         slopes.append(slope)
         actives.append(active)
-    residual_three = true(residual_two + collect(total))
-
-    final = spread(layer_norm(residual_three, norm_params[6], norm_params[7]))
+    residual_three = residual_two + collect(total)
+
+    final = spread(true(layer_norm(residual_three, gains[6], gains[7]).astype(BF16)))
     logits, targets, stats = [], [], []
     for half, part in enumerate(head):
         wanted = next_codes[half * books // 2 : (half + 1) * books // 2]
@@ -907,9 +907,8 @@
     ]
 
     grad, gain_final, shift_final = norm_back(
-        residual_three, norm_params[6], norm_params[7], grad_final
-    )
-    grad = near(grad)
+        residual_three, gains[6], gains[7], near(grad_final)
+    )
 
     rows_grad = spread(grad)
     grad_uppers, total = [], 0.0
@@ -1034,10 +1033,8 @@
 
     grad_table = add_table()
     norm_grads = [gain_one, shift_one, gain_two, shift_two, gain_three, shift_three]
-    norm_grads = jnp.take(
-        jnp.stack(norm_grads, 0).reshape(6, groups, -1), order_true, axis=1
-    ).reshape(6, width)
-    norm_grads = jnp.concatenate([norm_grads, gain_final[None], shift_final[None]], 0)
+    norm_grads = jnp.stack(norm_grads + [gain_final, shift_final], 0)
+    norm_grads = jnp.take(norm_grads.reshape(8, groups, -1), order_true, axis=1).reshape(8, width)
     loss_row = jnp.full((8, width), loss_local)
     norm_own = grid.total(jnp.concatenate([norm_grads, loss_row], 0), ("c",))
     tasks["normy"] = ("y", 0, [], 0, 3, lambda r: norm_own)

time: 972 us -> 968 us (level)
  waiting for transfers between devices: 304 us -> 317 us
    unnamed x465 -> x481, local copies, waits for them, and re-layouts: 70.6 us -> 74.5 us
  transfers between devices with their start and end apart: 89 -> 89, of which waited for: 35 -> 36; matrix products, arithmetic and copies ran while one was open for 32% -> 30% of each run, Pallas kernels for 7% -> 7%
where the time goes in v6:
time: 968 us; the launch traced here: 958 us
  waiting for transfers between devices  317 us (33%)
  matrix products  186 us (19%)
  local copies, waits for them, and re-layouts  137 us (14%)
  other arithmetic  136 us (14%)
  starting transfers between devices  85.2 us (9%)
  Pallas kernels  74 us (8%)
  between operations  22.7 us (2%)
    ppermute x38, waiting for transfers between devices, swap(): lax.ppermute(value, axis, [(i, i ^ step) for i in range(self.sizes[axis])])  219 us
    dot_general x42, matrix products, contract(): lax.dot_general(left, right, (((left_dim,), (right_dim,)), ((), ())), pre...  98.4 us
    ppermute x43, waiting for transfers between devices, rotate(): lax.ppermute(value, axis, [(i, (i + step) % size) for i in range(size)])  87.6 us
    unnamed x481, local copies, waits for them, and re-layouts  74.5 us
    ppermute x38, starting transfers between devices, swap(): lax.ppermute(value, axis, [(i, i ^ step) for i in range(self.sizes[axis])])  42.8 us
    ppermute x43, starting transfers between devices, rotate(): lax.ppermute(value, axis, [(i, (i + step) % size) for i in range(size)])  30.2 us
    dot_general x34, matrix products, times(): return jnp.einsum('brs,bst->brt', left, right, precision=HIGHEST)  25.6 us
    pallas_call x4, Pallas kernels, attend_back(): pl.pallas_call(functools.partial(attend_back_kernel, causal), grid=(count...  22.6 us
  transfers between devices with their start and end apart: 89, of which 36 were waited for; matrix products, arithmetic and copies ran while one was open for 30% of the time, Pallas kernels for 7%

profile of v6, /device:TPU:0, one launch (start us, length us, event | category | flops | bytes accessed | tf_op | source)
XLA Modules:
  0.0 957.8 jit_solution(1305370632519518740)
XLA Ops:
  20.3 10.0 %collective-permute-done.2 = bf16[256,1024]{0,1:T(8,128)(2,1)S(1)} collective-permute-done((bf16[256,1024]{0,1:T(8,128)(2,1)}, bf16[256,1024]{0,1:T(8,128)(2,1)S(1)}, u32[]{:S(2)}, u32[]{:S(2)}) %collective-permute-start.2) | collective-permute-done | bytes 524320 | tf_op jit(solution)/shard_map/ppermute | solution.py:83
  32.3 8.2 collective-permute-done.1
  52.5 6.5 collective-permute-done.7
  60.7 7.9 collective-permute-done.6
  93.1 5.4 collective-permute-done.10
  110.7 10.1 %collective-permute-done.14 = bf16[4,64,1024]{2,1,0:T(8,128)(2,1)S(1)} collective-permute-done((bf16[4,64,1024]{2,1,0:T(8,128)(2,1)S(1)}, bf16[4,64,1024]{2,1,0:T(8,128)(2,1)S(1)}, u32[]{:S(2)}, u32[]{:S(2)}) %collective-permute-start.14) | collective-permute-done | bytes 524320 | tf_op jit(solution)/shard_map/ppermute | solution.py:83
  121.7 6.7 fusion.14
  135.0 7.3 collective-permute-done.23
  142.3 4.1 collective-permute-done.20
  148.2 22.9 %collective-permute-done.24 = bf16[512,1024]{1,0:T(8,128)(2,1)S(1)} collective-permute-done((bf16[512,1024]{1,0:T(8,128)(2,1)S(1)}, bf16[512,1024]{1,0:T(8,128)(2,1)S(1)}, u32[]{:S(2)}, u32[]{:S(2)}) %collective-permute-start.24) | collective-permute-done | bytes 1048608 | tf_op jit(solution)/shard_map/ppermute | solution.py:83
  171.1 6.7 fusion.16
  178.1 3.7 multiply_sine_fusion
  188.3 3.8 shard_map.357
  204.3 4.0 convolution_convert_fusion.1.query_ref.key_ref.value_ref
  208.7 8.6 shard_map.360
  221.4 8.8 shard_map.358
  235.0 28.9 %collective-permute-done.26 = bf16[1024,1024]{0,1:T(8,128)(2,1)S(1)} collective-permute-done((bf16[1024,1024]{0,1:T(8,128)(2,1)S(1)}, bf16[1024,1024]{0,1:T(8,128)(2,1)S(1)}, u32[]{:S(2)}, u32[]{:S(2)}) %collective-permute-start.26) | collective-permute-done | bytes 2097184 | tf_op jit(solution)/shard_map/ppermute | solution.py:83
  292.2 12.3 %collective-permute-done.30 = bf16[512,1024]{0,1:T(8,128)(2,1)} collective-permute-done((bf16[512,1024]{0,1:T(8,128)(2,1)S(1)}, bf16[512,1024]{0,1:T(8,128)(2,1)}, u32[]{:S(2)}, u32[]{:S(2)}) %collective-permute-start.30) | collective-permute-done | bytes 1048608 | tf_op jit(solution)/shard_map/ppermute | solution.py:83
  314.6 3.5 fusion.52
  318.2 12.6 %shard_map.359 = (bf16[2,16,64,1024]{3,2,1,0:T(8,128)(2,1)}, bf16[2,16,64,1024]{3,2,1,0:T(8,128)(2,1)}) custom-call(s32[16]{0:T(128)} %add.1084.order_ref, bf16[16,4,64,1024]{3,2,1,0:T(8,128)(2,1)} %bitcast.640), custom_call_target="tpu_custom_call" | custom-call | flops 1024 | bytes 1024 | tf_op jit(solution)/shard_map/pallas_call | solution.py:208
  330.8 26.8 %collective-permute-done.33 = bf16[1024,1024]{0,1:T(8,128)(2,1)} collective-permute-done((bf16[1024,1024]{0,1:T(8,128)(2,1)}, bf16[1024,1024]{0,1:T(8,128)(2,1)}, u32[]{:S(2)}, u32[]{:S(2)}) %collective-permute-start.33) | collective-permute-done | bytes 2097184 | tf_op jit(solution)/shard_map/ppermute | solution.py:83
  362.6 10.1 %fusion.22 = (f32[1024,1024]{1,0:T(8,128)}, bf16[1024,1024]{1,0:T(8,128)(2,1)S(1)}) fusion(bf16[1024,1024]{1,0:T(8,128)(2,1)S(1)} %bitcast.677, bf16[1024,1024]{0,1:T(8,128)(2,1)} %constant_dynamic-update-slice_fusion.15), kind=kOutput, calls=%fused_computation.39 | convolution fusion | flops 2173698048 | bytes 10485760 | tf_op jit(solution)/shard_map/dot_general | solution.py:226
  372.6 9.5 fusion.27
  382.1 4.4 fusion.216
  392.2 3.9 collective-permute-done.36
  400.4 3.2 shard_map.364
  408.1 4.6 bitcast_reduce_fusion.1
  412.7 4.6 bitcast_reduce_fusion
  417.3 4.5 fusion.12
  423.7 6.2 fusion.7
  429.9 9.1 fusion.257
  439.1 4.6 bitcast_add_fusion
  447.1 3.7 collective-permute-done.39
  450.8 4.1 bitcast_add_fusion.4.from_ref
  455.0 3.6 shard_map.365
  458.6 3.1 multiply_reduce_fusion.1
  466.4 4.6 fusion.266
  477.8 4.4 multiply_convert_fusion
  482.2 4.7 fusion.258
  486.9 4.4 convolution_add_fusion.4
  497.0 4.6 fusion.30
  501.6 3.2 copy-done.51
  509.9 4.8 fusion.264
  514.7 3.9 multiply_reduce_fusion.2
  525.8 3.8 convolution_convert_fusion
  543.8 10.7 %collective-permute-done.47 = bf16[2,4,2,64,1024]{4,3,2,1,0:T(8,128)(2,1)} collective-permute-done((bf16[2,4,2,64,1024]{4,3,2,1,0:T(8,128)(2,1)}, bf16[2,4,2,64,1024]{4,3,2,1,0:T(8,128)(2,1)}, u32[]{:S(2)}, u32[]{:S(2)}) %collective-permute-start.47) | collective-permute-done | bytes 2097184 | tf_op jit(solution)/shard_map/ppermute | solution.py:83
  557.9 5.0 fusion.28
  589.3 8.6 shard_map.369
  597.9 8.4 shard_map.368
  606.4 3.2 fusion.70
  615.3 4.0 convert_add_fusion
  645.5 3.5 shard_map.370
  653.9 21.8 %collective-permute-done.54 = bf16[512,1024]{1,0:T(8,128)(2,1)} collective-permute-done((bf16[512,1024]{1,0:T(8,128)(2,1)}, bf16[512,1024]{1,0:T(8,128)(2,1)}, u32[]{:S(2)}, u32[]{:S(2)}) %collective-permute-start.54) | collective-permute-done | bytes 1048608 | tf_op jit(solution)/shard_map/ppermute | solution.py:83
  695.0 31.0 %collective-permute-done.57 = f32[16,1024]{1,0:T(8,128)S(1)} collective-permute-done((f32[16,1024]{1,0:T(8,128)S(1)}, f32[16,1024]{1,0:T(8,128)S(1)}, u32[]{:S(2)}, u32[]{:S(2)}) %collective-permute-start.57) | collective-permute-done | bytes 65568 | tf_op jit(solution)/shard_map/ppermute | solution.py:83
  758.2 6.3 collective-permute-done.62
  764.8 8.0 collective-permute-done.69
  773.1 7.5 collective-permute-done.67
  780.8 8.7 collective-permute-done.65
  815.8 21.7 %collective-permute-done.73 = bf16[128,1024]{1,0:T(8,128)(2,1)S(1)} collective-permute-done((bf16[128,1024]{1,0:T(8,128)(2,1)S(1)}, bf16[128,1024]{1,0:T(8,128)(2,1)S(1)}, u32[]{:S(2)}, u32[]{:S(2)}) %collective-permute-start.73) | collective-permute-done | bytes 262176 | tf_op jit(solution)/shard_map/ppermute | solution.py:80
  838.5 8.6 collective-permute-done.74
  850.9 8.4 collective-permute-done.77
  902.7 3.5 collective-permute-done.86
  912.0 9.3 collective-permute-start.84
  923.5 6.6 collective-permute-done.84
  (1016 shorter events, 423.8 us)
Async XLA Ops:
  7.2 310.9 %all-gather.3.cloned.1.call-start = ((), (), s32[]{:S(2)}) async-start(), calls=%async_computation | async-start | bytes 8912896 | tf_op jit(solution)/shard_map/all_gather | solution.py:694
  12.1 28.4 %collective-permute-start.1 = (bf16[512,1024]{0,1:T(8,128)(2,1)}, bf16[512,1024]{0,1:T(8,128)(2,1)S(1)}, u32[]{:S(2)}, u32[]{:S(2)}) collective-permute-start(bf16[512,1024]{0,1:T(8,128)(2,1)} %maximum_maximum_fusion), channel_id=1, source_target_pairs={{0,8},{8,16},{16,24},{24,0},{1,9},{9,17},{17,25},{25,1},{2,10},{10... | collective-permute-start | bytes 3145736 | tf_op jit(solution)/shard_map/ppermute | solution.py:80
  15.7 14.5 %collective-permute-start.2 = (bf16[256,1024]{0,1:T(8,128)(2,1)}, bf16[256,1024]{0,1:T(8,128)(2,1)S(1)}, u32[]{:S(2)}, u32[]{:S(2)}) collective-permute-start(bf16[256,1024]{0,1:T(8,128)(2,1)} %maximum_maximum_fusion.1), channel_id=1, source_target_pairs={{0,4},{4,0},{1,5},{5,1},{2,6},{6,2},{3,7},{7,3},{8,12},{12,8},{9,1... | collective-permute-start | bytes 1572872 | tf_op jit(solution)/shard_map/ppermute | solution.py:83
  17.2 25.1 %collective-permute-start.3 = (bf16[4,64,1024]{2,1,0:T(8,128)(2,1)S(1)}, bf16[4,64,1024]{2,1,0:T(8,128)(2,1)}, u32[]{:S(2)}, u32[]{:S(2)}) collective-permute-start(bf16[4,64,1024]{2,1,0:T(8,128)(2,1)S(1)} %get-tuple-element.126), channel_id=1, source_target_pairs={{0,2},{2,0},{1,3},{3,1},{4,6},{6,4},{5,7},{7,5},{8,10},{10,8},{9,1... | collective-permute-start | bytes 1572872 | tf_op jit(solution)/shard_map/ppermute | solution.py:83
  42.4 26.2 %collective-permute-start.6 = (bf16[512,1024]{0,1:T(8,128)(2,1)S(1)}, bf16[512,1024]{0,1:T(8,128)(2,1)}, u32[]{:S(2)}, u32[]{:S(2)}) collective-permute-start(bf16[512,1024]{0,1:T(8,128)(2,1)S(1)} %collective-permute-done.1), channel_id=1, source_target_pairs={{0,8},{8,16},{16,24},{24,0},{1,9},{9,17},{17,25},{25,1},{2,10},{10... | collective-permute-start | bytes 3145736 | tf_op jit(solution)/shard_map/ppermute | solution.py:80
  46.2 12.9 %collective-permute-start.7 = (bf16[256,1024]{0,1:T(8,128)(2,1)}, bf16[256,1024]{0,1:T(8,128)(2,1)S(1)}, u32[]{:S(2)}, u32[]{:S(2)}) collective-permute-start(bf16[256,1024]{0,1:T(8,128)(2,1)} %get-tuple-element.130), channel_id=1, source_target_pairs={{0,4},{4,0},{1,5},{5,1},{2,6},{6,2},{3,7},{7,3},{8,12},{12,8},{9,1... | collective-permute-start | bytes 1572872 | tf_op jit(solution)/shard_map/ppermute | solution.py:83
  47.7 25.2 %collective-permute-start.5 = (bf16[4,64,1024]{2,1,0:T(8,128)(2,1)}, bf16[4,64,1024]{2,1,0:T(8,128)(2,1)}, u32[]{:S(2)}, u32[]{:S(2)}) collective-permute-start(bf16[4,64,1024]{2,1,0:T(8,128)(2,1)} %bitcast.18), channel_id=1, source_target_pairs={{0,2},{2,0},{1,3},{3,1},{4,6},{6,4},{5,7},{7,5},{8,10},{10,8},{9,1... | collective-permute-start | bytes 1572872 | tf_op jit(solution)/shard_map/ppermute | solution.py:83
  48.2 24.6 %collective-permute-start.8 = (bf16[256,1024]{0,1:T(8,128)(2,1)}, bf16[256,1024]{0,1:T(8,128)(2,1)}, u32[]{:S(2)}, u32[]{:S(2)}) collective-permute-start(bf16[256,1024]{0,1:T(8,128)(2,1)} %pad_maximum_fusion.32), channel_id=1, source_target_pairs={{0,2},{2,0},{1,3},{3,1},{4,6},{6,4},{5,7},{7,5},{8,10},{10,8},{9,1... | collective-permute-start | bytes 1572872 | tf_op jit(solution)/shard_map/ppermute | solution.py:83
  72.9 25.5 %collective-permute-start.10 = (bf16[512,1024]{0,1:T(8,128)(2,1)}, bf16[512,1024]{0,1:T(8,128)(2,1)}, u32[]{:S(2)}, u32[]{:S(2)}) collective-permute-start(bf16[512,1024]{0,1:T(8,128)(2,1)} %collective-permute-done.6), channel_id=1, source_target_pairs={{0,8},{8,16},{16,24},{24,0},{1,9},{9,17},{17,25},{25,1},{2,10},{10... | collective-permute-start | bytes 3145736 | tf_op jit(solution)/shard_map/ppermute | solution.py:80
  73.8 16.3 %collective-permute-start.11 = (bf16[256,1024]{0,1:T(8,128)(2,1)}, bf16[256,1024]{0,1:T(8,128)(2,1)}, u32[]{:S(2)}, u32[]{:S(2)}) collective-permute-start(bf16[256,1024]{0,1:T(8,128)(2,1)} %get-tuple-element.134), channel_id=1, source_target_pairs={{0,4},{4,0},{1,5},{5,1},{2,6},{6,2},{3,7},{7,3},{8,12},{12,8},{9,1... | collective-permute-start | bytes 1572872 | tf_op jit(solution)/shard_map/ppermute | solution.py:83
  75.1 16.1 %collective-permute-start.9 = (bf16[4,64,1024]{2,1,0:T(8,128)(2,1)}, bf16[4,64,1024]{2,1,0:T(8,128)(2,1)}, u32[]{:S(2)}, u32[]{:S(2)}) collective-permute-start(bf16[4,64,1024]{2,1,0:T(8,128)(2,1)} %bitcast.697), channel_id=1, source_target_pairs={{0,2},{2,0},{1,3},{3,1},{4,6},{6,4},{5,7},{7,5},{8,10},{10,8},{9,1... | collective-permute-start | bytes 1572872 | tf_op jit(solution)/shard_map/ppermute | solution.py:83
  84.9 20.0 %collective-permute-start.13 = (bf16[256,1024]{0,1:T(8,128)(2,1)}, bf16[256,1024]{0,1:T(8,128)(2,1)}, u32[]{:S(2)}, u32[]{:S(2)}) collective-permute-start(bf16[256,1024]{0,1:T(8,128)(2,1)} %pad_maximum_fusion.33), channel_id=1, source_target_pairs={{0,2},{2,0},{1,3},{3,1},{4,6},{6,4},{5,7},{7,5},{8,10},{10,8},{9,1... | collective-permute-start | bytes 1572872 | tf_op jit(solution)/shard_map/ppermute | solution.py:83
  105.0 23.8 %collective-permute-start.16 = (bf16[256,1024]{0,1:T(8,128)(2,1)S(1)}, bf16[256,1024]{0,1:T(8,128)(2,1)S(1)}, u32[]{:S(2)}, u32[]{:S(2)}) collective-permute-start(bf16[256,1024]{0,1:T(8,128)(2,1)S(1)} %copy-done.158), channel_id=1, source_target_pairs={{0,4},{4,0},{1,5},{5,1},{2,6},{6,2},{3,7},{7,3},{8,12},{12,8},{9,1... | collective-permute-start | bytes 1572872 | tf_op jit(solution)/shard_map/ppermute | solution.py:83
  106.0 14.9 %collective-permute-start.14 = (bf16[4,64,1024]{2,1,0:T(8,128)(2,1)S(1)}, bf16[4,64,1024]{2,1,0:T(8,128)(2,1)S(1)}, u32[]{:S(2)}, u32[]{:S(2)}) collective-permute-start(bf16[4,64,1024]{2,1,0:T(8,128)(2,1)S(1)} %bitcast.699), channel_id=1, source_target_pairs={{0,2},{2,0},{1,3},{3,1},{4,6},{6,4},{5,7},{7,5},{8,10},{10,8},{9,1... | collective-permute-start | bytes 1572872 | tf_op jit(solution)/shard_map/ppermute | solution.py:83
  108.4 20.3 %collective-permute-start.17 = (s32[8,128]{1,0:T(8,128)S(1)}, s32[8,128]{1,0:T(8,128)S(1)}, u32[]{:S(2)}, u32[]{:S(2)}) collective-permute-start(s32[8,128]{1,0:T(8,128)S(1)} %broadcast_in_dim.260), channel_id=1, source_target_pairs={{0,8},{8,16},{16,24},{24,0},{1,9},{9,17},{17,25},{25,1},{2,10},{10... | collective-permute-start | bytes 12296 | tf_op jit(solution)/shard_map/ppermute | solution.py:80
  108.4 21.4 %collective-permute-start.18 = (bf16[256,1024]{0,1:T(8,128)(2,1)S(1)}, bf16[256,1024]{0,1:T(8,128)(2,1)S(1)}, u32[]{:S(2)}, u32[]{:S(2)}) collective-permute-start(bf16[256,1024]{0,1:T(8,128)(2,1)S(1)} %copy-done.153), channel_id=1, source_target_pairs={{0,8},{8,16},{16,24},{24,0},{1,9},{9,17},{17,25},{25,1},{2,10},{10... | collective-permute-start | bytes 1572872 | tf_op jit(solution)/shard_map/ppermute | solution.py:80
  108.4 21.4 %collective-permute-start.19 = (bf16[256,1024]{0,1:T(8,128)(2,1)S(1)}, bf16[256,1024]{0,1:T(8,128)(2,1)S(1)}, u32[]{:S(2)}, u32[]{:S(2)}) collective-permute-start(bf16[256,1024]{0,1:T(8,128)(2,1)S(1)} %pad_maximum_fusion.34), channel_id=1, source_target_pairs={{0,2},{2,0},{1,3},{3,1},{4,6},{6,4},{5,7},{7,5},{8,10},{10,8},{9,1... | collective-permute-start | bytes 1572872 | tf_op jit(solution)/shard_map/ppermute | solution.py:83
  129.8 16.6 %collective-permute-start.20 = (bf16[256,1024]{0,1:T(8,128)(2,1)S(1)}, bf16[256,1024]{0,1:T(8,128)(2,1)}, u32[]{:S(2)}, u32[]{:S(2)}) collective-permute-start(bf16[256,1024]{0,1:T(8,128)(2,1)S(1)} %collective-permute-done.18), channel_id=1, source_target_pairs={{0,8},{8,16},{16,24},{24,0},{1,9},{9,17},{17,25},{25,1},{2,10},{10... | collective-permute-start | bytes 1572872 | tf_op jit(solution)/shard_map/ppermute | solution.py:80
  130.1 16.3 %collective-permute-start.22 = (bf16[256,1024]{0,1:T(8,128)(2,1)S(1)}, bf16[256,1024]{0,1:T(8,128)(2,1)S(1)}, u32[]{:S(2)}, u32[]{:S(2)}) collective-permute-start(bf16[256,1024]{0,1:T(8,128)(2,1)S(1)} %pad_maximum_fusion.36), channel_id=1, source_target_pairs={{0,2},{2,0},{1,3},{3,1},{4,6},{6,4},{5,7},{7,5},{8,10},{10,8},{9,1... | collective-permute-start | bytes 1572872 | tf_op jit(solution)/shard_map/ppermute | solution.py:83
  131.7 10.6 %collective-permute-start.23 = (s32[8,128]{1,0:T(8,128)S(1)}, s32[8,128]{1,0:T(8,128)S(1)}, u32[]{:S(2)}, u32[]{:S(2)}) collective-permute-start(s32[8,128]{1,0:T(8,128)S(1)} %broadcast_add_fusion.1), channel_id=1, source_target_pairs={{0,16},{8,24},{16,0},{24,8},{1,17},{9,25},{17,1},{25,9},{2,18},{10... | collective-permute-start | bytes 12296 | tf_op jit(solution)/shard_map/ppermute | solution.py:80
  146.5 24.7 %collective-permute-start.24 = (bf16[512,1024]{1,0:T(8,128)(2,1)S(1)}, bf16[512,1024]{1,0:T(8,128)(2,1)S(1)}, u32[]{:S(2)}, u32[]{:S(2)}) collective-permute-start(bf16[512,1024]{1,0:T(8,128)(2,1)S(1)} %fusion.54), channel_id=1, source_target_pairs={{0,4},{4,0},{1,5},{5,1},{2,6},{6,2},{3,7},{7,3},{8,12},{12,8},{9,1... | collective-permute-start | bytes 3145736 | tf_op jit(solution)/shard_map/ppermute | solution.py:83
  201.1 62.9 %collective-permute-start.26 = (bf16[1024,1024]{0,1:T(8,128)(2,1)S(1)}, bf16[1024,1024]{0,1:T(8,128)(2,1)S(1)}, u32[]{:S(2)}, u32[]{:S(2)}) collective-permute-start(bf16[1024,1024]{0,1:T(8,128)(2,1)S(1)} %copy-done.140), channel_id=1, source_target_pairs={{0,2},{2,0},{1,3},{3,1},{4,6},{6,4},{5,7},{7,5},{8,10},{10,8},{9,1... | collective-permute-start | bytes 6291464 | tf_op jit(solution)/shard_map/ppermute | solution.py:83
  208.3 26.6 %collective-permute-start.27 = (bf16[256,1024]{0,1:T(8,128)(2,1)}, bf16[256,1024]{0,1:T(8,128)(2,1)}, u32[]{:S(2)}, u32[]{:S(2)}) collective-permute-start(bf16[256,1024]{0,1:T(8,128)(2,1)} %collective-permute-done.20), channel_id=1, source_target_pairs={{0,8},{8,16},{16,24},{24,0},{1,9},{9,17},{17,25},{25,1},{2,10},{10... | collective-permute-start | bytes 1572872 | tf_op jit(solution)/shard_map/ppermute | solution.py:80
  278.8 25.7 %collective-permute-start.30 = (bf16[512,1024]{0,1:T(8,128)(2,1)S(1)}, bf16[512,1024]{0,1:T(8,128)(2,1)}, u32[]{:S(2)}, u32[]{:S(2)}) collective-permute-start(bf16[512,1024]{0,1:T(8,128)(2,1)S(1)} %pad_maximum_fusion.16), channel_id=1, source_target_pairs={{0,4},{4,0},{1,5},{5,1},{2,6},{6,2},{3,7},{7,3},{8,12},{12,8},{9,1... | collective-permute-start | bytes 3145736 | tf_op jit(solution)/shard_map/ppermute | solution.py:83
  280.3 25.3 %collective-permute-start.31 = (bf16[512,1024]{0,1:T(8,128)(2,1)S(1)}, bf16[512,1024]{0,1:T(8,128)(2,1)}, u32[]{:S(2)}, u32[]{:S(2)}) collective-permute-start(bf16[512,1024]{0,1:T(8,128)(2,1)S(1)} %pad_maximum_fusion.17), channel_id=1, source_target_pairs={{0,2},{2,0},{1,3},{3,1},{4,6},{6,4},{5,7},{7,5},{8,10},{10,8},{9,1... | collective-permute-start | bytes 3145736 | tf_op jit(solution)/shard_map/ppermute | solution.py:83
  309.3 48.3 %collective-permute-start.33 = (bf16[1024,1024]{0,1:T(8,128)(2,1)}, bf16[1024,1024]{0,1:T(8,128)(2,1)}, u32[]{:S(2)}, u32[]{:S(2)}) collective-permute-start(bf16[1024,1024]{0,1:T(8,128)(2,1)} %constant_dynamic-update-slice_fusion.15), channel_id=1, source_target_pairs={{0,2},{2,0},{1,3},{3,1},{4,6},{6,4},{5,7},{7,5},{8,10},{10,8},{9,1... | collective-permute-start | bytes 6291464 | tf_op jit(solution)/shard_map/ppermute | solution.py:83
  312.7 48.1 %collective-permute-start.34 = (bf16[1024,1024]{0,1:T(8,128)(2,1)}, bf16[1024,1024]{0,1:T(8,128)(2,1)}, u32[]{:S(2)}, u32[]{:S(2)}) collective-permute-start(bf16[1024,1024]{0,1:T(8,128)(2,1)} %pad_maximum_fusion.2), channel_id=1, source_target_pairs={{0,4},{4,0},{1,5},{5,1},{2,6},{6,2},{3,7},{7,3},{8,12},{12,8},{9,1... | collective-permute-start | bytes 6291464 | tf_op jit(solution)/shard_map/ppermute | solution.py:83
  494.0 20.6 %collective-permute-start.41 = (f32[512,1024]{1,0:T(8,128)}, f32[512,1024]{1,0:T(8,128)}, u32[]{:S(2)}, u32[]{:S(2)}) collective-permute-start(f32[512,1024]{1,0:T(8,128)} %dynamic-slice_bitcast_fusion.2), channel_id=1, source_target_pairs={{0,1},{1,0},{2,3},{3,2},{4,5},{5,4},{6,7},{7,6},{8,9},{9,8},{10,11... | collective-permute-start | bytes 6291464 | tf_op jit(solution)/shard_map/ppermute | solution.py:80
  506.5 48.0 %collective-permute-start.47 = (bf16[2,4,2,64,1024]{4,3,2,1,0:T(8,128)(2,1)}, bf16[2,4,2,64,1024]{4,3,2,1,0:T(8,128)(2,1)}, u32[]{:S(2)}, u32[]{:S(2)}) collective-permute-start(bf16[2,4,2,64,1024]{4,3,2,1,0:T(8,128)(2,1)} %fusion.45), channel_id=1, source_target_pairs={{0,4},{4,0},{1,5},{5,1},{2,6},{6,2},{3,7},{7,3},{8,12},{12,8},{9,1... | collective-permute-start | bytes 6291464 | tf_op jit(solution)/shard_map/ppermute | solution.py:83
  507.7 47.7 %collective-permute-start.48 = (bf16[2,2,4,64,1024]{4,3,0,1,2:T(8,128)(2,1)}, bf16[2,2,4,64,1024]{4,3,0,1,2:T(8,128)(2,1)}, u32[]{:S(2)}, u32[]{:S(2)}) collective-permute-start(bf16[2,2,4,64,1024]{4,3,0,1,2:T(8,128)(2,1)} %fusion.46), channel_id=1, source_target_pairs={{0,2},{2,0},{1,3},{3,1},{4,6},{6,4},{5,7},{7,5},{8,10},{10,8},{9,1... | collective-permute-start | bytes 6291464 | tf_op jit(solution)/shard_map/ppermute | solution.py:83
  521.3 10.3 %collective-permute-start.42 = (bf16[512,1024]{1,0:T(8,128)(2,1)S(1)}, bf16[512,1024]{1,0:T(8,128)(2,1)S(1)}, u32[]{:S(2)}, u32[]{:S(2)}) collective-permute-start(bf16[512,1024]{1,0:T(8,128)(2,1)S(1)} %get-tuple-element.367), channel_id=1, source_target_pairs={{0,1},{1,0},{2,3},{3,2},{4,5},{5,4},{6,7},{7,6},{8,9},{9,8},{10,11... | collective-permute-start | bytes 3145736 | tf_op jit(solution)/shard_map/ppermute | solution.py:80
  543.7 30.3 %collective-permute-start.43 = (f32[512,1024]{1,0:T(8,128)S(1)}, f32[512,1024]{1,0:T(8,128)S(1)}, u32[]{:S(2)}, u32[]{:S(2)}) collective-permute-start(f32[512,1024]{1,0:T(8,128)S(1)} %dynamic-slice_bitcast_fusion.1), channel_id=1, source_target_pairs={{0,1},{1,0},{2,3},{3,2},{4,5},{5,4},{6,7},{7,6},{8,9},{9,8},{10,11... | collective-permute-start | bytes 6291464 | tf_op jit(solution)/shard_map/ppermute | solution.py:80
  564.1 49.7 %collective-permute-start.49 = (bf16[1024,1024]{1,0:T(8,128)(2,1)}, bf16[1024,1024]{1,0:T(8,128)(2,1)}, u32[]{:S(2)}, u32[]{:S(2)}) collective-permute-start(bf16[1024,1024]{1,0:T(8,128)(2,1)} %convolution_convert_fusion), channel_id=1, source_target_pairs={{0,2},{2,0},{1,3},{3,1},{4,6},{6,4},{5,7},{7,5},{8,10},{10,8},{9,1... | collective-permute-start | bytes 6291464 | tf_op jit(solution)/shard_map/ppermute | solution.py:83
  565.6 48.3 %collective-permute-start.50 = (bf16[1024,1024]{1,0:T(8,128)(2,1)}, bf16[1024,1024]{1,0:T(8,128)(2,1)}, u32[]{:S(2)}, u32[]{:S(2)}) collective-permute-start(bf16[1024,1024]{1,0:T(8,128)(2,1)} %pad_maximum_fusion.4), channel_id=1, source_target_pairs={{0,4},{4,0},{1,5},{5,1},{2,6},{6,2},{3,7},{7,3},{8,12},{12,8},{9,1... | collective-permute-start | bytes 6291464 | tf_op jit(solution)/shard_map/ppermute | solution.py:83
  566.4 47.5 %collective-permute-start.51 = (bf16[512,1024]{1,0:T(8,128)(2,1)}, bf16[512,1024]{1,0:T(8,128)(2,1)}, u32[]{:S(2)}, u32[]{:S(2)}) collective-permute-start(bf16[512,1024]{1,0:T(8,128)(2,1)} %pad_maximum_fusion.20), channel_id=1, source_target_pairs={{0,8},{8,16},{16,24},{24,0},{1,9},{9,17},{17,25},{25,1},{2,10},{10... | collective-permute-start | bytes 3145736 | tf_op jit(solution)/shard_map/ppermute | solution.py:80
  613.3 25.1 %collective-permute-start.45 = (f32[512,1024]{1,0:T(8,128)S(1)}, f32[512,1024]{1,0:T(8,128)S(1)}, u32[]{:S(2)}, u32[]{:S(2)}) collective-permute-start(f32[512,1024]{1,0:T(8,128)S(1)} %dynamic-slice_bitcast_fusion), channel_id=1, source_target_pairs={{0,1},{1,0},{2,3},{3,2},{4,5},{5,4},{6,7},{7,6},{8,9},{9,8},{10,11... | collective-permute-start | bytes 6291464 | tf_op jit(solution)/shard_map/ppermute | solution.py:80
  627.1 26.3 %collective-permute-start.52 = (bf16[1024,512]{1,0:T(8,128)(2,1)}, bf16[1024,512]{1,0:T(8,128)(2,1)}, u32[]{:S(2)}, u32[]{:S(2)}) collective-permute-start(bf16[1024,512]{1,0:T(8,128)(2,1)} %pad_maximum_fusion.18), channel_id=1, source_target_pairs={{0,2},{2,0},{1,3},{3,1},{4,6},{6,4},{5,7},{7,5},{8,10},{10,8},{9,1... | collective-permute-start | bytes 3145736 | tf_op jit(solution)/shard_map/ppermute | solution.py:83
  627.6 26.3 %collective-permute-start.53 = (bf16[1024,512]{1,0:T(8,128)(2,1)}, bf16[1024,512]{1,0:T(8,128)(2,1)}, u32[]{:S(2)}, u32[]{:S(2)}) collective-permute-start(bf16[1024,512]{1,0:T(8,128)(2,1)} %pad_maximum_fusion.19), channel_id=1, source_target_pairs={{0,4},{4,0},{1,5},{5,1},{2,6},{6,2},{3,7},{7,3},{8,12},{12,8},{9,1... | collective-permute-start | bytes 3145736 | tf_op jit(solution)/shard_map/ppermute | solution.py:83
  628.9 46.8 %collective-permute-start.54 = (bf16[512,1024]{1,0:T(8,128)(2,1)}, bf16[512,1024]{1,0:T(8,128)(2,1)}, u32[]{:S(2)}, u32[]{:S(2)}) collective-permute-start(bf16[512,1024]{1,0:T(8,128)(2,1)} %slice.1401), channel_id=1, source_target_pairs={{0,4},{4,0},{1,5},{5,1},{2,6},{6,2},{3,7},{7,3},{8,12},{12,8},{9,1... | collective-permute-start | bytes 3145736 | tf_op jit(solution)/shard_map/ppermute | solution.py:83
  629.7 46.0 %collective-permute-start.55 = (bf16[512,1024]{1,0:T(8,128)(2,1)}, bf16[512,1024]{1,0:T(8,128)(2,1)}, u32[]{:S(2)}, u32[]{:S(2)}) collective-permute-start(bf16[512,1024]{1,0:T(8,128)(2,1)} %fusion.50), channel_id=1, source_target_pairs={{0,2},{2,0},{1,3},{3,1},{4,6},{6,4},{5,7},{7,5},{8,10},{10,8},{9,1... | collective-permute-start | bytes 3145736 | tf_op jit(solution)/shard_map/ppermute | solution.py:83
  638.4 37.3 %collective-permute-start.56 = (bf16[512,1024]{1,0:T(8,128)(2,1)}, bf16[512,1024]{1,0:T(8,128)(2,1)}, u32[]{:S(2)}, u32[]{:S(2)}) collective-permute-start(bf16[512,1024]{1,0:T(8,128)(2,1)} %pad_maximum_fusion.21), channel_id=1, source_target_pairs={{0,8},{8,16},{16,24},{24,0},{1,9},{9,17},{17,25},{25,1},{2,10},{10... | collective-permute-start | bytes 3145736 | tf_op jit(solution)/shard_map/ppermute | solution.py:80
  653.4 34.3 %collective-permute-start.46 = (f32[16,1024]{1,0:T(8,128)S(1)}, f32[16,1024]{1,0:T(8,128)S(1)}, u32[]{:S(2)}, u32[]{:S(2)}) collective-permute-start(f32[16,1024]{1,0:T(8,128)S(1)} %concatenate.185), channel_id=1, source_target_pairs={{0,1},{1,0},{2,3},{3,2},{4,5},{5,4},{6,7},{7,6},{8,9},{9,8},{10,11... | collective-permute-start | bytes 196616 | tf_op jit(solution)/shard_map/ppermute | solution.py:89
  687.7 39.0 %collective-permute-start.60 = (bf16[768,1024]{1,0:T(8,128)(2,1)S(1)}, bf16[768,1024]{1,0:T(8,128)(2,1)S(1)}, u32[]{:S(2)}, u32[]{:S(2)}) collective-permute-start(bf16[768,1024]{1,0:T(8,128)(2,1)S(1)} %pad_maximum_fusion.7), channel_id=1, source_target_pairs={{0,8},{8,16},{16,24},{24,0},{1,9},{9,17},{17,25},{25,1},{2,10},{10... | collective-permute-start | bytes 4718600 | tf_op jit(solution)/shard_map/ppermute | solution.py:80
  689.2 37.6 %collective-permute-start.58 = (bf16[1536,512]{1,0:T(8,128)(2,1)S(1)}, bf16[1536,512]{1,0:T(8,128)(2,1)S(1)}, u32[]{:S(2)}, u32[]{:S(2)}) collective-permute-start(bf16[1536,512]{1,0:T(8,128)(2,1)S(1)} %pad_maximum_fusion.5), channel_id=1, source_target_pairs={{0,2},{2,0},{1,3},{3,1},{4,6},{6,4},{5,7},{7,5},{8,10},{10,8},{9,1... | collective-permute-start | bytes 4718600 | tf_op jit(solution)/shard_map/ppermute | solution.py:83
  692.9 33.2 %collective-permute-start.57 = (f32[16,1024]{1,0:T(8,128)S(1)}, f32[16,1024]{1,0:T(8,128)S(1)}, u32[]{:S(2)}, u32[]{:S(2)}) collective-permute-start(f32[16,1024]{1,0:T(8,128)S(1)} %pad_add_fusion.1), channel_id=1, source_target_pairs={{0,2},{2,0},{1,3},{3,1},{4,6},{6,4},{5,7},{7,5},{8,10},{10,8},{9,1... | collective-permute-start | bytes 196616 | tf_op jit(solution)/shard_map/ppermute | solution.py:83
  693.5 38.2 %collective-permute-start.59 = (bf16[1536,512]{1,0:T(8,128)(2,1)S(1)}, bf16[1536,512]{1,0:T(8,128)(2,1)S(1)}, u32[]{:S(2)}, u32[]{:S(2)}) collective-permute-start(bf16[1536,512]{1,0:T(8,128)(2,1)S(1)} %pad_maximum_fusion.6), channel_id=1, source_target_pairs={{0,4},{4,0},{1,5},{5,1},{2,6},{6,2},{3,7},{7,3},{8,12},{12,8},{9,1... | collective-permute-start | bytes 4718600 | tf_op jit(solution)/shard_map/ppermute | solution.py:83
  695.0 55.0 %collective-permute-start.64 = (bf16[512,1024]{1,0:T(8,128)(2,1)}, bf16[512,1024]{1,0:T(8,128)(2,1)}, u32[]{:S(2)}, u32[]{:S(2)}) collective-permute-start(bf16[512,1024]{1,0:T(8,128)(2,1)} %get-tuple-element.353), channel_id=1, source_target_pairs={{0,1},{1,0},{2,3},{3,2},{4,5},{5,4},{6,7},{7,6},{8,9},{9,8},{10,11... | collective-permute-start | bytes 3145736 | tf_op jit(solution)/shard_map/ppermute | solution.py:80
  740.3 15.9 %collective-permute-start.63 = (bf16[512,512]{1,0:T(8,128)(2,1)}, bf16[512,512]{1,0:T(8,128)(2,1)}, u32[]{:S(2)}, u32[]{:S(2)}) collective-permute-start(bf16[512,512]{1,0:T(8,128)(2,1)} %get-tuple-element.211), channel_id=1, source_target_pairs={{0,2},{2,0},{1,3},{3,1},{4,6},{6,4},{5,7},{7,5},{8,10},{10,8},{9,1... | collective-permute-start | bytes 1572872 | tf_op jit(solution)/shard_map/ppermute | solution.py:83
  749.1 15.4 %collective-permute-start.62 = (bf16[512,512]{1,0:T(8,128)(2,1)}, bf16[512,512]{1,0:T(8,128)(2,1)S(1)}, u32[]{:S(2)}, u32[]{:S(2)}) collective-permute-start(bf16[512,512]{1,0:T(8,128)(2,1)} %slice.1405), channel_id=1, source_target_pairs={{0,4},{4,0},{1,5},{5,1},{2,6},{6,2},{3,7},{7,3},{8,12},{12,8},{9,1... | collective-permute-start | bytes 1572872 | tf_op jit(solution)/shard_map/ppermute | solution.py:83
  752.3 28.4 %collective-permute-start.67 = (bf16[640,1024]{1,0:T(8,128)(2,1)}, bf16[640,1024]{1,0:T(8,128)(2,1)S(1)}, u32[]{:S(2)}, u32[]{:S(2)}) collective-permute-start(bf16[640,1024]{1,0:T(8,128)(2,1)} %get-tuple-element.213), channel_id=1, source_target_pairs={{0,2},{2,0},{1,3},{3,1},{4,6},{6,4},{5,7},{7,5},{8,10},{10,8},{9,1... | collective-permute-start | bytes 3932168 | tf_op jit(solution)/shard_map/ppermute | solution.py:83
  752.9 36.6 %collective-permute-start.65 = (bf16[640,1024]{1,0:T(8,128)(2,1)S(1)}, bf16[640,1024]{1,0:T(8,128)(2,1)S(1)}, u32[]{:S(2)}, u32[]{:S(2)}) collective-permute-start(bf16[640,1024]{1,0:T(8,128)(2,1)S(1)} %copy-done.120), channel_id=1, source_target_pairs={{0,4},{4,0},{1,5},{5,1},{2,6},{6,2},{3,7},{7,3},{8,12},{12,8},{9,1... | collective-permute-start | bytes 3932168 | tf_op jit(solution)/shard_map/ppermute | solution.py:83
  754.3 18.5 %collective-permute-start.69 = (bf16[384,1024]{1,0:T(8,128)(2,1)S(1)}, bf16[384,1024]{1,0:T(8,128)(2,1)S(1)}, u32[]{:S(2)}, u32[]{:S(2)}) collective-permute-start(bf16[384,1024]{1,0:T(8,128)(2,1)S(1)} %pad_maximum_fusion.24), channel_id=1, source_target_pairs={{0,8},{8,16},{16,24},{24,0},{1,9},{9,17},{17,25},{25,1},{2,10},{10... | collective-permute-start | bytes 2359304 | tf_op jit(solution)/shard_map/ppermute | solution.py:80
  808.9 40.1 %collective-permute-start.76 = (bf16[2,4,64,1024]{3,2,0,1:T(8,128)(2,1)S(1)}, bf16[2,4,64,1024]{3,2,0,1:T(8,128)(2,1)S(1)}, u32[]{:S(2)}, u32[]{:S(2)}) collective-permute-start(bf16[2,4,64,1024]{3,2,0,1:T(8,128)(2,1)S(1)} %fusion.97), channel_id=1, source_target_pairs={{0,2},{2,0},{1,3},{3,1},{4,6},{6,4},{5,7},{7,5},{8,10},{10,8},{9,1... | collective-permute-start | bytes 3145736 | tf_op jit(solution)/shard_map/ppermute | solution.py:83
  809.5 38.5 %collective-permute-start.78 = (bf16[384,1024]{1,0:T(8,128)(2,1)S(1)}, bf16[384,1024]{1,0:T(8,128)(2,1)S(1)}, u32[]{:S(2)}, u32[]{:S(2)}) collective-permute-start(bf16[384,1024]{1,0:T(8,128)(2,1)S(1)} %pad_maximum_fusion.25), channel_id=1, source_target_pairs={{0,8},{8,16},{16,24},{24,0},{1,9},{9,17},{17,25},{25,1},{2,10},{10... | collective-permute-start | bytes 2359304 | tf_op jit(solution)/shard_map/ppermute | solution.py:80
  810.1 27.4 %collective-permute-start.73 = (bf16[128,1024]{1,0:T(8,128)(2,1)S(1)}, bf16[128,1024]{1,0:T(8,128)(2,1)S(1)}, u32[]{:S(2)}, u32[]{:S(2)}) collective-permute-start(bf16[128,1024]{1,0:T(8,128)(2,1)S(1)} %get-tuple-element.218), channel_id=1, source_target_pairs={{0,8},{8,16},{16,24},{24,0},{1,9},{9,17},{17,25},{25,1},{2,10},{10... | collective-permute-start | bytes 786440 | tf_op jit(solution)/shard_map/ppermute | solution.py:80
  811.6 35.6 %collective-permute-start.74 = (bf16[128,1024]{1,0:T(8,128)(2,1)S(1)}, bf16[128,1024]{1,0:T(8,128)(2,1)S(1)}, u32[]{:S(2)}, u32[]{:S(2)}) collective-permute-start(bf16[128,1024]{1,0:T(8,128)(2,1)S(1)} %get-tuple-element.219), channel_id=1, source_target_pairs={{0,16},{8,24},{16,0},{24,8},{1,17},{9,25},{17,1},{25,9},{2,18},{10... | collective-permute-start | bytes 786440 | tf_op jit(solution)/shard_map/ppermute | solution.py:80
  813.9 33.2 %collective-permute-start.75 = (bf16[128,1024]{1,0:T(8,128)(2,1)S(1)}, bf16[128,1024]{1,0:T(8,128)(2,1)S(1)}, u32[]{:S(2)}, u32[]{:S(2)}) collective-permute-start(bf16[128,1024]{1,0:T(8,128)(2,1)S(1)} %get-tuple-element.220), channel_id=1, source_target_pairs={{0,24},{8,0},{16,8},{24,16},{1,25},{9,1},{17,9},{25,17},{2,26},{10... | collective-permute-start | bytes 786440 | tf_op jit(solution)/shard_map/ppermute | solution.py:80
  837.6 21.8 %collective-permute-start.77 = (bf16[2,4,64,1024]{3,2,0,1:T(8,128)(2,1)S(1)}, bf16[2,4,64,1024]{3,2,0,1:T(8,128)(2,1)S(1)}, u32[]{:S(2)}, u32[]{:S(2)}) collective-permute-start(bf16[2,4,64,1024]{3,2,0,1:T(8,128)(2,1)S(1)} %fusion.98), channel_id=1, source_target_pairs={{0,4},{4,0},{1,5},{5,1},{2,6},{6,2},{3,7},{7,3},{8,12},{12,8},{9,1... | collective-permute-start | bytes 3145736 | tf_op jit(solution)/shard_map/ppermute | solution.py:83
  863.7 11.0 %collective-permute-start.79 = (bf16[128,1024]{1,0:T(8,128)(2,1)}, bf16[128,1024]{1,0:T(8,128)(2,1)S(1)}, u32[]{:S(2)}, u32[]{:S(2)}) collective-permute-start(bf16[128,1024]{1,0:T(8,128)(2,1)} %get-tuple-element.224), channel_id=1, source_target_pairs={{0,8},{8,16},{16,24},{24,0},{1,9},{9,17},{17,25},{25,1},{2,10},{10... | collective-permute-start | bytes 786440 | tf_op jit(solution)/shard_map/ppermute | solution.py:80
  869.7 31.9 %collective-permute-start.85 = (bf16[256,1024]{1,0:T(8,128)(2,1)}, bf16[256,1024]{1,0:T(8,128)(2,1)}, u32[]{:S(2)}, u32[]{:S(2)}) collective-permute-start(bf16[256,1024]{1,0:T(8,128)(2,1)} %pad_maximum_fusion.37), channel_id=1, source_target_pairs={{0,8},{8,16},{16,24},{24,0},{1,9},{9,17},{17,25},{25,1},{2,10},{10... | collective-permute-start | bytes 1572872 | tf_op jit(solution)/shard_map/ppermute | solution.py:80
  872.2 34.0 %collective-permute-start.86 = (bf16[256,1024]{1,0:T(8,128)(2,1)}, bf16[256,1024]{1,0:T(8,128)(2,1)}, u32[]{:S(2)}, u32[]{:S(2)}) collective-permute-start(bf16[256,1024]{1,0:T(8,128)(2,1)} %pad_maximum_fusion.38), channel_id=1, source_target_pairs={{0,16},{8,24},{16,0},{24,8},{1,17},{9,25},{17,1},{25,9},{2,18},{10... | collective-permute-start | bytes 1572872 | tf_op jit(solution)/shard_map/ppermute | solution.py:80
  872.3 35.0 %collective-permute-start.87 = (bf16[256,1024]{1,0:T(8,128)(2,1)}, bf16[256,1024]{1,0:T(8,128)(2,1)}, u32[]{:S(2)}, u32[]{:S(2)}) collective-permute-start(bf16[256,1024]{1,0:T(8,128)(2,1)} %pad_maximum_fusion.39), channel_id=1, source_target_pairs={{0,24},{8,0},{16,8},{24,16},{1,25},{9,1},{17,9},{25,17},{2,26},{10... | collective-permute-start | bytes 1572872 | tf_op jit(solution)/shard_map/ppermute | solution.py:80
  887.4 23.5 %collective-permute-start.83 = (f32[12,32,128]{2,1,0:T(8,128)}, f32[12,32,128]{2,1,0:T(8,128)}, u32[]{:S(2)}, u32[]{:S(2)}) collective-permute-start(f32[12,32,128]{2,1,0:T(8,128)} %add.1225), channel_id=1, source_target_pairs={{0,8},{8,0},{16,24},{24,16},{1,9},{9,1},{17,25},{25,17},{2,10},{10... | collective-permute-start | bytes 589832 | tf_op jit(solution)/shard_map/ppermute | solution.py:89
  912.0 18.2 %collective-permute-start.84 = (f32[12,32,128]{2,1,0:T(8,128)S(1)}, f32[12,32,128]{2,1,0:T(8,128)S(1)}, u32[]{:S(2)}, u32[]{:S(2)}) collective-permute-start(f32[12,32,128]{2,1,0:T(8,128)S(1)} %add.1226), channel_id=1, source_target_pairs={{0,16},{8,24},{16,0},{24,8},{1,17},{9,25},{17,1},{25,9},{2,18},{10... | collective-permute-start | bytes 589832 | tf_op jit(solution)/shard_map/ppermute | solution.py:89
  (251 other events, 2287.8 us)
Sparse Core Ops, SparseCore 0:
  171.3 131.5 all-gather.2
